TPU v7x, 32 devices: a whole 2x2x4 slice. The times are simulated.
32 devices in a mesh: var: 4 (over y, core), patch: 8 (over z, x).
Axes of the slice: x: 2, y: 2, z: 4, core: 2. Of those that a mesh axis runs over, the one named last changes fastest.
Arguments:
- pixels: bfloat16 [2, 4, 8, 128, 192], P(None, None, 'patch', None, 'var'), may hold values from -6 to 6
- targets: bfloat16 [2, 4, 8, 128, 192], P(None, 'var', 'patch'), may hold values from -6 to 6
- masks: int32 [2, 4, 8, 128, 4], P(None, 'var', 'patch'), may hold values from 0 to 1
- lengths: int32 [2, 4, 8], P(None, 'var', 'patch'), may hold values from 32 to 128, as said below
- groups: int32 [2, 4, 8], P(None, 'var', 'patch'), may hold values from 0 to 4
- latitudes: int32 [2, 4, 8, 128], P(None, 'var', 'patch'), may hold values from 0 to 63
- step_count: int32 [1], replicated, may hold values from 1 to 20
- square_master: float32 [8, 1024, 1024], P(None, 'var', 'patch')
- square_first: float32 [8, 1024, 1024], P(None, 'var', 'patch'), may hold values from -1.5258789e-05 to 1.5258789e-05
- square_second: float32 [8, 1024, 1024], P(None, 'var', 'patch'), as said below
- dense_master: float32 [2, 1024, 4096], P(None, 'var', 'patch'), may hold values from -0.1875 to 0.1875
- dense_first: float32 [2, 1024, 4096], P(None, 'var', 'patch'), may hold values from -1.5258789e-05 to 1.5258789e-05
- dense_second: float32 [2, 1024, 4096], P(None, 'var', 'patch'), as said below
- head_master: float32 [1024, 192], P('var', 'patch'), may hold values from -0.1875 to 0.1875
- head_first: float32 [1024, 192], P('var', 'patch'), may hold values from -1.5258789e-05 to 1.5258789e-05
- head_second: float32 [1024, 192], P('var', 'patch'), as said below
- table_master: float32 [376, 1024], P('var', 'patch')
- table_first: float32 [376, 1024], P('var', 'patch'), may hold values from -1.5258789e-05 to 1.5258789e-05
- table_second: float32 [376, 1024], P('var', 'patch'), as said below
Outputs:
- loss: float32 [], replicated
- grad_norm: float32 [], replicated
- square_new: float32 [8, 1024, 1024], P(None, 'var', 'patch')
- square_first_new: float32 [8, 1024, 1024], P(None, 'var', 'patch')
- square_second_new: float32 [8, 1024, 1024], P(None, 'var', 'patch')
- square_copy: bfloat16 [8, 1024, 1024], P(None, 'var', 'patch')
- dense_new: float32 [2, 1024, 4096], P(None, 'var', 'patch')
- dense_first_new: float32 [2, 1024, 4096], P(None, 'var', 'patch')
- dense_second_new: float32 [2, 1024, 4096], P(None, 'var', 'patch')
- dense_copy: bfloat16 [2, 1024, 4096], P(None, 'var', 'patch')
- head_new: float32 [1024, 192], P('var', 'patch')
- head_first_new: float32 [1024, 192], P('var', 'patch')
- head_second_new: float32 [1024, 192], P('var', 'patch')
- head_copy: bfloat16 [1024, 192], P('var', 'patch')
- table_new: float32 [376, 1024], P('var', 'patch')
- table_first_new: float32 [376, 1024], P('var', 'patch')
- table_second_new: float32 [376, 1024], P('var', 'patch')
- table_copy: bfloat16 [376, 1024], P('var', 'patch')
Inputs may be any that keep to these rules, and one draw needn't show every extreme that they name: `lengths`: each item's number of used patch slots; some item has 128. `square_second`: positive. `dense_second`: positive. `head_second`: positive. `table_second`: positive.
All inputs are finite; a program needn't handle non-finite values.
Results may differ from a plain program's by a relative error of at most 0.011.
Values may be sent and summed in bfloat16 or wider, within the bound.
No kernel may reach another device: no remote copies, remote signals or barrier semaphores. Data moves between devices by JAX's collectives and lax.ppermute only.
A program may use at most 384 MiB of HBM per device.

v0:
```python
import math

import jax
import jax.numpy as jnp
from jax import lax
from jax.sharding import PartitionSpec as P

HEADS = 16
V = 48
PATCH_PIXELS = 4
SOURCES = 5
LATS = 64


HIGH = lax.Precision.HIGHEST
CLIP_AT = 0.01
LEARN_RATE = 0.01
TABLE_RATE = 0.3
WEIGHT_DECAY = 0.1
FIRST_DECAY = 0.5
SECOND_DECAY = 0.5
EPSILON = 1e-08
NORM_EPSILON = 1e-05


def latitude_table():
    levels = jnp.arange(2 * LATS).astype(jnp.float32)
    cosine = jnp.cos(((levels + 0.5) / (2 * LATS) - 0.5) * math.pi)
    scaled = cosine / jnp.mean(cosine)
    index = 2 * jnp.arange(LATS)[:, None] + jnp.arange(PATCH_PIXELS)[None, :] // 2
    return scaled[index]


def layer_norm(value, gain):
    center = value - jnp.mean(value, axis=-1, keepdims=True)
    spread = jnp.mean(center * center, axis=-1, keepdims=True)
    return center * lax.rsqrt(spread + NORM_EPSILON) * gain


def exact_gelu(value):
    return jax.nn.gelu(value, approximate=False)


def unchanged(value):
    return value


def softmax_vars(scores):
    return jax.nn.softmax(scores, axis=-2)


def aggregate_parts(tokens, key_proj, value_proj, normalize):
    width = tokens.shape[-1]
    var_scores = jnp.einsum("...vd,dh->...vh", tokens, key_proj, preferred_element_type=jnp.float32)
    var_probs = normalize(var_scores)
    var_low = var_probs.astype(jnp.bfloat16)
    projected = jnp.einsum(
        "...vd,de->...ve", tokens, value_proj, preferred_element_type=jnp.float32
    ).astype(jnp.bfloat16)
    heads = projected.reshape(projected.shape[:-1] + (HEADS, width // HEADS))
    partial_value = jnp.einsum(
        "...vh,...vhe->...he", var_low, heads, preferred_element_type=jnp.float32
    )
    return (
        partial_value.reshape(partial_value.shape[:-2] + (width,)),
        (var_probs, var_low, projected),
    )


def aggregate_back(g_agg, tokens, kept_agg, key_proj, value_proj, complete):
    var_probs, var_low, projected = kept_agg
    width = tokens.shape[-1]
    g_heads = g_agg.reshape(g_agg.shape[:-1] + (HEADS, width // HEADS))
    heads = projected.reshape(projected.shape[:-1] + (HEADS, width // HEADS))
    d_probs = jnp.einsum("...he,...vhe->...vh", g_heads, heads, preferred_element_type=jnp.float32)
    g_proj = (
        (var_low.astype(jnp.float32)[..., None] * g_heads.astype(jnp.float32)[..., None, :, :])
        .astype(jnp.bfloat16)
        .reshape(projected.shape)
    )
    dots = complete(jnp.sum(var_probs * d_probs, axis=-2))
    g_var = (var_probs * (d_probs - dots[..., None, :])).astype(jnp.bfloat16)
    flat_tok = tokens.reshape(-1, width)
    d_value = jnp.einsum(
        "nd,ne->de", flat_tok, g_proj.reshape(-1, width), preferred_element_type=jnp.float32
    )
    d_keyvec = jnp.einsum(
        "nd,nh->dh", flat_tok, g_var.reshape(-1, HEADS), preferred_element_type=jnp.float32
    )
    g_tok = (
        jnp.einsum("...ve,de->...vd", g_proj, value_proj, preferred_element_type=jnp.float32)
        + jnp.einsum("...vh,dh->...vd", g_var, key_proj, preferred_element_type=jnp.float32)
    ).astype(jnp.bfloat16)
    return (d_value, d_keyvec, g_tok)


def block_scores(queries, keys, length, scale):
    cap = keys.shape[0]
    raw = jnp.einsum("qhe,khe->hqk", queries, keys, preferred_element_type=jnp.float32) * scale
    keymask = jnp.arange(cap) < length
    return jnp.where(keymask[None, None, :], raw, -1e30)


def forward_block(gathered, weights, length, source):
    square, dense, outhead, variable_table = weights
    cap, width = gathered.shape
    size = width // HEADS
    scale = size ** (-0.5)
    base = 5 * V + cap
    gain_one = variable_table[base + SOURCES + 1].astype(jnp.float32)
    gain_two = variable_table[base + SOURCES + 2].astype(jnp.float32)
    onehot = (source == jnp.arange(SOURCES)).astype(jnp.float32)
    src_rows = variable_table[base : base + SOURCES].astype(jnp.float32)
    start = (
        jnp.dot(gathered, square[3], preferred_element_type=jnp.float32)
        + jnp.dot(onehot, src_rows, precision=HIGH)[None, :]
    )
    normed_one = layer_norm(start, gain_one).astype(jnp.bfloat16)
    wqkv = jnp.concatenate([square[4], square[5], square[6]], axis=1)
    qkv = jnp.dot(normed_one, wqkv, preferred_element_type=jnp.float32).astype(jnp.bfloat16)
    queries = qkv[:, :width].reshape(cap, HEADS, size)
    keys = qkv[:, width : 2 * width].reshape(cap, HEADS, size)
    values = qkv[:, 2 * width :].reshape(cap, HEADS, size)
    scores = block_scores(queries, keys, length, scale)
    logsum = jax.nn.logsumexp(scores, axis=-1)
    probs = jnp.exp(scores - logsum[..., None]).astype(jnp.bfloat16)
    attended = (
        jnp.einsum("hqk,khe->qhe", probs, values, preferred_element_type=jnp.float32)
        .reshape(cap, width)
        .astype(jnp.bfloat16)
    )
    middle = start + jnp.dot(attended, square[7], preferred_element_type=jnp.float32)
    normed_two = layer_norm(middle, gain_two).astype(jnp.bfloat16)
    hidden = jnp.dot(normed_two, dense[0], preferred_element_type=jnp.float32)
    active = exact_gelu(hidden).astype(jnp.bfloat16)
    final = middle + jnp.einsum("cf,df->cd", active, dense[1], preferred_element_type=jnp.float32)
    final_low = final.astype(jnp.bfloat16)
    predict = jnp.dot(final_low, outhead, preferred_element_type=jnp.float32)
    kept = (
        gathered,
        onehot,
        start,
        normed_one,
        wqkv,
        queries,
        keys,
        values,
        logsum,
        attended,
        middle,
        normed_two,
        hidden,
        active,
        final_low,
        gain_one,
        gain_two,
    )
    return (predict, kept)


def backward_block(grad_pred, kept, weights, length):
    square, dense, outhead, variable_table = weights
    (
        gathered,
        onehot,
        start,
        normed_one,
        wqkv,
        queries,
        keys,
        values,
        logsum,
        attended,
        middle,
        normed_two,
        hidden,
        active,
        final_low,
        gain_one,
        gain_two,
    ) = kept
    cap, width = gathered.shape
    size = width // HEADS
    scale = size ** (-0.5)
    g_pred = grad_pred.astype(jnp.bfloat16)
    d_head = jnp.einsum("cd,co->do", final_low, g_pred, preferred_element_type=jnp.float32)
    d_final = jnp.einsum("co,do->cd", g_pred, outhead, preferred_element_type=jnp.float32)
    g_final = d_final.astype(jnp.bfloat16)
    d_down = jnp.einsum("cd,cf->df", g_final, active, preferred_element_type=jnp.float32)
    d_active = jnp.dot(g_final, dense[1], preferred_element_type=jnp.float32)
    _, gelu_back = jax.vjp(exact_gelu, hidden)
    g_hidden = gelu_back(d_active)[0].astype(jnp.bfloat16)
    d_up = jnp.einsum("cd,cf->df", normed_two, g_hidden, preferred_element_type=jnp.float32)
    d_normed_two = jnp.einsum("cf,df->cd", g_hidden, dense[0], preferred_element_type=jnp.float32)
    _, norm_two_back = jax.vjp(layer_norm, middle, gain_two)
    d_mid_norm, d_gain_two = norm_two_back(d_normed_two)
    d_middle = d_final + d_mid_norm
    g_middle = d_middle.astype(jnp.bfloat16)
    d_wout = jnp.einsum("cd,ce->de", attended, g_middle, preferred_element_type=jnp.float32)
    g_att = (
        jnp.einsum("ce,de->cd", g_middle, square[7], preferred_element_type=jnp.float32)
        .astype(jnp.bfloat16)
        .reshape(cap, HEADS, size)
    )
    scores = block_scores(queries, keys, length, scale)
    probs = jnp.exp(scores - logsum[..., None])
    probs_low = probs.astype(jnp.bfloat16)
    d_probs = jnp.einsum("qhe,khe->hqk", g_att, values, preferred_element_type=jnp.float32)
    d_values = jnp.einsum("hqk,qhe->khe", probs_low, g_att, preferred_element_type=jnp.float32)
    g_scores = (probs * (d_probs - jnp.sum(probs * d_probs, axis=-1, keepdims=True))).astype(
        jnp.bfloat16
    )
    d_queries = (
        jnp.einsum("hqk,khe->qhe", g_scores, keys, preferred_element_type=jnp.float32) * scale
    )
    d_keys = (
        jnp.einsum("hqk,qhe->khe", g_scores, queries, preferred_element_type=jnp.float32) * scale
    )
    g_qkv = jnp.concatenate(
        [d_queries.reshape(cap, width), d_keys.reshape(cap, width), d_values.reshape(cap, width)],
        axis=1,
    ).astype(jnp.bfloat16)
    d_wqkv = jnp.einsum("cd,ce->de", normed_one, g_qkv, preferred_element_type=jnp.float32)
    d_normed_one = jnp.einsum("ce,de->cd", g_qkv, wqkv, preferred_element_type=jnp.float32)
    _, norm_one_back = jax.vjp(layer_norm, start, gain_one)
    d_start_norm, d_gain_one = norm_one_back(d_normed_one)
    d_start = d_middle + d_start_norm
    d_source = onehot[:, None] * jnp.sum(d_start, axis=0)[None, :]
    g_start = d_start.astype(jnp.bfloat16)
    d_wagg = jnp.einsum("cd,ce->de", gathered, g_start, preferred_element_type=jnp.float32)
    g_agg = jnp.einsum("ce,de->cd", g_start, square[3], preferred_element_type=jnp.float32).astype(
        jnp.bfloat16
    )
    parts = (
        d_wagg,
        d_wqkv[:, :width],
        d_wqkv[:, width : 2 * width],
        d_wqkv[:, 2 * width :],
        d_wout,
        d_up,
        d_down,
        d_head,
        d_source,
        d_gain_one,
        d_gain_two,
    )
    return (parts, g_agg)


def reduce_grads(grads):
    by_var = (
        lax.psum_scatter(
            grads[0].astype(jnp.bfloat16), "var", scatter_dimension=1, tiled=True
        ).astype(jnp.float32),
        lax.psum_scatter(
            grads[1].astype(jnp.bfloat16), "var", scatter_dimension=1, tiled=True
        ).astype(jnp.float32),
        lax.psum_scatter(
            grads[2].astype(jnp.bfloat16), "var", scatter_dimension=0, tiled=True
        ).astype(jnp.float32),
        lax.psum_scatter(
            grads[3].astype(jnp.bfloat16), "var", scatter_dimension=0, tiled=True
        ).astype(jnp.float32),
    )
    return (
        lax.psum_scatter(by_var[0], "patch", scatter_dimension=2, tiled=True),
        lax.psum_scatter(by_var[1], "patch", scatter_dimension=2, tiled=True),
        lax.psum_scatter(by_var[2], "patch", scatter_dimension=1, tiled=True),
        lax.psum_scatter(by_var[3], "patch", scatter_dimension=1, tiled=True),
    )


def add_all(left, right):
    return tuple((a + b for a, b in zip(left, right)))


def adam_update(master, first, second, grad, factor, steps, rate):
    clipped = grad * factor
    new_first = FIRST_DECAY * first + (1.0 - FIRST_DECAY) * clipped
    new_second = SECOND_DECAY * second + (1.0 - SECOND_DECAY) * clipped * clipped
    first_hat = new_first / (1.0 - jnp.power(FIRST_DECAY, steps))
    second_hat = new_second / (1.0 - jnp.power(SECOND_DECAY, steps))
    new_master = master - rate * (
        first_hat / (jnp.sqrt(second_hat) + EPSILON) + WEIGHT_DECAY * master
    )
    return (new_master, new_first, new_second, new_master.astype(jnp.bfloat16))


def body(
    pixels,
    targets,
    masks,
    lengths,
    groups,
    latitudes,
    step_count,
    square_master,
    square_first,
    square_second,
    dense_master,
    dense_first,
    dense_second,
    head_master,
    head_first,
    head_second,
    table_master,
    table_first,
    table_second,
):
    partly = (
        lax.all_gather(square_master.astype(jnp.bfloat16), "patch", axis=2, tiled=True),
        lax.all_gather(dense_master.astype(jnp.bfloat16), "patch", axis=2, tiled=True),
        lax.all_gather(head_master.astype(jnp.bfloat16), "patch", axis=1, tiled=True),
        lax.all_gather(table_master.astype(jnp.bfloat16), "patch", axis=1, tiled=True),
    )
    weights = (
        lax.all_gather(partly[0], "var", axis=1, tiled=True),
        lax.all_gather(partly[1], "var", axis=1, tiled=True),
        lax.all_gather(partly[2], "var", axis=0, tiled=True),
        lax.all_gather(partly[3], "var", axis=0, tiled=True),
    )
    square, dense, outhead, variable_table = weights
    micro_count = pixels.shape[0]
    items = pixels.shape[1]
    cap = pixels.shape[3]
    width = variable_table.shape[1]
    variable_count = V
    size = width // HEADS
    scale = size ** (-0.5)
    variables_per_shard = pixels.shape[4] // PATCH_PIXELS
    variable_index = lax.axis_index("var")
    lat_table = latitude_table()
    slots = jnp.arange(cap)
    weighted = []
    local_count = jnp.zeros((), jnp.float32)
    for micro in range(micro_count):
        valid = (
            masks[micro, 0, 0].astype(jnp.float32)
            * (slots < lengths[micro, 0, 0]).astype(jnp.float32)[:, None]
        )
        lat_onehot = (latitudes[micro, 0, 0][:, None] == jnp.arange(LATS)[None, :]).astype(
            jnp.float32
        )
        wpix = jnp.dot(lat_onehot, lat_table, precision=HIGH) * valid
        weighted.append(jnp.tile(wpix, (1, variable_count)))
        local_count = local_count + jnp.sum(valid)
    count = lax.psum(local_count, ("var", "patch"))
    patch_token_rows = lax.dynamic_slice_in_dim(
        variable_table,
        variable_index * variables_per_shard * PATCH_PIXELS,
        variables_per_shard * PATCH_PIXELS,
        0,
    ).reshape(variables_per_shard, PATCH_PIXELS, width)
    variable_rows = lax.dynamic_slice_in_dim(
        variable_table,
        PATCH_PIXELS * variable_count + variable_index * variables_per_shard,
        variables_per_shard,
        0,
    ).astype(jnp.float32)
    pos_rows = variable_table[
        (PATCH_PIXELS + 1) * variable_count : (PATCH_PIXELS + 1) * variable_count + cap
    ].astype(jnp.float32)
    base = (PATCH_PIXELS + 1) * variable_count + cap
    query = variable_table[base + SOURCES]
    qvec = jnp.dot(query[None, :], square[0], preferred_element_type=jnp.float32)[0].astype(
        jnp.bfloat16
    )
    key_proj = (
        jnp.einsum(
            "dhe,he->dh",
            square[1].reshape(width, HEADS, size),
            qvec.reshape(HEADS, size),
            preferred_element_type=jnp.float32,
        )
        * scale
    ).astype(jnp.bfloat16)
    value_proj = square[2]
    key_wide = square[1].astype(jnp.float32).reshape(width, HEADS, size)
    query_wide = square[0].astype(jnp.float32)
    loss_local = jnp.zeros((), jnp.float32)
    totals = None
    shards = None
    for micro in range(micro_count):
        pix = pixels[micro, :, 0].reshape(items, cap, variables_per_shard, PATCH_PIXELS)
        emb = (
            jnp.einsum("acjk,jkd->acjd", pix, patch_token_rows, preferred_element_type=jnp.float32)
            + variable_rows[None, None]
            + pos_rows[None, :, None]
        )
        tok_local = emb.astype(jnp.bfloat16)
        tokens = lax.all_to_all(tok_local, "var", split_axis=0, concat_axis=2, tiled=True)[0]
        partial_value, kept_agg = aggregate_parts(tokens, key_proj, value_proj, softmax_vars)
        gathered = partial_value.astype(jnp.bfloat16)
        length = lengths[micro, 0, 0]
        predict, kept = forward_block(gathered, weights, length, groups[micro, 0, 0])
        diff = predict - targets[micro, 0, 0].astype(jnp.float32)
        loss_local = loss_local + jnp.sum(weighted[micro] * diff * diff)
        grad_pred = 2.0 * weighted[micro] * diff / count
        parts, g_agg = backward_block(grad_pred, kept, weights, length)
        d_value, d_keyvec, g_tokens = aggregate_back(
            g_agg, tokens, kept_agg, key_proj, value_proj, unchanged
        )
        back = lax.all_to_all(g_tokens[None], "var", split_axis=2, concat_axis=0, tiled=True)
        d_wagg, d_bq, d_bk, d_bv, d_wout, d_up, d_down, d_head, d_source, d_gain_one, d_gain_two = (
            parts
        )
        d_wkey = (
            jnp.einsum(
                "dh,he->dhe",
                d_keyvec,
                qvec.reshape(HEADS, size).astype(jnp.float32),
                precision=HIGH,
            )
            * scale
        ).reshape(width, width)
        g_qvec = (jnp.einsum("dhe,dh->he", key_wide, d_keyvec, precision=HIGH) * scale).reshape(
            width
        )
        d_wquery = jnp.einsum("d,e->de", query.astype(jnp.float32), g_qvec, precision=HIGH)
        d_query = jnp.dot(query_wide, g_qvec, precision=HIGH)
        patch_gradient = jnp.einsum(
            "acjk,acjd->jkd", pix, back, preferred_element_type=jnp.float32
        ).reshape(variables_per_shard * PATCH_PIXELS, width)
        variable_row_gradient = jnp.sum(back, axis=(0, 1), dtype=jnp.float32)
        d_pos = jnp.sum(back, axis=(0, 2), dtype=jnp.float32)
        table_gradient = jnp.concatenate(
            [
                jnp.zeros(((PATCH_PIXELS + 1) * variable_count, width), jnp.float32),
                d_pos,
                d_source,
                d_query[None],
                d_gain_one[None],
                d_gain_two[None],
            ],
            axis=0,
        )
        table_gradient = lax.dynamic_update_slice_in_dim(
            table_gradient, patch_gradient, variable_index * variables_per_shard * PATCH_PIXELS, 0
        )
        table_gradient = lax.dynamic_update_slice_in_dim(
            table_gradient,
            variable_row_gradient,
            PATCH_PIXELS * variable_count + variable_index * variables_per_shard,
            0,
        )
        d_square = jnp.stack([d_wquery, d_wkey, d_value, d_wagg, d_bq, d_bk, d_bv, d_wout])
        d_dense = jnp.stack([d_up, d_down])
        grads = (d_square, d_dense, d_head, table_gradient)
        totals = grads if totals is None else add_all(totals, grads)
    shards = reduce_grads(totals)
    sumsq_local = (
        jnp.sum(shards[0] * shards[0])
        + jnp.sum(shards[1] * shards[1])
        + jnp.sum(shards[2] * shards[2])
        + jnp.sum(shards[3] * shards[3])
    )
    loss_sum, sumsq = lax.psum((loss_local, sumsq_local), ("var", "patch"))
    loss = loss_sum / count
    norm = jnp.sqrt(sumsq)
    factor = jnp.minimum(1.0, CLIP_AT / norm)
    steps = step_count[0].astype(jnp.float32)
    sq = adam_update(
        square_master, square_first, square_second, shards[0], factor, steps, LEARN_RATE
    )
    de = adam_update(dense_master, dense_first, dense_second, shards[1], factor, steps, LEARN_RATE)
    hd = adam_update(head_master, head_first, head_second, shards[2], factor, steps, LEARN_RATE)
    tb = adam_update(table_master, table_first, table_second, shards[3], factor, steps, TABLE_RATE)
    return (
        loss,
        norm,
        sq[0],
        sq[1],
        sq[2],
        sq[3],
        de[0],
        de[1],
        de[2],
        de[3],
        hd[0],
        hd[1],
        hd[2],
        hd[3],
        tb[0],
        tb[1],
        tb[2],
        tb[3],
    )


def solution(mesh):
    in_specs = (
        P(None, None, "patch", None, "var"),
        P(None, "var", "patch", None, None),
        P(None, "var", "patch", None, None),
        P(None, "var", "patch"),
        P(None, "var", "patch"),
        P(None, "var", "patch", None),
        P(),
        P(None, "var", "patch"),
        P(None, "var", "patch"),
        P(None, "var", "patch"),
        P(None, "var", "patch"),
        P(None, "var", "patch"),
        P(None, "var", "patch"),
        P("var", "patch"),
        P("var", "patch"),
        P("var", "patch"),
        P("var", "patch"),
        P("var", "patch"),
        P("var", "patch"),
    )
    out_specs = (
        P(),
        P(),
        P(None, "var", "patch"),
        P(None, "var", "patch"),
        P(None, "var", "patch"),
        P(None, "var", "patch"),
        P(None, "var", "patch"),
        P(None, "var", "patch"),
        P(None, "var", "patch"),
        P(None, "var", "patch"),
        P("var", "patch"),
        P("var", "patch"),
        P("var", "patch"),
        P("var", "patch"),
        P("var", "patch"),
        P("var", "patch"),
        P("var", "patch"),
        P("var", "patch"),
    )
    return jax.shard_map(body, mesh=mesh, in_specs=in_specs, out_specs=out_specs, check_vma=False)
```

profile of v0, /device:TPU:0, one launch (start us, length us, event | category | flops | bytes accessed | tf_op | source)
XLA Modules:
  0.0 2270.5 jit_solution(6580005277038901042)
XLA Ops:
  10.4 78.0 %all-gather.6.cloned.1.call-done = bf16[8,256,1024]{2,1,0:T(8,128)(2,1)} async-done(((bf16[8,256,128]{2,1,0:T(8,128)(2,1)}), bf16[8,256,1024]{2,1,0:T(8,128)(2,1)}) %all-gather.6.cloned.1.call-update) | async-done | bytes 4194320 | tf_op jit(solution)/shard_map/all_gather | solution.py:311
  89.2 27.1 %all_gather.24 = bf16[94,1024]{1,0:T(8,128)(2,1)S(1)} all-gather(bf16[94,128]{1,0:T(8,128)(2,1)S(1)} %convert_element_type.371), channel_id=1, replica_groups=mesh['var'=4,'patch'=8] {'patch'}, dimensions={1}, use_global_device_ids=true | all-gather | bytes 216576 | tf_op jit(solution)/shard_map/all_gather | solution.py:314
  116.4 8.6 all-gather
  154.2 217.0 %all-to-all-done.1 = bf16[4,128,12,1024]{1,3,2,0:T(8,128)(2,1)} async-done(((bf16[4,128,12,1024]{1,3,2,0:T(8,128)(2,1)}), bf16[4,128,12,1024]{1,3,2,0:T(8,128)(2,1)}, u32[]{:S(2)}, u32[]{:S(2)}) %all-to-all-start.1) | async-done | bytes 12582944 | tf_op jit(solution)/shard_map/all_to_all | solution.py:391
  382.5 254.2 %psum.22 = f32[]{:T(128)} all-reduce(f32[]{:T(128)S(6)} %add.341), channel_id=1, replica_groups=mesh['var'=4,'patch'=8] {'var','patch'}, use_global_device_ids=true, to_apply=%region_22.23 | all-reduce | flops 1 | bytes 8 | tf_op jit(solution)/shard_map/psum | solution.py:347
  640.3 30.5 %all_gather.30 = bf16[256,192]{0,1:T(8,128)(2,1)S(1)} all-gather(bf16[256,24]{0,1:T(8,128)(2,1)S(1)} %convert_element_type.392), channel_id=1, replica_groups=mesh['var'=4,'patch'=8] {'patch'}, dimensions={1}, use_global_device_ids=true | all-gather | bytes 110592 | tf_op jit(solution)/shard_map/all_gather | solution.py:313
  682.2 16.5 copy.122
  698.8 16.6 copy.112
  729.3 21.2 convolution_convert_fusion
  750.5 16.6 copy.193
  767.1 21.7 convolution_convert_fusion.1
  788.8 16.8 copy.192
  831.0 8.1 multiply_reduce_fusion.3
  855.8 8.4 fusion.58
  880.7 9.1 fusion.57
  891.6 9.4 convolution_bitcast_fusion
  907.4 8.3 convolution_bitcast_fusion.1
  915.7 9.0 convolution_bitcast_fusion.2
  931.2 8.3 convolution_bitcast_fusion.3
  940.6 27.8 %fusion.1 = bf16[2,1024,4096]{2,1,0:T(8,128)(2,1)} fusion(f32[1,1024,4096]{2,1,0:T(8,128)} %convolution_bitcast_fusion.2, f32[1,1024,4096]{2,1,0:T(8,128)} %convolution_bitcast_fusion.3, f32[1,1024,4096]{2,1,0:T(8,128)} %convolution_bitcast_fusion, f32[1,1024,4096]{2,1,0:T(8,128)} %convolution_bitcast_fusion.1), kind=kLoop, calls=%fused_computation.2 | loop fusion | flops 33554432 | bytes 83886080 | tf_op jit(solution)/shard_map/convert_element_type | solution.py:256
  969.6 14.5 copy.137
  984.1 21.0 reshape_squeeze.19
  1005.1 14.4 copy.128
  1019.6 20.1 reshape_squeeze.18
  1074.9 10.6 multiply_reduce_fusion
  1092.7 10.2 multiply_reduce_fusion.1
  1133.0 9.3 multiply_convert_fusion
  1142.3 34.6 %copy.144 = bf16[128,48,16,64]{3,2,1,0:T(8,128)(2,1)} copy(bf16[128,48,16,64]{0,3,2,1:T(8,128)(2,1)} %multiply_convert_fusion) | data formatting | bytes 25165824 | tf_op jit(solution)/shard_map/convert_element_type | solution.py:78
  1176.9 33.7 %convert_element_type.439 = bf16[6144,1024]{1,0:T(8,128)(2,1)} reshape(bf16[128,48,16,64]{3,2,1,0:T(8,128)(2,1)} %copy.144) | data formatting | bytes 25165824 | tf_op jit(solution)/shard_map/convert_element_type | solution.py:78
  1210.6 8.2 multiply_convert_fusion.1
  1218.8 34.6 %copy.135 = bf16[128,48,16,64]{3,2,1,0:T(8,128)(2,1)} copy(bf16[128,48,16,64]{0,3,2,1:T(8,128)(2,1)} %multiply_convert_fusion.1) | data formatting | bytes 25165824 | tf_op jit(solution)/shard_map/convert_element_type | solution.py:78
  1253.5 33.4 %convert_element_type.426 = bf16[6144,1024]{1,0:T(8,128)(2,1)} reshape(bf16[128,48,16,64]{3,2,1,0:T(8,128)(2,1)} %copy.135) | data formatting | bytes 25165824 | tf_op jit(solution)/shard_map/convert_element_type | solution.py:78
  1305.4 17.5 bitcast_dynamic-update-slice_fusion.4
  1325.5 17.5 bitcast_dynamic-update-slice_fusion.7
  1369.0 27.6 %add_convert_fusion = bf16[8,1024,1024]{2,1,0:T(8,128)(2,1)} fusion(f32[8,1024,1024]{2,1,0:T(8,128)} %bitcast_dynamic-update-slice_fusion.5, f32[8,1024,1024]{2,1,0:T(8,128)} %bitcast_dynamic-update-slice_fusion.2), kind=kLoop, calls=%fused_computation.3 | loop fusion | flops 16777216 | bytes 83886080 | tf_op jit(solution)/shard_map/convert_element_type | solution.py:253
  1396.6 24.8 %fusion.40 = f32[128,48,1024]{2,0,1:T(8,128)} fusion(bf16[128,48,1024]{0,2,1:T(8,128)(2,1)} %bitcast.453, bf16[8,1024,1024]{2,1,0:T(8,128)(2,1)} %all-gather.8.cloned.1.call-done), kind=kOutput, calls=%fused_computation.119 | convolution fusion | flops 12884901888 | bytes 39845888 | tf_op jit(solution)/shard_map/...ve,de->...vd/dot_general | solution.py:91
  1421.4 14.8 fusion.5
  1443.0 21.9 fusion.41
  1464.9 14.5 fusion.4
  1479.4 177.1 %all-to-all-done.3 = bf16[1,128,48,1024]{3,1,0,2:T(8,128)(2,1)} async-done(((bf16[1,128,48,1024]{3,1,0,2:T(8,128)(2,1)}), bf16[1,128,48,1024]{3,1,0,2:T(8,128)(2,1)}, u32[]{:S(2)}, u32[]{:S(2)}) %all-to-all-start.3) | async-done | bytes 12582944 | tf_op jit(solution)/shard_map/all_to_all | solution.py:403
  1679.5 8.9 convert_reduce_fusion
  1688.4 112.6 %all-to-all-done.2 = bf16[1,128,48,1024]{3,1,0,2:T(8,128)(2,1)} async-done(((bf16[1,128,48,1024]{3,1,0,2:T(8,128)(2,1)}), bf16[1,128,48,1024]{3,1,0,2:T(8,128)(2,1)}, u32[]{:S(2)}, u32[]{:S(2)}) %all-to-all-start.2) | async-done | bytes 12582944 | tf_op jit(solution)/shard_map/all_to_all | solution.py:403
  1801.0 8.1 convert_reduce_fusion.2
  1822.7 12.4 fusion
  1856.1 47.3 %reduce-scatter.22.cloned.1.call-done = f32[94,128]{1,0:T(8,128)} async-done(((f32[94,1024]{1,0:T(8,128)}), f32[94,128]{1,0:T(8,128)}) %reduce-scatter.22.cloned.1.call-update) | async-done | bytes 48144 | tf_op jit(solution)/shard_map/reduce_scatter | solution.py:269
  1904.9 150.5 %reduce-scatter.16.cloned.1.call-done = f32[2,256,512]{2,1,0:T(8,128)} async-done(((f32[2,256,4096]{2,1,0:T(8,128)}), f32[2,256,512]{2,1,0:T(8,128)}) %reduce-scatter.16.cloned.1.call-update) | async-done | bytes 1048592 | tf_op jit(solution)/shard_map/reduce_scatter | solution.py:267
  2057.6 150.3 %reduce-scatter.12.cloned.1.call-done = f32[8,256,128]{2,1,0:T(8,128)} async-done(((f32[8,256,1024]{2,1,0:T(8,128)}), f32[8,256,128]{2,1,0:T(8,128)}) %reduce-scatter.12.cloned.1.call-update) | async-done | bytes 1048592 | tf_op jit(solution)/shard_map/reduce_scatter | solution.py:266
  2212.6 39.1 %all-reduce.2 = (f32[]{:T(128)}, f32[]{:T(128)}) all-reduce(f32[]{:T(128)S(6)} %add.340, f32[]{:T(128)S(6)} %add.354), channel_id=1, replica_groups=mesh['var'=4,'patch'=8] {'var','patch'}, use_global_device_ids=true, to_apply=%region_19.20 | all-reduce | flops 2 | bytes 16 | tf_op jit(solution)/shard_map/psum | solution.py:457
  (596 shorter events, 339.4 us)
Async XLA Ops:
  7.2 81.2 %all-gather.6.cloned.1.call-start = ((), (), s32[]{:S(2)}) async-start(), calls=%async_computation.11 | async-start | bytes 4718592 | tf_op jit(solution)/shard_map/all_gather | solution.py:311
  9.5 368.1 %all-gather.10.cloned.1.call-start = ((), (), s32[]{:S(2)}) async-start(), calls=%async_computation.13 | async-start | bytes 4718592 | tf_op jit(solution)/shard_map/all_gather | solution.py:312
  10.4 705.0 %all-gather.8.cloned.1.call-start = ((), (), s32[]{:S(2)}) async-start(), calls=%async_computation.12 | async-start | bytes 20971520 | tf_op jit(solution)/shard_map/all_gather | solution.py:317
  125.1 555.5 %copy-start.57 = (bf16[376,1024]{1,0:T(8,128)(2,1)}, bf16[376,1024]{1,0:T(8,128)(2,1)S(1)}, u32[]{:S(2)}) copy-start(bf16[376,1024]{1,0:T(8,128)(2,1)S(1)} %reshape.566) | copy-start | bytes 2310148
  136.9 234.3 %all-to-all-start.1 = ((bf16[4,128,12,1024]{1,3,2,0:T(8,128)(2,1)}), bf16[4,128,12,1024]{1,3,2,0:T(8,128)(2,1)}, u32[]{:S(2)}, u32[]{:S(2)}) async-start(bf16[4,128,12,1024]{1,3,2,0:T(8,128)(2,1)} %copy.121), calls=%async_computation.1 | async-start | bytes 25165824 | tf_op jit(solution)/shard_map/all_to_all | solution.py:391
  371.2 327.6 %all-to-all-start = ((bf16[4,128,12,1024]{1,3,2,0:T(8,128)(2,1)}), bf16[4,128,12,1024]{1,3,2,0:T(8,128)(2,1)}, u32[]{:S(2)}, u32[]{:S(2)}) async-start(bf16[4,128,12,1024]{1,3,2,0:T(8,128)(2,1)} %copy.111), calls=%async_computation | async-start | bytes 25165824 | tf_op jit(solution)/shard_map/all_to_all | solution.py:391
  377.4 472.3 %all-gather.12.cloned.1.call-start = ((), (), s32[]{:S(2)}) async-start(), calls=%async_computation.14 | async-start | bytes 20971520 | tf_op jit(solution)/shard_map/all_gather | solution.py:318
  378.0 1293.8 %reduce-scatter.18.cloned.1.call-start = ((), (), s32[]{:S(2)}) async-start(), calls=%async_computation.19 | async-start | bytes 491520 | tf_op jit(solution)/shard_map/reduce_scatter | solution.py:258
  638.2 32.6 %copy-start.146 = (s32[2,1,1]{0,2,1:T(1,128)S(1)}, s32[2,1,1]{0,2,1:T(1,128)}, u32[]{:S(2)}) copy-start(s32[2,1,1]{0,2,1:T(1,128)} %param.23) | copy-start | bytes 28
  638.2 40.9 %copy-start.147 = (s32[2,1,1,128]{3,2,1,0:T(1,128)S(1)}, s32[2,1,1,128]{3,2,1,0:T(1,128)}, u32[]{:S(2)}) copy-start(s32[2,1,1,128]{3,2,1,0:T(1,128)} %param.24) | copy-start | bytes 3076
  681.2 186.3 %copy-start.85 = (f32[1,1024]{1,0:T(1,128)}, f32[1,1024]{1,0:T(1,128)S(1)}, u32[]{:S(2)}) copy-start(f32[1,1024]{1,0:T(1,128)S(1)} %get-tuple-element.75) | copy-start | bytes 12292
  831.0 41.9 %copy-start.7 = (f32[128,1024]{1,0:T(8,128)}, f32[128,1024]{1,0:T(8,128)S(1)}, u32[]{:S(2)}) copy-start(f32[128,1024]{1,0:T(8,128)S(1)} %get-tuple-element.117) | copy-start | bytes 1572868
  841.4 26.1 %copy-start.127 = (f32[128]{0:T(128)}, f32[128]{0:T(128)S(1)}, u32[]{:S(2)}) copy-start(f32[128]{0:T(128)S(1)} %get-tuple-element.132) | copy-start | bytes 1540
  875.9 31.5 %copy-start.139 = (f32[128]{0:T(128)}, f32[128]{0:T(128)S(1)}, u32[]{:S(2)}) copy-start(f32[128]{0:T(128)S(1)} %fusion.140) | copy-start | bytes 1540
  880.6 20.4 slice-start.9
  880.7 20.4 slice-start.10
  880.7 20.4 slice-start.11
  940.5 898.4 %reduce-scatter.14.cloned.1.call-start = ((), (), s32[]{:S(2)}) async-start(), calls=%async_computation.17 | async-start | bytes 20971520 | tf_op jit(solution)/shard_map/reduce_scatter | solution.py:255
  968.4 877.5 %reduce-scatter.10.cloned.1.call-start = ((), (), s32[]{:S(2)}) async-start(), calls=%async_computation.15 | async-start | bytes 20971520 | tf_op jit(solution)/shard_map/reduce_scatter | solution.py:252
  1056.7 32.5 %copy-start.17 = (f32[128,1024]{1,0:T(8,128)}, f32[128,1024]{1,0:T(8,128)S(1)}, u32[]{:S(2)}) copy-start(f32[128,1024]{1,0:T(8,128)S(1)} %add_add_fusion.7) | copy-start | bytes 1572868
  1176.9 33.7 %copy-start.23 = (f32[128,16,64]{0,2,1:T(8,128)S(1)}, f32[128,16,64]{0,2,1:T(8,128)}, u32[]{:S(2)}) copy-start(f32[128,16,64]{0,2,1:T(8,128)} %copy-done.22) | copy-start | bytes 1572868
  1176.9 33.7 %copy-start.64 = (f32[128,48,16]{0,2,1:T(8,128)S(1)}, f32[128,48,16]{0,2,1:T(8,128)}, u32[]{:S(2)}) copy-start(f32[128,48,16]{0,2,1:T(8,128)} %get-tuple-element.78) | copy-start | bytes 1179652
  1302.9 22.6 slice-start.3
  1396.6 24.8 %copy-start.58 = (bf16[128,48,16]{0,2,1:T(8,128)(2,1)S(1)}, bf16[128,48,16]{0,2,1:T(8,128)(2,1)}, u32[]{:S(2)}) copy-start(bf16[128,48,16]{0,2,1:T(8,128)(2,1)} %fusion.73) | copy-start | bytes 589828
  1396.6 24.8 %copy-start.62 = (f32[16,1,1024]{2,1,0:T(1,128)S(1)}, f32[16,1,1024]{2,1,0:T(1,128)}, u32[]{:S(2)}) copy-start(f32[16,1,1024]{2,1,0:T(1,128)} %copy-done.61) | copy-start | bytes 196612
  1436.2 220.3 %all-to-all-start.3 = ((bf16[1,128,48,1024]{3,1,0,2:T(8,128)(2,1)}), bf16[1,128,48,1024]{3,1,0,2:T(8,128)(2,1)}, u32[]{:S(2)}, u32[]{:S(2)}) async-start(bf16[1,128,48,1024]{3,1,0,2:T(8,128)(2,1)} %fusion.5), calls=%async_computation.9 | async-start | bytes 25165824 | tf_op jit(solution)/shard_map/all_to_all | solution.py:403
  1443.0 21.9 copy-start.60
  1479.4 184.9 %copy-start.115 = (f32[16,64]{1,0:T(8,128)S(1)}, f32[16,64]{1,0:T(8,128)}, u32[]{:S(2)}) copy-start(f32[16,64]{1,0:T(8,128)} %copy-done.114) | copy-start | bytes 12292
  1479.4 185.0 %copy-start.113 = (f32[16,64]{1,0:T(8,128)S(1)}, f32[16,64]{1,0:T(8,128)}, u32[]{:S(2)}) copy-start(f32[16,64]{1,0:T(8,128)} %copy-done.112) | copy-start | bytes 12292
  1479.4 185.1 %copy-start.121 = (f32[1024]{0:T(1024)S(1)}, f32[1024]{0:T(1024)}, u32[]{:S(2)}) copy-start(f32[1024]{0:T(1024)} %get-tuple-element.50) | copy-start | bytes 12292
  1479.4 185.8 %copy-start.122 = (f32[1024]{0:T(1024)S(1)}, f32[1024]{0:T(1024)}, u32[]{:S(2)}) copy-start(f32[1024]{0:T(1024)} %get-tuple-element.52) | copy-start | bytes 12292
  1656.5 144.5 %all-to-all-start.2 = ((bf16[1,128,48,1024]{3,1,0,2:T(8,128)(2,1)}), bf16[1,128,48,1024]{3,1,0,2:T(8,128)(2,1)}, u32[]{:S(2)}, u32[]{:S(2)}) async-start(bf16[1,128,48,1024]{3,1,0,2:T(8,128)(2,1)} %fusion.4), calls=%async_computation.8 | async-start | bytes 25165824 | tf_op jit(solution)/shard_map/all_to_all | solution.py:403
  1662.9 191.7 %reduce-scatter.20.cloned.1.call-start = ((), (), s32[]{:S(2)}) async-start(), calls=%async_computation.20 | async-start | bytes 221184 | tf_op jit(solution)/shard_map/reduce_scatter | solution.py:268
  1673.5 229.9 %reduce-scatter.22.cloned.1.call-start = ((), (), s32[]{:S(2)}) async-start(), calls=%async_computation.21 | async-start | bytes 442368 | tf_op jit(solution)/shard_map/reduce_scatter | solution.py:269
  1835.1 2.5 collective-permute-start
  1838.9 216.5 %reduce-scatter.16.cloned.1.call-start = ((), (), s32[]{:S(2)}) async-start(), calls=%async_computation.18 | async-start | bytes 9437184 | tf_op jit(solution)/shard_map/reduce_scatter | solution.py:267
  1845.6 362.3 %reduce-scatter.12.cloned.1.call-start = ((), (), s32[]{:S(2)}) async-start(), calls=%async_computation.16 | async-start | bytes 9437184 | tf_op jit(solution)/shard_map/reduce_scatter | solution.py:266
  1852.4 402.7 %copy-start.65 = (f32[2,256,512]{2,1,0:T(8,128)S(1)}, f32[2,256,512]{2,1,0:T(8,128)}, u32[]{:S(2)}) copy-start(f32[2,256,512]{2,1,0:T(8,128)} %param.31) | copy-start | bytes 3145732
  1852.4 401.3 %copy-start.102 = (f32[94,128]{1,0:T(8,128)S(1)}, f32[94,128]{1,0:T(8,128)}, u32[]{:S(2)}) copy-start(f32[94,128]{1,0:T(8,128)} %param.35) | copy-start | bytes 144388
  1852.5 401.3 %copy-start.116 = (f32[94,128]{1,0:T(8,128)S(1)}, f32[94,128]{1,0:T(8,128)}, u32[]{:S(2)}) copy-start(f32[94,128]{1,0:T(8,128)} %param.37) | copy-start | bytes 144388
  1852.5 401.3 %copy-start.117 = (f32[94,128]{1,0:T(8,128)S(1)}, f32[94,128]{1,0:T(8,128)}, u32[]{:S(2)}) copy-start(f32[94,128]{1,0:T(8,128)} %param.36) | copy-start | bytes 144388
  1852.5 402.0 %copy-start.110 = (f32[256,24]{0,1:T(8,128)S(1)}, f32[256,24]{0,1:T(8,128)}, u32[]{:S(2)}) copy-start(f32[256,24]{0,1:T(8,128)} %param.32) | copy-start | bytes 73732
  1852.5 402.0 %copy-start.119 = (f32[256,24]{0,1:T(8,128)S(1)}, f32[256,24]{0,1:T(8,128)}, u32[]{:S(2)}) copy-start(f32[256,24]{0,1:T(8,128)} %param.34) | copy-start | bytes 73732
  1852.5 402.0 %copy-start.120 = (f32[256,24]{0,1:T(8,128)S(1)}, f32[256,24]{0,1:T(8,128)}, u32[]{:S(2)}) copy-start(f32[256,24]{0,1:T(8,128)} %param.33) | copy-start | bytes 73732
  1852.5 402.6 %copy-start.25 = (f32[2,256,512]{2,1,0:T(8,128)S(1)}, f32[2,256,512]{2,1,0:T(8,128)}, u32[]{:S(2)}) copy-start(f32[2,256,512]{2,1,0:T(8,128)} %param.29) | copy-start | bytes 3145732
  1854.6 399.8 %copy-start.111 = (f32[256,24]{0,1:T(8,128)S(1)}, f32[256,24]{0,1:T(8,128)}, u32[]{:S(2)}) copy-start(f32[256,24]{0,1:T(8,128)} %reduce-scatter.20.cloned.1.call-done) | copy-start | bytes 73732
  1903.4 350.4 %copy-start.103 = (f32[94,128]{1,0:T(8,128)S(1)}, f32[94,128]{1,0:T(8,128)}, u32[]{:S(2)}) copy-start(f32[94,128]{1,0:T(8,128)} %reduce-scatter.22.cloned.1.call-done) | copy-start | bytes 144388
  2055.4 199.8 %copy-start.27 = (f32[2,256,512]{2,1,0:T(8,128)S(1)}, f32[2,256,512]{2,1,0:T(8,128)}, u32[]{:S(2)}) copy-start(f32[2,256,512]{2,1,0:T(8,128)} %reduce-scatter.16.cloned.1.call-done) | copy-start | bytes 3145732
  (144 other events, 797.6 us)
Sparse Core Ops, SparseCore 0:
  10.7 77.7 all-gather.5
  91.0 75.1 all-gather.9
  167.7 194.1 all-gather.7
  379.5 194.1 all-gather.11
  940.6 20.5 reduce-scatter.17
  968.5 125.9 reduce-scatter.13
  1396.7 201.7 reduce-scatter.9
  1673.6 62.4 reduce-scatter.19
  1839.0 64.3 reduce-scatter.21
  1906.9 148.4 reduce-scatter.15
  2059.4 148.3 reduce-scatter.11
where the time goes:
time: 2280 us; the launch traced here: 2270 us
  waiting for transfers between devices  934 us (41%)
  blocking collectives  380 us (17%)
  local copies, waits for them, and re-layouts  360 us (16%)
  matrix products  356 us (16%)
  other arithmetic  185 us (8%)
  between operations  28.3 us (1%)
  starting transfers between devices  27.6 us (1%)
    all_to_all x2, waiting for transfers between devices, body(): lax.all_to_all(g_tokens[None], 'var', split_axis=2, concat_axis=0, tiled=...  290 us
    psum x1, blocking collectives, body(): count = lax.psum(local_count, ('var', 'patch'))  254 us
    all_to_all x2, waiting for transfers between devices, body(): lax.all_to_all(tok_local, 'var', split_axis=0, concat_axis=2, tiled=True)[0]  217 us
    reduce_scatter x1, waiting for transfers between devices, reduce_grads(): lax.psum_scatter(by_var[1], 'patch', scatter_dimension=2, tiled=True)  150 us
    reduce_scatter x1, waiting for transfers between devices, reduce_grads(): lax.psum_scatter(by_var[0], 'patch', scatter_dimension=2, tiled=True)  150 us
    convert_element_type x4, local copies, waits for them, and re-layouts, aggregate_back(): g_proj = (var_low.astype(jnp.float32)[..., None] * g_heads.astype(jnp.flo...  136 us
    all_gather x1, waiting for transfers between devices, body(): lax.all_gather(square_master.astype(jnp.bfloat16), 'patch', axis=2, tiled...  78 us
    unnamed x366, local copies, waits for them, and re-layouts  68 us
  transfers between devices with their start and end apart: 16, of which 7 were waited for; matrix products, arithmetic and copies ran while one was open for 35% of the time, Pallas kernels for 0%

commit v1 on v0

v1 whole, which is shorter than its diff:
```python
import math

import jax
import jax.numpy as jnp
from jax import lax
from jax.sharding import Mesh
from jax.sharding import PartitionSpec as P

HEADS = 16
V = 48
PATCH_PIXELS = 4
SOURCES = 5
LATS = 64
PAD = 8

HIGH = lax.Precision.HIGHEST
CLIP_AT = 0.01
LEARN_RATE = 0.01
TABLE_RATE = 0.3
WEIGHT_DECAY = 0.1
FIRST_DECAY = 0.5
SECOND_DECAY = 0.5
EPSILON = 1e-08
NORM_EPSILON = 1e-05
AXES = ("y", "c", "z", "x")
BF = jnp.bfloat16
F32 = jnp.float32


class Grid:
    def __init__(self, mesh):
        nv, npatch = mesh.shape["var"], mesh.shape["patch"]
        self.sizes = {"y": nv // 2, "c": 2, "z": npatch // 2, "x": 2}
        self.mesh = Mesh(mesh.devices.reshape(tuple(self.sizes.values())), AXES)
        self.nv, self.np = nv, npatch
        self.fast = self.sizes["y"] == 2

    def flat(self, move):
        s = [self.sizes[a] for a in AXES]
        pairs = []
        for y in range(s[0]):
            for c in range(s[1]):
                for z in range(s[2]):
                    for x in range(s[3]):
                        ty, tc, tz, tx = move(y, c, z, x)
                        src = ((y * s[1] + c) * s[2] + z) * s[3] + x
                        dst = ((ty * s[1] + tc) * s[2] + tz) * s[3] + tx
                        pairs.append((src, dst))
        return pairs

    def permute(self, value, move):
        return lax.ppermute(value, AXES, self.flat(move))

    def swap(self, value, axis, bit=1):
        return lax.ppermute(value, axis, [(i, i ^ bit) for i in range(self.sizes[axis])])

    def total(self, value, axes=AXES):
        for axis in axes:
            bit = 1
            while bit < self.sizes[axis]:
                value = jax.tree.map(lambda v: v + self.swap(v, axis, bit), value)
                bit *= 2
        return value

    def spread(self, value, axes):
        count = math.prod(self.sizes[a] for a in axes)
        held = jnp.zeros((count,) + value.shape, value.dtype)
        held = lax.dynamic_update_index_in_dim(held, value, lax.axis_index(axes), 0)
        return self.total(held, axes)

    def along(self, first):
        def move(y, c, z, x):
            if (c == 0) == first:
                return (y ^ 1, c, z, x)
            return (y, c, z, x ^ 1)

        return move

    def flips(self, core, a, b):
        return jnp.where(core == 0, a, b), jnp.where(core == 0, b, a)

    def gather(self, piece):
        rows, w = piece.shape
        if not self.fast:
            return lax.all_gather(piece, AXES).reshape(self.nv, self.np, rows, w)
        nz = self.sizes["z"]
        y, c, z, x = (lax.axis_index(a) for a in AXES)
        line = jnp.zeros((nz, rows, w), piece.dtype)
        line = lax.dynamic_update_index_in_dim(line, piece, z, 0)
        for k in range(1, nz):
            got = lax.ppermute(piece, "z", [(i, (i + k) % nz) for i in range(nz)])
            line = lax.dynamic_update_index_in_dim(line, got, (z - k) % nz, 0)
        near = self.permute(line, self.along(False))
        far = [self.permute(v, self.along(True)) for v in (line, near)]
        mine = [[line, near], far]
        out = jnp.zeros((2, 2, nz, 2, rows, w), piece.dtype)
        for a in range(2):
            for b in range(2):
                fy, fx = self.flips(c, a, b)
                out = lax.dynamic_update_slice(
                    out, mine[a][b][None, None, :, None], (y ^ fy, c, 0, x ^ fx, 0, 0)
                )
                got = self.swap(mine[a][b], "c")
                fy, fx = self.flips(1 - c, a, b)
                out = lax.dynamic_update_slice(
                    out, got[None, None, :, None], (y ^ fy, 1 - c, 0, x ^ fx, 0, 0)
                )
        return out.reshape(self.nv, self.np, rows, w)

    def scatter(self, parts):
        nv, npatch, rows, w = parts.shape
        if not self.fast:
            flat = parts.reshape(nv * npatch * rows, w)
            return lax.psum_scatter(flat, AXES, scatter_dimension=0, tiled=True).astype(F32)
        nz = self.sizes["z"]
        y, c, z, x = (lax.axis_index(a) for a in AXES)
        cut = parts.reshape(2, 2, nz, 2, rows, w)

        def pick(core, a, b):
            fy, fx = self.flips(core, a, b)
            got = lax.dynamic_slice(
                cut, (y ^ fy, core, 0, x ^ fx, 0, 0), (1, 1, nz, 1, rows, w)
            )
            return got.reshape(nz, rows, w)

        def add(left, right):
            return (left.astype(F32) + right.astype(F32)).astype(BF)

        half = [
            [add(pick(c, a, b), self.swap(pick(1 - c, a, b), "c")) for b in range(2)]
            for a in range(2)
        ]
        quarter = [add(half[0][b], self.permute(half[1][b], self.along(True))) for b in range(2)]
        line = add(quarter[0], self.permute(quarter[1], self.along(False)))
        total = lax.dynamic_index_in_dim(line, z, 0, False).astype(F32)
        for k in range(1, nz):
            out = lax.dynamic_index_in_dim(line, (z + k) % nz, 0, False)
            got = lax.ppermute(out, "z", [(i, (i + k) % nz) for i in range(nz)])
            total = total + got.astype(F32)
        return total


def whole(chunks):
    nv, npatch, rows, w = chunks.shape
    return jnp.transpose(chunks, (0, 2, 1, 3)).reshape(nv * rows, npatch * w)


def chunked(value, nv, npatch):
    r, c = value.shape
    return jnp.transpose(value.reshape(nv, r // nv, npatch, c // npatch), (0, 2, 1, 3))


def latitude_table():
    levels = jnp.arange(2 * LATS).astype(F32)
    cosine = jnp.cos(((levels + 0.5) / (2 * LATS) - 0.5) * math.pi)
    scaled = cosine / jnp.mean(cosine)
    index = 2 * jnp.arange(LATS)[:, None] + jnp.arange(PATCH_PIXELS)[None, :] // 2
    return scaled[index]


def layer_norm(value, gain):
    center = value - jnp.mean(value, axis=-1, keepdims=True)
    spread = jnp.mean(center * center, axis=-1, keepdims=True)
    return center * lax.rsqrt(spread + NORM_EPSILON) * gain


def exact_gelu(value):
    return jax.nn.gelu(value, approximate=False)


def adam_update(master, first, second, grad, factor, steps, rate):
    clipped = grad * factor
    new_first = FIRST_DECAY * first + (1.0 - FIRST_DECAY) * clipped
    new_second = SECOND_DECAY * second + (1.0 - SECOND_DECAY) * clipped * clipped
    first_hat = new_first / (1.0 - jnp.power(FIRST_DECAY, steps))
    second_hat = new_second / (1.0 - jnp.power(SECOND_DECAY, steps))
    new_master = master - rate * (
        first_hat / (jnp.sqrt(second_hat) + EPSILON) + WEIGHT_DECAY * master
    )
    return (new_master, new_first, new_second, new_master.astype(BF))


def dot(a, b, dims, batch=((), ()), precision=None):
    return lax.dot_general(
        a, b, (dims, batch), precision=precision, preferred_element_type=F32
    )


NN = ((1,), (0,))
NT = ((1,), (1,))
TN = ((0,), (0,))


def body(
    grid,
    pixels,
    targets,
    masks,
    lengths,
    groups,
    latitudes,
    step_count,
    square_master,
    square_first,
    square_second,
    dense_master,
    dense_first,
    dense_second,
    head_master,
    head_first,
    head_second,
    table_master,
    table_first,
    table_second,
):
    nv, npatch = grid.nv, grid.np
    micro, items, _, cap, own_pixels = pixels.shape
    rows = micro * cap
    width = square_master.shape[1] * nv
    size = width // HEADS
    scale = size ** (-0.5)
    band, strip = square_master.shape[1:]
    ff_strip = dense_master.shape[2]
    ho = head_master.shape[1] * npatch
    base = 5 * V + cap
    table_band = table_master.shape[0]
    table_pad = -table_band % PAD
    my_band = lax.axis_index(("y", "c"))
    my_strip = lax.axis_index(("z", "x"))

    square_low = square_master.astype(BF)
    dense_low = dense_master.astype(BF)
    head_low = head_master.astype(BF)
    table_low = table_master.astype(BF)
    first = jnp.concatenate(
        [
            jnp.pad(table_low, ((0, table_pad), (0, 0))),
            square_low[2],
            square_low[3],
        ],
        axis=0,
    )
    first = grid.gather(first)
    table = whole(first[:, :, :table_band])
    start = table_band + table_pad
    wv = whole(first[:, :, start : start + band])
    wa = whole(first[:, :, start + band : start + 2 * band])
    second = grid.gather(square_low[4:8].reshape(4 * band, strip))
    wqkv = jnp.concatenate(
        [whole(second[:, :, k * band : (k + 1) * band]) for k in range(3)], axis=1
    )
    wo = whole(second[:, :, 3 * band :])
    w1 = whole(grid.gather(dense_low[0]))
    w2 = whole(grid.gather(dense_low[1]))
    head = whole(grid.gather(head_low))

    slots = jnp.arange(cap)
    lat_table = latitude_table()
    valid = masks[:, 0, 0].astype(F32) * (slots[None] < lengths[:, 0, 0][:, None]).astype(F32)[..., None]
    lat_onehot = (latitudes[:, 0, 0][..., None] == jnp.arange(LATS)).astype(F32)
    wpix = jnp.einsum("mcl,lk->mck", lat_onehot, lat_table, precision=HIGH) * valid
    weighted = jnp.tile(wpix.reshape(rows, PATCH_PIXELS), (1, V))
    count = grid.total(jnp.sum(valid))

    parts = pixels[:, :, 0]
    mine = lax.all_to_all(parts, ("y", "c"), split_axis=1, concat_axis=3, tiled=True)[:, 0]
    pix = jnp.transpose(mine.reshape(rows, V, PATCH_PIXELS), (0, 2, 1)).astype(F32)

    query = table[base + SOURCES]
    query_own = lax.dynamic_slice_in_dim(query, my_band * band, band)
    qv = dot(query_own[None], square_low[0], NN)[0]
    qv_own = grid.total(qv, ("y", "c")).astype(BF)
    col_head = (my_strip * strip + jnp.arange(strip)) // size
    head_mask = (col_head[:, None] == jnp.arange(HEADS)[None]).astype(F32)
    u_part = dot(square_low[1].astype(F32) * qv_own.astype(F32)[None], head_mask, NN, precision=HIGH)
    u_band = (grid.total(u_part, ("z", "x")) * scale).astype(BF)
    u = grid.spread(u_band, ("y", "c")).reshape(width, HEADS)
    rows_t = jnp.concatenate(
        [
            jnp.transpose(table[: PATCH_PIXELS * V].reshape(V, PATCH_PIXELS, width), (1, 0, 2)).reshape(-1, width),
            table[PATCH_PIXELS * V : base],
        ],
        axis=0,
    )
    tv = dot(rows_t, wv, NN)
    tu = dot(rows_t, u, NN)
    nk = PATCH_PIXELS * V
    n5 = nk + V
    scores = (
        jnp.einsum("ckv,kvh->chv", pix, tu[:nk].reshape(PATCH_PIXELS, V, HEADS), precision=HIGH)
        + tu[nk:n5].T[None]
        + jnp.tile(tu[n5:], (micro, 1))[:, :, None]
    )
    pa = jax.nn.softmax(scores, axis=-1)
    pal = pa.astype(BF).astype(F32)
    mass = jnp.sum(pal, axis=-1)
    fold = jnp.concatenate(
        [(pal[:, :, None] * pix[:, None]).reshape(rows, HEADS, nk), pal], axis=2
    )
    tv_heads = tv.reshape(-1, HEADS, size)
    pos_v = jnp.tile(tv_heads[n5:], (micro, 1, 1))
    agg = (
        jnp.einsum("chn,nhe->che", fold, tv_heads[:n5], precision=HIGH)
        + mass[:, :, None] * pos_v
    )
    gathered = agg.reshape(rows, width).astype(BF)

    gain_one = table[base + SOURCES + 1].astype(F32)
    gain_two = table[base + SOURCES + 2].astype(F32)
    onehot = (groups[:, 0, 0][:, None] == jnp.arange(SOURCES)).astype(F32)
    src = jnp.dot(onehot, table[base : base + SOURCES].astype(F32), precision=HIGH)
    x0 = dot(gathered, wa, NN) + jnp.repeat(src, cap, axis=0)
    h1 = layer_norm(x0, gain_one).astype(BF)
    qkv = dot(h1, wqkv, NN).astype(BF)
    q, k, vv = (
        qkv[:, i * width : (i + 1) * width].reshape(micro, cap, HEADS, size) for i in range(3)
    )
    keymask = slots[None] < lengths[:, 0, 0][:, None]
    raw = jnp.einsum("mqhe,mkhe->mhqk", q, k, preferred_element_type=F32) * scale
    probs = jax.nn.softmax(jnp.where(keymask[:, None, None], raw, -1e30), axis=-1)
    probs_low = probs.astype(BF)
    o = jnp.einsum("mhqk,mkhe->mqhe", probs_low, vv, preferred_element_type=F32)
    o = o.reshape(rows, width).astype(BF)
    x1 = x0 + dot(o, wo, NN)
    h2 = layer_norm(x1, gain_two).astype(BF)
    f = dot(h2, w1, NN)
    act = exact_gelu(f).astype(BF)
    x2 = x1 + dot(act, w2, NT)
    x2_low = x2.astype(BF)
    pred = dot(x2_low, head, NN)
    diff = pred - targets[:, 0, 0].astype(F32).reshape(rows, ho)
    loss_local = jnp.sum(weighted * diff * diff)
    dpred = (2.0 * weighted * diff / count).astype(BF)

    d_head = dot(x2_low, dpred, TN)
    dx2 = dot(dpred, head, NT)
    dx2_low = dx2.astype(BF)
    d_down = dot(dx2_low, act, TN)
    dact = dot(dx2_low, w2, NN)
    _, gelu_back = jax.vjp(exact_gelu, f)
    df = gelu_back(dact)[0].astype(BF)
    d_up = dot(h2, df, TN)
    dh2 = dot(df, w1, NT)
    _, norm_back = jax.vjp(layer_norm, x1, gain_two)
    dx1n, d_gain_two = norm_back(dh2)
    dx1 = dx2 + dx1n
    dx1_low = dx1.astype(BF)
    d_wo = dot(o, dx1_low, TN)
    do = dot(dx1_low, wo, NT).astype(BF).reshape(micro, cap, HEADS, size)
    dprobs = jnp.einsum("mqhe,mkhe->mhqk", do, vv, preferred_element_type=F32)
    dvv = jnp.einsum("mhqk,mqhe->mkhe", probs_low, do, preferred_element_type=F32)
    ds = (probs * (dprobs - jnp.sum(probs * dprobs, axis=-1, keepdims=True))).astype(BF)
    dq = jnp.einsum("mhqk,mkhe->mqhe", ds, k, preferred_element_type=F32) * scale
    dk = jnp.einsum("mhqk,mqhe->mkhe", ds, q, preferred_element_type=F32) * scale
    dqkv = jnp.concatenate([t.reshape(rows, width) for t in (dq, dk, dvv)], axis=1).astype(BF)
    d_wqkv = dot(h1, dqkv, TN)
    dh1 = dot(dqkv, wqkv, NT)
    _, norm_back = jax.vjp(layer_norm, x0, gain_one)
    dx0n, d_gain_one = norm_back(dh1)
    dx0 = dx1 + dx0n
    d_src = jnp.dot(onehot.T, jnp.sum(dx0.reshape(micro, cap, width), axis=1), precision=HIGH)
    dx0_low = dx0.astype(BF)
    d_wa = dot(gathered, dx0_low, TN)
    dagg = dot(dx0_low, wa, NT).astype(BF).astype(F32).reshape(rows, HEADS, size)

    dfold = jnp.einsum("che,nhe->chn", dagg, tv_heads[:n5], precision=HIGH)
    dpal = (
        jnp.sum(dfold[:, :, :nk].reshape(rows, HEADS, PATCH_PIXELS, V) * pix[:, None], axis=2)
        + dfold[:, :, nk:]
        + jnp.sum(dagg * pos_v, axis=-1)[:, :, None]
    )
    dsv = (pa * (dpal - jnp.sum(pa * dpal, axis=-1, keepdims=True))).astype(BF).astype(F32)
    g_rows = jnp.einsum("chn,che->nhe", fold, dagg, precision=HIGH).reshape(n5, width)
    g_pos = jnp.sum((mass[:, :, None] * dagg).reshape(micro, cap, width), axis=0)
    s_rows = jnp.concatenate(
        [
            jnp.einsum("ckv,chv->kvh", pix, dsv, precision=HIGH).reshape(nk, HEADS),
            jnp.sum(dsv, axis=0).T,
            jnp.sum(jnp.sum(dsv, axis=-1).reshape(micro, cap, HEADS), axis=0),
        ],
        axis=0,
    )
    g_table = jnp.concatenate(
        [
            jnp.transpose(g_rows[:nk].reshape(PATCH_PIXELS, V, width), (1, 0, 2)).reshape(nk, width),
            g_rows[nk:],
            g_pos,
            d_src,
            jnp.zeros((1, width), F32),
            d_gain_one[None],
            d_gain_two[None],
        ],
        axis=0,
    )
    s_table = jnp.concatenate(
        [
            jnp.transpose(s_rows[:nk].reshape(PATCH_PIXELS, V, HEADS), (1, 0, 2)).reshape(nk, HEADS),
            s_rows[nk:],
        ],
        axis=0,
    )

    def to_owner(value):
        return grid.scatter(chunked(value.astype(BF), nv, npatch))

    down_sum = to_owner(d_down)
    up_sum = to_owner(d_up)
    s_sum = grid.total(s_table)
    low_part = jnp.concatenate(
        [
            jnp.pad(chunked(g_table.astype(BF), nv, npatch), ((0, 0), (0, 0), (0, table_pad), (0, 0))),
            chunked(d_wa.astype(BF), nv, npatch),
        ],
        axis=2,
    )
    low_sum = grid.scatter(low_part)
    g_own = low_sum[:table_band]
    wa_sum = low_sum[table_band + table_pad :]
    attn_sum = grid.scatter(
        jnp.concatenate(
            [chunked(d_wqkv[:, i * width : (i + 1) * width].astype(BF), nv, npatch) for i in range(3)]
            + [chunked(d_wo.astype(BF), nv, npatch)],
            axis=2,
        )
    )
    head_sum = to_owner(d_head)

    g_low = g_own.astype(BF)
    g_column = grid.spread(g_low, ("y", "c")).reshape(nv * table_band, strip)[:base]
    g_line = jnp.transpose(grid.spread(g_low, ("z", "x")), (1, 0, 2)).reshape(table_band, width)
    table_own_band = lax.dynamic_slice_in_dim(table, my_band * band, band, 1)
    value_sum = dot(table_own_band[:base], g_column, TN)
    du_own = dot(table_own_band[:base].astype(F32), s_sum, TN, precision=HIGH)
    du_cols = dot(du_own, head_mask, NT, precision=HIGH)
    key_sum = du_cols * qv_own.astype(F32)[None] * scale
    dqv = grid.total(jnp.sum(square_low[1].astype(F32) * du_cols, axis=0) * scale, ("y", "c"))
    query_sum = query_own.astype(F32)[:, None] * dqv[None]
    dquery = jnp.sum(square_low[0].astype(F32) * dqv[None], axis=1)
    dquery = lax.dynamic_update_slice_in_dim(jnp.zeros((width,), F32), dquery, my_band * band, 0)
    dquery = grid.total(dquery)
    table_row = my_band * table_band + jnp.arange(table_band)
    s_pad = jnp.pad(s_sum, ((0, nv * table_band - base), (0, 0)))
    s_own = lax.dynamic_slice_in_dim(s_pad, my_band * table_band, table_band, 0)
    wv_rows = lax.dynamic_slice_in_dim(wv, my_strip * strip, strip, 0)
    u_rows = lax.dynamic_slice_in_dim(u, my_strip * strip, strip, 0)
    d_rows = dot(g_line, wv_rows, NT) + dot(s_own, u_rows.astype(F32), NT, precision=HIGH)
    dq_own = lax.dynamic_slice_in_dim(dquery, my_strip * strip, strip, 0)
    table_sum = jnp.where((table_row < base)[:, None], d_rows, g_own)
    table_sum = jnp.where((table_row == base + SOURCES)[:, None], dq_own[None], table_sum)
    square_sum = jnp.concatenate(
        [query_sum[None], key_sum[None], value_sum[None], wa_sum[None], attn_sum.reshape(4, band, strip)],
        axis=0,
    )
    dense_sum = jnp.stack([up_sum, down_sum])
    shards = (square_sum, dense_sum, head_sum, table_sum)
    sumsq = sum(jnp.sum(s * s) for s in shards)
    both = grid.total(jnp.stack([loss_local, sumsq]))
    loss = both[0] / count
    norm = jnp.sqrt(both[1])
    factor = jnp.minimum(1.0, CLIP_AT / norm)
    steps = step_count[0].astype(F32)
    sq = adam_update(square_master, square_first, square_second, shards[0], factor, steps, LEARN_RATE)
    de = adam_update(dense_master, dense_first, dense_second, shards[1], factor, steps, LEARN_RATE)
    hd = adam_update(head_master, head_first, head_second, shards[2], factor, steps, LEARN_RATE)
    tb = adam_update(table_master, table_first, table_second, shards[3], factor, steps, TABLE_RATE)
    return (loss, norm, *sq, *de, *hd, *tb)


def solution(mesh):
    grid = Grid(mesh)
    var, patch = ("y", "c"), ("z", "x")
    item = P(None, var, patch)
    weight = P(None, var, patch)
    flat = P(var, patch)
    in_specs = (
        P(None, None, patch, None, var),
        item,
        item,
        item,
        item,
        item,
        P(),
        *(weight,) * 6,
        *(flat,) * 6,
    )
    out_specs = (P(), P(), *(weight,) * 8, *(flat,) * 8)

    def step(*args):
        return body(grid, *args)

    return jax.shard_map(step, mesh=grid.mesh, in_specs=in_specs, out_specs=out_specs, check_vma=False)
```

time: 2280 us -> 853 us (0.37)
  waiting for transfers between devices: 934 us -> 243 us
  blocking collectives: 380 us -> 0 us
  matrix products: 356 us -> 86.7 us
  other arithmetic: 185 us -> 61.6 us
  starting transfers between devices: 27.6 us -> 147 us
  local copies, waits for them, and re-layouts: 360 us -> 291 us
    all_to_all x4 -> x1, waiting for transfers between devices: 507 us -> 0.01 us  [body(): lax.all_to_all(parts, ('y', 'c'), split_axis=1, concat_axis=3, tiled=True)]
    reduce_scatter x7 -> x0, waiting for transfers between devices: 348 us -> none  [the longest x1 150 us: reduce_grads(): lax.psum_scatter(by_var[1], 'patch', scatter_dimension=2, tiled=True)]
    psum x2 -> x0, blocking collectives: 293 us -> none  [the longest x1 254 us: body(): count = lax.psum(local_count, ('var', 'patch'))]
    dot_general x74 -> x40, matrix products: 356 us -> 84.5 us  [the longest x27 68.6 us: dot(): lax.dot_general(a, b, (dims, batch), precision=precision, preferred_eleme...]
    ppermute x0 -> x134, waiting for transfers between devices: none -> 243 us  [the longest x30 87 us: permute(): return lax.ppermute(value, AXES, self.flat(move))]
    ppermute x0 -> x134, starting transfers between devices: none -> 144 us  [the longest x74 67.2 us: swap(): lax.ppermute(value, axis, [(i, i ^ bit) for i in range(self.sizes[axis])])]
    convert_element_type x13 -> x6, local copies, waits for them, and re-layouts: 150 us -> 6.21 us  [the longest x2 4.26 us: body(): dot(dx0_low, wa, NT).astype(BF).astype(F32).reshape(rows, HEADS, size)]
    all_gather x4 -> x0, waiting for transfers between devices: 78 us -> none  [the longest x1 78 us: body(): lax.all_gather(square_master.astype(jnp.bfloat16), 'patch', axis=2, tiled...]
  transfers between devices with their start and end apart: 16 -> 135, of which waited for: 7 -> 52; matrix products, arithmetic and copies ran while one was open for 35% -> 37% of each run, Pallas kernels for 0% -> 0%
where the time goes in v1:
time: 853 us; the launch traced here: 845 us
  local copies, waits for them, and re-layouts  291 us (34%)
  waiting for transfers between devices  243 us (28%)
  starting transfers between devices  147 us (17%)
  matrix products  86.7 us (10%)
  other arithmetic  61.6 us (7%)
  between operations  15.1 us (2%)
    ppermute x30, waiting for transfers between devices, permute(): return lax.ppermute(value, AXES, self.flat(move))  87 us
    unnamed x255, local copies, waits for them, and re-layouts  69.3 us
    dot_general x27, matrix products, dot(): lax.dot_general(a, b, (dims, batch), precision=precision, preferred_eleme...  68.6 us
    ppermute x74, starting transfers between devices, swap(): lax.ppermute(value, axis, [(i, i ^ bit) for i in range(self.sizes[axis])])  67.2 us
    ppermute x74, waiting for transfers between devices, swap(): lax.ppermute(value, axis, [(i, i ^ bit) for i in range(self.sizes[axis])])  64.5 us
    ppermute x15, waiting for transfers between devices, scatter(): got = lax.ppermute(out, 'z', [(i, (i + k) % nz) for i in range(nz)])  52.4 us
    transpose x13, local copies, waits for them, and re-layouts, whole(): return jnp.transpose(chunks, (0, 2, 1, 3)).reshape(nv * rows, npatch * w)  42.5 us
    ppermute x15, waiting for transfers between devices, gather(): got = lax.ppermute(piece, 'z', [(i, (i + k) % nz) for i in range(nz)])  39.2 us
  transfers between devices with their start and end apart: 135, of which 52 were waited for; matrix products, arithmetic and copies ran while one was open for 37% of the time, Pallas kernels for 0%

profile of v1, /device:TPU:0, one launch (start us, length us, event | category | flops | bytes accessed | tf_op | source)
XLA Modules:
  0.0 844.9 jit_solution(4653329741603136263)
XLA Ops:
  1.4 4.0 collective-permute-start.48
  41.2 4.1 collective-permute-start.60
  77.9 13.1 %collective-permute-done.37 = bf16[256,512]{1,0:T(8,128)(2,1)S(1)} collective-permute-done((bf16[256,512]{1,0:T(8,128)(2,1)S(1)}, bf16[256,512]{1,0:T(8,128)(2,1)S(1)}, u32[]{:S(2)}, u32[]{:S(2)}) %collective-permute-start.37) | collective-permute-done | bytes 262176 | tf_op jit(solution)/shard_map/ppermute | solution.py:91
  91.7 13.4 %collective-permute-done.38 = bf16[256,512]{1,0:T(8,128)(2,1)S(1)} collective-permute-done((bf16[256,512]{1,0:T(8,128)(2,1)S(1)}, bf16[256,512]{1,0:T(8,128)(2,1)S(1)}, u32[]{:S(2)}, u32[]{:S(2)}) %collective-permute-start.38) | collective-permute-done | bytes 262176 | tf_op jit(solution)/shard_map/ppermute | solution.py:91
  105.0 4.3 collective-permute-start.27
  114.8 4.6 collective-permute-done.27
  122.7 7.6 collective-permute-done.28
  137.2 4.2 broadcast.447.clone
  146.1 4.3 broadcast.447.clone.1
  152.7 5.2 broadcast_in_dim.350
  165.1 9.4 %collective-permute-done.8 = bf16[4,608,128]{2,1,0:T(8,128)(2,1)S(1)} collective-permute-done((bf16[4,608,128]{2,1,0:T(8,128)(2,1)S(1)}, bf16[4,608,128]{2,1,0:T(8,128)(2,1)S(1)}, u32[]{:S(2)}, u32[]{:S(2)}) %collective-permute-start.8) | collective-permute-done | bytes 622624 | tf_op jit(solution)/shard_map/ppermute | solution.py:52
  181.8 15.3 %collective-permute-done.10 = f32[128]{0:T(128)S(1)} collective-permute-done((f32[128]{0:T(128)S(1)}, f32[128]{0:T(128)S(1)}, u32[]{:S(2)}, u32[]{:S(2)}) %collective-permute-start.10) | collective-permute-done | bytes 544 | tf_op jit(solution)/shard_map/ppermute | solution.py:55
  197.1 6.2 collective-permute-done.31
  203.3 4.6 collective-permute-start.11
  212.3 3.7 collective-permute-start.12
  272.0 10.2 %collective-permute-done.25 = bf16[4,1024,128]{2,1,0:T(8,128)(2,1)S(1)} collective-permute-done((bf16[4,1024,128]{2,1,0:T(8,128)(2,1)S(1)}, bf16[4,1024,128]{2,1,0:T(8,128)(2,1)S(1)}, u32[]{:S(2)}, u32[]{:S(2)}) %collective-permute-start.25) | collective-permute-done | bytes 1048608 | tf_op jit(solution)/shard_map/ppermute | solution.py:52
  282.7 10.7 %collective-permute-done.35 = bf16[4,256,512]{2,1,0:T(8,128)(2,1)S(1)} collective-permute-done((bf16[4,256,512]{2,1,0:T(8,128)(2,1)}, bf16[4,256,512]{2,1,0:T(8,128)(2,1)S(1)}, u32[]{:S(2)}, u32[]{:S(2)}) %collective-permute-start.35) | collective-permute-done | bytes 1048608 | tf_op jit(solution)/shard_map/ppermute | solution.py:52
  303.0 11.6 %copy.603 = bf16[4,256,8,512]{3,2,1,0:T(8,128)(2,1)} copy(bf16[4,256,8,512]{3,1,2,0:T(8,128)(2,1)} %bitcast.121) | data formatting | bytes 16777216 | tf_op jit(solution)/shard_map/transpose | solution.py:145
  314.6 12.2 %copy.707 = bf16[128,8,8,512]{3,1,2,0:T(8,128)(2,1)} copy(bf16[128,8,8,512]{3,2,1,0:T(8,128)(2,1)} %bitcast.783) | data formatting | bytes 16777216
  326.8 11.6 %copy.594 = bf16[4,256,8,512]{3,2,1,0:T(8,128)(2,1)} copy(bf16[4,256,8,512]{3,1,2,0:T(8,128)(2,1)} %bitcast.99) | data formatting | bytes 16777216 | tf_op jit(solution)/shard_map/transpose | solution.py:145
  338.4 12.3 %copy.706 = bf16[128,8,8,512]{3,1,2,0:T(8,128)(2,1)} copy(bf16[128,8,8,512]{3,2,1,0:T(8,128)(2,1)} %bitcast.784) | data formatting | bytes 16777216
  351.8 4.4 slice_bitcast_fusion.4
  383.0 15.4 %multiply_convert_fusion = (bf16[256,4096]{1,0:T(8,128)(2,1)S(1)}, f32[256,4096]{1,0:T(8,128)}, f32[256,4096]{1,0:T(8,128)}) fusion(bf16[1024,4096]{1,0:T(8,128)(2,1)} %bitcast.799, f32[256,1024]{1,0:T(8,128)S(1)} %get-tuple-element.143, f32[1024]{0:T(1024)S(1)} %bitcast.873, f32[256]{0:T(256)S(1)} %fusion.153, f32[256]{0:T(256)S(1)} %broadcast_multiply_fusion), kind=kOutput, calls=%fused_computation.11 | convolution fusion | flops 2216689664 | bytes 19929088 | tf_op jit(solution)/shard_map/dot_general | solution.py:184
  403.0 6.0 add_convert_fusion
  442.5 5.5 convolution_convert_fusion.2
  447.9 6.0 convolution_convert_fusion.1
  453.9 5.7 convolution_convert_fusion
  473.6 4.8 slice_bitcast_fusion.2
  481.9 18.9 %constant_dynamic-slice_fusion.14 = (bf16[1,1,4,1,1024,128]{5,3,2,4,1,0:T(2,128)(2,1)}, bf16[1,1,4,1,1024,128]{5,3,2,4,1,0:T(2,128)(2,1)}, bf16[1,1,4,1,1024,128...) fusion(bf16[2,2,4,2,1024,128]{5,3,2,4,1,0:T(2,128)(2,1)S(1)} %b, ...), kind=kLoop, calls=%fused_computation.393 | loop fusion | bytes 16777272 | tf_op jit(solution)/shard_map/dynamic_slice | solution.py:121
  528.2 3.7 concatenate.38
  535.2 12.3 %copy.719 = bf16[128,8,8,512]{3,2,1,0:T(8,128)(2,1)} copy(bf16[128,8,8,512]{3,1,2,0:T(8,128)(2,1)} %bitcast.774) | data formatting | bytes 16777216
  547.5 9.9 %copy.650 = bf16[4,256,8,512]{3,1,2,0:T(8,128)(2,1)} copy(bf16[4,256,8,512]{3,2,1,0:T(8,128)(2,1)} %bitcast.785) | data formatting | bytes 16777216 | tf_op jit(solution)/shard_map/reshape | solution.py:150
  561.8 4.2 dynamic-slice_bitcast_fusion.7
  566.1 12.5 %copy.720 = bf16[128,8,8,512]{3,2,1,0:T(8,128)(2,1)} copy(bf16[128,8,8,512]{3,1,2,0:T(8,128)(2,1)} %bitcast.773) | data formatting | bytes 16777216
  578.6 9.9 %copy.654 = bf16[4,256,8,512]{3,1,2,0:T(8,128)(2,1)} copy(bf16[4,256,8,512]{3,2,1,0:T(8,128)(2,1)} %bitcast.786) | data formatting | bytes 16777216 | tf_op jit(solution)/shard_map/reshape | solution.py:150
  588.5 4.3 dynamic-slice_bitcast_fusion.3
  621.4 5.4 collective-permute-done.71
  667.2 9.3 %collective-permute-done.127 = bf16[8,94,128]{2,1,0:T(8,128)(2,1)S(1)} collective-permute-done((bf16[8,94,128]{2,1,0:T(8,128)(2,1)}, bf16[8,94,128]{2,1,0:T(8,128)(2,1)S(1)}, u32[]{:S(2)}, u32[]{:S(2)}) %collective-permute-start.127) | collective-permute-done | bytes 192544 | tf_op jit(solution)/shard_map/ppermute | solution.py:55
  682.5 4.1 collective-permute-done.128
  698.5 14.2 %collective-permute-start.101 = (bf16[4,256,512]{2,1,0:T(8,128)(2,1)S(1)}, bf16[4,256,512]{2,1,0:T(8,128)(2,1)S(1)}, u32[]{:S(2)}, u32[]{:S(2)}) collective-permute-start(bf16[4,256,512]{2,1,0:T(8,128)(2,1)S(1)} %copy-done.61), channel_id=1, source_target_pairs={{0,8},{8,0},{1,9},{9,1},{2,10},{10,2},{3,11},{11,3},{4,12},{12,4},... | collective-permute-start | bytes 3145736 | tf_op jit(solution)/shard_map/ppermute | solution.py:55
  717.6 9.0 %collective-permute-done.83 = bf16[4,1024,128]{2,1,0:T(8,128)(2,1)S(1)} collective-permute-done((bf16[4,1024,128]{2,1,0:T(8,128)(2,1)S(1)}, bf16[4,1024,128]{2,1,0:T(8,128)(2,1)S(1)}, u32[]{:S(2)}, u32[]{:S(2)}) %collective-permute-start.83) | collective-permute-done | bytes 1048608 | tf_op jit(solution)/shard_map/ppermute | solution.py:52
  726.5 6.7 collective-permute-done.87
  735.9 13.1 %collective-permute-done.103 = bf16[4,256,512]{2,1,0:T(8,128)(2,1)S(1)} collective-permute-done((bf16[4,256,512]{2,1,0:T(8,128)(2,1)S(1)}, bf16[4,256,512]{2,1,0:T(8,128)(2,1)S(1)}, u32[]{:S(2)}, u32[]{:S(2)}) %collective-permute-start.103) | collective-permute-done | bytes 1048608 | tf_op jit(solution)/shard_map/ppermute | solution.py:52
  750.5 5.2 collective-permute-done.107
  760.6 24.3 %collective-permute-done.89 = bf16[1024,128]{1,0:T(8,128)(2,1)S(1)} collective-permute-done((bf16[1024,128]{1,0:T(8,128)(2,1)S(1)}, bf16[1024,128]{1,0:T(8,128)(2,1)S(1)}, u32[]{:S(2)}, u32[]{:S(2)}) %collective-permute-start.89) | collective-permute-done | bytes 262176 | tf_op jit(solution)/shard_map/ppermute | solution.py:138
  786.2 4.4 collective-permute-done.99
  793.7 13.7 %collective-permute-done.109 = bf16[256,512]{1,0:T(8,128)(2,1)S(1)} collective-permute-done((bf16[256,512]{1,0:T(8,128)(2,1)S(1)}, bf16[256,512]{1,0:T(8,128)(2,1)S(1)}, u32[]{:S(2)}, u32[]{:S(2)}) %collective-permute-start.109) | collective-permute-done | bytes 262176 | tf_op jit(solution)/shard_map/ppermute | solution.py:138
  834.4 4.1 fusion.178
  (810 shorter events, 420.5 us)
Async XLA Ops:
  1.4 53.0 %collective-permute-start.48 = (bf16[256,24]{0,1:T(8,128)(2,1)S(1)}, bf16[256,24]{0,1:T(8,128)(2,1)S(1)}, u32[]{:S(2)}, u32[]{:S(2)}) collective-permute-start(bf16[256,24]{0,1:T(8,128)(2,1)S(1)} %get-tuple-element.52), channel_id=1, source_target_pairs={{0,4},{2,6},{4,0},{6,2},{1,5},{3,7},{5,1},{7,3},{8,12},{10,14},{12... | collective-permute-start | bytes 36872 | tf_op jit(solution)/shard_map/ppermute | solution.py:91
  5.5 45.5 %collective-permute-start.47 = (bf16[256,24]{0,1:T(8,128)(2,1)S(1)}, bf16[256,24]{0,1:T(8,128)(2,1)S(1)}, u32[]{:S(2)}, u32[]{:S(2)}) collective-permute-start(bf16[256,24]{0,1:T(8,128)(2,1)S(1)} %get-tuple-element.52), channel_id=1, source_target_pairs={{0,2},{2,4},{4,6},{6,0},{1,3},{3,5},{5,7},{7,1},{8,10},{10,12},{12... | collective-permute-start | bytes 36872 | tf_op jit(solution)/shard_map/ppermute | solution.py:91
  7.0 47.4 %collective-permute-start.49 = (bf16[256,24]{0,1:T(8,128)(2,1)S(1)}, bf16[256,24]{0,1:T(8,128)(2,1)S(1)}, u32[]{:S(2)}, u32[]{:S(2)}) collective-permute-start(bf16[256,24]{0,1:T(8,128)(2,1)S(1)} %get-tuple-element.52), channel_id=1, source_target_pairs={{0,6},{2,0},{4,2},{6,4},{1,7},{3,1},{5,3},{7,5},{8,14},{10,8},{12,... | collective-permute-start | bytes 36872 | tf_op jit(solution)/shard_map/ppermute | solution.py:91
  14.9 45.6 %all-to-all-start = ((bf16[2,4,128,48]{2,3,0,1:T(8,128)(2,1)}), bf16[2,4,128,48]{2,3,0,1:T(8,128)(2,1)S(1)}, u32[]{:S(2)}, u32[]{:S(2)}) async-start(bf16[2,4,128,48]{2,3,0,1:T(8,128)(2,1)} %bitcast.764), calls=%async_computation | async-start | bytes 196608 | tf_op jit(solution)/shard_map/all_to_all | solution.py:266
  21.1 51.0 %collective-permute-start.1 = (bf16[608,128]{1,0:T(8,128)(2,1)}, bf16[608,128]{1,0:T(8,128)(2,1)}, u32[]{:S(2)}, u32[]{:S(2)}) collective-permute-start(bf16[608,128]{1,0:T(8,128)(2,1)} %fusion.112), channel_id=1, source_target_pairs={{0,4},{2,6},{4,0},{6,2},{1,5},{3,7},{5,1},{7,3},{8,12},{10,14},{12... | collective-permute-start | bytes 466952 | tf_op jit(solution)/shard_map/ppermute | solution.py:91
  62.7 81.0 %collective-permute-start.19 = (bf16[1024,128]{1,0:T(8,128)(2,1)S(1)}, bf16[1024,128]{1,0:T(8,128)(2,1)S(1)}, u32[]{:S(2)}, u32[]{:S(2)}) collective-permute-start(bf16[1024,128]{1,0:T(8,128)(2,1)S(1)} %bitcast.859), channel_id=1, source_target_pairs={{0,6},{2,0},{4,2},{6,4},{1,7},{3,1},{5,3},{7,5},{8,14},{10,8},{12,... | collective-permute-start | bytes 786440 | tf_op jit(solution)/shard_map/ppermute | solution.py:91
  68.4 67.8 %collective-permute-start.18 = (bf16[1024,128]{1,0:T(8,128)(2,1)S(1)}, bf16[1024,128]{1,0:T(8,128)(2,1)S(1)}, u32[]{:S(2)}, u32[]{:S(2)}) collective-permute-start(bf16[1024,128]{1,0:T(8,128)(2,1)S(1)} %bitcast.860), channel_id=1, source_target_pairs={{0,4},{2,6},{4,0},{6,2},{1,5},{3,7},{5,1},{7,3},{8,12},{10,14},{12... | collective-permute-start | bytes 786440 | tf_op jit(solution)/shard_map/ppermute | solution.py:91
  69.1 66.4 %collective-permute-start.17 = (bf16[1024,128]{1,0:T(8,128)(2,1)S(1)}, bf16[1024,128]{1,0:T(8,128)(2,1)S(1)}, u32[]{:S(2)}, u32[]{:S(2)}) collective-permute-start(bf16[1024,128]{1,0:T(8,128)(2,1)S(1)} %bitcast.861), channel_id=1, source_target_pairs={{0,2},{2,4},{4,6},{6,0},{1,3},{3,5},{5,7},{7,1},{8,10},{10,12},{12... | collective-permute-start | bytes 786440 | tf_op jit(solution)/shard_map/ppermute | solution.py:91
  75.2 29.8 %collective-permute-start.38 = (bf16[256,512]{1,0:T(8,128)(2,1)S(1)}, bf16[256,512]{1,0:T(8,128)(2,1)S(1)}, u32[]{:S(2)}, u32[]{:S(2)}) collective-permute-start(bf16[256,512]{1,0:T(8,128)(2,1)S(1)} %get-tuple-element.109), channel_id=1, source_target_pairs={{0,4},{2,6},{4,0},{6,2},{1,5},{3,7},{5,1},{7,3},{8,12},{10,14},{12... | collective-permute-start | bytes 786440 | tf_op jit(solution)/shard_map/ppermute | solution.py:91
  130.3 33.3 %collective-permute-start.6 = (bf16[4,608,128]{2,1,0:T(8,128)(2,1)S(1)}, bf16[4,608,128]{2,1,0:T(8,128)(2,1)S(1)}, u32[]{:S(2)}, u32[]{:S(2)}) collective-permute-start(bf16[4,608,128]{2,1,0:T(8,128)(2,1)S(1)} %bitcast_dynamic-update-slice_fusion.48), channel_id=1, source_target_pairs={{0,16},{1,17},{2,18},{3,19},{4,20},{5,21},{6,22},{7,23},{8,9},{9,8... | collective-permute-start | bytes 1867784 | tf_op jit(solution)/shard_map/ppermute | solution.py:52
  133.0 27.2 %collective-permute-start.4 = (bf16[4,608,128]{2,1,0:T(8,128)(2,1)S(1)}, bf16[4,608,128]{2,1,0:T(8,128)(2,1)S(1)}, u32[]{:S(2)}, u32[]{:S(2)}) collective-permute-start(bf16[4,608,128]{2,1,0:T(8,128)(2,1)S(1)} %bitcast_dynamic-update-slice_fusion.48), channel_id=1, source_target_pairs={{0,1},{1,0},{2,3},{3,2},{4,5},{5,4},{6,7},{7,6},{8,24},{9,25},{10,... | collective-permute-start | bytes 1867784 | tf_op jit(solution)/shard_map/ppermute | solution.py:52
  135.5 25.0 %collective-permute-start.3 = (bf16[4,608,128]{2,1,0:T(8,128)(2,1)S(1)}, bf16[4,608,128]{2,1,0:T(8,128)(2,1)S(1)}, u32[]{:S(2)}, u32[]{:S(2)}) collective-permute-start(bf16[4,608,128]{2,1,0:T(8,128)(2,1)S(1)} %bitcast_dynamic-update-slice_fusion.48), channel_id=1, source_target_pairs={{0,8},{8,0},{1,9},{9,1},{2,10},{10,2},{3,11},{11,3},{4,12},{12,4},... | collective-permute-start | bytes 1867784 | tf_op jit(solution)/shard_map/ppermute | solution.py:55
  136.2 27.7 %collective-permute-start.41 = (bf16[4,256,512]{2,1,0:T(8,128)(2,1)}, bf16[4,256,512]{2,1,0:T(8,128)(2,1)S(1)}, u32[]{:S(2)}, u32[]{:S(2)}) collective-permute-start(bf16[4,256,512]{2,1,0:T(8,128)(2,1)} %bitcast_dynamic-update-slice_fusion.38), channel_id=1, source_target_pairs={{0,1},{1,0},{2,3},{3,2},{4,5},{5,4},{6,7},{7,6},{8,24},{9,25},{10,... | collective-permute-start | bytes 3145736 | tf_op jit(solution)/shard_map/ppermute | solution.py:52
  160.7 101.6 %collective-permute-start.23 = (bf16[4,1024,128]{2,1,0:T(8,128)(2,1)}, bf16[4,1024,128]{2,1,0:T(8,128)(2,1)}, u32[]{:S(2)}, u32[]{:S(2)}) collective-permute-start(bf16[4,1024,128]{2,1,0:T(8,128)(2,1)} %bitcast_dynamic-update-slice_fusion.44), channel_id=1, source_target_pairs={{0,16},{1,17},{2,18},{3,19},{4,20},{5,21},{6,22},{7,23},{8,9},{9,8... | collective-permute-start | bytes 3145736 | tf_op jit(solution)/shard_map/ppermute | solution.py:52
  163.6 54.1 %collective-permute-start.21 = (bf16[4,1024,128]{2,1,0:T(8,128)(2,1)}, bf16[4,1024,128]{2,1,0:T(8,128)(2,1)S(1)}, u32[]{:S(2)}, u32[]{:S(2)}) collective-permute-start(bf16[4,1024,128]{2,1,0:T(8,128)(2,1)} %bitcast_dynamic-update-slice_fusion.44), channel_id=1, source_target_pairs={{0,1},{1,0},{2,3},{3,2},{4,5},{5,4},{6,7},{7,6},{8,24},{9,25},{10,... | collective-permute-start | bytes 3145736 | tf_op jit(solution)/shard_map/ppermute | solution.py:52
  174.5 37.8 %collective-permute-start.20 = (bf16[4,1024,128]{2,1,0:T(8,128)(2,1)}, bf16[4,1024,128]{2,1,0:T(8,128)(2,1)S(1)}, u32[]{:S(2)}, u32[]{:S(2)}) collective-permute-start(bf16[4,1024,128]{2,1,0:T(8,128)(2,1)} %bitcast_dynamic-update-slice_fusion.44), channel_id=1, source_target_pairs={{0,8},{8,0},{1,9},{9,1},{2,10},{10,2},{3,11},{11,3},{4,12},{12,4},... | collective-permute-start | bytes 3145736 | tf_op jit(solution)/shard_map/ppermute | solution.py:55
  178.5 24.8 %collective-permute-start.31 = (bf16[4,256,512]{2,1,0:T(8,128)(2,1)}, bf16[4,256,512]{2,1,0:T(8,128)(2,1)}, u32[]{:S(2)}, u32[]{:S(2)}) collective-permute-start(bf16[4,256,512]{2,1,0:T(8,128)(2,1)} %bitcast_dynamic-update-slice_fusion.41), channel_id=1, source_target_pairs={{0,1},{1,0},{2,3},{3,2},{4,5},{5,4},{6,7},{7,6},{8,24},{9,25},{10,... | collective-permute-start | bytes 3145736 | tf_op jit(solution)/shard_map/ppermute | solution.py:52
  197.0 65.8 %collective-permute-start.33 = (bf16[4,256,512]{2,1,0:T(8,128)(2,1)}, bf16[4,256,512]{2,1,0:T(8,128)(2,1)}, u32[]{:S(2)}, u32[]{:S(2)}) collective-permute-start(bf16[4,256,512]{2,1,0:T(8,128)(2,1)} %bitcast_dynamic-update-slice_fusion.41), channel_id=1, source_target_pairs={{0,16},{1,17},{2,18},{3,19},{4,20},{5,21},{6,22},{7,23},{8,9},{9,8... | collective-permute-start | bytes 3145736 | tf_op jit(solution)/shard_map/ppermute | solution.py:52
  210.2 45.8 %collective-permute-start.43 = (bf16[4,256,512]{2,1,0:T(8,128)(2,1)}, bf16[4,256,512]{2,1,0:T(8,128)(2,1)}, u32[]{:S(2)}, u32[]{:S(2)}) collective-permute-start(bf16[4,256,512]{2,1,0:T(8,128)(2,1)} %bitcast_dynamic-update-slice_fusion.38), channel_id=1, source_target_pairs={{0,16},{1,17},{2,18},{3,19},{4,20},{5,21},{6,22},{7,23},{8,9},{9,8... | collective-permute-start | bytes 3145736 | tf_op jit(solution)/shard_map/ppermute | solution.py:52
  217.7 46.6 %collective-permute-start.32 = (bf16[4,256,512]{2,1,0:T(8,128)(2,1)}, bf16[4,256,512]{2,1,0:T(8,128)(2,1)}, u32[]{:S(2)}, u32[]{:S(2)}) collective-permute-start(bf16[4,256,512]{2,1,0:T(8,128)(2,1)} %collective-permute-done.31), channel_id=1, source_target_pairs={{0,8},{8,0},{1,9},{9,1},{2,10},{10,2},{3,11},{11,3},{4,12},{12,4},... | collective-permute-start | bytes 3145736 | tf_op jit(solution)/shard_map/ppermute | solution.py:55
  262.9 30.5 %collective-permute-start.35 = (bf16[4,256,512]{2,1,0:T(8,128)(2,1)}, bf16[4,256,512]{2,1,0:T(8,128)(2,1)S(1)}, u32[]{:S(2)}, u32[]{:S(2)}) collective-permute-start(bf16[4,256,512]{2,1,0:T(8,128)(2,1)} %collective-permute-done.31), channel_id=1, source_target_pairs={{0,16},{1,17},{2,18},{3,19},{4,20},{5,21},{6,22},{7,23},{8,9},{9,8... | collective-permute-start | bytes 3145736 | tf_op jit(solution)/shard_map/ppermute | solution.py:52
  268.9 26.6 %collective-permute-start.22 = (bf16[4,1024,128]{2,1,0:T(8,128)(2,1)S(1)}, bf16[4,1024,128]{2,1,0:T(8,128)(2,1)S(1)}, u32[]{:S(2)}, u32[]{:S(2)}) collective-permute-start(bf16[4,1024,128]{2,1,0:T(8,128)(2,1)S(1)} %copy-done.56), channel_id=1, source_target_pairs={{0,8},{8,0},{1,9},{9,1},{2,10},{10,2},{3,11},{11,3},{4,12},{12,4},... | collective-permute-start | bytes 3145736 | tf_op jit(solution)/shard_map/ppermute | solution.py:55
  270.9 28.2 %collective-permute-start.24 = (bf16[4,1024,128]{2,1,0:T(8,128)(2,1)}, bf16[4,1024,128]{2,1,0:T(8,128)(2,1)S(1)}, u32[]{:S(2)}, u32[]{:S(2)}) collective-permute-start(bf16[4,1024,128]{2,1,0:T(8,128)(2,1)} %collective-permute-done.23), channel_id=1, source_target_pairs={{0,8},{8,0},{1,9},{9,1},{2,10},{10,2},{3,11},{11,3},{4,12},{12,4},... | collective-permute-start | bytes 3145736 | tf_op jit(solution)/shard_map/ppermute | solution.py:55
  282.2 68.5 %collective-permute-start.26 = (bf16[4,1024,128]{2,1,0:T(8,128)(2,1)S(1)}, bf16[4,1024,128]{2,1,0:T(8,128)(2,1)S(1)}, u32[]{:S(2)}, u32[]{:S(2)}) collective-permute-start(bf16[4,1024,128]{2,1,0:T(8,128)(2,1)S(1)} %collective-permute-done.25), channel_id=1, source_target_pairs={{0,8},{8,0},{1,9},{9,1},{2,10},{10,2},{3,11},{11,3},{4,12},{12,4},... | collective-permute-start | bytes 3145736 | tf_op jit(solution)/shard_map/ppermute | solution.py:55
  462.3 153.6 %collective-permute-start.111 = (bf16[4,256,24]{1,2,0:T(8,128)(2,1)}, bf16[4,256,24]{1,2,0:T(8,128)(2,1)}, u32[]{:S(2)}, u32[]{:S(2)}) collective-permute-start(bf16[4,256,24]{1,2,0:T(8,128)(2,1)} %get-tuple-element.116), channel_id=1, source_target_pairs={{0,8},{8,0},{1,9},{9,1},{2,10},{10,2},{3,11},{11,3},{4,12},{12,4},... | collective-permute-start | bytes 147464 | tf_op jit(solution)/shard_map/ppermute | solution.py:55
  462.8 137.5 %collective-permute-start.115 = (bf16[4,256,24]{1,2,0:T(8,128)(2,1)}, bf16[4,256,24]{1,2,0:T(8,128)(2,1)}, u32[]{:S(2)}, u32[]{:S(2)}) collective-permute-start(bf16[4,256,24]{1,2,0:T(8,128)(2,1)} %get-tuple-element.119), channel_id=1, source_target_pairs={{0,8},{8,0},{1,9},{9,1},{2,10},{10,2},{3,11},{11,3},{4,12},{12,4},... | collective-permute-start | bytes 147464 | tf_op jit(solution)/shard_map/ppermute | solution.py:55
  472.3 31.5 %collective-permute-start.62 = (f32[368,16]{0,1:T(8,128)S(1)}, f32[368,16]{0,1:T(8,128)S(1)}, u32[]{:S(2)}, u32[]{:S(2)}) collective-permute-start(f32[368,16]{0,1:T(8,128)S(1)} %pad_maximum_fusion.18), channel_id=1, source_target_pairs={{0,16},{16,0},{1,17},{17,1},{2,18},{18,2},{3,19},{19,3},{4,20},{20... | collective-permute-start | bytes 70664 | tf_op jit(solution)/shard_map/ppermute | solution.py:55
  505.3 98.3 %collective-permute-start.114 = (bf16[4,256,24]{1,2,0:T(8,128)(2,1)}, bf16[4,256,24]{1,2,0:T(8,128)(2,1)}, u32[]{:S(2)}, u32[]{:S(2)}) collective-permute-start(bf16[4,256,24]{1,2,0:T(8,128)(2,1)} %get-tuple-element.117), channel_id=1, source_target_pairs={{0,8},{8,0},{1,9},{9,1},{2,10},{10,2},{3,11},{11,3},{4,12},{12,4},... | collective-permute-start | bytes 147464 | tf_op jit(solution)/shard_map/ppermute | solution.py:55
  505.7 94.4 %collective-permute-start.112 = (bf16[4,256,24]{1,2,0:T(8,128)(2,1)}, bf16[4,256,24]{1,2,0:T(8,128)(2,1)}, u32[]{:S(2)}, u32[]{:S(2)}) collective-permute-start(bf16[4,256,24]{1,2,0:T(8,128)(2,1)} %get-tuple-element.118), channel_id=1, source_target_pairs={{0,8},{8,0},{1,9},{9,1},{2,10},{10,2},{3,11},{11,3},{4,12},{12,4},... | collective-permute-start | bytes 147464 | tf_op jit(solution)/shard_map/ppermute | solution.py:55
  534.2 23.2 %collective-permute-start.66 = (f32[368,16]{0,1:T(8,128)S(1)}, f32[368,16]{0,1:T(8,128)S(1)}, u32[]{:S(2)}, u32[]{:S(2)}) collective-permute-start(f32[368,16]{0,1:T(8,128)S(1)} %add.967), channel_id=1, source_target_pairs={{0,1},{1,0},{2,3},{3,2},{4,5},{5,4},{6,7},{7,6},{8,9},{9,8},{10,11... | collective-permute-start | bytes 70664 | tf_op jit(solution)/shard_map/ppermute | solution.py:55
  560.3 28.2 %collective-permute-start.67 = (f32[128]{0:T(128)S(1)}, f32[128]{0:T(128)S(1)}, u32[]{:S(2)}, u32[]{:S(2)}) collective-permute-start(f32[128]{0:T(128)S(1)} %broadcast_multiply_fusion.2), channel_id=1, source_target_pairs={{0,16},{16,0},{1,17},{17,1},{2,18},{18,2},{3,19},{19,3},{4,20},{20... | collective-permute-start | bytes 1544 | tf_op jit(solution)/shard_map/ppermute | solution.py:55
  620.0 24.4 %collective-permute-start.92 = (bf16[4,256,512]{2,1,0:T(8,128)(2,1)S(1)}, bf16[4,256,512]{2,1,0:T(8,128)(2,1)S(1)}, u32[]{:S(2)}, u32[]{:S(2)}) collective-permute-start(bf16[4,256,512]{2,1,0:T(8,128)(2,1)S(1)} %copy-done.65), channel_id=1, source_target_pairs={{0,8},{8,0},{1,9},{9,1},{2,10},{10,2},{3,11},{11,3},{4,12},{12,4},... | collective-permute-start | bytes 3145736 | tf_op jit(solution)/shard_map/ppermute | solution.py:55
  620.1 25.0 %collective-permute-start.95 = (bf16[4,256,512]{2,1,0:T(8,128)(2,1)S(1)}, bf16[4,256,512]{2,1,0:T(8,128)(2,1)S(1)}, u32[]{:S(2)}, u32[]{:S(2)}) collective-permute-start(bf16[4,256,512]{2,1,0:T(8,128)(2,1)S(1)} %copy-done.64), channel_id=1, source_target_pairs={{0,8},{8,0},{1,9},{9,1},{2,10},{10,2},{3,11},{11,3},{4,12},{12,4},... | collective-permute-start | bytes 3145736 | tf_op jit(solution)/shard_map/ppermute | solution.py:55
  658.7 23.7 %collective-permute-start.84 = (bf16[4,1024,128]{2,1,0:T(8,128)(2,1)}, bf16[4,1024,128]{2,1,0:T(8,128)(2,1)}, u32[]{:S(2)}, u32[]{:S(2)}) collective-permute-start(bf16[4,1024,128]{2,1,0:T(8,128)(2,1)} %bitcast.759), channel_id=1, source_target_pairs={{0,8},{8,0},{1,9},{9,1},{2,10},{10,2},{3,11},{11,3},{4,12},{12,4},... | collective-permute-start | bytes 3145736 | tf_op jit(solution)/shard_map/ppermute | solution.py:55
  660.3 27.2 %collective-permute-start.86 = (bf16[4,1024,128]{2,1,0:T(8,128)(2,1)}, bf16[4,1024,128]{2,1,0:T(8,128)(2,1)}, u32[]{:S(2)}, u32[]{:S(2)}) collective-permute-start(bf16[4,1024,128]{2,1,0:T(8,128)(2,1)} %fusion.27), channel_id=1, source_target_pairs={{0,16},{1,17},{2,18},{3,19},{4,20},{5,21},{6,22},{7,23},{8,9},{9,8... | collective-permute-start | bytes 3145736 | tf_op jit(solution)/shard_map/ppermute | solution.py:52
  667.2 23.9 %collective-permute-start.102 = (bf16[4,256,512]{2,1,0:T(8,128)(2,1)}, bf16[4,256,512]{2,1,0:T(8,128)(2,1)S(1)}, u32[]{:S(2)}, u32[]{:S(2)}) collective-permute-start(bf16[4,256,512]{2,1,0:T(8,128)(2,1)} %get-tuple-element.65), channel_id=1, source_target_pairs={{0,8},{8,0},{1,9},{9,1},{2,10},{10,2},{3,11},{11,3},{4,12},{12,4},... | collective-permute-start | bytes 3145736 | tf_op jit(solution)/shard_map/ppermute | solution.py:55
  686.6 26.1 %collective-permute-start.93 = (bf16[4,256,512]{2,1,0:T(8,128)(2,1)S(1)}, bf16[4,256,512]{2,1,0:T(8,128)(2,1)S(1)}, u32[]{:S(2)}, u32[]{:S(2)}) collective-permute-start(bf16[4,256,512]{2,1,0:T(8,128)(2,1)S(1)} %copy-done.59), channel_id=1, source_target_pairs={{0,16},{1,17},{2,18},{3,19},{4,20},{5,21},{6,22},{7,23},{8,9},{9,8... | collective-permute-start | bytes 3145736 | tf_op jit(solution)/shard_map/ppermute | solution.py:52
  687.5 26.1 %collective-permute-start.97 = (bf16[4,256,512]{2,1,0:T(8,128)(2,1)S(1)}, bf16[4,256,512]{2,1,0:T(8,128)(2,1)S(1)}, u32[]{:S(2)}, u32[]{:S(2)}) collective-permute-start(bf16[4,256,512]{2,1,0:T(8,128)(2,1)S(1)} %add_convert_fusion.5), channel_id=1, source_target_pairs={{0,1},{1,0},{2,3},{3,2},{4,5},{5,4},{6,7},{7,6},{8,24},{9,25},{10,... | collective-permute-start | bytes 3145736 | tf_op jit(solution)/shard_map/ppermute | solution.py:52
  691.1 35.4 %collective-permute-start.83 = (bf16[4,1024,128]{2,1,0:T(8,128)(2,1)S(1)}, bf16[4,1024,128]{2,1,0:T(8,128)(2,1)S(1)}, u32[]{:S(2)}, u32[]{:S(2)}) collective-permute-start(bf16[4,1024,128]{2,1,0:T(8,128)(2,1)S(1)} %copy-done.60), channel_id=1, source_target_pairs={{0,16},{1,17},{2,18},{3,19},{4,20},{5,21},{6,22},{7,23},{8,9},{9,8... | collective-permute-start | bytes 3145736 | tf_op jit(solution)/shard_map/ppermute | solution.py:52
  694.0 39.3 %collective-permute-start.87 = (bf16[4,1024,128]{2,1,0:T(8,128)(2,1)S(1)}, bf16[4,1024,128]{2,1,0:T(8,128)(2,1)S(1)}, u32[]{:S(2)}, u32[]{:S(2)}) collective-permute-start(bf16[4,1024,128]{2,1,0:T(8,128)(2,1)S(1)} %add_convert_fusion.8), channel_id=1, source_target_pairs={{0,1},{1,0},{2,3},{3,2},{4,5},{5,4},{6,7},{7,6},{8,24},{9,25},{10,... | collective-permute-start | bytes 3145736 | tf_op jit(solution)/shard_map/ppermute | solution.py:52
  698.5 36.9 %collective-permute-start.101 = (bf16[4,256,512]{2,1,0:T(8,128)(2,1)S(1)}, bf16[4,256,512]{2,1,0:T(8,128)(2,1)S(1)}, u32[]{:S(2)}, u32[]{:S(2)}) collective-permute-start(bf16[4,256,512]{2,1,0:T(8,128)(2,1)S(1)} %copy-done.61), channel_id=1, source_target_pairs={{0,8},{8,0},{1,9},{9,1},{2,10},{10,2},{3,11},{11,3},{4,12},{12,4},... | collective-permute-start | bytes 3145736 | tf_op jit(solution)/shard_map/ppermute | solution.py:55
  712.7 36.3 %collective-permute-start.103 = (bf16[4,256,512]{2,1,0:T(8,128)(2,1)S(1)}, bf16[4,256,512]{2,1,0:T(8,128)(2,1)S(1)}, u32[]{:S(2)}, u32[]{:S(2)}) collective-permute-start(bf16[4,256,512]{2,1,0:T(8,128)(2,1)S(1)} %get-tuple-element.67), channel_id=1, source_target_pairs={{0,16},{1,17},{2,18},{3,19},{4,20},{5,21},{6,22},{7,23},{8,9},{9,8... | collective-permute-start | bytes 3145736 | tf_op jit(solution)/shard_map/ppermute | solution.py:52
  713.6 42.1 %collective-permute-start.107 = (bf16[4,256,512]{2,1,0:T(8,128)(2,1)S(1)}, bf16[4,256,512]{2,1,0:T(8,128)(2,1)S(1)}, u32[]{:S(2)}, u32[]{:S(2)}) collective-permute-start(bf16[4,256,512]{2,1,0:T(8,128)(2,1)S(1)} %get-tuple-element.68), channel_id=1, source_target_pairs={{0,1},{1,0},{2,3},{3,2},{4,5},{5,4},{6,7},{7,6},{8,24},{9,25},{10,... | collective-permute-start | bytes 3145736 | tf_op jit(solution)/shard_map/ppermute | solution.py:52
  726.5 58.7 %collective-permute-start.98 = (bf16[256,512]{1,0:T(8,128)(2,1)S(1)}, bf16[256,512]{1,0:T(8,128)(2,1)S(1)}, u32[]{:S(2)}, u32[]{:S(2)}) collective-permute-start(bf16[256,512]{1,0:T(8,128)(2,1)S(1)} %get-tuple-element.95), channel_id=1, source_target_pairs={{0,2},{2,4},{4,6},{6,0},{1,3},{3,5},{5,7},{7,1},{8,10},{10,12},{12... | collective-permute-start | bytes 786440 | tf_op jit(solution)/shard_map/ppermute | solution.py:138
  733.3 53.0 %collective-permute-start.100 = (bf16[256,512]{1,0:T(8,128)(2,1)S(1)}, bf16[256,512]{1,0:T(8,128)(2,1)S(1)}, u32[]{:S(2)}, u32[]{:S(2)}) collective-permute-start(bf16[256,512]{1,0:T(8,128)(2,1)S(1)} %get-tuple-element.96), channel_id=1, source_target_pairs={{0,6},{2,0},{4,2},{6,4},{1,7},{3,1},{5,3},{7,5},{8,14},{10,8},{12,... | collective-permute-start | bytes 786440 | tf_op jit(solution)/shard_map/ppermute | solution.py:138
  755.7 29.2 %collective-permute-start.89 = (bf16[1024,128]{1,0:T(8,128)(2,1)S(1)}, bf16[1024,128]{1,0:T(8,128)(2,1)S(1)}, u32[]{:S(2)}, u32[]{:S(2)}) collective-permute-start(bf16[1024,128]{1,0:T(8,128)(2,1)S(1)} %get-tuple-element.103), channel_id=1, source_target_pairs={{0,4},{2,6},{4,0},{6,2},{1,5},{3,7},{5,1},{7,3},{8,12},{10,14},{12... | collective-permute-start | bytes 786440 | tf_op jit(solution)/shard_map/ppermute | solution.py:138
  757.7 33.0 %collective-permute-start.99 = (bf16[256,512]{1,0:T(8,128)(2,1)S(1)}, bf16[256,512]{1,0:T(8,128)(2,1)S(1)}, u32[]{:S(2)}, u32[]{:S(2)}) collective-permute-start(bf16[256,512]{1,0:T(8,128)(2,1)S(1)} %get-tuple-element.97), channel_id=1, source_target_pairs={{0,4},{2,6},{4,0},{6,2},{1,5},{3,7},{5,1},{7,3},{8,12},{10,14},{12... | collective-permute-start | bytes 786440 | tf_op jit(solution)/shard_map/ppermute | solution.py:138
  760.6 30.1 %collective-permute-start.108 = (bf16[256,512]{1,0:T(8,128)(2,1)S(1)}, bf16[256,512]{1,0:T(8,128)(2,1)S(1)}, u32[]{:S(2)}, u32[]{:S(2)}) collective-permute-start(bf16[256,512]{1,0:T(8,128)(2,1)S(1)} %get-tuple-element.98), channel_id=1, source_target_pairs={{0,2},{2,4},{4,6},{6,0},{1,3},{3,5},{5,7},{7,1},{8,10},{10,12},{12... | collective-permute-start | bytes 786440 | tf_op jit(solution)/shard_map/ppermute | solution.py:138
  (203 other events, 2694.8 us)

commit v2 on v1

--- a/solution.py
+++ b/solution.py
@@ -2,7 +2,10 @@
 
 import jax
 import jax.numpy as jnp
+import numpy as np
 from jax import lax
+from jax.experimental import pallas as pl
+from jax.experimental.pallas import tpu as pltpu
 from jax.sharding import Mesh
 from jax.sharding import PartitionSpec as P
 
@@ -33,7 +36,7 @@
         self.sizes = {"y": nv // 2, "c": 2, "z": npatch // 2, "x": 2}
         self.mesh = Mesh(mesh.devices.reshape(tuple(self.sizes.values())), AXES)
         self.nv, self.np = nv, npatch
-        self.fast = self.sizes["y"] == 2
+        self.fast = self.sizes["y"] == 2 and self.sizes["z"] == 4
 
     def flat(self, move):
         s = [self.sizes[a] for a in AXES]
@@ -76,68 +79,57 @@
 
         return move
 
-    def flips(self, core, a, b):
-        return jnp.where(core == 0, a, b), jnp.where(core == 0, b, a)
-
     def gather(self, piece):
-        rows, w = piece.shape
-        if not self.fast:
-            return lax.all_gather(piece, AXES).reshape(self.nv, self.np, rows, w)
-        nz = self.sizes["z"]
-        y, c, z, x = (lax.axis_index(a) for a in AXES)
-        line = jnp.zeros((nz, rows, w), piece.dtype)
-        line = lax.dynamic_update_index_in_dim(line, piece, z, 0)
-        for k in range(1, nz):
-            got = lax.ppermute(piece, "z", [(i, (i + k) % nz) for i in range(nz)])
-            line = lax.dynamic_update_index_in_dim(line, got, (z - k) % nz, 0)
-        near = self.permute(line, self.along(False))
-        far = [self.permute(v, self.along(True)) for v in (line, near)]
-        mine = [[line, near], far]
-        out = jnp.zeros((2, 2, nz, 2, rows, w), piece.dtype)
-        for a in range(2):
-            for b in range(2):
-                fy, fx = self.flips(c, a, b)
-                out = lax.dynamic_update_slice(
-                    out, mine[a][b][None, None, :, None], (y ^ fy, c, 0, x ^ fx, 0, 0)
-                )
-                got = self.swap(mine[a][b], "c")
-                fy, fx = self.flips(1 - c, a, b)
-                out = lax.dynamic_update_slice(
-                    out, got[None, None, :, None], (y ^ fy, 1 - c, 0, x ^ fx, 0, 0)
-                )
-        return out.reshape(self.nv, self.np, rows, w)
+        return lax.all_gather(piece, AXES).reshape(self.nv, self.np, *piece.shape)
 
     def scatter(self, parts):
         nv, npatch, rows, w = parts.shape
-        if not self.fast:
-            flat = parts.reshape(nv * npatch * rows, w)
-            return lax.psum_scatter(flat, AXES, scatter_dimension=0, tiled=True).astype(F32)
-        nz = self.sizes["z"]
-        y, c, z, x = (lax.axis_index(a) for a in AXES)
-        cut = parts.reshape(2, 2, nz, 2, rows, w)
-
-        def pick(core, a, b):
-            fy, fx = self.flips(core, a, b)
-            got = lax.dynamic_slice(
-                cut, (y ^ fy, core, 0, x ^ fx, 0, 0), (1, 1, nz, 1, rows, w)
-            )
-            return got.reshape(nz, rows, w)
+        flat = parts.reshape(nv * npatch * rows, w)
+        return lax.psum_scatter(flat, AXES, scatter_dimension=0, tiled=True).astype(F32)
+
+    def gate(self, values, before):
+        return lax.optimization_barrier((values, before))[0] if before else values
+
+    def hop(self, value, *steps):
+        for axis, bit in steps:
+            value = value + self.swap(value, axis, bit)
+        return value
+
+    def begin(self, before, *moves):
+        operands = self.gate([v for _, v in moves], before)
+        return [fn(v) for (fn, _), v in zip(moves, operands)]
+
+    def far_z(self, piece):
+        return self.swap(piece, "z", 2)
+
+    def next_z(self, pair):
+        return self.swap(pair, "z", 1)
+
+    def near(self, line):
+        return self.permute(line, self.along(False))
+
+    def far(self, both):
+        return self.permute(both, self.along(True))
+
+    def core(self, value):
+        return self.swap(value, "c")
+
+    def phase(self, state, number):
+        kept, sent = state
+        if number == 0:
+            return kept, self.swap(sent, "c")
+        if number in (1, 2):
+            return kept, self.permute(sent, self.along(number == 1))
+        return kept, self.swap(sent, "z", 1 if number == 3 else 2)
+
+    def split(self, state):
+        kept, got = state
 
         def add(left, right):
             return (left.astype(F32) + right.astype(F32)).astype(BF)
 
-        half = [
-            [add(pick(c, a, b), self.swap(pick(1 - c, a, b), "c")) for b in range(2)]
-            for a in range(2)
-        ]
-        quarter = [add(half[0][b], self.permute(half[1][b], self.along(True))) for b in range(2)]
-        line = add(quarter[0], self.permute(quarter[1], self.along(False)))
-        total = lax.dynamic_index_in_dim(line, z, 0, False).astype(F32)
-        for k in range(1, nz):
-            out = lax.dynamic_index_in_dim(line, (z + k) % nz, 0, False)
-            got = lax.ppermute(out, "z", [(i, (i + k) % nz) for i in range(nz)])
-            total = total + got.astype(F32)
-        return total
+        half = kept.shape[0] // 2
+        return add(kept[:half], got[:half]), add(kept[half:], got[half:])
 
 
 def whole(chunks):
@@ -466,6 +458,1101 @@
     return (loss, norm, *sq, *de, *hd, *tb)
 
 
+NZ = 4
+BANDS = 4
+STRIPS = 8
+NT_DIMS = (((1,), (1,)), ((), ()))
+NN_DIMS = (((1,), (0,)), ((), ()))
+TN_DIMS = (((0,), (0,)), ((), ()))
+VMEM_LIMIT = 56 * 1024 * 1024
+
+
+def mm(a, b):
+    return lax.dot_general(a, b, NN_DIMS, preferred_element_type=F32)
+
+
+def mm_nt(a, b):
+    return lax.dot_general(a, b, NT_DIMS, preferred_element_type=F32)
+
+
+def mm_tn(a, b):
+    return lax.dot_general(a, b, TN_DIMS, preferred_element_type=F32)
+
+
+def zflip(k):
+    return (k % 2) * 2 + k // 2
+
+
+def span(index, extent):
+    return pl.ds(pl.multiple_of(index * extent, extent), extent)
+
+
+def spots(core):
+    out = []
+    for owner in (core, 1 - core):
+        for a in range(2):
+            for b in range(2):
+                out.append((a, b, owner) if owner == 0 else (b, a, owner))
+    return out
+
+
+def by_core(co, fn):
+    for core in range(2):
+
+        @pl.when(co[1] == core)
+        def _(core=core):
+            fn(core)
+
+
+def forward_step(co, k, x_ref, chunks, row, band, w, put):
+    back = co[2] ^ zflip(k)
+
+    def run(core):
+        places = spots(core)
+        for fx in range(2):
+            total = None
+            for index, (fy, px, owner) in enumerate(places):
+                if px != fx:
+                    continue
+                r = (co[0] ^ fy) * 2 + owner
+                part = mm(x_ref[:, span(r, band)], chunks[index][0, row : row + band])
+                total = part if total is None else total + part
+            put(back * 2 + (co[3] ^ fx), total)
+
+    by_core(co, run)
+
+
+def backward_step(co, k, dy_ref, chunks, row, band, w, acc_ref, fresh):
+    back = co[2] ^ zflip(k)
+
+    def run(core):
+        places = spots(core)
+        for owner in range(2):
+            for fy in range(2):
+                total = None
+                for index, (py, fx, who) in enumerate(places):
+                    if (py, who) != (fy, owner):
+                        continue
+                    p = back * 2 + (co[3] ^ fx)
+                    part = mm_nt(dy_ref[:, span(p, w)], chunks[index][0, row : row + band])
+                    total = part if total is None else total + part
+                r = (co[0] ^ fy) * 2 + owner
+
+                @pl.when(fresh)
+                def _():
+                    acc_ref[:, span(r, band)] = total
+
+                @pl.when(jnp.logical_not(fresh))
+                def _():
+                    acc_ref[:, span(r, band)] += total
+
+    by_core(co, run)
+
+
+def smem():
+    return pl.BlockSpec(memory_space=pltpu.SMEM)
+
+
+def full(shape):
+    zeros = (0,) * len(shape)
+    return pl.BlockSpec(shape, lambda i: zeros)
+
+
+def steps_of(rows, w, first=0, block=0):
+    def at(b):
+        return pl.BlockSpec(
+            (1, rows, w), lambda i: (b * NZ + jnp.clip(i - first, 0, NZ - 1), block, 0)
+        )
+
+    return [at(0), at(1)] * 4
+
+
+def twice(arrays):
+    return [v for v in arrays for _ in range(2)]
+
+
+def call(kernel, name, grid, in_specs, outs, out_specs, scratch, flops, moved, *args):
+    return pl.pallas_call(
+        kernel,
+        name=name,
+        grid=grid,
+        in_specs=in_specs,
+        out_shape=outs,
+        out_specs=out_specs,
+        scratch_shapes=scratch,
+        compiler_params=pltpu.CompilerParams(
+            vmem_limit_bytes=VMEM_LIMIT
+        ),
+        cost_estimate=pl.CostEstimate(flops=flops, bytes_accessed=moved, transcendentals=0),
+    )(*args)
+
+
+def shape(*dims, dtype=F32):
+    return jax.ShapeDtypeStruct(dims, dtype)
+
+
+def norm(value, gain):
+    center = value - jnp.mean(value, axis=-1, keepdims=True)
+    spread = jnp.mean(center * center, axis=-1, keepdims=True)
+    return center * lax.rsqrt(spread + NORM_EPSILON) * gain
+
+
+def norm_grad(value, gain, grad):
+    center = value - jnp.mean(value, axis=-1, keepdims=True)
+    spread = jnp.mean(center * center, axis=-1, keepdims=True)
+    inverse = lax.rsqrt(spread + NORM_EPSILON)
+    unit = center * inverse
+    inner = grad * gain
+    out = inverse * (
+        inner
+        - jnp.mean(inner, axis=-1, keepdims=True)
+        - unit * jnp.mean(inner * unit, axis=-1, keepdims=True)
+    )
+    return out, jnp.sum(grad * unit, axis=0, keepdims=True)
+
+
+def half_masks(rows):
+    lane = lax.broadcasted_iota(jnp.int32, (rows, 128), 1)
+    return [(lane < 64).astype(BF), (lane >= 64).astype(BF)]
+
+
+def assemble_kernel(co, *refs, band, offset, tall, extra):
+    chunks, (table_ref, more_ref, value_ref) = refs[:8], refs[8:]
+    k = pl.program_id(0)
+    back = co[2] ^ zflip(k)
+
+    def run(core):
+        for index, (fy, fx, owner) in enumerate(spots(core)):
+            r = (co[0] ^ fy) * 2 + owner
+            p = back * 2 + (co[3] ^ fx)
+            table_ref[span(r, tall), span(p, 128)] = chunks[index][0, offset : offset + tall]
+            more_ref[r, p] = chunks[index][0, offset + tall : offset + tall + extra]
+            value_ref[span(r, band), span(p, 128)] = chunks[index][0, :band]
+
+    by_core(co, run)
+
+
+def square_kernel(co, *refs, band):
+    chunks, outs = refs[:8], refs[8:]
+    k = pl.program_id(0)
+
+    def run(core):
+        for index, (fy, fx, owner) in enumerate(spots(core)):
+            r = (co[0] ^ fy) * 2 + owner
+            p = (co[2] ^ zflip(k)) * 2 + (co[3] ^ fx)
+            for part, out_ref in enumerate(outs):
+                out_ref[span(r, band), span(p, 128)] = chunks[index][0, part * band : (part + 1) * band]
+
+    by_core(co, run)
+
+
+def product_kernel(co, x_ref, *refs, band, w):
+    chunks, out_ref = refs[:8], refs[8]
+
+    def put(p, total):
+        out_ref[:, span(p, w)] = total.astype(out_ref.dtype)
+
+    forward_step(co, pl.program_id(0), x_ref, chunks, 0, band, w, put)
+
+
+def pool_kernel(x_ref, e_ref, tu_ref, tv_ref, agg_ref, a_ref, pa_ref):
+    j = pl.program_id(0)
+    x, e = x_ref[...], e_ref[...]
+    rows, n = x.shape
+    masks = half_masks(n)
+    lane = lax.broadcasted_iota(jnp.int32, (n, 128), 1)
+    keep = lax.broadcasted_iota(jnp.int32, (rows, 128), 1) < V
+    total = None
+    for half in range(2):
+        column = jnp.sum(jnp.where(lane == 2 * j + half, tu_ref[...], 0.0), axis=1, keepdims=True)
+        m = e.astype(F32) * column
+        high = m.astype(BF)
+        rest = (m - high.astype(F32)).astype(BF)
+        s = mm(x, high) + mm(x, rest)
+        s = jnp.where(keep, s, -1e30)
+        s = jnp.exp(s - jnp.max(s, axis=-1, keepdims=True))
+        pa = s / jnp.sum(s, axis=-1, keepdims=True)
+        wide = mm_nt(pa.astype(BF), e)
+        a = (x.astype(F32) * wide).astype(BF)
+        pa_ref[half] = pa
+        a_ref[half] = a
+        part = mm(a, tv_ref[...] * masks[half])
+        total = part if total is None else total + part
+    agg_ref[...] = total.astype(BF)
+
+
+def enter_kernel(co, agg_ref, src_ref, gain_ref, *refs, band):
+    chunks, (x0_ref, h1_ref) = refs[:8], refs[8:]
+    k = pl.program_id(0)
+
+    def put(p, total):
+        x0_ref[:, span(p, 128)] = total
+
+    forward_step(co, k, agg_ref, chunks, 0, band, 128, put)
+
+    @pl.when(k == NZ - 1)
+    def _():
+        cap = x0_ref.shape[0] // src_ref.shape[0]
+        for m in range(src_ref.shape[0]):
+            x0_ref[m * cap : (m + 1) * cap] += src_ref[m : m + 1]
+        h1_ref[...] = norm(x0_ref[...], gain_ref[...]).astype(BF)
+
+
+def attend_kernel(co, lens, x0_ref, h1_ref, gain_ref, *refs, band, scale):
+    qkv_chunks, o_chunks = refs[:8], refs[8:16]
+    qkv_ref, p_ref, o_ref, x1_ref, h2_ref = refs[16:]
+    i = pl.program_id(0)
+    micro = lens.shape[0]
+    width = x0_ref.shape[1]
+    cap = x0_ref.shape[0] // micro
+
+    @pl.when(i < NZ)
+    def _():
+        for part in range(3):
+
+            def put(p, total, part=part):
+                col = pl.multiple_of(part * width + p * 128, 128)
+                qkv_ref[:, pl.ds(col, 128)] = total.astype(BF)
+
+            forward_step(co, i, h1_ref, qkv_chunks, part * band, band, 128, put)
+
+    @pl.when(i == NZ - 1)
+    def _():
+        masks = half_masks(cap)
+        key = lax.broadcasted_iota(jnp.int32, (cap, cap), 1)
+
+        @pl.loop(0, width // 128)
+        def _(j):
+            for m in range(micro):
+                rows = slice(m * cap, (m + 1) * cap)
+                q = qkv_ref[rows, span(j, 128)]
+                kk = qkv_ref[rows, pl.ds(pl.multiple_of(width + j * 128, 128), 128)]
+                vv = qkv_ref[rows, pl.ds(pl.multiple_of(2 * width + j * 128, 128), 128)]
+                total = None
+                for half in range(2):
+                    s = mm_nt(q * masks[half], kk) * scale
+                    s = jnp.where(key < lens[m], s, -1e30)
+                    s = jnp.exp(s - jnp.max(s, axis=-1, keepdims=True))
+                    p = s / jnp.sum(s, axis=-1, keepdims=True)
+                    p_ref[2 * j + half, m] = p
+                    part = mm(p.astype(BF), vv * masks[half])
+                    total = part if total is None else total + part
+                o_ref[rows, span(j, 128)] = total.astype(BF)
+
+    @pl.when(i >= NZ)
+    def _():
+        def put(p, total):
+            x1_ref[:, span(p, 128)] = x0_ref[:, span(p, 128)] + total
+
+        forward_step(co, i - NZ, o_ref, o_chunks, 0, band, 128, put)
+
+    @pl.when(i == 2 * NZ - 1)
+    def _():
+        h2_ref[...] = norm(x1_ref[...], gain_ref[...]).astype(BF)
+
+
+def up_kernel(co, h2_ref, *refs, band, w):
+    chunks, (act_ref, slope_ref) = refs[:8], refs[8:]
+
+    def put(p, f):
+        bell = jnp.exp(-0.5 * f * f)
+        t = 1.0 / (1.0 + (0.3275911 * 0.5**0.5) * jnp.abs(f))
+        tail = t * (1.061405429 * 0.5)
+        for term in (-1.453152027, 1.421413741, -0.284496736, 0.254829592):
+            tail = t * (0.5 * term + tail)
+        tail = tail * bell
+        share = jnp.where(f < 0.0, tail, 1.0 - tail)
+        act_ref[:, span(p, w)] = (f * share).astype(BF)
+        slope_ref[:, span(p, w)] = share + f * bell * ((2.0 * math.pi) ** -0.5)
+
+    forward_step(co, pl.program_id(0), h2_ref, chunks, 0, band, w, put)
+
+
+def down_kernel(co, count, x1_ref, act_ref, slope_ref, head_ref, target_ref, weight_ref, *refs, band, w):
+    chunks = refs[:8]
+    loss_ref, dx2_ref, dx2_low_ref, dhead_ref, df_ref = refs[8:13]
+    acc_ref = refs[13]
+    i = pl.program_id(0)
+
+    @pl.when(i < NZ)
+    def _():
+        backward_step(co, i, act_ref, chunks, 0, band, w, acc_ref, i == 0)
+
+    @pl.when(i == NZ - 1)
+    def _():
+        x2 = (x1_ref[...] + acc_ref[...]).astype(BF)
+        diff = mm(x2, head_ref[...]) - target_ref[...].astype(F32)
+        weighted = weight_ref[...] * diff
+        loss_ref[...] = jnp.broadcast_to(jnp.sum(weighted * diff), loss_ref.shape)
+        dpred = (2.0 * weighted / count[0]).astype(BF)
+        dhead_ref[...] = mm_tn(x2, dpred).astype(BF)
+        dx2 = mm_nt(dpred, head_ref[...])
+        dx2_ref[...] = dx2
+        dx2_low_ref[...] = dx2.astype(BF)
+
+    @pl.when(i >= NZ)
+    def _():
+        def put(p, dact):
+            df_ref[:, span(p, w)] = (dact * slope_ref[:, span(p, w)]).astype(BF)
+
+        forward_step(co, i - NZ, dx2_low_ref, chunks, 0, band, w, put)
+
+
+def owner_place(co, i, owner):
+    a, b, k = i // (2 * NZ), (i // NZ) % 2, i % NZ
+    fy = jnp.where(owner == 0, a, b)
+    fx = jnp.where(owner == 0, b, a)
+    return (co[0] ^ fy) * 2 + owner, (co[2] ^ zflip(k)) * 2 + (co[3] ^ fx)
+
+
+def targets(co, keep_ref, send_ref):
+    return [
+        (out, owner, j)
+        for out, owner in ((keep_ref, co[1]), (send_ref, 1 - co[1]))
+        for j in range(NZ)
+    ]
+
+
+def grad_kernel(co, x_ref, dy_ref, keep_ref, send_ref, xt_ref, *, band, w):
+    i = pl.program_id(0)
+
+    @pl.when(i == 0)
+    def _():
+        xt_ref[...] = x_ref[...].T
+
+    for out_ref, owner, j in targets(co, keep_ref, send_ref):
+        r, p = owner_place(co, i * NZ + j, owner)
+        out_ref[j] = mm(xt_ref[span(r, band)], dy_ref[:, span(p, w)]).astype(BF)
+
+
+def qkv_grad_kernel(co, h1_ref, dqkv_ref, keep_ref, send_ref, ht_ref, *, band):
+    i = pl.program_id(0)
+    width = h1_ref.shape[1]
+
+    @pl.when(i == 0)
+    def _():
+        ht_ref[...] = h1_ref[...].T
+
+    for out_ref, owner, j in targets(co, keep_ref, send_ref):
+        r, p = owner_place(co, i * NZ + j, owner)
+        h1 = ht_ref[span(r, band)]
+        for part in range(3):
+            col = pl.multiple_of(part * width + p * 128, 128)
+            got = mm(h1, dqkv_ref[:, pl.ds(col, 128)])
+            out_ref[j, part * band : (part + 1) * band] = got.astype(BF)
+
+
+def pair_grad_kernel(co, o_ref, agg_ref, dx1_ref, dx0_ref, keep_ref, send_ref, ot_ref, at_ref, *, band):
+    i = pl.program_id(0)
+
+    @pl.when(i == 0)
+    def _():
+        ot_ref[...] = o_ref[...].T
+        at_ref[...] = agg_ref[...].T
+
+    for out_ref, owner, j in targets(co, keep_ref, send_ref):
+        r, p = owner_place(co, i * NZ + j, owner)
+        got = mm(ot_ref[span(r, band)], dx1_ref[:, span(p, 128)])
+        out_ref[j, :band] = got.astype(BF)
+        got = mm(at_ref[span(r, band)], dx0_ref[:, span(p, 128)])
+        out_ref[j, band:] = got.astype(BF)
+
+
+def rows_kernel(co, g_ref, head_ref, keep_ref, send_ref, *, tall):
+    i = pl.program_id(0)
+    for out_ref, owner, j in targets(co, keep_ref, send_ref):
+        r, p = owner_place(co, i * NZ + j, owner)
+        out_ref[j, :tall] = g_ref[span(r, tall), span(p, 128)]
+        out_ref[j, tall:] = head_ref[r, p]
+
+
+def up_back_kernel(co, df_ref, x1_ref, gain_ref, dx2_ref, *refs, band, w):
+    chunks, (dx1_ref, dx1_low_ref, dgain_ref, acc_ref) = refs[:8], refs[8:]
+    k = pl.program_id(0)
+    backward_step(co, k, df_ref, chunks, 0, band, w, acc_ref, k == 0)
+
+    @pl.when(k == NZ - 1)
+    def _():
+        out, dgain = norm_grad(x1_ref[...], gain_ref[...], acc_ref[...])
+        dx1 = dx2_ref[...] + out
+        dx1_ref[...] = dx1
+        dx1_low_ref[...] = dx1.astype(BF)
+        dgain_ref[...] = dgain
+
+
+def attend_back_kernel(co, dx1_low_ref, qkv_ref, p_ref, *refs, band, scale):
+    o_chunks = refs[:8]
+    dqkv_ref, acc_ref, do_ref = refs[8:]
+    i = pl.program_id(0)
+    micro = p_ref.shape[1]
+    width = dx1_low_ref.shape[1]
+    cap = dx1_low_ref.shape[0] // micro
+
+    @pl.when(i < NZ)
+    def _():
+        backward_step(co, i, dx1_low_ref, o_chunks, 0, band, 128, acc_ref, i == 0)
+
+    @pl.when(i == NZ - 1)
+    def _():
+        do_ref[...] = acc_ref[...].astype(BF)
+        masks = half_masks(cap)
+
+        @pl.loop(0, width // 128)
+        def _(j):
+            for m in range(micro):
+                rows = slice(m * cap, (m + 1) * cap)
+                k_at = pl.ds(pl.multiple_of(width + j * 128, 128), 128)
+                v_at = pl.ds(pl.multiple_of(2 * width + j * 128, 128), 128)
+                q, kk, vv = qkv_ref[rows, span(j, 128)], qkv_ref[rows, k_at], qkv_ref[rows, v_at]
+                do = do_ref[rows, span(j, 128)]
+                dq = dk = dv = None
+                for half in range(2):
+                    p = p_ref[2 * j + half, m]
+                    do_half = do * masks[half]
+                    dp = mm_nt(do_half, vv)
+                    moved = p * dp
+                    ds = (moved - p * jnp.sum(moved, axis=-1, keepdims=True)).astype(BF)
+                    parts = (
+                        mm(ds, kk * masks[half]),
+                        mm_tn(ds, q * masks[half]),
+                        mm_tn(p.astype(BF), do_half),
+                    )
+                    if dq is None:
+                        dq, dk, dv = parts
+                    else:
+                        dq, dk, dv = dq + parts[0], dk + parts[1], dv + parts[2]
+                dqkv_ref[rows, span(j, 128)] = (dq * scale).astype(BF)
+                dqkv_ref[rows, k_at] = (dk * scale).astype(BF)
+                dqkv_ref[rows, v_at] = dv.astype(BF)
+
+
+def leave_kernel(co, dx1_ref, dqkv_ref, x0_ref, gain_ref, *refs, band):
+    qkv_chunks, a_chunks = refs[:8], refs[8:16]
+    dx0_low_ref, dgain_ref, dsum_ref, dagg_ref, acc_ref = refs[16:]
+    i = pl.program_id(0)
+    micro = dsum_ref.shape[0]
+    width = x0_ref.shape[1]
+    cap = x0_ref.shape[0] // micro
+
+    @pl.when(i < NZ)
+    def _():
+        back = co[2] ^ zflip(i)
+
+        def run(core):
+            places = spots(core)
+            for owner in range(2):
+                for fy in range(2):
+                    total = None
+                    for index, (py, fx, who) in enumerate(places):
+                        if (py, who) != (fy, owner):
+                            continue
+                        p = back * 2 + (co[3] ^ fx)
+                        for part in range(3):
+                            col = pl.multiple_of(part * width + p * 128, 128)
+                            got = mm_nt(
+                                dqkv_ref[:, pl.ds(col, 128)],
+                                qkv_chunks[index][0, part * band : (part + 1) * band],
+                            )
+                            total = got if total is None else total + got
+                    r = (co[0] ^ fy) * 2 + owner
+
+                    @pl.when(i == 0)
+                    def _():
+                        acc_ref[:, span(r, band)] = total
+
+                    @pl.when(i > 0)
+                    def _():
+                        acc_ref[:, span(r, band)] += total
+
+        by_core(co, run)
+
+    @pl.when(i == NZ - 1)
+    def _():
+        out, dgain = norm_grad(x0_ref[...], gain_ref[...], acc_ref[...])
+        dx0 = dx1_ref[...] + out
+        dx0_low_ref[...] = dx0.astype(BF)
+        dgain_ref[...] = dgain
+        for m in range(micro):
+            dsum_ref[m : m + 1] = jnp.sum(dx0[m * cap : (m + 1) * cap], axis=0, keepdims=True)
+
+    @pl.when(i >= NZ)
+    def _():
+        backward_step(co, i - NZ, dx0_low_ref, a_chunks, 0, band, 128, acc_ref, i == NZ)
+
+    @pl.when(i == 2 * NZ - 1)
+    def _():
+        dagg_ref[...] = acc_ref[...].astype(BF)
+
+
+def pool_back_kernel(x_ref, e_ref, tv_ref, a_ref, pa_ref, dagg_ref, g_ref, s_ref):
+    x, e, dagg = x_ref[...].astype(F32), e_ref[...], dagg_ref[...]
+    masks = half_masks(dagg.shape[0])
+    total = None
+    for half in range(2):
+        part = dagg * masks[half]
+        moved = mm_nt(part, tv_ref[...]) * x
+        high = moved.astype(BF)
+        rest = (moved - high.astype(F32)).astype(BF)
+        dpal = mm(high, e) + mm(rest, e)
+        pa = pa_ref[half]
+        inner = pa * dpal
+        ds = (inner - pa * jnp.sum(inner, axis=-1, keepdims=True)).astype(BF)
+        s_ref[0, half : half + 1] = jnp.sum(mm_nt(ds, e) * x, axis=0, keepdims=True)
+        got = mm_tn(a_ref[half], part)
+        total = got if total is None else total + got
+    g_ref[...] = total
+
+
+def table_layout(cap, band, tall):
+    n = BANDS * tall
+    nk = PATCH_PIXELS * V
+    select = np.zeros((nk, n), np.float32)
+    fixed = np.zeros((cap, n), np.float32)
+    var_of = np.zeros((n, 128), np.float32)
+    for row in range(5 * V + cap):
+        lane = (row // band) * tall + row % band
+        if row < nk:
+            select[row, lane] = 1.0
+            var_of[lane, row // PATCH_PIXELS] = 1.0
+        elif row < 5 * V:
+            fixed[:, lane] = 1.0
+            var_of[lane, row - nk] = 1.0
+        else:
+            fixed[row - 5 * V, lane] = 1.0
+            var_of[lane, :V] = 1.0
+    return select, fixed, var_of
+
+
+def fast_body(
+    grid,
+    pixels,
+    targets,
+    masks,
+    lengths,
+    groups,
+    latitudes,
+    step_count,
+    square_master,
+    square_first,
+    square_second,
+    dense_master,
+    dense_first,
+    dense_second,
+    head_master,
+    head_first,
+    head_second,
+    table_master,
+    table_first,
+    table_second,
+):
+    micro, items, _, cap, own_pixels = pixels.shape
+    rows = micro * cap
+    band, strip = square_master.shape[1:]
+    width = band * BANDS
+    size = width // HEADS
+    scale = size ** (-0.5)
+    w = dense_master.shape[2]
+    ff = w * STRIPS
+    ho = head_master.shape[1] * STRIPS
+    base = 5 * V + cap
+    table_band = table_master.shape[0]
+    tall = table_band + -table_band % 16
+    n = BANDS * tall
+    head_rows = head_master.size // strip
+    y, c, z, x = (lax.axis_index(a) for a in AXES)
+    co = jnp.stack([y, c, z, x]).astype(jnp.int32)
+    my_band = y * 2 + c
+    my_strip = z * 2 + x
+    select, fixed, var_of = table_layout(cap, table_band, tall)
+
+    def lane_of(row):
+        return (row // table_band) * tall + row % table_band
+
+    square_low = square_master.astype(BF)
+    dense_low = dense_master.astype(BF)
+    low_rows = 2 * band + tall + head_rows
+    low = jnp.concatenate(
+        [
+            square_low[2],
+            square_low[3],
+            jnp.pad(table_master.astype(BF), ((0, tall - table_band), (0, 0))),
+            head_master.astype(BF).reshape(head_rows, strip),
+        ],
+        axis=0,
+    )
+    attn = square_low[4:8].reshape(4 * band, strip)
+    slots = jnp.arange(cap)
+    lens = lengths[:, 0, 0]
+    valid = masks[:, 0, 0].astype(F32) * (slots[None] < lens[:, None]).astype(F32)[..., None]
+    lat_onehot = (latitudes[:, 0, 0][..., None] == jnp.arange(LATS)).astype(F32)
+    wpix = jnp.einsum("mcl,lk->mck", lat_onehot, latitude_table(), precision=HIGH) * valid
+    weighted = jnp.tile(wpix.reshape(rows, PATCH_PIXELS), (1, V))
+    var_of = jnp.asarray(var_of, BF)
+    query_row = base + SOURCES
+    col_head = (my_strip * strip + jnp.arange(strip)) // size
+    head_mask = (col_head[:, None] == jnp.arange(HEADS)[None]).astype(F32)
+    wide, line, one = full((rows, width)), full((1, width)), shape(1, width)
+    pair = pl.BlockSpec((rows, 128), lambda j: (0, j))
+    src_at = lane_of(base)
+    row = jnp.where(my_band == query_row // table_band, 1.0, 0.0) * table_master[query_row % table_band]
+    first_pack = lax.dynamic_update_slice_in_dim(
+        jnp.zeros((width,), F32), row.astype(BF).astype(F32), my_strip * strip, 0
+    )
+    first_pack = jnp.concatenate([first_pack, jnp.broadcast_to(jnp.sum(valid), (128,))])
+    first_pack = grid.hop(first_pack, ("z", 1), ("z", 2))
+
+    bundles = [low, attn, dense_low[0], dense_low[1], square_low[:2].reshape(2 * band, strip)]
+    stack, join = lambda i, v: jnp.stack([bundles[i], v]), lambda a, b: jnp.concatenate([a, b], axis=0)
+    z2, z1, near, far, core = grid.far_z, grid.next_z, grid.near, grid.far, grid.core
+    (a0,) = grid.begin([first_pack], (z2, bundles[0]))
+    p0 = stack(0, a0)
+    b0, a1 = got = grid.begin([a0], (z1, p0), (z2, bundles[1]))
+    l0, p1 = join(p0, b0), stack(1, a1)
+    pack = grid.hop(first_pack, ("x", 1), ("y", 1), ("c", 1))
+    query, count = pack[:width].astype(BF), pack[width]
+    query_own = lax.dynamic_slice_in_dim(query, my_band * band, band)
+    spread = jnp.tile(jnp.asarray(fixed), (micro, 1))
+    for fy in range(2):
+        for fc in range(2):
+            other = (y ^ fy) * 2 + (c ^ fc)
+            piece = lax.dynamic_index_in_dim(pixels[:, :, 0], other, 1, False)
+            if fy or fc:
+                piece = grid.permute(piece, lambda a, b, d, e, fy=fy, fc=fc: (a ^ fy, b ^ fc, d, e))
+            pick = lax.dynamic_slice_in_dim(
+                jnp.asarray(select, BF), other * own_pixels, own_pixels, 0
+            )
+            spread = spread + mm(piece.reshape(rows, own_pixels), pick)
+    spread = spread.astype(BF)
+    qv = dot(query_own[None], square_low[0], NN)[0]
+    qv_own = grid.hop(qv, ("y", 1), ("c", 1)).astype(BF)
+    u_part = dot(square_low[1].astype(F32) * qv_own.astype(F32)[None], head_mask, NN, precision=HIGH)
+    u_part = lax.dynamic_update_slice_in_dim(jnp.zeros((width, HEADS), F32), u_part, my_band * band, 0)
+    u_part = grid.hop(u_part, ("x", 1))
+    n0, b1 = got = grid.begin([got, qv_own, spread], (near, l0), (z1, p1))
+    f0, l1 = join(l0, n0), join(p1, b1)
+    u_part = grid.hop(u_part, ("y", 1), ("c", 1))
+    r0, n1, a2 = got = grid.begin([got, u_part], (far, f0), (near, l1), (z2, bundles[2]))
+    f1, p2 = join(l1, n1), stack(2, a2)
+    (b2,) = grid.begin([], (z1, p2))
+    u_part = grid.hop(u_part, ("z", 1))
+    l2 = join(p2, b2)
+    c0, d0, r1, a3 = got = grid.begin(
+        [got, b2, u_part], (core, f0), (core, r0), (far, f1), (z2, bundles[3])
+    )
+    p3 = stack(3, a3)
+    (b3,) = grid.begin([], (z1, p3))
+    u_part = grid.hop(u_part, ("z", 2))
+    l3 = join(p3, b3)
+    low = twice([f0, r0, c0, d0])
+    n2, c1, d1, a4 = got = grid.begin(
+        [got, b3, u_part], (near, l2), (core, f1), (core, r1), (z2, bundles[4])
+    )
+    f2, p4 = join(l2, n2), stack(4, a4)
+    u = (u_part * scale).astype(BF)
+    table, heads, wv = call(
+        lambda *r: assemble_kernel(*r, band=band, offset=2 * band, tall=tall, extra=head_rows),
+        "assemble",
+        (NZ,),
+        [smem()] + steps_of(low_rows, 128),
+        (
+            shape(n, width, dtype=BF),
+            shape(BANDS, STRIPS, head_rows, 128, dtype=BF),
+            shape(width, width, dtype=BF),
+        ),
+        (full((n, width)), full((BANDS, STRIPS, head_rows, 128)), full((width, width))),
+        [],
+        0,
+        1 << 23,
+        co,
+        *low,
+    )
+    head = whole(heads.reshape(BANDS, STRIPS, band, ho // STRIPS))
+    tv = call(
+        lambda *r: product_kernel(*r, band=band, w=128),
+        "table_values",
+        (NZ,),
+        [smem(), full((n, width))] + steps_of(band, 128),
+        shape(n, width, dtype=BF),
+        full((n, width)),
+        [],
+        2 * n * width * width,
+        1 << 22,
+        co,
+        table,
+        *low,
+    )
+    tu = jnp.pad(dot(table, u, NN), ((0, 0), (0, 128 - HEADS)))
+    attn = twice([f1, r1, c1, d1])
+    r2, n3, b4 = got = grid.begin([got, tv, u], (far, f2), (near, l3), (z1, p4))
+    f3, l4 = join(l3, n3), join(p4, b4)
+    tu, head, weighted = grid.gate((tu, head, weighted), [n2])
+    tu = grid.gate(tu, [head, weighted])
+    agg, fold, pa = call(
+        pool_kernel,
+        "pool",
+        (HEADS // 2,),
+        [full((rows, n)), full((n, 128)), full((n, 128)), pl.BlockSpec((n, 128), lambda j: (0, j))],
+        (shape(rows, width, dtype=BF), shape(HEADS, rows, n, dtype=BF), shape(HEADS, rows, 128)),
+        (
+            pair,
+            pl.BlockSpec((2, rows, n), lambda j: (j, 0, 0)),
+            pl.BlockSpec((2, rows, 128), lambda j: (j, 0, 0)),
+        ),
+        [],
+        12 * HEADS * rows * n * 128,
+        1 << 23,
+        spread,
+        var_of,
+        tu,
+        tv,
+    )
+
+    gain_one = table[lane_of(base + SOURCES + 1)].astype(F32)[None]
+    gain_two = table[lane_of(base + SOURCES + 2)].astype(F32)[None]
+    onehot = (groups[:, 0, 0][:, None] == jnp.arange(SOURCES)).astype(F32)
+    src = dot(onehot, table[src_at : src_at + SOURCES].astype(F32), NN, precision=HIGH)
+    x0, h1 = call(
+        lambda *r: enter_kernel(*r, band=band),
+        "enter",
+        (NZ,),
+        [smem(), wide, full((micro, width)), line] + steps_of(band, 128, 0, 1),
+        (shape(rows, width), shape(rows, width, dtype=BF)),
+        (wide, wide),
+        [],
+        2 * rows * width * width,
+        1 << 22,
+        co,
+        agg,
+        src,
+        gain_one,
+        *low,
+    )
+    c2, d2, r3, n4 = got = grid.begin(
+        [got, h1], (core, f2), (core, r2), (far, f3), (near, l4)
+    )
+    f4 = join(l4, n4)
+    up = twice([f2, r2, c2, d2])
+    qkv, probs, o, x1, h2 = call(
+        lambda *r: attend_kernel(*r, band=band, scale=scale),
+        "attend",
+        (2 * NZ,),
+        [smem(), smem(), wide, wide, line]
+        + steps_of(3 * band, 128)
+        + steps_of(band, 128, NZ, 3),
+        (
+            shape(rows, 3 * width, dtype=BF),
+            shape(HEADS, micro, cap, cap),
+            shape(rows, width, dtype=BF),
+            shape(rows, width),
+            shape(rows, width, dtype=BF),
+        ),
+        (full((rows, 3 * width)), full((HEADS, micro, cap, cap)), wide, wide, wide),
+        [],
+        8 * rows * width * width + 8 * rows * cap * width,
+        1 << 24,
+        co,
+        lens,
+        x0,
+        h1,
+        gain_two,
+        *attn,
+        *attn,
+    )
+    c3, d3, r4 = got = grid.begin([got, h2], (core, f3), (core, r3), (far, f4))
+    down = twice([f3, r3, c3, d3])
+    act, slope = call(
+        lambda *r: up_kernel(*r, band=band, w=w),
+        "up",
+        (NZ,),
+        [smem(), wide] + steps_of(band, w),
+        (shape(rows, ff, dtype=BF), shape(rows, ff)),
+        (full((rows, ff)), full((rows, ff))),
+        [],
+        2 * rows * width * ff,
+        1 << 24,
+        co,
+        h2,
+        *up,
+    )
+    wq_parts = [f4, r4, *grid.begin([got, act], (core, f4), (core, r4))]
+    act = grid.gate(act, [r4])
+    loss_part, dx2, dx2_low, d_head, df = call(
+        lambda *r: down_kernel(*r, band=band, w=w),
+        "down",
+        (2 * NZ,),
+        [smem(), smem(), wide, full((rows, ff)), full((rows, ff)), full((width, ho)), full((rows, ho)), full((rows, ho))]
+        + [pl.BlockSpec((1, band, w), lambda i, b=b: (b * NZ + i % NZ, 0, 0)) for b in range(2)] * 4,
+        (
+            shape(8, 128),
+            shape(rows, width),
+            shape(rows, width, dtype=BF),
+            shape(width, ho, dtype=BF),
+            shape(rows, ff, dtype=BF),
+        ),
+        (full((8, 128)), wide, wide, full((width, ho)), full((rows, ff))),
+        [pltpu.VMEM((rows, width), F32)],
+        4 * rows * width * ff,
+        1 << 25,
+        co,
+        count[None],
+        x1,
+        act,
+        slope,
+        head,
+        targets[:, 0, 0].reshape(rows, ho),
+        weighted,
+        *down,
+    )
+
+    place = lambda height, wid: pl.BlockSpec((NZ, height, wid), lambda i: (i, 0, 0))
+
+    turned = [pltpu.VMEM((width, rows), BF)]
+
+    def sent(kernel, name, height, wid, flops, scratch, *args):
+        out = shape(4 * NZ, height, wid, dtype=BF)
+        return call(
+            kernel,
+            name,
+            (NZ,),
+            [smem()] + [full(a.shape) for a in args],
+            (out, out),
+            (place(height, wid),) * 2,
+            scratch,
+            flops,
+            32 * height * wid * 2 + 4 * 1024 * 1024,
+            co,
+            *args,
+        )
+
+    dense_grad = lambda *r: grad_kernel(*r, band=band, w=w)
+    flow, done = {}, {}
+
+    def stage(work, before):
+        gated = grid.gate([flow[name] for name, _ in work], before)
+        arrived = []
+        for (name, number), state in zip(work, gated):
+            state = grid.phase(state, number)
+            arrived.append(state[1])
+            if number < 4:
+                flow[name] = grid.split(state)
+            else:
+                done[name] = state[0].astype(F32) + state[1].astype(F32)
+        return arrived
+
+    flow["down"] = sent(dense_grad, "down_grad", band, w, 2 * rows * width * ff, turned, dx2_low, act)
+    df = grid.gate(df, [flow["down"]])
+    flow["up"] = sent(dense_grad, "up_grad", band, w, 2 * rows * width * ff, turned, h2, df)
+    got = stage([("down", 0)], [])
+    df = grid.gate(df, [flow["up"], flow["down"]])
+    dx1, dx1_low, d_gain_two = call(
+        lambda *r: up_back_kernel(*r, band=band, w=w),
+        "up_back",
+        (NZ,),
+        [smem(), full((rows, ff)), wide, line, wide] + steps_of(band, w),
+        (shape(rows, width), shape(rows, width, dtype=BF), one),
+        (wide, wide, line),
+        [pltpu.VMEM((rows, width), F32)],
+        2 * rows * width * ff,
+        1 << 24,
+        co,
+        df,
+        x1,
+        gain_two,
+        dx2,
+        *up,
+    )
+    dqkv = call(
+        lambda *r: attend_back_kernel(*r, band=band, scale=scale),
+        "attend_back",
+        (NZ,),
+        [smem(), wide, full((rows, 3 * width)), full((HEADS, micro, cap, cap))]
+        + steps_of(band, 128, 0, 3),
+        shape(rows, 3 * width, dtype=BF),
+        full((rows, 3 * width)),
+        [pltpu.VMEM((rows, width), F32), pltpu.VMEM((rows, width), BF)],
+        2 * rows * width * width + 12 * rows * cap * width,
+        1 << 22,
+        co,
+        dx1_low,
+        qkv,
+        probs,
+        *attn,
+    )
+    got = stage([("down", 1), ("up", 0)], [got, flow["up"]])
+    dqkv = grid.gate(dqkv, [got, flow["up"], flow["down"]])
+    got = stage([("down", 2), ("up", 1)], [got, dqkv])
+    flow["qkv"] = sent(
+        lambda *r: qkv_grad_kernel(*r, band=band),
+        "qkv_grad",
+        3 * band,
+        128,
+        6 * rows * width * width,
+        turned,
+        h1,
+        dqkv,
+    )
+    dx0_low, d_gain_one, dx0_sum, dagg = call(
+        lambda *r: leave_kernel(*r, band=band),
+        "leave",
+        (2 * NZ,),
+        [smem(), wide, full((rows, 3 * width)), wide, line]
+        + steps_of(3 * band, 128)
+        + steps_of(band, 128, NZ, 1),
+        (
+            shape(rows, width, dtype=BF),
+            one,
+            shape(micro, width),
+            shape(rows, width, dtype=BF),
+        ),
+        (wide, line, full((micro, width)), wide),
+        [pltpu.VMEM((rows, width), F32)],
+        8 * rows * width * width,
+        1 << 23,
+        co,
+        dx1,
+        dqkv,
+        x0,
+        gain_one,
+        *attn,
+        *low,
+    )
+    got_core = stage([("qkv", 0)], [])
+    dx0_low, dx1_low = grid.gate((dx0_low, dx1_low), [got, got_core, flow["down"], flow["up"]])
+    got = stage([("down", 3), ("up", 2), ("qkv", 1)], [got, got_core, dagg])
+    flow["pair"] = sent(
+        lambda *r: pair_grad_kernel(*r, band=band),
+        "pair_grad",
+        2 * band,
+        128,
+        4 * rows * width * width,
+        turned * 2,
+        o,
+        agg,
+        dx1_low,
+        dx0_low,
+    )
+    dagg = grid.gate(dagg, [flow["pair"]])
+    got_core = stage([("pair", 0)], [])
+    g_rows, s_rows = call(
+        pool_back_kernel,
+        "pool_back",
+        (HEADS // 2,),
+        [
+            full((rows, n)),
+            full((n, 128)),
+            pl.BlockSpec((n, 128), lambda j: (0, j)),
+            pl.BlockSpec((2, rows, n), lambda j: (j, 0, 0)),
+            pl.BlockSpec((2, rows, 128), lambda j: (j, 0, 0)),
+            pair,
+        ],
+        (shape(n, width), shape(HEADS // 2, 2, n)),
+        (pl.BlockSpec((n, 128), lambda j: (0, j)), pl.BlockSpec((1, 2, n), lambda j: (j, 0, 0))),
+        [],
+        14 * HEADS * rows * n * 128,
+        1 << 23,
+        spread,
+        var_of,
+        tv,
+        fold,
+        pa,
+        dagg,
+    )
+    extra = jnp.concatenate(
+        [
+            jnp.zeros((src_at, width), F32),
+            dot(onehot, dx0_sum, TN, precision=HIGH),
+            jnp.zeros((1, width), F32),
+            d_gain_one,
+            d_gain_two,
+            jnp.zeros((n - src_at - SOURCES - 3, width), F32),
+        ],
+        axis=0,
+    )
+    s_rows = grid.gate(s_rows, got)
+    got = stage([("down", 4), ("up", 3), ("qkv", 2), ("pair", 1)], [got, got_core, g_rows])
+    s_sum = grid.hop(s_rows.reshape(HEADS, n), ("c", 1), ("y", 1))
+    flow["rows"] = sent(
+        lambda *r: rows_kernel(*r, tall=tall),
+        "rows",
+        tall + head_rows,
+        128,
+        0,
+        [],
+        (g_rows + extra).astype(BF),
+        chunked(d_head, BANDS, STRIPS).reshape(BANDS, STRIPS, head_rows, 128),
+    )
+    got_core = stage([("rows", 0)], [])
+    got = stage([("up", 4), ("qkv", 3), ("pair", 2), ("rows", 1)], [got, got_core, s_sum])
+    s_sum = grid.hop(s_sum, ("x", 1))
+    got = stage([("qkv", 4), ("pair", 3), ("rows", 2)], [got, s_sum])
+    wq_parts = grid.gate(wq_parts, got)
+    s_sum = grid.hop(s_sum, ("z", 1))
+    got = stage([("pair", 4), ("rows", 3)], [got, s_sum])
+    s_sum = grid.hop(s_sum, ("z", 2))
+    got = stage([("rows", 4)], [got, s_sum])
+    wq, wk = call(
+        lambda *r: square_kernel(*r, band=band),
+        "squares",
+        (NZ,),
+        [smem()] + steps_of(2 * band, 128),
+        (shape(width, width, dtype=BF),) * 2,
+        (full((width, width)),) * 2,
+        [],
+        0,
+        1 << 20,
+        co,
+        *twice(wq_parts),
+    )
+    u_heads = (jnp.arange(width)[:, None] // size == jnp.arange(HEADS)[None]).astype(F32)
+    du = dot(table.astype(F32), s_sum, ((0,), (1,)), precision=HIGH)
+    du_cols = dot(lax.dynamic_slice_in_dim(du, my_band * band, band), head_mask, NT, precision=HIGH)
+    dqv_heads = dot(du, wk.astype(F32), TN, precision=HIGH) * scale
+    dqv_all = jnp.sum(dqv_heads * u_heads.T, axis=0)
+    dqv = lax.dynamic_slice_in_dim(dqv_all, my_strip * strip, strip)
+    dq_own = jnp.sum(
+        lax.dynamic_slice_in_dim(wq, my_strip * strip, strip, 0).astype(F32) * dqv_all[None], axis=1
+    )
+    table_own = lax.dynamic_slice_in_dim(table, my_band * band, band, 1)
+    g_own = done["rows"][0][:tall]
+    g_low = g_own.astype(BF)
+    g_column = grid.spread(g_low, ("y", "c")).reshape(n, strip)
+    g_line = jnp.transpose(grid.spread(g_low, ("z", "x")), (1, 0, 2)).reshape(tall, width)
+    down_sum, up_sum = done["down"][0], done["up"][0]
+    wa_sum = done["pair"][0][band:]
+    attn_sum = (done["qkv"][0].reshape(3, band, strip), done["pair"][0][:band])
+    head_sum = done["rows"][0][tall:].reshape(head_master.shape)
+
+    row_of = np.full((n,), base + SOURCES + 3)
+    for row in range(base + SOURCES + 3):
+        row_of[lane_of(row)] = row
+    row_of = jnp.asarray(row_of)
+    g_column = jnp.where((row_of < base)[:, None], g_column, 0.0).astype(BF)
+    value_sum = dot(table_own, g_column, TN)
+    key_sum = du_cols * qv_own.astype(F32)[None] * scale
+    query_sum = query_own.astype(F32)[:, None] * dqv[None]
+    s_own = lax.dynamic_slice_in_dim(s_sum, my_band * tall, tall, 1)
+    wv_rows = lax.dynamic_slice_in_dim(wv, my_strip * strip, strip, 0)
+    u_rows = lax.dynamic_slice_in_dim(u, my_strip * strip, strip, 0).astype(F32)
+    d_rows = dot(g_line, wv_rows, NT) + dot(s_own, u_rows, ((0,), (1,)), precision=HIGH)
+    own_row = lax.dynamic_slice_in_dim(row_of, my_band * tall, tall)[:, None]
+    table_sum = jnp.where(own_row < base, d_rows, g_own)
+    table_sum = jnp.where(own_row == base + SOURCES, dq_own[None], table_sum)[:table_band]
+    square_sums = (query_sum, key_sum, value_sum, wa_sum, *attn_sum)
+    sumsq = sum(jnp.sum(s * s) for s in (*square_sums, up_sum, down_sum, head_sum, table_sum))
+    both = grid.total(jnp.stack([loss_part[0, 0], sumsq]))
+    loss = both[0] / count
+    grad_norm = jnp.sqrt(both[1])
+    factor = jnp.minimum(1.0, CLIP_AT / grad_norm)
+    steps = step_count[0].astype(F32)
+    square_sum = jnp.concatenate([s.reshape(-1, band, strip) for s in square_sums], axis=0)
+    dense_sum = jnp.stack([up_sum, down_sum])
+    sq = adam_update(square_master, square_first, square_second, square_sum, factor, steps, LEARN_RATE)
+    de = adam_update(dense_master, dense_first, dense_second, dense_sum, factor, steps, LEARN_RATE)
+    hd = adam_update(head_master, head_first, head_second, head_sum, factor, steps, LEARN_RATE)
+    tb = adam_update(table_master, table_first, table_second, table_sum, factor, steps, TABLE_RATE)
+    return (loss, grad_norm, *sq, *de, *hd, *tb)
+
+
 def solution(mesh):
     grid = Grid(mesh)
     var, patch = ("y", "c"), ("z", "x")
@@ -486,6 +1573,6 @@
     out_specs = (P(), P(), *(weight,) * 8, *(flat,) * 8)
 
     def step(*args):
-        return body(grid, *args)
+        return (fast_body if grid.fast else body)(grid, *args)
 
     return jax.shard_map(step, mesh=grid.mesh, in_specs=in_specs, out_specs=out_specs, check_vma=False)

time: 853 us -> 583 us (0.68)
  local copies, waits for them, and re-layouts: 291 us -> 40.6 us
  Pallas kernels: 0 us -> 180 us
  matrix products: 86.7 us -> 12.9 us
  waiting for transfers between devices: 243 us -> 170 us
  starting transfers between devices: 147 us -> 83.5 us
  other arithmetic: 61.6 us -> 74.9 us
    pallas_call x0 -> x17, Pallas kernels: none -> 180 us  [call(): pl.pallas_call(kernel, name=name, grid=grid, in_specs=in_specs, out_shape...]
    ppermute x30 -> x0, waiting for transfers between devices: 91.6 us -> none  [the longest x15 52.4 us: scatter(): got = lax.ppermute(out, 'z', [(i, (i + k) % nz) for i in range(nz)])]
    ppermute x74 -> x62, waiting for transfers between devices: 64.5 us -> 138 us  [swap(): lax.ppermute(value, axis, [(i, i ^ bit) for i in range(self.sizes[axis])])]
    unnamed x255 -> x150, local copies, waits for them, and re-layouts: 69.3 us -> 9.16 us
    dot_general x27 -> x11, matrix products: 68.6 us -> 10.2 us  [dot(): lax.dot_general(a, b, (dims, batch), precision=precision, preferred_eleme...]
    ppermute x30 -> x23, waiting for transfers between devices: 87 us -> 32.4 us  [permute(): return lax.ppermute(value, AXES, self.flat(move))]
    dynamic_update_slice x57 -> x0, local copies, waits for them, and re-layouts: 47.7 us -> none  [the longest x20 22.2 us: gather(): lax.dynamic_update_slice(out, mine[a][b][None, None, :, None], (y ^ fy, c...]
    ppermute x30 -> x0, starting transfers between devices: 44.1 us -> none  [the longest x15 27.6 us: gather(): got = lax.ppermute(piece, 'z', [(i, (i + k) % nz) for i in range(nz)])]
  transfers between devices with their start and end apart: 135 -> 85, of which waited for: 52 -> 42; matrix products, arithmetic and copies ran while one was open for 37% -> 15% of each run, Pallas kernels for 0% -> 24%
where the time goes in v2:
time: 583 us; the launch traced here: 577 us
  Pallas kernels  180 us (31%)
  waiting for transfers between devices  170 us (29%)
  starting transfers between devices  83.5 us (14%)
  other arithmetic  74.9 us (13%)
  local copies, waits for them, and re-layouts  40.6 us (7%)
  between operations  14.6 us (3%)
  matrix products  12.9 us (2%)
    pallas_call x17, Pallas kernels, call(): pl.pallas_call(kernel, name=name, grid=grid, in_specs=in_specs, out_shape...  180 us
    ppermute x62, waiting for transfers between devices, swap(): lax.ppermute(value, axis, [(i, i ^ bit) for i in range(self.sizes[axis])])  138 us
    ppermute x62, starting transfers between devices, swap(): lax.ppermute(value, axis, [(i, i ^ bit) for i in range(self.sizes[axis])])  60.6 us
    ppermute x23, waiting for transfers between devices, permute(): return lax.ppermute(value, AXES, self.flat(move))  32.4 us
    convert_element_type x20, other arithmetic, add(): return (left.astype(F32) + right.astype(F32)).astype(BF)  29.1 us
    ppermute x23, starting transfers between devices, permute(): return lax.ppermute(value, AXES, self.flat(move))  22.9 us
  transfers between devices with their start and end apart: 85, of which 42 were waited for; matrix products, arithmetic and copies ran while one was open for 15% of the time, Pallas kernels for 24%

profile of v2, /device:TPU:0, one launch (start us, length us, event | category | flops | bytes accessed | tf_op | source)
XLA Modules:
  0.0 576.9 jit_solution(3992784145489301853)
XLA Ops:
  4.2 3.1 collective-permute-start
  32.7 6.8 %collective-permute-done.8 = bf16[656,128]{1,0:T(8,128)(2,1)S(1)} collective-permute-done((bf16[656,128]{1,0:T(8,128)(2,1)S(1)}, bf16[656,128]{1,0:T(8,128)(2,1)S(1)}, u32[]{:S(2)}, u32[]{:S(2)}) %collective-permute-start.8) | collective-permute-done | bytes 167968 | tf_op jit(solution)/shard_map/ppermute | solution.py:58
  39.9 3.0 collective-permute-start.9
  43.8 10.1 %collective-permute-done.10 = bf16[1024,128]{1,0:T(8,128)(2,1)S(1)} collective-permute-done((bf16[1024,128]{1,0:T(8,128)(2,1)S(1)}, bf16[1024,128]{1,0:T(8,128)(2,1)S(1)}, u32[]{:S(2)}, u32[]{:S(2)}) %collective-permute-start.10) | collective-permute-done | bytes 262176 | tf_op jit(solution)/shard_map/ppermute | solution.py:58
  59.3 3.4 collective-permute-done.16
  62.8 3.7 collective-permute-start.17
  73.0 12.3 %collective-permute-done.20 = bf16[256,512]{1,0:T(8,128)(2,1)S(1)} collective-permute-done((bf16[256,512]{1,0:T(8,128)(2,1)S(1)}, bf16[256,512]{1,0:T(8,128)(2,1)S(1)}, u32[]{:S(2)}, u32[]{:S(2)}) %collective-permute-start.20) | collective-permute-done | bytes 262176 | tf_op jit(solution)/shard_map/ppermute | solution.py:58
  87.5 12.0 %collective-permute-done.22 = f32[1024,16]{0,1:T(8,128)S(1)} collective-permute-done((f32[1024,16]{0,1:T(8,128)S(1)}, f32[1024,16]{0,1:T(8,128)S(1)}, u32[]{:S(2)}, u32[]{:S(2)}) %collective-permute-start.22) | collective-permute-done | bytes 65568 | tf_op jit(solution)/shard_map/ppermute | solution.py:58
  101.7 13.7 %collective-permute-done.27 = bf16[256,512]{1,0:T(8,128)(2,1)S(1)} collective-permute-done((bf16[256,512]{1,0:T(8,128)(2,1)S(1)}, bf16[256,512]{1,0:T(8,128)(2,1)S(1)}, u32[]{:S(2)}, u32[]{:S(2)}) %collective-permute-start.27) | collective-permute-done | bytes 262176 | tf_op jit(solution)/shard_map/ppermute | solution.py:58
  119.6 9.0 %collective-permute-done.25 = f32[1024,16]{0,1:T(8,128)S(1)} collective-permute-done((f32[1024,16]{0,1:T(8,128)S(1)}, f32[1024,16]{0,1:T(8,128)S(1)}, u32[]{:S(2)}, u32[]{:S(2)}) %collective-permute-start.25) | collective-permute-done | bytes 65568 | tf_op jit(solution)/shard_map/ppermute | solution.py:58
  137.0 5.9 %assemble.1 = (bf16[384,1024]{1,0:T(8,128)(2,1)}, bf16[4,8,48,128]{3,2,1,0:T(8,128)(2,1)}, bf16[1024,1024]{1,0:T(8,128)(2,1)}) custom-call(s32[4]{0:T(128)} %pad_add_fusion.1.r_0_, bf16[8,656,128]{2,1,0:T(8,128)(2,1)} %copy-done.3, bf16[8,656,128]{2,1,0:T(8,128)(2,1)} %copy-done.3, bf16[8,656,128]{2,1,0:T(8,128)(2,1)} %copy-done.4, ...), custom_call_target="tpu_custom_call" | custom-call | bytes 8388608 | tf_op jit(solution)/shard_map/assemble/pallas_call | solution.py:575
  143.0 5.5 table_values.1.tv_ref
  162.7 4.7 reshape.369
  172.7 14.0 %pool.1 = (bf16[256,1024]{1,0:T(8,128)(2,1)}, bf16[16,256,384]{2,1,0:T(8,128)(2,1)}, f32[16,256,128]{2,1,0:T(8,128)}) custom-call(bf16[256,384]{1,0:T(8,128)(2,1)} %fusion.2.x_ref, bf16[384,128]{1,0:T(8,128)(2,1)} %constant.171.clone.e_ref, f32[384,128]{1,0:T(8,128)} %pad.10.tu_ref, bf16[384,1024]{1,0:T(8,128)(2,1)} %table_values.1.tv_ref), custom_call_target="tpu_custom_call" | custom-call | flops 2415919104 | bytes 8388608 | tf_op jit(solution)/shard_map/pool/pallas_call | solution.py:575
  186.7 5.5 enter.1
  197.7 20.9 %attend.1 = (bf16[256,3072]{1,0:T(8,128)(2,1)}, f32[16,2,128,128]{3,2,1,0:T(8,128)}, bf16[256,1024]{1,0:T(8,128)(2,1)}, f32[256,1024]{1,0:T(8,128)}, bf16[256,1024]{1,0:T(8,128)(2,1)}) custom-call(s32[4]{0:T(128)} %pad_add_fusion.1.r_0_, s32[2]{0:T(128)} %bitcast.177, f32[256,1024]{1,0:T(8,128)} %get-tuple-element.165.r_2_.r_3_, ...), custom_call_target="tpu_custom_call" | custom-call | flops 2415919104 | bytes 16777216 | tf_op jit(solution)/shard_map/attend/pallas_call | solution.py:575
  221.2 6.5 %collective-permute-done.38.r_10_.r_11_ = bf16[8,256,512]{2,1,0:T(8,128)(2,1)} collective-permute-done((bf16[8,256,512]{2,1,0:T(8,128)(2,1)}, bf16[8,256,512]{2,1,0:T(8,128)(2,1)}, u32[]{:S(2)}, u32[]{:S(2)}) %collective-permute-start.38) | collective-permute-done | bytes 2097184 | tf_op jit(solution)/shard_map/ppermute | solution.py:55
  233.7 11.1 %up.1 = (bf16[256,4096]{1,0:T(8,128)(2,1)}, f32[256,4096]{1,0:T(8,128)}) custom-call(s32[4]{0:T(128)} %pad_add_fusion.1.r_0_, bf16[256,1024]{1,0:T(8,128)(2,1)} %get-tuple-element.170.r_1_, bf16[8,256,512]{2,1,0:T(8,128)(2,1)} %pad_maximum_fusion.1.r_2_.r_3_.r_5_.r_6_, bf16[8,256,512]{2,1,0:T(8,128)(2,1)} %pad_maximum_fusion.1.r_2_.r_3_.r_5_.r_6_, ...), custom_call_target="tpu_custom_call" | custom-call | flops 2147483648 | bytes 16777216 | tf_op jit(solution)/shard_map/up/pallas_call | solution.py:575
  246.2 20.4 %down.1 = (f32[8,128]{1,0:T(8,128)}, f32[256,1024]{1,0:T(8,128)}, bf16[256,1024]{1,0:T(8,128)(2,1)}, bf16[1024,192]{1,0:T(8,128)(2,1)}, bf16[256,4096]{1,0:T(8,128)(2,1)}) custom-call(s32[4]{0:T(128)} %pad_add_fusion.1.r_0_, f32[1]{0:T(128)} %slice.418.r_1_, f32[256,1024]{1,0:T(8,128)} %get-tuple-element.169.r_2_, ...), custom_call_target="tpu_custom_call" | custom-call | flops 4294967296 | bytes 33554432 | tf_op jit(solution)/shard_map/down/pallas_call | solution.py:575
  266.6 6.5 %down_grad.1 = (bf16[16,256,512]{2,1,0:T(8,128)(2,1)}, bf16[16,256,512]{2,1,0:T(8,128)(2,1)}) custom-call(s32[4]{0:T(128)} %pad_add_fusion.1.r_0_, bf16[256,1024]{1,0:T(8,128)(2,1)} %get-tuple-element.189.r_1_, bf16[256,4096]{1,0:T(8,128)(2,1)} %get-tuple-element.181.r_3_.r_2_), custom_call_target="tpu_custom_call" | custom-call | flops 2147483648 | bytes 12582912 | tf_op jit(solution)/shard_map/down_grad/pallas_call | solution.py:575
  273.6 6.7 %up_grad.1 = (bf16[16,256,512]{2,1,0:T(8,128)(2,1)}, bf16[16,256,512]{2,1,0:T(8,128)(2,1)}) custom-call(s32[4]{0:T(128)} %pad_add_fusion.1.r_0_, bf16[256,1024]{1,0:T(8,128)(2,1)} %get-tuple-element.170.r_1_, bf16[256,4096]{1,0:T(8,128)(2,1)} %get-tuple-element.195.r_2_.r_1_), custom_call_target="tpu_custom_call" | custom-call | flops 2147483648 | bytes 12582912 | tf_op jit(solution)/shard_map/up_grad/pallas_call | solution.py:575
  280.7 3.8 add_convert_fusion.2
  286.0 12.8 %up_back.1 = (f32[256,1024]{1,0:T(8,128)}, bf16[256,1024]{1,0:T(8,128)(2,1)}, f32[1,1024]{1,0:T(1,128)}) custom-call(s32[4]{0:T(128)} %pad_add_fusion.1.r_0_, bf16[256,4096]{1,0:T(8,128)(2,1)} %get-tuple-element.195.r_2_.r_1_, f32[256,1024]{1,0:T(8,128)} %get-tuple-element.169.r_2_, f32[1,1024]{1,0:T(1,128)} %get-tuple-element.386.r_4_.r_3_, ...), custom_call_target="tpu_custom_call" | custom-call | flops 2147483648 | bytes 16777216 | tf_op jit(solution)/shard_map/up_back/pallas_call | solution.py:575
  298.9 15.4 %attend_back.1.r_2_ = bf16[256,3072]{1,0:T(8,128)(2,1)} custom-call(s32[4]{0:T(128)} %pad_add_fusion.1.r_0_, bf16[256,1024]{1,0:T(8,128)(2,1)} %get-tuple-element.214.r_1_.r_3_, bf16[256,3072]{1,0:T(8,128)(2,1)} %get-tuple-element.199.r_2_, f32[16,2,128,128]{3,2,1,0:T(8,128)} %get-tuple-element.200.r_3_, bf16[8,1024,128]{2,1,0:T(8,128)(2,1)} %copy-done, ...), custom_call_target="tpu_custom_call" | custom-call | flops 939524096 | bytes 4194304 | tf_op jit(solution)/shard_map/attend_back/pallas_call | solution.py:575
  314.3 3.7 add_convert_fusion.10
  318.0 3.8 add_convert_fusion
  321.8 7.1 %qkv_grad.1 = (bf16[16,768,128]{2,1,0:T(8,128)(2,1)}, bf16[16,768,128]{2,1,0:T(8,128)(2,1)}) custom-call(s32[4]{0:T(128)} %pad_add_fusion.1.r_0_, bf16[256,1024]{1,0:T(8,128)(2,1)} %get-tuple-element.166.r_3_.r_1_, bf16[256,3072]{1,0:T(8,128)(2,1)} %attend_back.1.r_2_), custom_call_target="tpu_custom_call" | custom-call | flops 1610612736 | bytes 10485760 | tf_op jit(solution)/shard_map/qkv_grad/pallas_call | solution.py:575
  331.1 20.0 %leave.1 = (bf16[256,1024]{1,0:T(8,128)(2,1)}, f32[1,1024]{1,0:T(1,128)}, f32[2,1024]{1,0:T(2,128)}, bf16[256,1024]{1,0:T(8,128)(2,1)}) custom-call(s32[4]{0:T(128)} %pad_add_fusion.1.r_0_, f32[256,1024]{1,0:T(8,128)} %get-tuple-element.197.r_1_, bf16[256,3072]{1,0:T(8,128)(2,1)} %attend_back.1.r_2_, f32[256,1024]{1,0:T(8,128)} %get-tuple-element.165.r_2_.r_3_, ...), custom_call_target="tpu_custom_call" | custom-call | flops 2147483648 | bytes 8388608 | tf_op jit(solution)/shard_map/leave/pallas_call | solution.py:575
  351.1 5.4 collective-permute-done.46
  357.8 8.8 %collective-permute-done.47 = bf16[8,256,512]{2,1,0:T(8,128)(2,1)} collective-permute-done((bf16[8,256,512]{2,1,0:T(8,128)(2,1)}, bf16[8,256,512]{2,1,0:T(8,128)(2,1)}, u32[]{:S(2)}, u32[]{:S(2)}) %collective-permute-start.47) | collective-permute-done | bytes 2097184 | tf_op jit(solution)/shard_map/ppermute | solution.py:55
  366.6 3.5 add_convert_fusion.8
  370.1 4.3 add_convert_fusion.4
  376.4 6.3 %pair_grad.1 = (bf16[16,512,128]{2,1,0:T(8,128)(2,1)}, bf16[16,512,128]{2,1,0:T(8,128)(2,1)}) custom-call(s32[4]{0:T(128)} %pad_add_fusion.1.r_0_, bf16[256,1024]{1,0:T(8,128)(2,1)} %get-tuple-element.207.r_1_, bf16[256,1024]{1,0:T(8,128)(2,1)} %get-tuple-element.164.r_1_.r_2_, bf16[256,1024]{1,0:T(8,128)(2,1)} %get-tuple-element.214.r_1_.r_3_, ...), custom_call_target="tpu_custom_call" | custom-call | flops 1073741824 | bytes 8388608 | tf_op jit(solution)/shard_map/pair_grad/pallas_call | solution.py:575
  389.8 3.5 reshape.374.r_2_
  394.9 3.2 concatenate.64
  398.1 13.1 %pool_back.1 = (f32[384,1024]{1,0:T(8,128)}, f32[8,2,384]{2,1,0:T(2,128)}) custom-call(bf16[256,384]{1,0:T(8,128)(2,1)} %fusion.2.x_ref, bf16[384,128]{1,0:T(8,128)(2,1)} %constant.171.clone.e_ref, bf16[384,1024]{1,0:T(8,128)(2,1)} %table_values.1.tv_ref, bf16[16,256,384]{2,1,0:T(8,128)(2,1)} %get-tuple-element.186.a_ref, ...), custom_call_target="tpu_custom_call" | custom-call | flops 2818572288 | bytes 8388608 | tf_op jit(solution)/shard_map/pool_back/pallas_call | solution.py:575
  414.9 3.2 rows.1
  439.1 5.2 collective-permute-done.60
  446.9 7.2 %collective-permute-done.61 = bf16[4,768,128]{2,1,0:T(8,128)(2,1)S(1)} collective-permute-done((bf16[4,768,128]{2,1,0:T(8,128)(2,1)S(1)}, bf16[4,768,128]{2,1,0:T(8,128)(2,1)S(1)}, u32[]{:S(2)}, u32[]{:S(2)}) %collective-permute-start.61) | collective-permute-done | bytes 786464 | tf_op jit(solution)/shard_map/ppermute | solution.py:55
  460.7 4.3 collective-permute-done.67
  465.1 5.5 collective-permute-done.65
  470.9 5.8 collective-permute-done.68
  482.5 4.4 collective-permute-done.69
  488.7 5.8 %squares.1 = (bf16[1024,1024]{1,0:T(8,128)(2,1)}, bf16[1024,1024]{1,0:T(8,128)(2,1)}) custom-call(s32[4]{0:T(128)} %pad_add_fusion.1.r_0_, bf16[8,512,128]{2,1,0:T(8,128)(2,1)} %copy-done.10, bf16[8,512,128]{2,1,0:T(8,128)(2,1)} %copy-done.10, bf16[8,512,128]{2,1,0:T(8,128)(2,1)} %collective-permute-done.40.r_3_.r_4_, ...), custom_call_target="tpu_custom_call" | custom-call | bytes 1048576 | tf_op jit(solution)/shard_map/squares/pallas_call | solution.py:575
  522.1 8.8 %collective-permute-done.78 = bf16[8,96,128]{2,1,0:T(8,128)(2,1)} collective-permute-done((bf16[8,96,128]{2,1,0:T(8,128)(2,1)}, bf16[8,96,128]{2,1,0:T(8,128)(2,1)}, u32[]{:S(2)}, u32[]{:S(2)}) %collective-permute-start.78) | collective-permute-done | bytes 196640 | tf_op jit(solution)/shard_map/ppermute | solution.py:58
  550.0 3.5 collective-permute-done.82
  554.2 3.8 collective-permute-done.83
  568.1 3.8 fusion.69
  (449 shorter events, 201.4 us)
Async XLA Ops:
  8.1 34.7 %collective-permute-start.5 = (bf16[2,128,48]{1,2,0:T(8,128)(2,1)S(1)}, bf16[2,128,48]{1,2,0:T(8,128)(2,1)S(1)}, u32[]{:S(2)}, u32[]{:S(2)}) collective-permute-start(bf16[2,128,48]{1,2,0:T(8,128)(2,1)S(1)} %get-tuple-element.409), channel_id=1, source_target_pairs={{0,8},{1,9},{2,10},{3,11},{4,12},{5,13},{6,14},{7,15},{8,0},{9,1},... | collective-permute-start | bytes 73736 | tf_op jit(solution)/shard_map/ppermute | solution.py:55
  8.2 31.4 %collective-permute-start.7 = (bf16[2,128,48]{1,2,0:T(8,128)(2,1)S(1)}, bf16[2,128,48]{1,2,0:T(8,128)(2,1)S(1)}, u32[]{:S(2)}, u32[]{:S(2)}) collective-permute-start(bf16[2,128,48]{1,2,0:T(8,128)(2,1)S(1)} %get-tuple-element.411), channel_id=1, source_target_pairs={{0,24},{1,25},{2,26},{3,27},{4,28},{5,29},{6,30},{7,31},{8,16},{9,... | collective-permute-start | bytes 73736 | tf_op jit(solution)/shard_map/ppermute | solution.py:55
  9.8 22.6 %collective-permute-start.6 = (bf16[2,128,48]{1,2,0:T(8,128)(2,1)S(1)}, bf16[2,128,48]{1,2,0:T(8,128)(2,1)S(1)}, u32[]{:S(2)}, u32[]{:S(2)}) collective-permute-start(bf16[2,128,48]{1,2,0:T(8,128)(2,1)S(1)} %get-tuple-element.412), channel_id=1, source_target_pairs={{0,16},{1,17},{2,18},{3,19},{4,20},{5,21},{6,22},{7,23},{8,24},{9,... | collective-permute-start | bytes 73736 | tf_op jit(solution)/shard_map/ppermute | solution.py:55
  30.9 26.7 %collective-permute-start.15 = (f32[1024,16]{0,1:T(8,128)S(1)}, f32[1024,16]{0,1:T(8,128)S(1)}, u32[]{:S(2)}, u32[]{:S(2)}) collective-permute-start(f32[1024,16]{0,1:T(8,128)S(1)} %get-tuple-element.419), channel_id=1, source_target_pairs={{0,1},{1,0},{2,3},{3,2},{4,5},{5,4},{6,7},{7,6},{8,9},{9,8},{10,11... | collective-permute-start | bytes 196616 | tf_op jit(solution)/shard_map/ppermute | solution.py:58
  39.5 14.3 %collective-permute-start.10 = (bf16[1024,128]{1,0:T(8,128)(2,1)S(1)}, bf16[1024,128]{1,0:T(8,128)(2,1)S(1)}, u32[]{:S(2)}, u32[]{:S(2)}) collective-permute-start(bf16[1024,128]{1,0:T(8,128)(2,1)S(1)} %bitcast.148), channel_id=1, source_target_pairs={{0,4},{2,6},{4,0},{6,2},{1,5},{3,7},{5,1},{7,3},{8,12},{10,14},{12... | collective-permute-start | bytes 786440 | tf_op jit(solution)/shard_map/ppermute | solution.py:58
  39.9 16.1 %collective-permute-start.9 = (bf16[2,656,128]{2,1,0:T(8,128)(2,1)S(1)}, bf16[2,656,128]{2,1,0:T(8,128)(2,1)S(1)}, u32[]{:S(2)}, u32[]{:S(2)}) collective-permute-start(bf16[2,656,128]{2,1,0:T(8,128)(2,1)S(1)} %pad_maximum_fusion.13), channel_id=1, source_target_pairs={{0,2},{2,0},{4,6},{6,4},{1,3},{3,1},{5,7},{7,5},{8,10},{10,8},{12,... | collective-permute-start | bytes 1007624 | tf_op jit(solution)/shard_map/ppermute | solution.py:58
  56.0 12.8 %collective-permute-start.14 = (bf16[2,1024,128]{2,1,0:T(8,128)(2,1)S(1)}, bf16[2,1024,128]{2,1,0:T(8,128)(2,1)S(1)}, u32[]{:S(2)}, u32[]{:S(2)}) collective-permute-start(bf16[2,1024,128]{2,1,0:T(8,128)(2,1)S(1)} %pad_maximum_fusion.9), channel_id=1, source_target_pairs={{0,2},{2,0},{4,6},{6,4},{1,3},{3,1},{5,7},{7,5},{8,10},{10,8},{12,... | collective-permute-start | bytes 1572872 | tf_op jit(solution)/shard_map/ppermute | solution.py:58
  56.1 12.9 %collective-permute-start.13 = (bf16[4,656,128]{2,1,0:T(8,128)(2,1)S(1)}, bf16[4,656,128]{2,1,0:T(8,128)(2,1)S(1)}, u32[]{:S(2)}, u32[]{:S(2)}) collective-permute-start(bf16[4,656,128]{2,1,0:T(8,128)(2,1)S(1)} %pad_maximum_fusion.8), channel_id=1, source_target_pairs={{0,1},{1,0},{2,3},{3,2},{4,5},{5,4},{6,7},{7,6},{8,24},{9,25},{10,... | collective-permute-start | bytes 2015240 | tf_op jit(solution)/shard_map/ppermute | solution.py:55
  69.1 30.6 %collective-permute-start.18 = (bf16[8,656,128]{2,1,0:T(8,128)(2,1)S(1)}, bf16[8,656,128]{2,1,0:T(8,128)(2,1)S(1)}, u32[]{:S(2)}, u32[]{:S(2)}) collective-permute-start(bf16[8,656,128]{2,1,0:T(8,128)(2,1)S(1)} %pad_maximum_fusion.3.r_1_.r_2_.r_3_.r_4_.r_5_.r_13_.r_14_), channel_id=1, source_target_pairs={{0,16},{1,17},{2,18},{3,19},{4,20},{5,21},{6,22},{7,23},{8,9},{9,8... | collective-permute-start | bytes 4030472 | tf_op jit(solution)/shard_map/ppermute | solution.py:55
  70.7 28.8 %collective-permute-start.19 = (bf16[4,1024,128]{2,1,0:T(8,128)(2,1)S(1)}, bf16[4,1024,128]{2,1,0:T(8,128)(2,1)S(1)}, u32[]{:S(2)}, u32[]{:S(2)}) collective-permute-start(bf16[4,1024,128]{2,1,0:T(8,128)(2,1)S(1)} %pad_maximum_fusion.4), channel_id=1, source_target_pairs={{0,1},{1,0},{2,3},{3,2},{4,5},{5,4},{6,7},{7,6},{8,24},{9,25},{10,... | collective-permute-start | bytes 3145736 | tf_op jit(solution)/shard_map/ppermute | solution.py:55
  72.2 13.1 %collective-permute-start.20 = (bf16[256,512]{1,0:T(8,128)(2,1)S(1)}, bf16[256,512]{1,0:T(8,128)(2,1)S(1)}, u32[]{:S(2)}, u32[]{:S(2)}) collective-permute-start(bf16[256,512]{1,0:T(8,128)(2,1)S(1)} %get-tuple-element.152), channel_id=1, source_target_pairs={{0,4},{2,6},{4,0},{6,2},{1,5},{3,7},{5,1},{7,3},{8,12},{10,14},{12... | collective-permute-start | bytes 786440 | tf_op jit(solution)/shard_map/ppermute | solution.py:58
  85.4 14.4 %collective-permute-start.21 = (bf16[2,256,512]{2,1,0:T(8,128)(2,1)S(1)}, bf16[2,256,512]{2,1,0:T(8,128)(2,1)S(1)}, u32[]{:S(2)}, u32[]{:S(2)}) collective-permute-start(bf16[2,256,512]{2,1,0:T(8,128)(2,1)S(1)} %pad_maximum_fusion.10), channel_id=1, source_target_pairs={{0,2},{2,0},{4,6},{6,4},{1,3},{3,1},{5,7},{7,5},{8,10},{10,8},{12,... | collective-permute-start | bytes 1572872 | tf_op jit(solution)/shard_map/ppermute | solution.py:58
  85.4 14.1 %collective-permute-start.22 = (f32[1024,16]{0,1:T(8,128)S(1)}, f32[1024,16]{0,1:T(8,128)S(1)}, u32[]{:S(2)}, u32[]{:S(2)}) collective-permute-start(f32[1024,16]{0,1:T(8,128)S(1)} %add.492), channel_id=1, source_target_pairs={{0,2},{2,0},{4,6},{6,4},{1,3},{3,1},{5,7},{7,5},{8,10},{10,8},{12,... | collective-permute-start | bytes 196616 | tf_op jit(solution)/shard_map/ppermute | solution.py:58
  99.8 31.0 %collective-permute-start.26 = (bf16[8,1024,128]{2,1,0:T(8,128)(2,1)S(1)}, bf16[8,1024,128]{2,1,0:T(8,128)(2,1)S(1)}, u32[]{:S(2)}, u32[]{:S(2)}) collective-permute-start(bf16[8,1024,128]{2,1,0:T(8,128)(2,1)S(1)} %pad_maximum_fusion.r_5_.r_6_.r_13_.r_14_.r_4_), channel_id=1, source_target_pairs={{0,16},{1,17},{2,18},{3,19},{4,20},{5,21},{6,22},{7,23},{8,9},{9,8... | collective-permute-start | bytes 6291464 | tf_op jit(solution)/shard_map/ppermute | solution.py:55
  100.4 30.3 %collective-permute-start.23 = (bf16[8,656,128]{2,1,0:T(8,128)(2,1)S(1)}, bf16[8,656,128]{2,1,0:T(8,128)(2,1)S(1)}, u32[]{:S(2)}, u32[]{:S(2)}) collective-permute-start(bf16[8,656,128]{2,1,0:T(8,128)(2,1)S(1)} %pad_maximum_fusion.3.r_1_.r_2_.r_3_.r_4_.r_5_.r_13_.r_14_), channel_id=1, source_target_pairs={{0,8},{8,0},{1,9},{9,1},{2,10},{10,2},{3,11},{11,3},{4,12},{12,4},... | collective-permute-start | bytes 4030472 | tf_op jit(solution)/shard_map/ppermute | solution.py:58
  100.4 30.3 %collective-permute-start.24 = (bf16[8,656,128]{2,1,0:T(8,128)(2,1)S(1)}, bf16[8,656,128]{2,1,0:T(8,128)(2,1)S(1)}, u32[]{:S(2)}, u32[]{:S(2)}) collective-permute-start(bf16[8,656,128]{2,1,0:T(8,128)(2,1)S(1)} %collective-permute-done.18.r_3_.r_4_.r_5_.r_6_.r_7_.r_15_.r_16_), channel_id=1, source_target_pairs={{0,8},{8,0},{1,9},{9,1},{2,10},{10,2},{3,11},{11,3},{4,12},{12,4},... | collective-permute-start | bytes 4030472 | tf_op jit(solution)/shard_map/ppermute | solution.py:58
  100.9 14.5 %collective-permute-start.27 = (bf16[256,512]{1,0:T(8,128)(2,1)S(1)}, bf16[256,512]{1,0:T(8,128)(2,1)S(1)}, u32[]{:S(2)}, u32[]{:S(2)}) collective-permute-start(bf16[256,512]{1,0:T(8,128)(2,1)S(1)} %get-tuple-element.158), channel_id=1, source_target_pairs={{0,4},{2,6},{4,0},{6,2},{1,5},{3,7},{5,1},{7,3},{8,12},{10,14},{12... | collective-permute-start | bytes 786440 | tf_op jit(solution)/shard_map/ppermute | solution.py:58
  115.4 15.3 %collective-permute-start.28 = (bf16[2,256,512]{2,1,0:T(8,128)(2,1)S(1)}, bf16[2,256,512]{2,1,0:T(8,128)(2,1)S(1)}, u32[]{:S(2)}, u32[]{:S(2)}) collective-permute-start(bf16[2,256,512]{2,1,0:T(8,128)(2,1)S(1)} %pad_maximum_fusion.11), channel_id=1, source_target_pairs={{0,2},{2,0},{4,6},{6,4},{1,3},{3,1},{5,7},{7,5},{8,10},{10,8},{12,... | collective-permute-start | bytes 1572872 | tf_op jit(solution)/shard_map/ppermute | solution.py:58
  115.5 13.0 %collective-permute-start.25 = (f32[1024,16]{0,1:T(8,128)S(1)}, f32[1024,16]{0,1:T(8,128)S(1)}, u32[]{:S(2)}, u32[]{:S(2)}) collective-permute-start(f32[1024,16]{0,1:T(8,128)S(1)} %add.493), channel_id=1, source_target_pairs={{0,4},{2,6},{4,0},{6,2},{1,5},{3,7},{5,1},{7,3},{8,12},{10,14},{12... | collective-permute-start | bytes 196616 | tf_op jit(solution)/shard_map/ppermute | solution.py:58
  131.9 21.0 %collective-permute-start.30 = (bf16[8,1024,128]{2,1,0:T(8,128)(2,1)S(1)}, bf16[8,1024,128]{2,1,0:T(8,128)(2,1)S(1)}, u32[]{:S(2)}, u32[]{:S(2)}) collective-permute-start(bf16[8,1024,128]{2,1,0:T(8,128)(2,1)S(1)} %pad_maximum_fusion.r_5_.r_6_.r_13_.r_14_.r_4_), channel_id=1, source_target_pairs={{0,8},{8,0},{1,9},{9,1},{2,10},{10,2},{3,11},{11,3},{4,12},{12,4},... | collective-permute-start | bytes 6291464 | tf_op jit(solution)/shard_map/ppermute | solution.py:58
  132.3 20.6 %collective-permute-start.31 = (bf16[8,1024,128]{2,1,0:T(8,128)(2,1)S(1)}, bf16[8,1024,128]{2,1,0:T(8,128)(2,1)}, u32[]{:S(2)}, u32[]{:S(2)}) collective-permute-start(bf16[8,1024,128]{2,1,0:T(8,128)(2,1)S(1)} %collective-permute-done.26.r_7_.r_8_.r_15_.r_16_.r_6_), channel_id=1, source_target_pairs={{0,8},{8,0},{1,9},{9,1},{2,10},{10,2},{3,11},{11,3},{4,12},{12,4},... | collective-permute-start | bytes 6291464 | tf_op jit(solution)/shard_map/ppermute | solution.py:58
  132.4 17.8 %collective-permute-start.29 = (bf16[4,256,512]{2,1,0:T(8,128)(2,1)}, bf16[4,256,512]{2,1,0:T(8,128)(2,1)}, u32[]{:S(2)}, u32[]{:S(2)}) collective-permute-start(bf16[4,256,512]{2,1,0:T(8,128)(2,1)} %pad_maximum_fusion.5), channel_id=1, source_target_pairs={{0,1},{1,0},{2,3},{3,2},{4,5},{5,4},{6,7},{7,6},{8,24},{9,25},{10,... | collective-permute-start | bytes 3145736 | tf_op jit(solution)/shard_map/ppermute | solution.py:55
  133.6 14.9 %collective-permute-start.32 = (bf16[512,128]{1,0:T(8,128)(2,1)}, bf16[512,128]{1,0:T(8,128)(2,1)S(1)}, u32[]{:S(2)}, u32[]{:S(2)}) collective-permute-start(bf16[512,128]{1,0:T(8,128)(2,1)} %bitcast.29), channel_id=1, source_target_pairs={{0,4},{2,6},{4,0},{6,2},{1,5},{3,7},{5,1},{7,3},{8,12},{10,14},{12... | collective-permute-start | bytes 393224 | tf_op jit(solution)/shard_map/ppermute | solution.py:58
  154.2 41.9 %collective-permute-start.33 = (bf16[8,256,512]{2,1,0:T(8,128)(2,1)}, bf16[8,256,512]{2,1,0:T(8,128)(2,1)S(1)}, u32[]{:S(2)}, u32[]{:S(2)}) collective-permute-start(bf16[8,256,512]{2,1,0:T(8,128)(2,1)} %pad_maximum_fusion.1.r_2_.r_3_.r_5_.r_6_), channel_id=1, source_target_pairs={{0,16},{1,17},{2,18},{3,19},{4,20},{5,21},{6,22},{7,23},{8,9},{9,8... | collective-permute-start | bytes 6291464 | tf_op jit(solution)/shard_map/ppermute | solution.py:55
  160.2 33.0 %collective-permute-start.34 = (bf16[4,256,512]{2,1,0:T(8,128)(2,1)}, bf16[4,256,512]{2,1,0:T(8,128)(2,1)}, u32[]{:S(2)}, u32[]{:S(2)}) collective-permute-start(bf16[4,256,512]{2,1,0:T(8,128)(2,1)} %pad_maximum_fusion.6), channel_id=1, source_target_pairs={{0,1},{1,0},{2,3},{3,2},{4,5},{5,4},{6,7},{7,6},{8,24},{9,25},{10,... | collective-permute-start | bytes 3145736 | tf_op jit(solution)/shard_map/ppermute | solution.py:55
  172.4 19.7 %collective-permute-start.35 = (bf16[2,512,128]{2,1,0:T(8,128)(2,1)}, bf16[2,512,128]{2,1,0:T(8,128)(2,1)S(1)}, u32[]{:S(2)}, u32[]{:S(2)}) collective-permute-start(bf16[2,512,128]{2,1,0:T(8,128)(2,1)} %pad_maximum_fusion.14), channel_id=1, source_target_pairs={{0,2},{2,0},{4,6},{6,4},{1,3},{3,1},{5,7},{7,5},{8,10},{10,8},{12,... | collective-permute-start | bytes 786440 | tf_op jit(solution)/shard_map/ppermute | solution.py:58
  196.0 23.7 %collective-permute-start.36 = (bf16[8,256,512]{2,1,0:T(8,128)(2,1)}, bf16[8,256,512]{2,1,0:T(8,128)(2,1)S(1)}, u32[]{:S(2)}, u32[]{:S(2)}) collective-permute-start(bf16[8,256,512]{2,1,0:T(8,128)(2,1)} %pad_maximum_fusion.1.r_2_.r_3_.r_5_.r_6_), channel_id=1, source_target_pairs={{0,8},{8,0},{1,9},{9,1},{2,10},{10,2},{3,11},{11,3},{4,12},{12,4},... | collective-permute-start | bytes 6291464 | tf_op jit(solution)/shard_map/ppermute | solution.py:58
  196.0 23.8 %collective-permute-start.37 = (bf16[8,256,512]{2,1,0:T(8,128)(2,1)S(1)}, bf16[8,256,512]{2,1,0:T(8,128)(2,1)S(1)}, u32[]{:S(2)}, u32[]{:S(2)}) collective-permute-start(bf16[8,256,512]{2,1,0:T(8,128)(2,1)S(1)} %collective-permute-done.33.r_4_.r_5_.r_7_.r_8_), channel_id=1, source_target_pairs={{0,8},{8,0},{1,9},{9,1},{2,10},{10,2},{3,11},{11,3},{4,12},{12,4},... | collective-permute-start | bytes 6291464 | tf_op jit(solution)/shard_map/ppermute | solution.py:58
  196.5 31.1 %collective-permute-start.38 = (bf16[8,256,512]{2,1,0:T(8,128)(2,1)}, bf16[8,256,512]{2,1,0:T(8,128)(2,1)}, u32[]{:S(2)}, u32[]{:S(2)}) collective-permute-start(bf16[8,256,512]{2,1,0:T(8,128)(2,1)} %pad_maximum_fusion.2.r_8_.r_9_), channel_id=1, source_target_pairs={{0,16},{1,17},{2,18},{3,19},{4,20},{5,21},{6,22},{7,23},{8,9},{9,8... | collective-permute-start | bytes 6291464 | tf_op jit(solution)/shard_map/ppermute | solution.py:55
  197.0 21.5 %collective-permute-start.39 = (bf16[4,512,128]{2,1,0:T(8,128)(2,1)S(1)}, bf16[4,512,128]{2,1,0:T(8,128)(2,1)}, u32[]{:S(2)}, u32[]{:S(2)}) collective-permute-start(bf16[4,512,128]{2,1,0:T(8,128)(2,1)S(1)} %pad_maximum_fusion.12), channel_id=1, source_target_pairs={{0,1},{1,0},{2,3},{3,2},{4,5},{5,4},{6,7},{7,6},{8,24},{9,25},{10,... | collective-permute-start | bytes 1572872 | tf_op jit(solution)/shard_map/ppermute | solution.py:55
  227.7 17.1 %collective-permute-start.41 = (bf16[8,256,512]{2,1,0:T(8,128)(2,1)}, bf16[8,256,512]{2,1,0:T(8,128)(2,1)S(1)}, u32[]{:S(2)}, u32[]{:S(2)}) collective-permute-start(bf16[8,256,512]{2,1,0:T(8,128)(2,1)} %pad_maximum_fusion.2.r_8_.r_9_), channel_id=1, source_target_pairs={{0,8},{8,0},{1,9},{9,1},{2,10},{10,2},{3,11},{11,3},{4,12},{12,4},... | collective-permute-start | bytes 6291464 | tf_op jit(solution)/shard_map/ppermute | solution.py:58
  227.7 17.1 %collective-permute-start.42 = (bf16[8,256,512]{2,1,0:T(8,128)(2,1)}, bf16[8,256,512]{2,1,0:T(8,128)(2,1)}, u32[]{:S(2)}, u32[]{:S(2)}) collective-permute-start(bf16[8,256,512]{2,1,0:T(8,128)(2,1)} %collective-permute-done.38.r_10_.r_11_), channel_id=1, source_target_pairs={{0,8},{8,0},{1,9},{9,1},{2,10},{10,2},{3,11},{11,3},{4,12},{12,4},... | collective-permute-start | bytes 6291464 | tf_op jit(solution)/shard_map/ppermute | solution.py:58
  228.2 16.6 %collective-permute-start.40 = (bf16[8,512,128]{2,1,0:T(8,128)(2,1)S(1)}, bf16[8,512,128]{2,1,0:T(8,128)(2,1)}, u32[]{:S(2)}, u32[]{:S(2)}) collective-permute-start(bf16[8,512,128]{2,1,0:T(8,128)(2,1)S(1)} %pad_maximum_fusion.7.r_1_.r_2_), channel_id=1, source_target_pairs={{0,16},{1,17},{2,18},{3,19},{4,20},{5,21},{6,22},{7,23},{8,9},{9,8... | collective-permute-start | bytes 3145736 | tf_op jit(solution)/shard_map/ppermute | solution.py:55
  284.6 33.4 %collective-permute-start.45 = (bf16[16,256,512]{2,1,0:T(8,128)(2,1)}, bf16[16,256,512]{2,1,0:T(8,128)(2,1)}, u32[]{:S(2)}, u32[]{:S(2)}) collective-permute-start(bf16[16,256,512]{2,1,0:T(8,128)(2,1)} %get-tuple-element.202), channel_id=1, source_target_pairs={{0,8},{8,0},{1,9},{9,1},{2,10},{10,2},{3,11},{11,3},{4,12},{12,4},... | collective-permute-start | bytes 12582920 | tf_op jit(solution)/shard_map/ppermute | solution.py:58
  284.9 29.4 %collective-permute-start.44 = (bf16[8,256,512]{2,1,0:T(8,128)(2,1)}, bf16[8,256,512]{2,1,0:T(8,128)(2,1)}, u32[]{:S(2)}, u32[]{:S(2)}) collective-permute-start(bf16[8,256,512]{2,1,0:T(8,128)(2,1)} %get-tuple-element.201), channel_id=1, source_target_pairs={{0,16},{1,17},{2,18},{3,19},{4,20},{5,21},{6,22},{7,23},{8,9},{9,8... | collective-permute-start | bytes 6291464 | tf_op jit(solution)/shard_map/ppermute | solution.py:55
  328.9 41.1 %collective-permute-start.48 = (bf16[16,768,128]{2,1,0:T(8,128)(2,1)}, bf16[16,768,128]{2,1,0:T(8,128)(2,1)}, u32[]{:S(2)}, u32[]{:S(2)}) collective-permute-start(bf16[16,768,128]{2,1,0:T(8,128)(2,1)} %get-tuple-element.211), channel_id=1, source_target_pairs={{0,8},{8,0},{1,9},{9,1},{2,10},{10,2},{3,11},{11,3},{4,12},{12,4},... | collective-permute-start | bytes 9437192 | tf_op jit(solution)/shard_map/ppermute | solution.py:58
  329.0 37.6 %collective-permute-start.47 = (bf16[8,256,512]{2,1,0:T(8,128)(2,1)}, bf16[8,256,512]{2,1,0:T(8,128)(2,1)}, u32[]{:S(2)}, u32[]{:S(2)}) collective-permute-start(bf16[8,256,512]{2,1,0:T(8,128)(2,1)} %get-tuple-element.210), channel_id=1, source_target_pairs={{0,16},{1,17},{2,18},{3,19},{4,20},{5,21},{6,22},{7,23},{8,9},{9,8... | collective-permute-start | bytes 6291464 | tf_op jit(solution)/shard_map/ppermute | solution.py:55
  330.4 26.1 %collective-permute-start.46 = (bf16[4,256,512]{2,1,0:T(8,128)(2,1)S(1)}, bf16[4,256,512]{2,1,0:T(8,128)(2,1)S(1)}, u32[]{:S(2)}, u32[]{:S(2)}) collective-permute-start(bf16[4,256,512]{2,1,0:T(8,128)(2,1)S(1)} %copy-done.47), channel_id=1, source_target_pairs={{0,1},{1,0},{2,3},{3,2},{4,5},{5,4},{6,7},{7,6},{8,24},{9,25},{10,... | collective-permute-start | bytes 3145736 | tf_op jit(solution)/shard_map/ppermute | solution.py:55
  374.4 36.8 %collective-permute-start.51 = (bf16[8,768,128]{2,1,0:T(8,128)(2,1)}, bf16[8,768,128]{2,1,0:T(8,128)(2,1)}, u32[]{:S(2)}, u32[]{:S(2)}) collective-permute-start(bf16[8,768,128]{2,1,0:T(8,128)(2,1)} %get-tuple-element.223), channel_id=1, source_target_pairs={{0,16},{1,17},{2,18},{3,19},{4,20},{5,21},{6,22},{7,23},{8,9},{9,8... | collective-permute-start | bytes 4718600 | tf_op jit(solution)/shard_map/ppermute | solution.py:55
  375.4 35.8 %collective-permute-start.50 = (bf16[4,256,512]{2,1,0:T(8,128)(2,1)}, bf16[4,256,512]{2,1,0:T(8,128)(2,1)}, u32[]{:S(2)}, u32[]{:S(2)}) collective-permute-start(bf16[4,256,512]{2,1,0:T(8,128)(2,1)} %get-tuple-element.222), channel_id=1, source_target_pairs={{0,1},{1,0},{2,3},{3,2},{4,5},{5,4},{6,7},{7,6},{8,24},{9,25},{10,... | collective-permute-start | bytes 3145736 | tf_op jit(solution)/shard_map/ppermute | solution.py:55
  382.7 48.0 %collective-permute-start.59 = (bf16[16,512,128]{2,1,0:T(8,128)(2,1)}, bf16[16,512,128]{2,1,0:T(8,128)(2,1)}, u32[]{:S(2)}, u32[]{:S(2)}) collective-permute-start(bf16[16,512,128]{2,1,0:T(8,128)(2,1)} %get-tuple-element.217), channel_id=1, source_target_pairs={{0,8},{8,0},{1,9},{9,1},{2,10},{10,2},{3,11},{11,3},{4,12},{12,4},... | collective-permute-start | bytes 6291464 | tf_op jit(solution)/shard_map/ppermute | solution.py:58
  382.8 28.3 %collective-permute-start.49 = (bf16[2,256,512]{2,1,0:T(8,128)(2,1)}, bf16[2,256,512]{2,1,0:T(8,128)(2,1)}, u32[]{:S(2)}, u32[]{:S(2)}) collective-permute-start(bf16[2,256,512]{2,1,0:T(8,128)(2,1)} %get-tuple-element.221), channel_id=1, source_target_pairs={{0,2},{2,0},{4,6},{6,4},{1,3},{3,1},{5,7},{7,5},{8,10},{10,8},{12,... | collective-permute-start | bytes 1572872 | tf_op jit(solution)/shard_map/ppermute | solution.py:58
  388.5 99.1 %collective-permute-start.57 = (bf16[8,512,128]{2,1,0:T(8,128)(2,1)S(1)}, bf16[8,512,128]{2,1,0:T(8,128)(2,1)}, u32[]{:S(2)}, u32[]{:S(2)}) collective-permute-start(bf16[8,512,128]{2,1,0:T(8,128)(2,1)S(1)} %pad_maximum_fusion.7.r_1_.r_2_), channel_id=1, source_target_pairs={{0,8},{8,0},{1,9},{9,1},{2,10},{10,2},{3,11},{11,3},{4,12},{12,4},... | collective-permute-start | bytes 3145736 | tf_op jit(solution)/shard_map/ppermute | solution.py:58
  418.1 17.6 %collective-permute-start.63 = (bf16[16,144,128]{2,1,0:T(8,128)(2,1)}, bf16[16,144,128]{2,1,0:T(8,128)(2,1)S(1)}, u32[]{:S(2)}, u32[]{:S(2)}) collective-permute-start(bf16[16,144,128]{2,1,0:T(8,128)(2,1)} %get-tuple-element.242), channel_id=1, source_target_pairs={{0,8},{8,0},{1,9},{9,1},{2,10},{10,2},{3,11},{11,3},{4,12},{12,4},... | collective-permute-start | bytes 1769480 | tf_op jit(solution)/shard_map/ppermute | solution.py:58
  434.6 19.4 %collective-permute-start.61 = (bf16[4,768,128]{2,1,0:T(8,128)(2,1)S(1)}, bf16[4,768,128]{2,1,0:T(8,128)(2,1)S(1)}, u32[]{:S(2)}, u32[]{:S(2)}) collective-permute-start(bf16[4,768,128]{2,1,0:T(8,128)(2,1)S(1)} %get-tuple-element.234), channel_id=1, source_target_pairs={{0,1},{1,0},{2,3},{3,2},{4,5},{5,4},{6,7},{7,6},{8,24},{9,25},{10,... | collective-permute-start | bytes 2359304 | tf_op jit(solution)/shard_map/ppermute | solution.py:55
  435.7 18.6 %collective-permute-start.62 = (bf16[8,512,128]{2,1,0:T(8,128)(2,1)S(1)}, bf16[8,512,128]{2,1,0:T(8,128)(2,1)S(1)}, u32[]{:S(2)}, u32[]{:S(2)}) collective-permute-start(bf16[8,512,128]{2,1,0:T(8,128)(2,1)S(1)} %get-tuple-element.236), channel_id=1, source_target_pairs={{0,16},{1,17},{2,18},{3,19},{4,20},{5,21},{6,22},{7,23},{8,9},{9,8... | collective-permute-start | bytes 3145736 | tf_op jit(solution)/shard_map/ppermute | solution.py:55
  436.9 50.8 %collective-permute-start.58 = (bf16[8,512,128]{2,1,0:T(8,128)(2,1)}, bf16[8,512,128]{2,1,0:T(8,128)(2,1)S(1)}, u32[]{:S(2)}, u32[]{:S(2)}) collective-permute-start(bf16[8,512,128]{2,1,0:T(8,128)(2,1)} %collective-permute-done.40.r_3_.r_4_), channel_id=1, source_target_pairs={{0,8},{8,0},{1,9},{9,1},{2,10},{10,2},{3,11},{11,3},{4,12},{12,4},... | collective-permute-start | bytes 3145736 | tf_op jit(solution)/shard_map/ppermute | solution.py:58
  518.2 12.7 %collective-permute-start.78 = (bf16[8,96,128]{2,1,0:T(8,128)(2,1)}, bf16[8,96,128]{2,1,0:T(8,128)(2,1)}, u32[]{:S(2)}, u32[]{:S(2)}) collective-permute-start(bf16[8,96,128]{2,1,0:T(8,128)(2,1)} %get-tuple-element.413), channel_id=1, source_target_pairs={{0,4},{2,6},{4,0},{6,2},{1,5},{3,7},{5,1},{7,3},{8,12},{10,14},{12... | collective-permute-start | bytes 589832 | tf_op jit(solution)/shard_map/ppermute | solution.py:58
  (109 other events, 1438.4 us)

commit v3 on v2

--- a/solution.py
+++ b/solution.py
@@ -88,13 +88,39 @@
         return lax.psum_scatter(flat, AXES, scatter_dimension=0, tiled=True).astype(F32)
 
     def gate(self, values, before):
-        return lax.optimization_barrier((values, before))[0] if before else values
+        empty = isinstance(before, list) and not before
+        return values if empty else lax.optimization_barrier((values, before))[0]
 
     def hop(self, value, *steps):
         for axis, bit in steps:
             value = value + self.swap(value, axis, bit)
         return value
 
+    def rounds(self, value, axes):
+        if "c" in axes:
+            value = value + self.swap(value, "c")
+        if "y" in axes:
+            both = self.permute(value, lambda y, c, z, x: (y ^ 1, c, z, x ^ 1))
+            value = (value + self.swap(value, "x")) + (self.swap(value, "y") + both)
+        elif "x" in axes:
+            value = value + self.swap(value, "x")
+        if "z" in axes:
+            third = self.swap(value, "z", 3)
+            value = (value + self.swap(value, "z", 1)) + (self.swap(value, "z", 2) + third)
+        return value
+
+    def collect(self, value, axis):
+        count = self.sizes[axis]
+        here = lax.axis_index(axis)
+        got = [value] + [self.swap(value, axis, flip) for flip in range(1, count)]
+        out = []
+        for place in range(count):
+            piece = got[count - 1]
+            for flip in range(count - 1):
+                piece = jnp.where((here ^ flip) == place, got[flip], piece)
+            out.append(piece)
+        return jnp.stack(out)
+
     def begin(self, before, *moves):
         operands = self.gate([v for _, v in moves], before)
         return [fn(v) for (fn, _), v in zip(moves, operands)]
@@ -113,23 +139,6 @@
 
     def core(self, value):
         return self.swap(value, "c")
-
-    def phase(self, state, number):
-        kept, sent = state
-        if number == 0:
-            return kept, self.swap(sent, "c")
-        if number in (1, 2):
-            return kept, self.permute(sent, self.along(number == 1))
-        return kept, self.swap(sent, "z", 1 if number == 3 else 2)
-
-    def split(self, state):
-        kept, got = state
-
-        def add(left, right):
-            return (left.astype(F32) + right.astype(F32)).astype(BF)
-
-        half = kept.shape[0] // 2
-        return add(kept[:half], got[:half]), add(kept[half:], got[half:])
 
 
 def whole(chunks):
@@ -549,6 +558,65 @@
     by_core(co, run)
 
 
+def by_place(co, fn):
+    for core in range(2):
+        for x in range(2):
+
+            @pl.when((co[1] == core) & (co[3] == x))
+            def _(core=core, x=x):
+                fn(core, x)
+
+
+def pair_of(chunks, core, x, flip_y, owner, rows):
+    found = [None, None]
+    for index, (fy, fx, who) in enumerate(spots(core)):
+        if (fy, who) == (flip_y, owner):
+            found[fx ^ x] = chunks[index][0, rows]
+    return jnp.concatenate(found, axis=1)
+
+
+def forward_pair(co, k, x_ref, chunks, row, band, put):
+    back = co[2] ^ zflip(k)
+
+    def run(core, x):
+        total = None
+        for owner in range(2):
+            for fy in range(2):
+                r = (co[0] ^ fy) * 2 + owner
+                w = pair_of(chunks, core, x, fy, owner, slice(row, row + band))
+                part = mm(x_ref[:, span(r, band)], w)
+                total = part if total is None else total + part
+        put(back, total)
+
+    by_place(co, run)
+
+
+def backward_pair(co, k, dy_ref, chunks, parts, band, acc_ref, fresh):
+    back = co[2] ^ zflip(k)
+    width = dy_ref.shape[1] // parts
+
+    def run(core, x):
+        for owner in range(2):
+            for fy in range(2):
+                total = None
+                for part in range(parts):
+                    w = pair_of(chunks, core, x, fy, owner, slice(part * band, (part + 1) * band))
+                    col = pl.multiple_of(part * width + back * 256, 256)
+                    got = mm_nt(dy_ref[:, pl.ds(col, 256)], w)
+                    total = got if total is None else total + got
+                r = (co[0] ^ fy) * 2 + owner
+
+                @pl.when(fresh)
+                def _():
+                    acc_ref[:, span(r, band)] = total
+
+                @pl.when(jnp.logical_not(fresh))
+                def _():
+                    acc_ref[:, span(r, band)] += total
+
+    by_place(co, run)
+
+
 def smem():
     return pl.BlockSpec(memory_space=pltpu.SMEM)
 
@@ -626,7 +694,11 @@
             r = (co[0] ^ fy) * 2 + owner
             p = back * 2 + (co[3] ^ fx)
             table_ref[span(r, tall), span(p, 128)] = chunks[index][0, offset : offset + tall]
-            more_ref[r, p] = chunks[index][0, offset + tall : offset + tall + extra]
+            more = chunks[index][0, offset + tall : offset + tall + extra].astype(F32)
+            half = extra // 2
+            for part in range(2):
+                col = pl.multiple_of(r * band + part * 128, 128)
+                more_ref[span(p, half), pl.ds(col, 128)] = more[part * half : (part + 1) * half]
             value_ref[span(r, band), span(p, 128)] = chunks[index][0, :band]
 
     by_core(co, run)
@@ -646,39 +718,42 @@
     by_core(co, run)
 
 
-def product_kernel(co, x_ref, *refs, band, w):
+def product_kernel(co, x_ref, *refs, band):
     chunks, out_ref = refs[:8], refs[8]
 
     def put(p, total):
-        out_ref[:, span(p, w)] = total.astype(out_ref.dtype)
-
-    forward_step(co, pl.program_id(0), x_ref, chunks, 0, band, w, put)
+        out_ref[:, span(p, 256)] = total.astype(out_ref.dtype)
+
+    forward_pair(co, pl.program_id(0), x_ref, chunks, 0, band, put)
 
 
 def pool_kernel(x_ref, e_ref, tu_ref, tv_ref, agg_ref, a_ref, pa_ref):
     j = pl.program_id(0)
     x, e = x_ref[...], e_ref[...]
+    wide_x, wide_e = x.astype(F32), e.astype(F32)
     rows, n = x.shape
     masks = half_masks(n)
     lane = lax.broadcasted_iota(jnp.int32, (n, 128), 1)
     keep = lax.broadcasted_iota(jnp.int32, (rows, 128), 1) < V
-    total = None
-    for half in range(2):
-        column = jnp.sum(jnp.where(lane == 2 * j + half, tu_ref[...], 0.0), axis=1, keepdims=True)
-        m = e.astype(F32) * column
-        high = m.astype(BF)
-        rest = (m - high.astype(F32)).astype(BF)
-        s = mm(x, high) + mm(x, rest)
-        s = jnp.where(keep, s, -1e30)
-        s = jnp.exp(s - jnp.max(s, axis=-1, keepdims=True))
-        pa = s / jnp.sum(s, axis=-1, keepdims=True)
-        wide = mm_nt(pa.astype(BF), e)
-        a = (x.astype(F32) * wide).astype(BF)
-        pa_ref[half] = pa
-        a_ref[half] = a
-        part = mm(a, tv_ref[...] * masks[half])
-        total = part if total is None else total + part
-    agg_ref[...] = total.astype(BF)
+    for pair in range(2):
+        total = None
+        for half in range(2):
+            head = 2 * pair + half
+            column = jnp.sum(jnp.where(lane == 4 * j + head, tu_ref[...], 0.0), axis=1, keepdims=True)
+            m = wide_e * column
+            high = m.astype(BF)
+            rest = (m - high.astype(F32)).astype(BF)
+            s = mm(x, high) + mm(x, rest)
+            s = jnp.where(keep, s, -1e30)
+            s = jnp.exp(s - jnp.max(s, axis=-1, keepdims=True))
+            pa = s * (1.0 / jnp.sum(s, axis=-1, keepdims=True))
+            wide = mm_nt(pa.astype(BF), e)
+            a = (wide_x * wide).astype(BF)
+            pa_ref[head] = pa
+            a_ref[head] = a
+            part = mm(a, tv_ref[:, pair * 128 : (pair + 1) * 128] * masks[half])
+            total = part if total is None else total + part
+        agg_ref[:, pair * 128 : (pair + 1) * 128] = total.astype(BF)
 
 
 def enter_kernel(co, agg_ref, src_ref, gain_ref, *refs, band):
@@ -686,9 +761,9 @@
     k = pl.program_id(0)
 
     def put(p, total):
-        x0_ref[:, span(p, 128)] = total
-
-    forward_step(co, k, agg_ref, chunks, 0, band, 128, put)
+        x0_ref[:, span(p, 256)] = total
+
+    forward_pair(co, k, agg_ref, chunks, 0, band, put)
 
     @pl.when(k == NZ - 1)
     def _():
@@ -711,17 +786,17 @@
         for part in range(3):
 
             def put(p, total, part=part):
-                col = pl.multiple_of(part * width + p * 128, 128)
-                qkv_ref[:, pl.ds(col, 128)] = total.astype(BF)
-
-            forward_step(co, i, h1_ref, qkv_chunks, part * band, band, 128, put)
+                col = pl.multiple_of(part * width + p * 256, 256)
+                qkv_ref[:, pl.ds(col, 256)] = total.astype(BF)
+
+            forward_pair(co, i, h1_ref, qkv_chunks, part * band, band, put)
 
     @pl.when(i == NZ - 1)
     def _():
         masks = half_masks(cap)
         key = lax.broadcasted_iota(jnp.int32, (cap, cap), 1)
 
-        @pl.loop(0, width // 128)
+        @pl.loop(0, width // 128, unroll=2)
         def _(j):
             for m in range(micro):
                 rows = slice(m * cap, (m + 1) * cap)
@@ -733,7 +808,7 @@
                     s = mm_nt(q * masks[half], kk) * scale
                     s = jnp.where(key < lens[m], s, -1e30)
                     s = jnp.exp(s - jnp.max(s, axis=-1, keepdims=True))
-                    p = s / jnp.sum(s, axis=-1, keepdims=True)
+                    p = s * (1.0 / jnp.sum(s, axis=-1, keepdims=True))
                     p_ref[2 * j + half, m] = p
                     part = mm(p.astype(BF), vv * masks[half])
                     total = part if total is None else total + part
@@ -742,9 +817,9 @@
     @pl.when(i >= NZ)
     def _():
         def put(p, total):
-            x1_ref[:, span(p, 128)] = x0_ref[:, span(p, 128)] + total
-
-        forward_step(co, i - NZ, o_ref, o_chunks, 0, band, 128, put)
+            x1_ref[:, span(p, 256)] = x0_ref[:, span(p, 256)] + total
+
+        forward_pair(co, i - NZ, o_ref, o_chunks, 0, band, put)
 
     @pl.when(i == 2 * NZ - 1)
     def _():
@@ -763,7 +838,7 @@
         tail = tail * bell
         share = jnp.where(f < 0.0, tail, 1.0 - tail)
         act_ref[:, span(p, w)] = (f * share).astype(BF)
-        slope_ref[:, span(p, w)] = share + f * bell * ((2.0 * math.pi) ** -0.5)
+        slope_ref[:, span(p, w)] = (share + f * bell * ((2.0 * math.pi) ** -0.5)).astype(BF)
 
     forward_step(co, pl.program_id(0), h2_ref, chunks, 0, band, w, put)
 
@@ -781,19 +856,20 @@
     @pl.when(i == NZ - 1)
     def _():
         x2 = (x1_ref[...] + acc_ref[...]).astype(BF)
-        diff = mm(x2, head_ref[...]) - target_ref[...].astype(F32)
+        head = head_ref[...].astype(BF)
+        diff = mm_nt(x2, head) - target_ref[...].astype(F32)
         weighted = weight_ref[...] * diff
         loss_ref[...] = jnp.broadcast_to(jnp.sum(weighted * diff), loss_ref.shape)
         dpred = (2.0 * weighted / count[0]).astype(BF)
-        dhead_ref[...] = mm_tn(x2, dpred).astype(BF)
-        dx2 = mm_nt(dpred, head_ref[...])
+        dhead_ref[...] = mm_tn(dpred, x2)
+        dx2 = mm(dpred, head)
         dx2_ref[...] = dx2
         dx2_low_ref[...] = dx2.astype(BF)
 
     @pl.when(i >= NZ)
     def _():
         def put(p, dact):
-            df_ref[:, span(p, w)] = (dact * slope_ref[:, span(p, w)]).astype(BF)
+            df_ref[:, span(p, w)] = (dact * slope_ref[:, span(p, w)].astype(F32)).astype(BF)
 
         forward_step(co, i - NZ, dx2_low_ref, chunks, 0, band, w, put)
 
@@ -825,45 +901,70 @@
         out_ref[j] = mm(xt_ref[span(r, band)], dy_ref[:, span(p, w)]).astype(BF)
 
 
-def qkv_grad_kernel(co, h1_ref, dqkv_ref, keep_ref, send_ref, ht_ref, *, band):
-    i = pl.program_id(0)
+def pair_places(co, k, keep_ref, send_ref):
+    out = []
+    for out_ref, owner in ((keep_ref, co[1]), (send_ref, 1 - co[1])):
+        for fy in range(2):
+            at = []
+            for half in range(2):
+                fx = co[3] ^ half
+                at.append(jnp.where(owner == 0, fy * 2 + fx, fx * 2 + fy))
+            out.append((out_ref, (co[0] ^ fy) * 2 + owner, co[2] ^ zflip(k), at))
+    return out
+
+
+def attention_grad_kernel(co, h1_ref, o_ref, dqkv_ref, dx1_ref, keep_ref, send_ref, ht_ref, ot_ref, *, band):
+    k = pl.program_id(0)
     width = h1_ref.shape[1]
 
-    @pl.when(i == 0)
+    @pl.when(k == 0)
     def _():
         ht_ref[...] = h1_ref[...].T
-
-    for out_ref, owner, j in targets(co, keep_ref, send_ref):
-        r, p = owner_place(co, i * NZ + j, owner)
-        h1 = ht_ref[span(r, band)]
-        for part in range(3):
-            col = pl.multiple_of(part * width + p * 128, 128)
-            got = mm(h1, dqkv_ref[:, pl.ds(col, 128)])
-            out_ref[j, part * band : (part + 1) * band] = got.astype(BF)
-
-
-def pair_grad_kernel(co, o_ref, agg_ref, dx1_ref, dx0_ref, keep_ref, send_ref, ot_ref, at_ref, *, band):
-    i = pl.program_id(0)
-
-    @pl.when(i == 0)
-    def _():
         ot_ref[...] = o_ref[...].T
+
+    for out_ref, r, back, at in pair_places(co, k, keep_ref, send_ref):
+        for part in range(4):
+            if part < 3:
+                col = pl.multiple_of(part * width + back * 256, 256)
+                got = mm(ht_ref[span(r, band)], dqkv_ref[:, pl.ds(col, 256)])
+            else:
+                got = mm(ot_ref[span(r, band)], dx1_ref[:, span(back, 256)])
+            for half in range(2):
+                out_ref[at[half], 0, part * band : (part + 1) * band] = got[
+                    :, half * 128 : (half + 1) * 128
+                ].astype(BF)
+
+
+def low_grad_kernel(
+    co, groups, agg_ref, dx0_ref, g_ref, sum_ref, gain_ref, head_ref, keep_ref, send_ref, at_ref, gl_ref, *, band, tall, top
+):
+    k = pl.program_id(0)
+    n = g_ref.shape[0]
+    piece = head_ref.shape[0] // STRIPS
+
+    @pl.when(k == 0)
+    def _():
         at_ref[...] = agg_ref[...].T
-
-    for out_ref, owner, j in targets(co, keep_ref, send_ref):
-        r, p = owner_place(co, i * NZ + j, owner)
-        got = mm(ot_ref[span(r, band)], dx1_ref[:, span(p, 128)])
-        out_ref[j, :band] = got.astype(BF)
-        got = mm(at_ref[span(r, band)], dx0_ref[:, span(p, 128)])
-        out_ref[j, band:] = got.astype(BF)
-
-
-def rows_kernel(co, g_ref, head_ref, keep_ref, send_ref, *, tall):
-    i = pl.program_id(0)
-    for out_ref, owner, j in targets(co, keep_ref, send_ref):
-        r, p = owner_place(co, i * NZ + j, owner)
-        out_ref[j, :tall] = g_ref[span(r, tall), span(p, 128)]
-        out_ref[j, tall:] = head_ref[r, p]
+        gl_ref[: n - 16] = g_ref[: n - 16].astype(BF)
+        last = g_ref[n - 16 :]
+        row = lax.broadcasted_iota(jnp.int32, last.shape, 0)
+        for m in range(sum_ref.shape[0]):
+            last += jnp.where(row == top + groups[m], sum_ref[m : m + 1], 0.0)
+        for m in range(2):
+            last += jnp.where(row == top + SOURCES + 1 + m, gain_ref[m : m + 1], 0.0)
+        gl_ref[n - 16 :] = last.astype(BF)
+
+    for out_ref, r, back, at in pair_places(co, k, keep_ref, send_ref):
+        got = mm(at_ref[span(r, band)], dx0_ref[:, span(back, 256)])
+        for half in range(2):
+            p = back * 2 + half
+            out_ref[at[half], 0, :band] = got[:, half * 128 : (half + 1) * 128].astype(BF)
+            out_ref[at[half], 0, band : band + tall] = gl_ref[span(r, tall), span(p, 128)]
+            head = [
+                head_ref[span(p, piece), pl.ds(pl.multiple_of(r * band + part * 128, 128), 128)]
+                for part in range(2)
+            ]
+            out_ref[at[half], 0, band + tall :] = jnp.concatenate(head, axis=0).astype(BF)
 
 
 def up_back_kernel(co, df_ref, x1_ref, gain_ref, dx2_ref, *refs, band, w):
@@ -890,14 +991,14 @@
 
     @pl.when(i < NZ)
     def _():
-        backward_step(co, i, dx1_low_ref, o_chunks, 0, band, 128, acc_ref, i == 0)
+        backward_pair(co, i, dx1_low_ref, o_chunks, 1, band, acc_ref, i == 0)
 
     @pl.when(i == NZ - 1)
     def _():
         do_ref[...] = acc_ref[...].astype(BF)
         masks = half_masks(cap)
 
-        @pl.loop(0, width // 128)
+        @pl.loop(0, width // 128, unroll=2)
         def _(j):
             for m in range(micro):
                 rows = slice(m * cap, (m + 1) * cap)
@@ -936,35 +1037,7 @@
 
     @pl.when(i < NZ)
     def _():
-        back = co[2] ^ zflip(i)
-
-        def run(core):
-            places = spots(core)
-            for owner in range(2):
-                for fy in range(2):
-                    total = None
-                    for index, (py, fx, who) in enumerate(places):
-                        if (py, who) != (fy, owner):
-                            continue
-                        p = back * 2 + (co[3] ^ fx)
-                        for part in range(3):
-                            col = pl.multiple_of(part * width + p * 128, 128)
-                            got = mm_nt(
-                                dqkv_ref[:, pl.ds(col, 128)],
-                                qkv_chunks[index][0, part * band : (part + 1) * band],
-                            )
-                            total = got if total is None else total + got
-                    r = (co[0] ^ fy) * 2 + owner
-
-                    @pl.when(i == 0)
-                    def _():
-                        acc_ref[:, span(r, band)] = total
-
-                    @pl.when(i > 0)
-                    def _():
-                        acc_ref[:, span(r, band)] += total
-
-        by_core(co, run)
+        backward_pair(co, i, dqkv_ref, qkv_chunks, 3, band, acc_ref, i == 0)
 
     @pl.when(i == NZ - 1)
     def _():
@@ -977,7 +1050,7 @@
 
     @pl.when(i >= NZ)
     def _():
-        backward_step(co, i - NZ, dx0_low_ref, a_chunks, 0, band, 128, acc_ref, i == NZ)
+        backward_pair(co, i - NZ, dx0_low_ref, a_chunks, 1, band, acc_ref, i == NZ)
 
     @pl.when(i == 2 * NZ - 1)
     def _():
@@ -985,22 +1058,22 @@
 
 
 def pool_back_kernel(x_ref, e_ref, tv_ref, a_ref, pa_ref, dagg_ref, g_ref, s_ref):
-    x, e, dagg = x_ref[...].astype(F32), e_ref[...], dagg_ref[...]
-    masks = half_masks(dagg.shape[0])
-    total = None
-    for half in range(2):
-        part = dagg * masks[half]
-        moved = mm_nt(part, tv_ref[...]) * x
-        high = moved.astype(BF)
-        rest = (moved - high.astype(F32)).astype(BF)
-        dpal = mm(high, e) + mm(rest, e)
-        pa = pa_ref[half]
-        inner = pa * dpal
-        ds = (inner - pa * jnp.sum(inner, axis=-1, keepdims=True)).astype(BF)
-        s_ref[0, half : half + 1] = jnp.sum(mm_nt(ds, e) * x, axis=0, keepdims=True)
-        got = mm_tn(a_ref[half], part)
-        total = got if total is None else total + got
-    g_ref[...] = total
+    x, e = x_ref[...].astype(F32), e_ref[...]
+    masks = half_masks(x.shape[0])
+    for pair in range(2):
+        at = slice(pair * 128, (pair + 1) * 128)
+        total = None
+        for half in range(2):
+            head = 2 * pair + half
+            part = dagg_ref[:, at] * masks[half]
+            dpal = mm((mm_nt(part, tv_ref[:, at]) * x).astype(BF), e)
+            pa = pa_ref[head]
+            inner = pa * dpal
+            ds = (inner - pa * jnp.sum(inner, axis=-1, keepdims=True)).astype(BF)
+            s_ref[0, head : head + 1] = jnp.sum(mm_nt(ds, e) * x, axis=0, keepdims=True)
+            got = mm_tn(a_ref[head], part)
+            total = got if total is None else total + got
+        g_ref[:, at] = total
 
 
 def table_layout(cap, band, tall):
@@ -1076,7 +1149,9 @@
             square_low[2],
             square_low[3],
             jnp.pad(table_master.astype(BF), ((0, tall - table_band), (0, 0))),
-            head_master.astype(BF).reshape(head_rows, strip),
+            jnp.transpose(
+                head_master.astype(BF).T.reshape(ho // STRIPS, 2, strip), (1, 0, 2)
+            ).reshape(head_rows, strip),
         ],
         axis=0,
     )
@@ -1092,23 +1167,24 @@
     col_head = (my_strip * strip + jnp.arange(strip)) // size
     head_mask = (col_head[:, None] == jnp.arange(HEADS)[None]).astype(F32)
     wide, line, one = full((rows, width)), full((1, width)), shape(1, width)
-    pair = pl.BlockSpec((rows, 128), lambda j: (0, j))
+    pair = pl.BlockSpec((rows, 256), lambda j: (0, j))
     src_at = lane_of(base)
     row = jnp.where(my_band == query_row // table_band, 1.0, 0.0) * table_master[query_row % table_band]
     first_pack = lax.dynamic_update_slice_in_dim(
         jnp.zeros((width,), F32), row.astype(BF).astype(F32), my_strip * strip, 0
     )
     first_pack = jnp.concatenate([first_pack, jnp.broadcast_to(jnp.sum(valid), (128,))])
-    first_pack = grid.hop(first_pack, ("z", 1), ("z", 2))
 
     bundles = [low, attn, dense_low[0], dense_low[1], square_low[:2].reshape(2 * band, strip)]
     stack, join = lambda i, v: jnp.stack([bundles[i], v]), lambda a, b: jnp.concatenate([a, b], axis=0)
     z2, z1, near, far, core = grid.far_z, grid.next_z, grid.near, grid.far, grid.core
-    (a0,) = grid.begin([first_pack], (z2, bundles[0]))
+    (a0,) = grid.begin([], (z2, bundles[0]))
+    first_pack = grid.hop(grid.gate(first_pack, [a0]), ("z", 1), ("z", 2))
     p0 = stack(0, a0)
-    b0, a1 = got = grid.begin([a0], (z1, p0), (z2, bundles[1]))
+    b0, a1 = got = grid.begin([a0, first_pack], (z1, p0), (z2, bundles[1]))
     l0, p1 = join(p0, b0), stack(1, a1)
-    pack = grid.hop(first_pack, ("x", 1), ("y", 1), ("c", 1))
+    pack = grid.hop(first_pack, ("x", 1))
+    pack = grid.hop(pack, ("y", 1), ("c", 1))
     query, count = pack[:width].astype(BF), pack[width]
     query_own = lax.dynamic_slice_in_dim(query, my_band * band, band)
     spread = jnp.tile(jnp.asarray(fixed), (micro, 1))
@@ -1130,45 +1206,41 @@
     u_part = grid.hop(u_part, ("x", 1))
     n0, b1 = got = grid.begin([got, qv_own, spread], (near, l0), (z1, p1))
     f0, l1 = join(l0, n0), join(p1, b1)
-    u_part = grid.hop(u_part, ("y", 1), ("c", 1))
+    u_part = grid.hop(u_part, ("y", 1), ("c", 1), ("z", 1))
     r0, n1, a2 = got = grid.begin([got, u_part], (far, f0), (near, l1), (z2, bundles[2]))
     f1, p2 = join(l1, n1), stack(2, a2)
     (b2,) = grid.begin([], (z1, p2))
-    u_part = grid.hop(u_part, ("z", 1))
     l2 = join(p2, b2)
     c0, d0, r1, a3 = got = grid.begin(
         [got, b2, u_part], (core, f0), (core, r0), (far, f1), (z2, bundles[3])
     )
     p3 = stack(3, a3)
-    (b3,) = grid.begin([], (z1, p3))
     u_part = grid.hop(u_part, ("z", 2))
-    l3 = join(p3, b3)
     low = twice([f0, r0, c0, d0])
-    n2, c1, d1, a4 = got = grid.begin(
-        [got, b3, u_part], (near, l2), (core, f1), (core, r1), (z2, bundles[4])
-    )
-    f2, p4 = join(l2, n2), stack(4, a4)
+    n2, c1, d1, b3 = got = grid.begin(
+        [got, u_part], (near, l2), (core, f1), (core, r1), (z1, p3)
+    )
+    f2, l3 = join(l2, n2), join(p3, b3)
     u = (u_part * scale).astype(BF)
-    table, heads, wv = call(
+    table, head, wv = call(
         lambda *r: assemble_kernel(*r, band=band, offset=2 * band, tall=tall, extra=head_rows),
         "assemble",
         (NZ,),
         [smem()] + steps_of(low_rows, 128),
         (
             shape(n, width, dtype=BF),
-            shape(BANDS, STRIPS, head_rows, 128, dtype=BF),
+            shape(ho, width),
             shape(width, width, dtype=BF),
         ),
-        (full((n, width)), full((BANDS, STRIPS, head_rows, 128)), full((width, width))),
+        (full((n, width)), full((ho, width)), full((width, width))),
         [],
         0,
         1 << 23,
         co,
         *low,
     )
-    head = whole(heads.reshape(BANDS, STRIPS, band, ho // STRIPS))
     tv = call(
-        lambda *r: product_kernel(*r, band=band, w=128),
+        lambda *r: product_kernel(*r, band=band),
         "table_values",
         (NZ,),
         [smem(), full((n, width))] + steps_of(band, 128),
@@ -1183,20 +1255,20 @@
     )
     tu = jnp.pad(dot(table, u, NN), ((0, 0), (0, 128 - HEADS)))
     attn = twice([f1, r1, c1, d1])
-    r2, n3, b4 = got = grid.begin([got, tv, u], (far, f2), (near, l3), (z1, p4))
-    f3, l4 = join(l3, n3), join(p4, b4)
-    tu, head, weighted = grid.gate((tu, head, weighted), [n2])
-    tu = grid.gate(tu, [head, weighted])
+    r2, n3, a4 = got = grid.begin([got, u, tv], (far, f2), (near, l3), (z2, bundles[4]))
+    f3, p4 = join(l3, n3), stack(4, a4)
+    tu, weighted = grid.gate((tu, weighted), [n2])
+    tu = grid.gate(tu, [weighted])
     agg, fold, pa = call(
         pool_kernel,
         "pool",
-        (HEADS // 2,),
-        [full((rows, n)), full((n, 128)), full((n, 128)), pl.BlockSpec((n, 128), lambda j: (0, j))],
+        (HEADS // 4,),
+        [full((rows, n)), full((n, 128)), full((n, 128)), pl.BlockSpec((n, 256), lambda j: (0, j))],
         (shape(rows, width, dtype=BF), shape(HEADS, rows, n, dtype=BF), shape(HEADS, rows, 128)),
         (
             pair,
-            pl.BlockSpec((2, rows, n), lambda j: (j, 0, 0)),
-            pl.BlockSpec((2, rows, 128), lambda j: (j, 0, 0)),
+            pl.BlockSpec((4, rows, n), lambda j: (j, 0, 0)),
+            pl.BlockSpec((4, rows, 128), lambda j: (j, 0, 0)),
         ),
         [],
         12 * HEADS * rows * n * 128,
@@ -1227,10 +1299,8 @@
         gain_one,
         *low,
     )
-    c2, d2, r3, n4 = got = grid.begin(
-        [got, h1], (core, f2), (core, r2), (far, f3), (near, l4)
-    )
-    f4 = join(l4, n4)
+    c2, d2, r3, b4 = got = grid.begin([got, h1], (core, f2), (core, r2), (far, f3), (z1, p4))
+    l4 = join(p4, b4)
     up = twice([f2, r2, c2, d2])
     qkv, probs, o, x1, h2 = call(
         lambda *r: attend_kernel(*r, band=band, scale=scale),
@@ -1258,14 +1328,15 @@
         *attn,
         *attn,
     )
-    c3, d3, r4 = got = grid.begin([got, h2], (core, f3), (core, r3), (far, f4))
+    c3, d3, n4 = got = grid.begin([got, h2], (core, f3), (core, r3), (near, l4))
+    f4 = join(l4, n4)
     down = twice([f3, r3, c3, d3])
     act, slope = call(
         lambda *r: up_kernel(*r, band=band, w=w),
         "up",
         (NZ,),
         [smem(), wide] + steps_of(band, w),
-        (shape(rows, ff, dtype=BF), shape(rows, ff)),
+        (shape(rows, ff, dtype=BF), shape(rows, ff, dtype=BF)),
         (full((rows, ff)), full((rows, ff))),
         [],
         2 * rows * width * ff,
@@ -1274,22 +1345,23 @@
         h2,
         *up,
     )
-    wq_parts = [f4, r4, *grid.begin([got, act], (core, f4), (core, r4))]
-    act = grid.gate(act, [r4])
+    act = grid.gate(act, [n4])
+    (r4,) = grid.begin([act], (far, f4))
+    wq_parts = [f4, r4, *grid.begin([], (core, f4), (core, r4))]
     loss_part, dx2, dx2_low, d_head, df = call(
         lambda *r: down_kernel(*r, band=band, w=w),
         "down",
         (2 * NZ,),
-        [smem(), smem(), wide, full((rows, ff)), full((rows, ff)), full((width, ho)), full((rows, ho)), full((rows, ho))]
+        [smem(), smem(), wide, full((rows, ff)), full((rows, ff)), full((ho, width)), full((rows, ho)), full((rows, ho))]
         + [pl.BlockSpec((1, band, w), lambda i, b=b: (b * NZ + i % NZ, 0, 0)) for b in range(2)] * 4,
         (
             shape(8, 128),
             shape(rows, width),
             shape(rows, width, dtype=BF),
-            shape(width, ho, dtype=BF),
+            shape(ho, width),
             shape(rows, ff, dtype=BF),
         ),
-        (full((8, 128)), wide, wide, full((width, ho)), full((rows, ff))),
+        (full((8, 128)), wide, wide, full((ho, width)), full((rows, ff))),
         [pltpu.VMEM((rows, width), F32)],
         4 * rows * width * ff,
         1 << 25,
@@ -1324,26 +1396,48 @@
             *args,
         )
 
+    def sent_pairs(kernel, name, height, flops, scratch, *args):
+        out = shape(4, NZ, height, 128, dtype=BF)
+        block = pl.BlockSpec((4, 1, height, 128), lambda k: (0, k, 0, 0))
+        keep, send = call(
+            kernel,
+            name,
+            (NZ,),
+            [smem()] + [smem() if a.ndim == 1 else full(a.shape) for a in args],
+            (out, out),
+            (block, block),
+            scratch,
+            flops,
+            32 * height * 128 * 2,
+            co,
+            *args,
+        )
+        return keep.reshape(4 * NZ, height, 128), send.reshape(4 * NZ, height, 128)
+
     dense_grad = lambda *r: grad_kernel(*r, band=band, w=w)
-    flow, done = {}, {}
-
-    def stage(work, before):
-        gated = grid.gate([flow[name] for name, _ in work], before)
-        arrived = []
-        for (name, number), state in zip(work, gated):
-            state = grid.phase(state, number)
-            arrived.append(state[1])
-            if number < 4:
-                flow[name] = grid.split(state)
-            else:
-                done[name] = state[0].astype(F32) + state[1].astype(F32)
-        return arrived
-
+    flow = {}
     flow["down"] = sent(dense_grad, "down_grad", band, w, 2 * rows * width * ff, turned, dx2_low, act)
     df = grid.gate(df, [flow["down"]])
     flow["up"] = sent(dense_grad, "up_grad", band, w, 2 * rows * width * ff, turned, h2, df)
-    got = stage([("down", 0)], [])
-    df = grid.gate(df, [flow["up"], flow["down"]])
+    far, near, core, z1, z2 = grid.far, grid.near, grid.core, grid.next_z, grid.far_z
+
+    def plus(left, right):
+        return (left.astype(F32) + right.astype(F32)).astype(BF)
+
+    def quarters(kept, got):
+        return [plus(kept[i * NZ : (i + 1) * NZ], got[i * NZ : (i + 1) * NZ]) for i in range(4)]
+
+    def halves(kept, got):
+        return plus(kept[:2], got[:2]), plus(kept[2:], got[2:])
+
+    def ends(kept, got):
+        return plus(kept[:1], got[:1]), plus(kept[1:], got[1:])
+
+    (got,) = grid.begin([r4], (core, flow["down"][1]))
+    dq = quarters(flow["down"][0], got)
+    df = grid.gate(df, [flow["up"], dq])
+    (f1d,) = grid.begin([dq, flow["up"]], (far, dq[3]))
+    got = core(flow["up"][1])
     dx1, dx1_low, d_gain_two = call(
         lambda *r: up_back_kernel(*r, band=band, w=w),
         "up_back",
@@ -1361,6 +1455,10 @@
         dx2,
         *up,
     )
+    uq = quarters(flow["up"][0], got)
+    d_side = plus(dq[1], f1d)
+    dx1_low = grid.gate(dx1_low, [f1d, uq])
+    (f0d,) = grid.begin([f1d, uq, dx1], (far, dq[2]))
     dqkv = call(
         lambda *r: attend_back_kernel(*r, band=band, scale=scale),
         "attend_back",
@@ -1378,19 +1476,24 @@
         probs,
         *attn,
     )
-    got = stage([("down", 1), ("up", 0)], [got, flow["up"]])
-    dqkv = grid.gate(dqkv, [got, flow["up"], flow["down"]])
-    got = stage([("down", 2), ("up", 1)], [got, dqkv])
-    flow["qkv"] = sent(
-        lambda *r: qkv_grad_kernel(*r, band=band),
-        "qkv_grad",
-        3 * band,
-        128,
-        6 * rows * width * width,
-        turned,
+    d_line = plus(dq[0], f0d)
+    dqkv = grid.gate(dqkv, [f0d, d_side])
+    (f1u,) = grid.begin([f0d, dqkv], (far, uq[3]))
+    flow["attn"] = sent_pairs(
+        lambda *r: attention_grad_kernel(*r, band=band),
+        "attention_grad",
+        4 * band,
+        8 * rows * width * width,
+        turned * 2,
         h1,
+        o,
         dqkv,
-    )
+        dx1_low,
+    )
+    u_side = plus(uq[1], f1u)
+    dqkv = grid.gate(dqkv, [f1u, flow["attn"]])
+    f0u, nd = grid.begin([f1u, flow["attn"]], (far, uq[2]), (near, d_side))
+    got = core(grid.gate(flow["attn"][1], f1u))
     dx0_low, d_gain_one, dx0_sum, dagg = call(
         lambda *r: leave_kernel(*r, band=band),
         "leave",
@@ -1416,37 +1519,24 @@
         *attn,
         *low,
     )
-    got_core = stage([("qkv", 0)], [])
-    dx0_low, dx1_low = grid.gate((dx0_low, dx1_low), [got, got_core, flow["down"], flow["up"]])
-    got = stage([("down", 3), ("up", 2), ("qkv", 1)], [got, got_core, dagg])
-    flow["pair"] = sent(
-        lambda *r: pair_grad_kernel(*r, band=band),
-        "pair_grad",
-        2 * band,
-        128,
-        4 * rows * width * width,
-        turned * 2,
-        o,
-        agg,
-        dx1_low,
-        dx0_low,
-    )
-    dagg = grid.gate(dagg, [flow["pair"]])
-    got_core = stage([("pair", 0)], [])
+    u_line = plus(uq[0], f0u)
+    d_half = halves(d_line, nd)
+    dagg = grid.gate(dagg, [f0u, nd])
+    nu, z1d = grid.begin([f0u, nd, dagg], (near, u_side), (z1, d_half[1]))
     g_rows, s_rows = call(
         pool_back_kernel,
         "pool_back",
-        (HEADS // 2,),
+        (HEADS // 4,),
         [
             full((rows, n)),
             full((n, 128)),
-            pl.BlockSpec((n, 128), lambda j: (0, j)),
-            pl.BlockSpec((2, rows, n), lambda j: (j, 0, 0)),
-            pl.BlockSpec((2, rows, 128), lambda j: (j, 0, 0)),
+            pl.BlockSpec((n, 256), lambda j: (0, j)),
+            pl.BlockSpec((4, rows, n), lambda j: (j, 0, 0)),
+            pl.BlockSpec((4, rows, 128), lambda j: (j, 0, 0)),
             pair,
         ],
-        (shape(n, width), shape(HEADS // 2, 2, n)),
-        (pl.BlockSpec((n, 128), lambda j: (0, j)), pl.BlockSpec((1, 2, n), lambda j: (j, 0, 0))),
+        (shape(n, width), shape(HEADS // 4, 4, n)),
+        (pl.BlockSpec((n, 256), lambda j: (0, j)), pl.BlockSpec((1, 4, n), lambda j: (j, 0, 0))),
         [],
         14 * HEADS * rows * n * 128,
         1 << 23,
@@ -1457,39 +1547,45 @@
         pa,
         dagg,
     )
-    extra = jnp.concatenate(
-        [
-            jnp.zeros((src_at, width), F32),
-            dot(onehot, dx0_sum, TN, precision=HIGH),
-            jnp.zeros((1, width), F32),
-            d_gain_one,
-            d_gain_two,
-            jnp.zeros((n - src_at - SOURCES - 3, width), F32),
-        ],
-        axis=0,
-    )
-    s_rows = grid.gate(s_rows, got)
-    got = stage([("down", 4), ("up", 3), ("qkv", 2), ("pair", 1)], [got, got_core, g_rows])
-    s_sum = grid.hop(s_rows.reshape(HEADS, n), ("c", 1), ("y", 1))
-    flow["rows"] = sent(
-        lambda *r: rows_kernel(*r, tall=tall),
-        "rows",
-        tall + head_rows,
-        128,
-        0,
-        [],
-        (g_rows + extra).astype(BF),
-        chunked(d_head, BANDS, STRIPS).reshape(BANDS, STRIPS, head_rows, 128),
-    )
-    got_core = stage([("rows", 0)], [])
-    got = stage([("up", 4), ("qkv", 3), ("pair", 2), ("rows", 1)], [got, got_core, s_sum])
-    s_sum = grid.hop(s_sum, ("x", 1))
-    got = stage([("qkv", 4), ("pair", 3), ("rows", 2)], [got, s_sum])
-    wq_parts = grid.gate(wq_parts, got)
-    s_sum = grid.hop(s_sum, ("z", 1))
-    got = stage([("pair", 4), ("rows", 3)], [got, s_sum])
-    s_sum = grid.hop(s_sum, ("z", 2))
-    got = stage([("rows", 4)], [got, s_sum])
+    aq = quarters(flow["attn"][0], got)
+    u_half = halves(u_line, nu)
+    d_end = ends(d_half[0], z1d)
+    dx0_low = grid.gate(dx0_low, [g_rows, nu, z1d])
+    f1a, z1u = grid.begin([nu, z1d, g_rows], (far, aq[3]), (z1, u_half[1]))
+    flow["low"] = sent_pairs(
+        lambda *r: low_grad_kernel(*r, band=band, tall=tall, top=src_at - (n - 16)),
+        "low_grad",
+        band + tall + head_rows,
+        2 * rows * width * width,
+        [*turned, pltpu.VMEM((n, width), BF)],
+        groups[:, 0, 0],
+        agg,
+        dx0_low,
+        g_rows,
+        dx0_sum,
+        jnp.concatenate([d_gain_one, d_gain_two], axis=0),
+        d_head,
+    )
+    a_side = plus(aq[1], f1a)
+    u_end = ends(u_half[0], z1u)
+    lk, ls = flow["low"]
+    f0a, na, z2d, z2u, got = grid.begin(
+        [f1a, z1u, lk], (far, aq[2]), (near, a_side), (z2, d_end[1]), (z2, u_end[1]), (core, ls)
+    )
+    lq = [plus(lk[: 2 * NZ], got[: 2 * NZ]), plus(lk[2 * NZ :], got[2 * NZ :])]
+    fl = far(lq[1])
+    down_sum = (d_end[0].astype(F32) + z2d.astype(F32))[0]
+    up_sum = (u_end[0].astype(F32) + z2u.astype(F32))[0]
+    a_half = halves(plus(aq[0], f0a), na)
+    l_side, l_line = plus(lq[0][NZ:], fl[NZ:]), plus(lq[0][:NZ], fl[:NZ])
+    nl, z1a = grid.begin([f0a, na, z2d, z2u, fl], (near, l_side), (z1, a_half[1]))
+    l_half = halves(l_line, nl)
+    z1l = z1(l_half[1])
+    s_sum = grid.hop(grid.gate(s_rows.reshape(HEADS, n), nl), ("x", 1), ("c", 1), ("y", 1))
+    a_end, l_end = ends(a_half[0], z1a), ends(l_half[0], z1l)
+    z2l, z2a = grid.begin([z1a, z1l], (z2, l_end[1]), (z2, a_end[1]))
+    s_sum = grid.hop(grid.gate(s_sum, [z1a, z1l]), ("z", 1), ("z", 2))
+    wq_parts = grid.gate(wq_parts, z2l)
     wq, wk = call(
         lambda *r: square_kernel(*r, band=band),
         "squares",
@@ -1503,6 +1599,9 @@
         co,
         *twice(wq_parts),
     )
+    low_sum, attn_sum = (
+        (kept[0].astype(F32) + got.astype(F32))[0] for kept, got in ((l_end, z2l), (a_end, z2a))
+    )
     u_heads = (jnp.arange(width)[:, None] // size == jnp.arange(HEADS)[None]).astype(F32)
     du = dot(table.astype(F32), s_sum, ((0,), (1,)), precision=HIGH)
     du_cols = dot(lax.dynamic_slice_in_dim(du, my_band * band, band), head_mask, NT, precision=HIGH)
@@ -1513,14 +1612,14 @@
         lax.dynamic_slice_in_dim(wq, my_strip * strip, strip, 0).astype(F32) * dqv_all[None], axis=1
     )
     table_own = lax.dynamic_slice_in_dim(table, my_band * band, band, 1)
-    g_own = done["rows"][0][:tall]
+    g_own = low_sum[band : band + tall]
     g_low = g_own.astype(BF)
-    g_column = grid.spread(g_low, ("y", "c")).reshape(n, strip)
-    g_line = jnp.transpose(grid.spread(g_low, ("z", "x")), (1, 0, 2)).reshape(tall, width)
-    down_sum, up_sum = done["down"][0], done["up"][0]
-    wa_sum = done["pair"][0][band:]
-    attn_sum = (done["qkv"][0].reshape(3, band, strip), done["pair"][0][:band])
-    head_sum = done["rows"][0][tall:].reshape(head_master.shape)
+    g_column = grid.collect(grid.collect(g_low, "c"), "y").reshape(n, strip)
+    g_line = grid.collect(grid.collect(g_low, "x"), "z").reshape(STRIPS, tall, strip)
+    g_line = jnp.transpose(g_line, (1, 0, 2)).reshape(tall, width)
+    wa_sum = low_sum[:band]
+    head_sum = low_sum[band + tall :].reshape(2, ho // STRIPS, strip)
+    head_sum = jnp.transpose(head_sum, (1, 0, 2)).reshape(ho // STRIPS, band).T
 
     row_of = np.full((n,), base + SOURCES + 3)
     for row in range(base + SOURCES + 3):
@@ -1537,9 +1636,9 @@
     own_row = lax.dynamic_slice_in_dim(row_of, my_band * tall, tall)[:, None]
     table_sum = jnp.where(own_row < base, d_rows, g_own)
     table_sum = jnp.where(own_row == base + SOURCES, dq_own[None], table_sum)[:table_band]
-    square_sums = (query_sum, key_sum, value_sum, wa_sum, *attn_sum)
+    square_sums = (query_sum, key_sum, value_sum, wa_sum, attn_sum)
     sumsq = sum(jnp.sum(s * s) for s in (*square_sums, up_sum, down_sum, head_sum, table_sum))
-    both = grid.total(jnp.stack([loss_part[0, 0], sumsq]))
+    both = grid.rounds(jnp.stack([loss_part[0, 0], sumsq]), AXES)
     loss = both[0] / count
     grad_norm = jnp.sqrt(both[1])
     factor = jnp.minimum(1.0, CLIP_AT / grad_norm)

time: 583 us -> 535 us (0.918)
  local copies, waits for them, and re-layouts: 40.6 us -> 20.5 us
  Pallas kernels: 180 us -> 166 us
  waiting for transfers between devices: 170 us -> 159 us
    ppermute x62 -> x61, waiting for transfers between devices: 138 us -> 92.3 us  [swap(): lax.ppermute(value, axis, [(i, i ^ bit) for i in range(self.sizes[axis])])]
    ppermute x23 -> x25, waiting for transfers between devices: 32.4 us -> 66.3 us  [permute(): return lax.ppermute(value, AXES, self.flat(move))]
    pallas_call x17 -> x16, Pallas kernels: 180 us -> 166 us  [call(): pl.pallas_call(kernel, name=name, grid=grid, in_specs=in_specs, out_shape...]
    reshape x5 -> x2, local copies, waits for them, and re-layouts: 9.29 us -> 0.83 us  [the longest x1 0.75 us: fast_body(): s_rows.reshape(HEADS, n)]
    add x13 -> x4, other arithmetic: 8.34 us -> 0.77 us  [the longest x1 0.72 us: rounds(): value = value + self.swap(value, 'c')]
    ppermute x23 -> x25, starting transfers between devices: 22.9 us -> 27 us  [permute(): return lax.ppermute(value, AXES, self.flat(move))]
    ppermute x62 -> x61, starting transfers between devices: 60.6 us -> 61.6 us  [swap(): lax.ppermute(value, axis, [(i, i ^ bit) for i in range(self.sizes[axis])])]
    convert_element_type x22 -> x19, other arithmetic: 31.6 us -> 31.1 us  [plus(): return (left.astype(F32) + right.astype(F32)).astype(BF)]
  transfers between devices with their start and end apart: 85 -> 86, of which waited for: 42 -> 44; matrix products, arithmetic and copies ran while one was open for 15% -> 15% of each run, Pallas kernels for 24% -> 31%
where the time goes in v3:
time: 535 us; the launch traced here: 529 us
  Pallas kernels  166 us (31%)
  waiting for transfers between devices  159 us (30%)
  starting transfers between devices  88.5 us (17%)
  other arithmetic  70.8 us (13%)
  local copies, waits for them, and re-layouts  20.5 us (4%)
  between operations  13.7 us (3%)
  matrix products  10.2 us (2%)
    pallas_call x16, Pallas kernels, call(): pl.pallas_call(kernel, name=name, grid=grid, in_specs=in_specs, out_shape...  166 us
    ppermute x61, waiting for transfers between devices, swap(): lax.ppermute(value, axis, [(i, i ^ bit) for i in range(self.sizes[axis])])  92.3 us
    ppermute x25, waiting for transfers between devices, permute(): return lax.ppermute(value, AXES, self.flat(move))  66.3 us
    ppermute x61, starting transfers between devices, swap(): lax.ppermute(value, axis, [(i, i ^ bit) for i in range(self.sizes[axis])])  61.6 us
    convert_element_type x19, other arithmetic, plus(): return (left.astype(F32) + right.astype(F32)).astype(BF)  31.1 us
    ppermute x25, starting transfers between devices, permute(): return lax.ppermute(value, AXES, self.flat(move))  27 us
  transfers between devices with their start and end apart: 86, of which 44 were waited for; matrix products, arithmetic and copies ran while one was open for 15% of the time, Pallas kernels for 31%

profile of v3, /device:TPU:0, one launch (start us, length us, event | category | flops | bytes accessed | tf_op | source)
XLA Modules:
  0.0 528.6 jit_solution(1240759724648752575)
XLA Ops:
  2.2 2.6 collective-permute-start.8
  7.8 3.1 collective-permute-start
  13.0 5.7 %collective-permute-done = bf16[656,128]{1,0:T(8,128)(2,1)S(1)} collective-permute-done((bf16[656,128]{1,0:T(8,128)(2,1)S(1)}, bf16[656,128]{1,0:T(8,128)(2,1)S(1)}, u32[]{:S(2)}, u32[]{:S(2)}) %collective-permute-start) | collective-permute-done | bytes 167968 | tf_op jit(solution)/shard_map/ppermute | solution.py:58
  19.7 2.6 collective-permute-done.1
  45.8 9.4 %collective-permute-done.10 = bf16[1024,128]{1,0:T(8,128)(2,1)S(1)} collective-permute-done((bf16[1024,128]{1,0:T(8,128)(2,1)S(1)}, bf16[1024,128]{1,0:T(8,128)(2,1)S(1)}, u32[]{:S(2)}, u32[]{:S(2)}) %collective-permute-start.10) | collective-permute-done | bytes 262176 | tf_op jit(solution)/shard_map/ppermute | solution.py:58
  61.1 3.5 collective-permute-done.16
  64.6 4.2 collective-permute-start.17
  70.9 3.3 collective-permute-done.18
  79.6 11.7 %collective-permute-done.21 = bf16[256,512]{1,0:T(8,128)(2,1)S(1)} collective-permute-done((bf16[256,512]{1,0:T(8,128)(2,1)S(1)}, bf16[256,512]{1,0:T(8,128)(2,1)S(1)}, u32[]{:S(2)}, u32[]{:S(2)}) %collective-permute-start.21) | collective-permute-done | bytes 262176 | tf_op jit(solution)/shard_map/ppermute | solution.py:58
  91.4 10.8 %collective-permute-done.20 = bf16[4,1024,128]{2,1,0:T(8,128)(2,1)S(1)} collective-permute-done((bf16[4,1024,128]{2,1,0:T(8,128)(2,1)S(1)}, bf16[4,1024,128]{2,1,0:T(8,128)(2,1)S(1)}, u32[]{:S(2)}, u32[]{:S(2)}) %collective-permute-start.20) | collective-permute-done | bytes 1048608 | tf_op jit(solution)/shard_map/ppermute | solution.py:55
  108.7 9.3 %collective-permute-done.25 = f32[1024,16]{0,1:T(8,128)S(1)} collective-permute-done((f32[1024,16]{0,1:T(8,128)S(1)}, f32[1024,16]{0,1:T(8,128)S(1)}, u32[]{:S(2)}, u32[]{:S(2)}) %collective-permute-start.25) | collective-permute-done | bytes 65568 | tf_op jit(solution)/shard_map/ppermute | solution.py:58
  119.2 4.2 collective-permute-done.27
  124.3 6.6 %collective-permute-done.26.r_7_.r_8_.r_15_.r_16_.r_6_ = bf16[8,1024,128]{2,1,0:T(8,128)(2,1)S(1)} collective-permute-done((bf16[8,1024,128]{2,1,0:T(8,128)(2,1)S(1)}, bf16[8,1024,128]{2,1,0:T(8,128)(2,1)S(1)}, u32[]{:S(2)}, u32[]{:S(2)}) %collective-permute-start.26) | collective-permute-done | bytes 2097184 | tf_op jit(solution)/shard_map/ppermute | solution.py:55
  133.7 6.1 %assemble.1 = (bf16[384,1024]{1,0:T(8,128)(2,1)}, f32[192,1024]{1,0:T(8,128)}, bf16[1024,1024]{1,0:T(8,128)(2,1)}) custom-call(s32[4]{0:T(128)} %pad_add_fusion.r_0_, bf16[8,656,128]{2,1,0:T(8,128)(2,1)} %copy-done.3, bf16[8,656,128]{2,1,0:T(8,128)(2,1)} %copy-done.3, bf16[8,656,128]{2,1,0:T(8,128)(2,1)} %copy-done.4, bf16[8,656,128]{2,1,0:T(8,128)(2,1)} %copy-done.4, ...), custom_call_target="tpu_custom_call" | custom-call | bytes 8388608 | tf_op jit(solution)/shard_map/assemble/pallas_call | solution.py:643
  139.8 4.9 table_values.1.tv_ref
  146.8 2.8 pad_maximum_fusion.1.r_2_.r_3_.r_5_.r_6_
  162.3 12.9 %pool.1 = (bf16[256,1024]{1,0:T(8,128)(2,1)}, bf16[16,256,384]{2,1,0:T(8,128)(2,1)}, f32[16,256,128]{2,1,0:T(8,128)}) custom-call(bf16[256,384]{1,0:T(8,128)(2,1)} %fusion.8.x_ref, bf16[384,128]{1,0:T(8,128)(2,1)} %constant.157.clone.e_ref, f32[384,128]{1,0:T(8,128)} %pad.10.tu_ref, bf16[384,1024]{1,0:T(8,128)(2,1)} %table_values.1.tv_ref), custom_call_target="tpu_custom_call" | custom-call | flops 2415919104 | bytes 8388608 | tf_op jit(solution)/shard_map/pool/pallas_call | solution.py:643
  175.1 5.2 enter.1
  180.4 3.9 collective-permute-done.33
  185.9 2.5 collective-permute-done.32.r_4_.r_5_.r_7_.r_8_
  190.7 19.3 %attend.1 = (bf16[256,3072]{1,0:T(8,128)(2,1)}, f32[16,2,128,128]{3,2,1,0:T(8,128)}, bf16[256,1024]{1,0:T(8,128)(2,1)}, f32[256,1024]{1,0:T(8,128)}, bf16[256,1024]{1,0:T(8,128)(2,1)}) custom-call(s32[4]{0:T(128)} %pad_add_fusion.r_0_, s32[2]{0:T(128)} %bitcast.241, f32[256,1024]{1,0:T(8,128)} %get-tuple-element.139.r_2_.r_3_, ...), custom_call_target="tpu_custom_call" | custom-call | flops 2415919104 | bytes 16777216 | tf_op jit(solution)/shard_map/attend/pallas_call | solution.py:643
  211.0 4.3 collective-permute-done.37.r_10_.r_11_
  216.4 10.5 %up.1 = (bf16[256,4096]{1,0:T(8,128)(2,1)}, bf16[256,4096]{1,0:T(8,128)(2,1)}) custom-call(s32[4]{0:T(128)} %pad_add_fusion.r_0_, bf16[256,1024]{1,0:T(8,128)(2,1)} %get-tuple-element.144.r_1_, bf16[8,256,512]{2,1,0:T(8,128)(2,1)} %pad_maximum_fusion.1.r_2_.r_3_.r_5_.r_6_, bf16[8,256,512]{2,1,0:T(8,128)(2,1)} %pad_maximum_fusion.1.r_2_.r_3_.r_5_.r_6_, ...), custom_call_target="tpu_custom_call" | custom-call | flops 2147483648 | bytes 16777216 | tf_op jit(solution)/shard_map/up/pallas_call | solution.py:643
  234.7 19.9 %down.1 = (f32[8,128]{1,0:T(8,128)}, f32[256,1024]{1,0:T(8,128)}, bf16[256,1024]{1,0:T(8,128)(2,1)}, f32[192,1024]{1,0:T(8,128)}, bf16[256,4096]{1,0:T(8,128)(2,1)}) custom-call(s32[4]{0:T(128)} %pad_add_fusion.r_0_, f32[1]{0:T(128)} %slice.357.r_1_, f32[256,1024]{1,0:T(8,128)} %get-tuple-element.143.r_2_, bf16[256,4096]{1,0:T(8,128)(2,1)} %get-tuple-element.155.r_3_.r_2_, ...), custom_call_target="tpu_custom_call" | custom-call | flops 4294967296 | bytes 33554432 | tf_op jit(solution)/shard_map/down/pallas_call | solution.py:643
  254.6 6.6 %down_grad.1 = (bf16[16,256,512]{2,1,0:T(8,128)(2,1)}, bf16[16,256,512]{2,1,0:T(8,128)(2,1)}) custom-call(s32[4]{0:T(128)} %pad_add_fusion.r_0_, bf16[256,1024]{1,0:T(8,128)(2,1)} %get-tuple-element.164.r_1_, bf16[256,4096]{1,0:T(8,128)(2,1)} %get-tuple-element.155.r_3_.r_2_), custom_call_target="tpu_custom_call" | custom-call | flops 2147483648 | bytes 12582912 | tf_op jit(solution)/shard_map/down_grad/pallas_call | solution.py:643
  261.2 6.7 %up_grad.1 = (bf16[16,256,512]{2,1,0:T(8,128)(2,1)}, bf16[16,256,512]{2,1,0:T(8,128)(2,1)}) custom-call(s32[4]{0:T(128)} %pad_add_fusion.r_0_, bf16[256,1024]{1,0:T(8,128)(2,1)} %get-tuple-element.144.r_1_, bf16[256,4096]{1,0:T(8,128)(2,1)} %get-tuple-element.172.r_2_.r_1_), custom_call_target="tpu_custom_call" | custom-call | flops 2147483648 | bytes 12582912 | tf_op jit(solution)/shard_map/up_grad/pallas_call | solution.py:643
  268.7 3.7 add_convert_fusion.10
  273.0 13.0 %up_back.1 = (f32[256,1024]{1,0:T(8,128)}, bf16[256,1024]{1,0:T(8,128)(2,1)}, f32[1,1024]{1,0:T(1,128)}) custom-call(s32[4]{0:T(128)} %pad_add_fusion.r_0_, bf16[256,4096]{1,0:T(8,128)(2,1)} %get-tuple-element.172.r_2_.r_1_, f32[256,1024]{1,0:T(8,128)} %get-tuple-element.143.r_2_, f32[1,1024]{1,0:T(1,128)} %get-tuple-element.278.r_4_.r_3_, ...), custom_call_target="tpu_custom_call" | custom-call | flops 2147483648 | bytes 16777216 | tf_op jit(solution)/shard_map/up_back/pallas_call | solution.py:643
  286.0 3.9 add_convert_fusion.6
  291.5 14.3 %attend_back.1.r_3_.r_2_ = bf16[256,3072]{1,0:T(8,128)(2,1)} custom-call(s32[4]{0:T(128)} %pad_add_fusion.r_0_, bf16[256,1024]{1,0:T(8,128)(2,1)} %get-tuple-element.177.r_1_.r_4_, bf16[256,3072]{1,0:T(8,128)(2,1)} %get-tuple-element.178.r_2_, f32[16,2,128,128]{3,2,1,0:T(8,128)} %get-tuple-element.179.r_3_, bf16[8,1024,128]{2,1,0:T(8,128)(2,1)} %copy-done, ...), custom_call_target="tpu_custom_call" | custom-call | flops 939524096 | bytes 4194304 | tf_op jit(solution)/shard_map/attend_back/pallas_call | solution.py:643
  307.9 7.4 %attention_grad.1 = (bf16[4,4,1024,128]{3,2,1,0:T(8,128)(2,1)}, bf16[4,4,1024,128]{3,2,1,0:T(8,128)(2,1)}) custom-call(s32[4]{0:T(128)} %pad_add_fusion.r_0_, bf16[256,1024]{1,0:T(8,128)(2,1)} %get-tuple-element.140.r_3_.r_1_, bf16[256,1024]{1,0:T(8,128)(2,1)} %get-tuple-element.183.r_2_, bf16[256,3072]{1,0:T(8,128)(2,1)} %attend_back.1.r_3_.r_2_, ...), custom_call_target="tpu_custom_call" | custom-call | flops 2147483648 | bytes 8388608 | tf_op jit(solution)/shard_map/attention_grad/pallas_call | solution.py:643
  315.3 7.1 %collective-permute-done.47 = bf16[4,256,512]{2,1,0:T(8,128)(2,1)S(1)} collective-permute-done((bf16[4,256,512]{2,1,0:T(8,128)(2,1)}, bf16[4,256,512]{2,1,0:T(8,128)(2,1)S(1)}, u32[]{:S(2)}, u32[]{:S(2)}) %collective-permute-start.47) | collective-permute-done | bytes 1048608 | tf_op jit(solution)/shard_map/ppermute | solution.py:55
  326.0 17.4 %leave.1 = (bf16[256,1024]{1,0:T(8,128)(2,1)}, f32[1,1024]{1,0:T(1,128)}, f32[2,1024]{1,0:T(2,128)}, bf16[256,1024]{1,0:T(8,128)(2,1)}) custom-call(s32[4]{0:T(128)} %pad_add_fusion.r_0_, f32[256,1024]{1,0:T(8,128)} %get-tuple-element.174.r_1_, bf16[256,3072]{1,0:T(8,128)(2,1)} %attend_back.1.r_3_.r_2_, f32[256,1024]{1,0:T(8,128)} %get-tuple-element.139.r_2_.r_3_, ...), custom_call_target="tpu_custom_call" | custom-call | flops 2147483648 | bytes 8388608 | tf_op jit(solution)/shard_map/leave/pallas_call | solution.py:643
  344.7 3.3 collective-permute-done.48
  352.3 11.1 %pool_back.1 = (f32[384,1024]{1,0:T(8,128)}, f32[4,4,384]{2,1,0:T(4,128)}) custom-call(bf16[256,384]{1,0:T(8,128)(2,1)} %fusion.8.x_ref, bf16[384,128]{1,0:T(8,128)(2,1)} %constant.157.clone.e_ref, bf16[384,1024]{1,0:T(8,128)(2,1)} %table_values.1.tv_ref, bf16[16,256,384]{2,1,0:T(8,128)(2,1)} %get-tuple-element.161.a_ref, ...), custom_call_target="tpu_custom_call" | custom-call | flops 2818572288 | bytes 8388608 | tf_op jit(solution)/shard_map/pool_back/pallas_call | solution.py:643
  372.9 5.3 low_grad.1
  378.1 6.0 %collective-permute-done.54 = bf16[2,256,512]{2,1,0:T(8,128)(2,1)} collective-permute-done((bf16[2,256,512]{2,1,0:T(8,128)(2,1)}, bf16[2,256,512]{2,1,0:T(8,128)(2,1)}, u32[]{:S(2)}, u32[]{:S(2)}) %collective-permute-start.54) | collective-permute-done | bytes 524320 | tf_op jit(solution)/shard_map/ppermute | solution.py:58
  385.2 2.7 add_convert_fusion.1
  395.7 18.3 %collective-permute-done.57 = bf16[4,1024,128]{2,1,0:T(8,128)(2,1)S(1)} collective-permute-done((bf16[4,1024,128]{2,1,0:T(8,128)(2,1)S(1)}, bf16[4,1024,128]{2,1,0:T(8,128)(2,1)S(1)}, u32[]{:S(2)}, u32[]{:S(2)}) %collective-permute-start.57) | collective-permute-done | bytes 1048608 | tf_op jit(solution)/shard_map/ppermute | solution.py:55
  416.8 6.1 %collective-permute-done.56 = bf16[8,400,128]{2,1,0:T(8,128)(2,1)S(1)} collective-permute-done((bf16[8,400,128]{2,1,0:T(8,128)(2,1)S(1)}, bf16[8,400,128]{2,1,0:T(8,128)(2,1)S(1)}, u32[]{:S(2)}, u32[]{:S(2)}) %collective-permute-start.56) | collective-permute-done | bytes 819232 | tf_op jit(solution)/shard_map/ppermute | solution.py:55
  440.0 2.5 multiply_reduce_fusion.2
  444.6 3.5 collective-permute-done.66
  456.3 7.8 %collective-permute-done.68 = f32[16,384]{1,0:T(8,128)S(1)} collective-permute-done((f32[16,384]{1,0:T(8,128)S(1)}, f32[16,384]{1,0:T(8,128)S(1)}, u32[]{:S(2)}, u32[]{:S(2)}) %collective-permute-start.68) | collective-permute-done | bytes 24608 | tf_op jit(solution)/shard_map/ppermute | solution.py:58
  468.5 5.8 %squares.1 = (bf16[1024,1024]{1,0:T(8,128)(2,1)}, bf16[1024,1024]{1,0:T(8,128)(2,1)}) custom-call(s32[4]{0:T(128)} %pad_add_fusion.r_0_, bf16[8,512,128]{2,1,0:T(8,128)(2,1)} %copy-done.10, bf16[8,512,128]{2,1,0:T(8,128)(2,1)} %copy-done.10, bf16[8,512,128]{2,1,0:T(8,128)(2,1)} %collective-permute-done.42.r_3_.r_4_, ...), custom_call_target="tpu_custom_call" | custom-call | bytes 1048576 | tf_op jit(solution)/shard_map/squares/pallas_call | solution.py:643
  474.4 2.5 fusion.11
  510.8 2.5 collective-permute-start.83
  519.2 4.5 fusion.76
  523.7 2.5 fusion.74
  (441 shorter events, 181.2 us)
Async XLA Ops:
  1.6 36.1 %collective-permute-start.6 = (bf16[2,128,48]{1,2,0:T(8,128)(2,1)S(1)}, bf16[2,128,48]{1,2,0:T(8,128)(2,1)S(1)}, u32[]{:S(2)}, u32[]{:S(2)}) collective-permute-start(bf16[2,128,48]{1,2,0:T(8,128)(2,1)S(1)} %get-tuple-element.293), channel_id=1, source_target_pairs={{0,8},{1,9},{2,10},{3,11},{4,12},{5,13},{6,14},{7,15},{8,0},{9,1},... | collective-permute-start | bytes 73736 | tf_op jit(solution)/shard_map/ppermute | solution.py:55
  2.2 32.1 %collective-permute-start.8 = (bf16[2,128,48]{1,2,0:T(8,128)(2,1)S(1)}, bf16[2,128,48]{1,2,0:T(8,128)(2,1)S(1)}, u32[]{:S(2)}, u32[]{:S(2)}) collective-permute-start(bf16[2,128,48]{1,2,0:T(8,128)(2,1)S(1)} %get-tuple-element.295), channel_id=1, source_target_pairs={{0,24},{1,25},{2,26},{3,27},{4,28},{5,29},{6,30},{7,31},{8,16},{9,... | collective-permute-start | bytes 73736 | tf_op jit(solution)/shard_map/ppermute | solution.py:55
  4.8 27.3 %collective-permute-start.7 = (bf16[2,128,48]{1,2,0:T(8,128)(2,1)S(1)}, bf16[2,128,48]{1,2,0:T(8,128)(2,1)S(1)}, u32[]{:S(2)}, u32[]{:S(2)}) collective-permute-start(bf16[2,128,48]{1,2,0:T(8,128)(2,1)S(1)} %get-tuple-element.296), channel_id=1, source_target_pairs={{0,16},{1,17},{2,18},{3,19},{4,20},{5,21},{6,22},{7,23},{8,24},{9,... | collective-permute-start | bytes 73736 | tf_op jit(solution)/shard_map/ppermute | solution.py:55
  39.8 15.4 %collective-permute-start.10 = (bf16[1024,128]{1,0:T(8,128)(2,1)S(1)}, bf16[1024,128]{1,0:T(8,128)(2,1)S(1)}, u32[]{:S(2)}, u32[]{:S(2)}) collective-permute-start(bf16[1024,128]{1,0:T(8,128)(2,1)S(1)} %bitcast.205), channel_id=1, source_target_pairs={{0,4},{2,6},{4,0},{6,2},{1,5},{3,7},{5,1},{7,3},{8,12},{10,14},{12... | collective-permute-start | bytes 786440 | tf_op jit(solution)/shard_map/ppermute | solution.py:58
  41.9 14.9 %collective-permute-start.9 = (bf16[2,656,128]{2,1,0:T(8,128)(2,1)S(1)}, bf16[2,656,128]{2,1,0:T(8,128)(2,1)S(1)}, u32[]{:S(2)}, u32[]{:S(2)}) collective-permute-start(bf16[2,656,128]{2,1,0:T(8,128)(2,1)S(1)} %pad_maximum_fusion.13), channel_id=1, source_target_pairs={{0,2},{2,0},{4,6},{6,4},{1,3},{3,1},{5,7},{7,5},{8,10},{10,8},{12,... | collective-permute-start | bytes 1007624 | tf_op jit(solution)/shard_map/ppermute | solution.py:58
  44.2 15.3 %collective-permute-start.15 = (f32[1024,16]{0,1:T(8,128)S(1)}, f32[1024,16]{0,1:T(8,128)S(1)}, u32[]{:S(2)}, u32[]{:S(2)}) collective-permute-start(f32[1024,16]{0,1:T(8,128)S(1)} %get-tuple-element.307), channel_id=1, source_target_pairs={{0,1},{1,0},{2,3},{3,2},{4,5},{5,4},{6,7},{7,6},{8,9},{9,8},{10,11... | collective-permute-start | bytes 196616 | tf_op jit(solution)/shard_map/ppermute | solution.py:58
  56.9 17.3 %collective-permute-start.14 = (bf16[2,1024,128]{2,1,0:T(8,128)(2,1)S(1)}, bf16[2,1024,128]{2,1,0:T(8,128)(2,1)S(1)}, u32[]{:S(2)}, u32[]{:S(2)}) collective-permute-start(bf16[2,1024,128]{2,1,0:T(8,128)(2,1)S(1)} %pad_maximum_fusion.9), channel_id=1, source_target_pairs={{0,2},{2,0},{4,6},{6,4},{1,3},{3,1},{5,7},{7,5},{8,10},{10,8},{12,... | collective-permute-start | bytes 1572872 | tf_op jit(solution)/shard_map/ppermute | solution.py:58
  58.0 16.3 %collective-permute-start.13 = (bf16[4,656,128]{2,1,0:T(8,128)(2,1)S(1)}, bf16[4,656,128]{2,1,0:T(8,128)(2,1)S(1)}, u32[]{:S(2)}, u32[]{:S(2)}) collective-permute-start(bf16[4,656,128]{2,1,0:T(8,128)(2,1)S(1)} %pad_maximum_fusion.8), channel_id=1, source_target_pairs={{0,1},{1,0},{2,3},{3,2},{4,5},{5,4},{6,7},{7,6},{8,24},{9,25},{10,... | collective-permute-start | bytes 2015240 | tf_op jit(solution)/shard_map/ppermute | solution.py:55
  74.5 30.2 %collective-permute-start.19 = (bf16[8,656,128]{2,1,0:T(8,128)(2,1)S(1)}, bf16[8,656,128]{2,1,0:T(8,128)(2,1)S(1)}, u32[]{:S(2)}, u32[]{:S(2)}) collective-permute-start(bf16[8,656,128]{2,1,0:T(8,128)(2,1)S(1)} %pad_maximum_fusion.3.r_1_.r_2_.r_3_.r_4_.r_5_.r_13_.r_14_), channel_id=1, source_target_pairs={{0,16},{1,17},{2,18},{3,19},{4,20},{5,21},{6,22},{7,23},{8,9},{9,8... | collective-permute-start | bytes 4030472 | tf_op jit(solution)/shard_map/ppermute | solution.py:55
  76.1 26.1 %collective-permute-start.20 = (bf16[4,1024,128]{2,1,0:T(8,128)(2,1)S(1)}, bf16[4,1024,128]{2,1,0:T(8,128)(2,1)S(1)}, u32[]{:S(2)}, u32[]{:S(2)}) collective-permute-start(bf16[4,1024,128]{2,1,0:T(8,128)(2,1)S(1)} %pad_maximum_fusion.4), channel_id=1, source_target_pairs={{0,1},{1,0},{2,3},{3,2},{4,5},{5,4},{6,7},{7,6},{8,24},{9,25},{10,... | collective-permute-start | bytes 3145736 | tf_op jit(solution)/shard_map/ppermute | solution.py:55
  104.7 26.1 %collective-permute-start.26 = (bf16[8,1024,128]{2,1,0:T(8,128)(2,1)S(1)}, bf16[8,1024,128]{2,1,0:T(8,128)(2,1)S(1)}, u32[]{:S(2)}, u32[]{:S(2)}) collective-permute-start(bf16[8,1024,128]{2,1,0:T(8,128)(2,1)S(1)} %pad_maximum_fusion.r_5_.r_6_.r_13_.r_14_.r_4_), channel_id=1, source_target_pairs={{0,16},{1,17},{2,18},{3,19},{4,20},{5,21},{6,22},{7,23},{8,9},{9,8... | collective-permute-start | bytes 6291464 | tf_op jit(solution)/shard_map/ppermute | solution.py:55
  105.3 18.9 %collective-permute-start.23 = (bf16[8,656,128]{2,1,0:T(8,128)(2,1)S(1)}, bf16[8,656,128]{2,1,0:T(8,128)(2,1)S(1)}, u32[]{:S(2)}, u32[]{:S(2)}) collective-permute-start(bf16[8,656,128]{2,1,0:T(8,128)(2,1)S(1)} %pad_maximum_fusion.3.r_1_.r_2_.r_3_.r_4_.r_5_.r_13_.r_14_), channel_id=1, source_target_pairs={{0,8},{8,0},{1,9},{9,1},{2,10},{10,2},{3,11},{11,3},{4,12},{12,4},... | collective-permute-start | bytes 4030472 | tf_op jit(solution)/shard_map/ppermute | solution.py:58
  105.3 18.9 %collective-permute-start.24 = (bf16[8,656,128]{2,1,0:T(8,128)(2,1)S(1)}, bf16[8,656,128]{2,1,0:T(8,128)(2,1)S(1)}, u32[]{:S(2)}, u32[]{:S(2)}) collective-permute-start(bf16[8,656,128]{2,1,0:T(8,128)(2,1)S(1)} %collective-permute-done.19.r_3_.r_4_.r_5_.r_6_.r_7_.r_15_.r_16_), channel_id=1, source_target_pairs={{0,8},{8,0},{1,9},{9,1},{2,10},{10,2},{3,11},{11,3},{4,12},{12,4},... | collective-permute-start | bytes 4030472 | tf_op jit(solution)/shard_map/ppermute | solution.py:58
  107.6 15.7 %collective-permute-start.27 = (bf16[256,512]{1,0:T(8,128)(2,1)S(1)}, bf16[256,512]{1,0:T(8,128)(2,1)S(1)}, u32[]{:S(2)}, u32[]{:S(2)}) collective-permute-start(bf16[256,512]{1,0:T(8,128)(2,1)S(1)} %get-tuple-element.133), channel_id=1, source_target_pairs={{0,4},{2,6},{4,0},{6,2},{1,5},{3,7},{5,1},{7,3},{8,12},{10,14},{12... | collective-permute-start | bytes 786440 | tf_op jit(solution)/shard_map/ppermute | solution.py:58
  130.8 18.8 %collective-permute-start.29 = (bf16[8,1024,128]{2,1,0:T(8,128)(2,1)S(1)}, bf16[8,1024,128]{2,1,0:T(8,128)(2,1)S(1)}, u32[]{:S(2)}, u32[]{:S(2)}) collective-permute-start(bf16[8,1024,128]{2,1,0:T(8,128)(2,1)S(1)} %pad_maximum_fusion.r_5_.r_6_.r_13_.r_14_.r_4_), channel_id=1, source_target_pairs={{0,8},{8,0},{1,9},{9,1},{2,10},{10,2},{3,11},{11,3},{4,12},{12,4},... | collective-permute-start | bytes 6291464 | tf_op jit(solution)/shard_map/ppermute | solution.py:58
  130.8 18.8 %collective-permute-start.30 = (bf16[8,1024,128]{2,1,0:T(8,128)(2,1)S(1)}, bf16[8,1024,128]{2,1,0:T(8,128)(2,1)}, u32[]{:S(2)}, u32[]{:S(2)}) collective-permute-start(bf16[8,1024,128]{2,1,0:T(8,128)(2,1)S(1)} %collective-permute-done.26.r_7_.r_8_.r_15_.r_16_.r_6_), channel_id=1, source_target_pairs={{0,8},{8,0},{1,9},{9,1},{2,10},{10,2},{3,11},{11,3},{4,12},{12,4},... | collective-permute-start | bytes 6291464 | tf_op jit(solution)/shard_map/ppermute | solution.py:58
  131.3 15.5 %collective-permute-start.28 = (bf16[4,256,512]{2,1,0:T(8,128)(2,1)}, bf16[4,256,512]{2,1,0:T(8,128)(2,1)}, u32[]{:S(2)}, u32[]{:S(2)}) collective-permute-start(bf16[4,256,512]{2,1,0:T(8,128)(2,1)} %pad_maximum_fusion.5), channel_id=1, source_target_pairs={{0,1},{1,0},{2,3},{3,2},{4,5},{5,4},{6,7},{7,6},{8,24},{9,25},{10,... | collective-permute-start | bytes 3145736 | tf_op jit(solution)/shard_map/ppermute | solution.py:55
  131.9 13.8 %collective-permute-start.31 = (bf16[2,256,512]{2,1,0:T(8,128)(2,1)}, bf16[2,256,512]{2,1,0:T(8,128)(2,1)S(1)}, u32[]{:S(2)}, u32[]{:S(2)}) collective-permute-start(bf16[2,256,512]{2,1,0:T(8,128)(2,1)} %pad_maximum_fusion.11), channel_id=1, source_target_pairs={{0,2},{2,0},{4,6},{6,4},{1,3},{3,1},{5,7},{7,5},{8,10},{10,8},{12,... | collective-permute-start | bytes 1572872 | tf_op jit(solution)/shard_map/ppermute | solution.py:58
  150.9 37.5 %collective-permute-start.32 = (bf16[8,256,512]{2,1,0:T(8,128)(2,1)}, bf16[8,256,512]{2,1,0:T(8,128)(2,1)S(1)}, u32[]{:S(2)}, u32[]{:S(2)}) collective-permute-start(bf16[8,256,512]{2,1,0:T(8,128)(2,1)} %pad_maximum_fusion.1.r_2_.r_3_.r_5_.r_6_), channel_id=1, source_target_pairs={{0,16},{1,17},{2,18},{3,19},{4,20},{5,21},{6,22},{7,23},{8,9},{9,8... | collective-permute-start | bytes 6291464 | tf_op jit(solution)/shard_map/ppermute | solution.py:55
  158.0 26.4 %collective-permute-start.33 = (bf16[4,256,512]{2,1,0:T(8,128)(2,1)}, bf16[4,256,512]{2,1,0:T(8,128)(2,1)S(1)}, u32[]{:S(2)}, u32[]{:S(2)}) collective-permute-start(bf16[4,256,512]{2,1,0:T(8,128)(2,1)} %pad_maximum_fusion.6), channel_id=1, source_target_pairs={{0,1},{1,0},{2,3},{3,2},{4,5},{5,4},{6,7},{7,6},{8,24},{9,25},{10,... | collective-permute-start | bytes 3145736 | tf_op jit(solution)/shard_map/ppermute | solution.py:55
  161.0 19.4 %collective-permute-start.34 = (bf16[512,128]{1,0:T(8,128)(2,1)S(1)}, bf16[512,128]{1,0:T(8,128)(2,1)S(1)}, u32[]{:S(2)}, u32[]{:S(2)}) collective-permute-start(bf16[512,128]{1,0:T(8,128)(2,1)S(1)} %bitcast.219), channel_id=1, source_target_pairs={{0,4},{2,6},{4,0},{6,2},{1,5},{3,7},{5,1},{7,3},{8,12},{10,14},{12... | collective-permute-start | bytes 393224 | tf_op jit(solution)/shard_map/ppermute | solution.py:58
  188.4 22.5 %collective-permute-start.35 = (bf16[8,256,512]{2,1,0:T(8,128)(2,1)}, bf16[8,256,512]{2,1,0:T(8,128)(2,1)S(1)}, u32[]{:S(2)}, u32[]{:S(2)}) collective-permute-start(bf16[8,256,512]{2,1,0:T(8,128)(2,1)} %pad_maximum_fusion.1.r_2_.r_3_.r_5_.r_6_), channel_id=1, source_target_pairs={{0,8},{8,0},{1,9},{9,1},{2,10},{10,2},{3,11},{11,3},{4,12},{12,4},... | collective-permute-start | bytes 6291464 | tf_op jit(solution)/shard_map/ppermute | solution.py:58
  188.4 22.5 %collective-permute-start.36 = (bf16[8,256,512]{2,1,0:T(8,128)(2,1)S(1)}, bf16[8,256,512]{2,1,0:T(8,128)(2,1)S(1)}, u32[]{:S(2)}, u32[]{:S(2)}) collective-permute-start(bf16[8,256,512]{2,1,0:T(8,128)(2,1)S(1)} %collective-permute-done.32.r_4_.r_5_.r_7_.r_8_), channel_id=1, source_target_pairs={{0,8},{8,0},{1,9},{9,1},{2,10},{10,2},{3,11},{11,3},{4,12},{12,4},... | collective-permute-start | bytes 6291464 | tf_op jit(solution)/shard_map/ppermute | solution.py:58
  188.9 26.4 %collective-permute-start.37 = (bf16[8,256,512]{2,1,0:T(8,128)(2,1)}, bf16[8,256,512]{2,1,0:T(8,128)(2,1)}, u32[]{:S(2)}, u32[]{:S(2)}) collective-permute-start(bf16[8,256,512]{2,1,0:T(8,128)(2,1)} %pad_maximum_fusion.2.r_8_.r_9_), channel_id=1, source_target_pairs={{0,16},{1,17},{2,18},{3,19},{4,20},{5,21},{6,22},{7,23},{8,9},{9,8... | collective-permute-start | bytes 6291464 | tf_op jit(solution)/shard_map/ppermute | solution.py:55
  190.5 19.6 %collective-permute-start.38 = (bf16[2,512,128]{2,1,0:T(8,128)(2,1)S(1)}, bf16[2,512,128]{2,1,0:T(8,128)(2,1)S(1)}, u32[]{:S(2)}, u32[]{:S(2)}) collective-permute-start(bf16[2,512,128]{2,1,0:T(8,128)(2,1)S(1)} %pad_maximum_fusion.14), channel_id=1, source_target_pairs={{0,2},{2,0},{4,6},{6,4},{1,3},{3,1},{5,7},{7,5},{8,10},{10,8},{12,... | collective-permute-start | bytes 786440 | tf_op jit(solution)/shard_map/ppermute | solution.py:58
  215.3 18.1 %collective-permute-start.40 = (bf16[8,256,512]{2,1,0:T(8,128)(2,1)}, bf16[8,256,512]{2,1,0:T(8,128)(2,1)S(1)}, u32[]{:S(2)}, u32[]{:S(2)}) collective-permute-start(bf16[8,256,512]{2,1,0:T(8,128)(2,1)} %pad_maximum_fusion.2.r_8_.r_9_), channel_id=1, source_target_pairs={{0,8},{8,0},{1,9},{9,1},{2,10},{10,2},{3,11},{11,3},{4,12},{12,4},... | collective-permute-start | bytes 6291464 | tf_op jit(solution)/shard_map/ppermute | solution.py:58
  215.3 18.1 %collective-permute-start.41 = (bf16[8,256,512]{2,1,0:T(8,128)(2,1)}, bf16[8,256,512]{2,1,0:T(8,128)(2,1)}, u32[]{:S(2)}, u32[]{:S(2)}) collective-permute-start(bf16[8,256,512]{2,1,0:T(8,128)(2,1)} %collective-permute-done.37.r_10_.r_11_), channel_id=1, source_target_pairs={{0,8},{8,0},{1,9},{9,1},{2,10},{10,2},{3,11},{11,3},{4,12},{12,4},... | collective-permute-start | bytes 6291464 | tf_op jit(solution)/shard_map/ppermute | solution.py:58
  228.8 32.4 %collective-permute-start.42 = (bf16[8,512,128]{2,1,0:T(8,128)(2,1)S(1)}, bf16[8,512,128]{2,1,0:T(8,128)(2,1)}, u32[]{:S(2)}, u32[]{:S(2)}) collective-permute-start(bf16[8,512,128]{2,1,0:T(8,128)(2,1)S(1)} %pad_maximum_fusion.7.r_1_.r_2_), channel_id=1, source_target_pairs={{0,16},{1,17},{2,18},{3,19},{4,20},{5,21},{6,22},{7,23},{8,9},{9,8... | collective-permute-start | bytes 3145736 | tf_op jit(solution)/shard_map/ppermute | solution.py:55
  268.0 18.0 %collective-permute-start.45 = (bf16[16,256,512]{2,1,0:T(8,128)(2,1)}, bf16[16,256,512]{2,1,0:T(8,128)(2,1)}, u32[]{:S(2)}, u32[]{:S(2)}) collective-permute-start(bf16[16,256,512]{2,1,0:T(8,128)(2,1)} %get-tuple-element.169), channel_id=1, source_target_pairs={{0,8},{8,0},{1,9},{9,1},{2,10},{10,2},{3,11},{11,3},{4,12},{12,4},... | collective-permute-start | bytes 12582920 | tf_op jit(solution)/shard_map/ppermute | solution.py:58
  272.4 17.5 %collective-permute-start.44 = (bf16[4,256,512]{2,1,0:T(8,128)(2,1)}, bf16[4,256,512]{2,1,0:T(8,128)(2,1)}, u32[]{:S(2)}, u32[]{:S(2)}) collective-permute-start(bf16[4,256,512]{2,1,0:T(8,128)(2,1)} %get-tuple-element.176), channel_id=1, source_target_pairs={{0,16},{1,17},{2,18},{3,19},{4,20},{5,21},{6,22},{7,23},{8,9},{9,8... | collective-permute-start | bytes 3145736 | tf_op jit(solution)/shard_map/ppermute | solution.py:55
  289.9 17.4 %collective-permute-start.46 = (bf16[4,256,512]{2,1,0:T(8,128)(2,1)}, bf16[4,256,512]{2,1,0:T(8,128)(2,1)S(1)}, u32[]{:S(2)}, u32[]{:S(2)}) collective-permute-start(bf16[4,256,512]{2,1,0:T(8,128)(2,1)} %get-tuple-element.180), channel_id=1, source_target_pairs={{0,16},{1,17},{2,18},{3,19},{4,20},{5,21},{6,22},{7,23},{8,9},{9,8... | collective-permute-start | bytes 3145736 | tf_op jit(solution)/shard_map/ppermute | solution.py:55
  307.3 15.1 %collective-permute-start.47 = (bf16[4,256,512]{2,1,0:T(8,128)(2,1)}, bf16[4,256,512]{2,1,0:T(8,128)(2,1)S(1)}, u32[]{:S(2)}, u32[]{:S(2)}) collective-permute-start(bf16[4,256,512]{2,1,0:T(8,128)(2,1)} %get-tuple-element.182), channel_id=1, source_target_pairs={{0,16},{1,17},{2,18},{3,19},{4,20},{5,21},{6,22},{7,23},{8,9},{9,8... | collective-permute-start | bytes 3145736 | tf_op jit(solution)/shard_map/ppermute | solution.py:55
  322.4 45.4 %collective-permute-start.52 = (bf16[16,1024,128]{2,1,0:T(8,128)(2,1)}, bf16[16,1024,128]{2,1,0:T(8,128)(2,1)}, u32[]{:S(2)}, u32[]{:S(2)}) collective-permute-start(bf16[16,1024,128]{2,1,0:T(8,128)(2,1)} %bitcast.243), channel_id=1, source_target_pairs={{0,8},{8,0},{1,9},{9,1},{2,10},{10,2},{3,11},{11,3},{4,12},{12,4},... | collective-permute-start | bytes 12582920 | tf_op jit(solution)/shard_map/ppermute | solution.py:58
  322.4 25.6 %collective-permute-start.48 = (bf16[4,256,512]{2,1,0:T(8,128)(2,1)S(1)}, bf16[4,256,512]{2,1,0:T(8,128)(2,1)}, u32[]{:S(2)}, u32[]{:S(2)}) collective-permute-start(bf16[4,256,512]{2,1,0:T(8,128)(2,1)S(1)} %copy-done.46), channel_id=1, source_target_pairs={{0,16},{1,17},{2,18},{3,19},{4,20},{5,21},{6,22},{7,23},{8,9},{9,8... | collective-permute-start | bytes 3145736 | tf_op jit(solution)/shard_map/ppermute | solution.py:55
  323.0 25.0 %collective-permute-start.49 = (bf16[4,256,512]{2,1,0:T(8,128)(2,1)S(1)}, bf16[4,256,512]{2,1,0:T(8,128)(2,1)}, u32[]{:S(2)}, u32[]{:S(2)}) collective-permute-start(bf16[4,256,512]{2,1,0:T(8,128)(2,1)S(1)} %add_convert_fusion.5), channel_id=1, source_target_pairs={{0,1},{1,0},{2,3},{3,2},{4,5},{5,4},{6,7},{7,6},{8,24},{9,25},{10,... | collective-permute-start | bytes 3145736 | tf_op jit(solution)/shard_map/ppermute | solution.py:55
  350.4 15.1 %collective-permute-start.50 = (bf16[4,256,512]{2,1,0:T(8,128)(2,1)}, bf16[4,256,512]{2,1,0:T(8,128)(2,1)}, u32[]{:S(2)}, u32[]{:S(2)}) collective-permute-start(bf16[4,256,512]{2,1,0:T(8,128)(2,1)} %add_convert_fusion.4), channel_id=1, source_target_pairs={{0,1},{1,0},{2,3},{3,2},{4,5},{5,4},{6,7},{7,6},{8,24},{9,25},{10,... | collective-permute-start | bytes 3145736 | tf_op jit(solution)/shard_map/ppermute | solution.py:55
  352.1 17.4 %collective-permute-start.51 = (bf16[2,256,512]{2,1,0:T(8,128)(2,1)}, bf16[2,256,512]{2,1,0:T(8,128)(2,1)S(1)}, u32[]{:S(2)}, u32[]{:S(2)}) collective-permute-start(bf16[2,256,512]{2,1,0:T(8,128)(2,1)} %get-tuple-element.195), channel_id=1, source_target_pairs={{0,2},{2,0},{4,6},{6,4},{1,3},{3,1},{5,7},{7,5},{8,10},{10,8},{12,... | collective-permute-start | bytes 1572872 | tf_op jit(solution)/shard_map/ppermute | solution.py:58
  369.5 15.7 %collective-permute-start.53 = (bf16[4,1024,128]{2,1,0:T(8,128)(2,1)S(1)}, bf16[4,1024,128]{2,1,0:T(8,128)(2,1)}, u32[]{:S(2)}, u32[]{:S(2)}) collective-permute-start(bf16[4,1024,128]{2,1,0:T(8,128)(2,1)S(1)} %fusion.1), channel_id=1, source_target_pairs={{0,16},{1,17},{2,18},{3,19},{4,20},{5,21},{6,22},{7,23},{8,9},{9,8... | collective-permute-start | bytes 3145736 | tf_op jit(solution)/shard_map/ppermute | solution.py:55
  370.2 14.0 %collective-permute-start.54 = (bf16[2,256,512]{2,1,0:T(8,128)(2,1)}, bf16[2,256,512]{2,1,0:T(8,128)(2,1)}, u32[]{:S(2)}, u32[]{:S(2)}) collective-permute-start(bf16[2,256,512]{2,1,0:T(8,128)(2,1)} %get-tuple-element.204), channel_id=1, source_target_pairs={{0,2},{2,0},{4,6},{6,4},{1,3},{3,1},{5,7},{7,5},{8,10},{10,8},{12,... | collective-permute-start | bytes 1572872 | tf_op jit(solution)/shard_map/ppermute | solution.py:58
  388.0 25.9 %collective-permute-start.57 = (bf16[4,1024,128]{2,1,0:T(8,128)(2,1)S(1)}, bf16[4,1024,128]{2,1,0:T(8,128)(2,1)S(1)}, u32[]{:S(2)}, u32[]{:S(2)}) collective-permute-start(bf16[4,1024,128]{2,1,0:T(8,128)(2,1)S(1)} %get-tuple-element.207), channel_id=1, source_target_pairs={{0,16},{1,17},{2,18},{3,19},{4,20},{5,21},{6,22},{7,23},{8,9},{9,8... | collective-permute-start | bytes 3145736 | tf_op jit(solution)/shard_map/ppermute | solution.py:55
  388.7 26.9 %collective-permute-start.58 = (bf16[4,1024,128]{2,1,0:T(8,128)(2,1)S(1)}, bf16[4,1024,128]{2,1,0:T(8,128)(2,1)S(1)}, u32[]{:S(2)}, u32[]{:S(2)}) collective-permute-start(bf16[4,1024,128]{2,1,0:T(8,128)(2,1)S(1)} %get-tuple-element.208), channel_id=1, source_target_pairs={{0,1},{1,0},{2,3},{3,2},{4,5},{5,4},{6,7},{7,6},{8,24},{9,25},{10,... | collective-permute-start | bytes 3145736 | tf_op jit(solution)/shard_map/ppermute | solution.py:55
  392.1 30.9 %collective-permute-start.56 = (bf16[8,400,128]{2,1,0:T(8,128)(2,1)S(1)}, bf16[8,400,128]{2,1,0:T(8,128)(2,1)S(1)}, u32[]{:S(2)}, u32[]{:S(2)}) collective-permute-start(bf16[8,400,128]{2,1,0:T(8,128)(2,1)S(1)} %get-tuple-element.273), channel_id=1, source_target_pairs={{0,16},{1,17},{2,18},{3,19},{4,20},{5,21},{6,22},{7,23},{8,9},{9,8... | collective-permute-start | bytes 2457608 | tf_op jit(solution)/shard_map/ppermute | solution.py:55
  392.7 31.1 %collective-permute-start.59 = (bf16[1,256,512]{2,1,0:T(8,128)(2,1)S(1)}, bf16[1,256,512]{2,1,0:T(8,128)(2,1)S(1)}, u32[]{:S(2)}, u32[]{:S(2)}) collective-permute-start(bf16[1,256,512]{2,1,0:T(8,128)(2,1)S(1)} %add_convert_fusion.27), channel_id=1, source_target_pairs={{0,4},{2,6},{4,0},{6,2},{1,5},{3,7},{5,1},{7,3},{8,12},{10,14},{12... | collective-permute-start | bytes 786440 | tf_op jit(solution)/shard_map/ppermute | solution.py:58
  394.5 29.4 %collective-permute-start.60 = (bf16[1,256,512]{2,1,0:T(8,128)(2,1)S(1)}, bf16[1,256,512]{2,1,0:T(8,128)(2,1)S(1)}, u32[]{:S(2)}, u32[]{:S(2)}) collective-permute-start(bf16[1,256,512]{2,1,0:T(8,128)(2,1)S(1)} %add_convert_fusion.26), channel_id=1, source_target_pairs={{0,4},{2,6},{4,0},{6,2},{1,5},{3,7},{5,1},{7,3},{8,12},{10,14},{12... | collective-permute-start | bytes 786440 | tf_op jit(solution)/shard_map/ppermute | solution.py:58
  427.1 40.5 %collective-permute-start.69 = (bf16[8,512,128]{2,1,0:T(8,128)(2,1)S(1)}, bf16[8,512,128]{2,1,0:T(8,128)(2,1)S(1)}, u32[]{:S(2)}, u32[]{:S(2)}) collective-permute-start(bf16[8,512,128]{2,1,0:T(8,128)(2,1)S(1)} %pad_maximum_fusion.7.r_1_.r_2_), channel_id=1, source_target_pairs={{0,8},{8,0},{1,9},{9,1},{2,10},{10,2},{3,11},{11,3},{4,12},{12,4},... | collective-permute-start | bytes 3145736 | tf_op jit(solution)/shard_map/ppermute | solution.py:58
  427.1 40.5 %collective-permute-start.70 = (bf16[8,512,128]{2,1,0:T(8,128)(2,1)}, bf16[8,512,128]{2,1,0:T(8,128)(2,1)}, u32[]{:S(2)}, u32[]{:S(2)}) collective-permute-start(bf16[8,512,128]{2,1,0:T(8,128)(2,1)} %collective-permute-done.42.r_3_.r_4_), channel_id=1, source_target_pairs={{0,8},{8,0},{1,9},{9,1},{2,10},{10,2},{3,11},{11,3},{4,12},{12,4},... | collective-permute-start | bytes 3145736 | tf_op jit(solution)/shard_map/ppermute | solution.py:58
  429.6 15.1 %collective-permute-start.65 = (bf16[2,1024,128]{2,1,0:T(8,128)(2,1)}, bf16[2,1024,128]{2,1,0:T(8,128)(2,1)S(1)}, u32[]{:S(2)}, u32[]{:S(2)}) collective-permute-start(bf16[2,1024,128]{2,1,0:T(8,128)(2,1)} %get-tuple-element.213), channel_id=1, source_target_pairs={{0,2},{2,0},{4,6},{6,4},{1,3},{3,1},{5,7},{7,5},{8,10},{10,8},{12,... | collective-permute-start | bytes 1572872 | tf_op jit(solution)/shard_map/ppermute | solution.py:58
  455.0 40.2 %collective-permute-start.74 = (bf16[1,1024,128]{2,1,0:T(8,128)(2,1)}, bf16[1,1024,128]{2,1,0:T(8,128)(2,1)}, u32[]{:S(2)}, u32[]{:S(2)}) collective-permute-start(bf16[1,1024,128]{2,1,0:T(8,128)(2,1)} %add_convert_fusion.25), channel_id=1, source_target_pairs={{0,4},{2,6},{4,0},{6,2},{1,5},{3,7},{5,1},{7,3},{8,12},{10,14},{12... | collective-permute-start | bytes 786440 | tf_op jit(solution)/shard_map/ppermute | solution.py:58
  (115 other events, 1639.0 us)

commit v4 on v3

--- a/solution.py
+++ b/solution.py
@@ -1257,8 +1257,9 @@
     attn = twice([f1, r1, c1, d1])
     r2, n3, a4 = got = grid.begin([got, u, tv], (far, f2), (near, l3), (z2, bundles[4]))
     f3, p4 = join(l3, n3), stack(4, a4)
-    tu, weighted = grid.gate((tu, weighted), [n2])
-    tu = grid.gate(tu, [weighted])
+    aims = targets[:, 0, 0].reshape(rows, ho)
+    tu, weighted, aims = grid.gate((tu, weighted, aims), [n2])
+    tu = grid.gate(tu, [weighted, aims])
     agg, fold, pa = call(
         pool_kernel,
         "pool",
@@ -1371,7 +1372,7 @@
         act,
         slope,
         head,
-        targets[:, 0, 0].reshape(rows, ho),
+        aims,
         weighted,
         *down,
     )
@@ -1569,23 +1570,21 @@
     a_side = plus(aq[1], f1a)
     u_end = ends(u_half[0], z1u)
     lk, ls = flow["low"]
-    f0a, na, z2d, z2u, got = grid.begin(
-        [f1a, z1u, lk], (far, aq[2]), (near, a_side), (z2, d_end[1]), (z2, u_end[1]), (core, ls)
+    f0a, z2d, z2u, got = grid.begin(
+        [f1a, z1u, lk], (far, aq[2]), (z2, d_end[1]), (z2, u_end[1]), (core, ls)
     )
     lq = [plus(lk[: 2 * NZ], got[: 2 * NZ]), plus(lk[2 * NZ :], got[2 * NZ :])]
     fl = far(lq[1])
     down_sum = (d_end[0].astype(F32) + z2d.astype(F32))[0]
     up_sum = (u_end[0].astype(F32) + z2u.astype(F32))[0]
-    a_half = halves(plus(aq[0], f0a), na)
+    a_line = plus(aq[0], f0a)
     l_side, l_line = plus(lq[0][NZ:], fl[NZ:]), plus(lq[0][:NZ], fl[:NZ])
-    nl, z1a = grid.begin([f0a, na, z2d, z2u, fl], (near, l_side), (z1, a_half[1]))
+    nl, na = grid.begin([f0a, z2d, z2u, fl], (near, l_side), (near, a_side))
     l_half = halves(l_line, nl)
     z1l = z1(l_half[1])
-    s_sum = grid.hop(grid.gate(s_rows.reshape(HEADS, n), nl), ("x", 1), ("c", 1), ("y", 1))
-    a_end, l_end = ends(a_half[0], z1a), ends(l_half[0], z1l)
-    z2l, z2a = grid.begin([z1a, z1l], (z2, l_end[1]), (z2, a_end[1]))
-    s_sum = grid.hop(grid.gate(s_sum, [z1a, z1l]), ("z", 1), ("z", 2))
-    wq_parts = grid.gate(wq_parts, z2l)
+    a_half, l_end = halves(a_line, na), ends(l_half[0], z1l)
+    s_sum = grid.hop(grid.gate(s_rows.reshape(HEADS, n), [f0a, z2d, z2u, fl]), ("c", 1), ("z", 1), ("z", 2))
+    wq_parts = grid.gate(wq_parts, fl)
     wq, wk = call(
         lambda *r: square_kernel(*r, band=band),
         "squares",
@@ -1599,6 +1598,10 @@
         co,
         *twice(wq_parts),
     )
+    z2l, z1a = grid.begin([na, z1l, s_sum, wq, wk], (z2, l_end[1]), (z1, a_half[1]))
+    s_sum = grid.hop(grid.gate(s_sum, z2l), ("x", 1), ("y", 1))
+    a_end = ends(a_half[0], z1a)
+    (z2a,) = grid.begin([z1a], (z2, a_end[1]))
     low_sum, attn_sum = (
         (kept[0].astype(F32) + got.astype(F32))[0] for kept, got in ((l_end, z2l), (a_end, z2a))
     )
@@ -1613,7 +1616,7 @@
     )
     table_own = lax.dynamic_slice_in_dim(table, my_band * band, band, 1)
     g_own = low_sum[band : band + tall]
-    g_low = g_own.astype(BF)
+    g_low = grid.gate(g_own.astype(BF), z1a)
     g_column = grid.collect(grid.collect(g_low, "c"), "y").reshape(n, strip)
     g_line = grid.collect(grid.collect(g_low, "x"), "z").reshape(STRIPS, tall, strip)
     g_line = jnp.transpose(g_line, (1, 0, 2)).reshape(tall, width)

time: 535 us -> 530 us (level)
  waiting for transfers between devices: 159 us -> 147 us
  other arithmetic: 70.8 us -> 77.4 us
    ppermute x25, waiting for transfers between devices: 66.3 us -> 50.1 us  [permute(): return lax.ppermute(value, AXES, self.flat(move))]
    convert_element_type x19 -> x18, other arithmetic: 31.1 us -> 32.2 us  [plus(): return (left.astype(F32) + right.astype(F32)).astype(BF)]
  transfers between devices with their start and end apart: 86 -> 86, of which waited for: 44 -> 47; matrix products, arithmetic and copies ran while one was open for 15% -> 16% of each run, Pallas kernels for 31% -> 32%
where the time goes in v4:
time: 530 us; the launch traced here: 523 us
  Pallas kernels  166 us (31%)
  waiting for transfers between devices  147 us (28%)
  starting transfers between devices  87.7 us (17%)
  other arithmetic  77.4 us (15%)
  local copies, waits for them, and re-layouts  22.7 us (4%)
  between operations  13.6 us (3%)
  matrix products  8.64 us (2%)
    pallas_call x16, Pallas kernels, call(): pl.pallas_call(kernel, name=name, grid=grid, in_specs=in_specs, out_shape...  166 us
    ppermute x61, waiting for transfers between devices, swap(): lax.ppermute(value, axis, [(i, i ^ bit) for i in range(self.sizes[axis])])  96.9 us
    ppermute x61, starting transfers between devices, swap(): lax.ppermute(value, axis, [(i, i ^ bit) for i in range(self.sizes[axis])])  59.9 us
    ppermute x25, waiting for transfers between devices, permute(): return lax.ppermute(value, AXES, self.flat(move))  50.1 us
    convert_element_type x18, other arithmetic, plus(): return (left.astype(F32) + right.astype(F32)).astype(BF)  32.2 us
    ppermute x25, starting transfers between devices, permute(): return lax.ppermute(value, AXES, self.flat(move))  27.8 us
  transfers between devices with their start and end apart: 86, of which 47 were waited for; matrix products, arithmetic and copies ran while one was open for 16% of the time, Pallas kernels for 32%

profile of v4, /device:TPU:0, one launch (start us, length us, event | category | flops | bytes accessed | tf_op | source)
XLA Modules:
  0.0 523.4 jit_solution(16546475765211228303)
XLA Ops:
  2.2 2.6 collective-permute-start.8
  7.8 3.1 collective-permute-start
  13.0 5.7 %collective-permute-done = bf16[656,128]{1,0:T(8,128)(2,1)S(1)} collective-permute-done((bf16[656,128]{1,0:T(8,128)(2,1)S(1)}, bf16[656,128]{1,0:T(8,128)(2,1)S(1)}, u32[]{:S(2)}, u32[]{:S(2)}) %collective-permute-start) | collective-permute-done | bytes 167968 | tf_op jit(solution)/shard_map/ppermute | solution.py:58
  19.7 2.6 collective-permute-done.1
  45.8 9.4 %collective-permute-done.10 = bf16[1024,128]{1,0:T(8,128)(2,1)S(1)} collective-permute-done((bf16[1024,128]{1,0:T(8,128)(2,1)S(1)}, bf16[1024,128]{1,0:T(8,128)(2,1)S(1)}, u32[]{:S(2)}, u32[]{:S(2)}) %collective-permute-start.10) | collective-permute-done | bytes 262176 | tf_op jit(solution)/shard_map/ppermute | solution.py:58
  61.1 3.5 collective-permute-done.16
  64.6 4.2 collective-permute-start.17
  70.9 3.3 collective-permute-done.18
  79.6 11.7 %collective-permute-done.21 = bf16[256,512]{1,0:T(8,128)(2,1)S(1)} collective-permute-done((bf16[256,512]{1,0:T(8,128)(2,1)S(1)}, bf16[256,512]{1,0:T(8,128)(2,1)S(1)}, u32[]{:S(2)}, u32[]{:S(2)}) %collective-permute-start.21) | collective-permute-done | bytes 262176 | tf_op jit(solution)/shard_map/ppermute | solution.py:58
  91.4 10.8 %collective-permute-done.20 = bf16[4,1024,128]{2,1,0:T(8,128)(2,1)S(1)} collective-permute-done((bf16[4,1024,128]{2,1,0:T(8,128)(2,1)S(1)}, bf16[4,1024,128]{2,1,0:T(8,128)(2,1)S(1)}, u32[]{:S(2)}, u32[]{:S(2)}) %collective-permute-start.20) | collective-permute-done | bytes 1048608 | tf_op jit(solution)/shard_map/ppermute | solution.py:55
  108.7 9.3 %collective-permute-done.25 = f32[1024,16]{0,1:T(8,128)S(1)} collective-permute-done((f32[1024,16]{0,1:T(8,128)S(1)}, f32[1024,16]{0,1:T(8,128)S(1)}, u32[]{:S(2)}, u32[]{:S(2)}) %collective-permute-start.25) | collective-permute-done | bytes 65568 | tf_op jit(solution)/shard_map/ppermute | solution.py:58
  119.2 4.2 collective-permute-done.27
  124.3 6.6 %collective-permute-done.26.r_7_.r_8_.r_15_.r_16_.r_6_ = bf16[8,1024,128]{2,1,0:T(8,128)(2,1)S(1)} collective-permute-done((bf16[8,1024,128]{2,1,0:T(8,128)(2,1)S(1)}, bf16[8,1024,128]{2,1,0:T(8,128)(2,1)S(1)}, u32[]{:S(2)}, u32[]{:S(2)}) %collective-permute-start.26) | collective-permute-done | bytes 2097184 | tf_op jit(solution)/shard_map/ppermute | solution.py:55
  133.7 6.1 %assemble.1 = (bf16[384,1024]{1,0:T(8,128)(2,1)}, f32[192,1024]{1,0:T(8,128)}, bf16[1024,1024]{1,0:T(8,128)(2,1)}) custom-call(s32[4]{0:T(128)} %pad_add_fusion.r_0_, bf16[8,656,128]{2,1,0:T(8,128)(2,1)} %copy-done.3, bf16[8,656,128]{2,1,0:T(8,128)(2,1)} %copy-done.3, bf16[8,656,128]{2,1,0:T(8,128)(2,1)} %copy-done.4, bf16[8,656,128]{2,1,0:T(8,128)(2,1)} %copy-done.4, ...), custom_call_target="tpu_custom_call" | custom-call | bytes 8388608 | tf_op jit(solution)/shard_map/assemble/pallas_call | solution.py:643
  139.8 4.9 table_values.1.tv_ref
  146.8 2.8 pad_maximum_fusion.1.r_2_.r_3_.r_5_.r_6_
  163.1 12.9 %pool.1 = (bf16[256,1024]{1,0:T(8,128)(2,1)}, bf16[16,256,384]{2,1,0:T(8,128)(2,1)}, f32[16,256,128]{2,1,0:T(8,128)}) custom-call(bf16[256,384]{1,0:T(8,128)(2,1)} %fusion.8.x_ref, bf16[384,128]{1,0:T(8,128)(2,1)} %constant.157.clone.e_ref, f32[384,128]{1,0:T(8,128)} %pad.10.tu_ref, bf16[384,1024]{1,0:T(8,128)(2,1)} %table_values.1.tv_ref), custom_call_target="tpu_custom_call" | custom-call | flops 2415919104 | bytes 8388608 | tf_op jit(solution)/shard_map/pool/pallas_call | solution.py:643
  176.0 5.2 %enter.1 = (f32[256,1024]{1,0:T(8,128)}, bf16[256,1024]{1,0:T(8,128)(2,1)}) custom-call(s32[4]{0:T(128)} %pad_add_fusion.r_0_, bf16[256,1024]{1,0:T(8,128)(2,1)} %get-tuple-element.141.r_1_.r_2_, f32[2,1024]{1,0:T(2,128)} %fusion.49.r_2_, f32[1,1024]{1,0:T(1,128)} %get-tuple-element.285.r_3_.r_4_, bf16[8,656,128]{2,1,0:T(8,128)(2,1)} %copy-done.3, ...), custom_call_target="tpu_custom_call" | custom-call | flops 536870912 | bytes 4194304 | tf_op jit(solution)/shard_map/enter/pallas_call | solution.py:643
  181.3 3.9 collective-permute-done.33
  190.8 19.3 %attend.1 = (bf16[256,3072]{1,0:T(8,128)(2,1)}, f32[16,2,128,128]{3,2,1,0:T(8,128)}, bf16[256,1024]{1,0:T(8,128)(2,1)}, f32[256,1024]{1,0:T(8,128)}, bf16[256,1024]{1,0:T(8,128)(2,1)}) custom-call(s32[4]{0:T(128)} %pad_add_fusion.r_0_, s32[2]{0:T(128)} %bitcast.239, f32[256,1024]{1,0:T(8,128)} %get-tuple-element.142.r_2_.r_3_, ...), custom_call_target="tpu_custom_call" | custom-call | flops 2415919104 | bytes 16777216 | tf_op jit(solution)/shard_map/attend/pallas_call | solution.py:643
  211.0 4.3 collective-permute-done.37.r_10_.r_11_
  216.4 10.5 %up.1 = (bf16[256,4096]{1,0:T(8,128)(2,1)}, bf16[256,4096]{1,0:T(8,128)(2,1)}) custom-call(s32[4]{0:T(128)} %pad_add_fusion.r_0_, bf16[256,1024]{1,0:T(8,128)(2,1)} %get-tuple-element.147.r_1_, bf16[8,256,512]{2,1,0:T(8,128)(2,1)} %pad_maximum_fusion.1.r_2_.r_3_.r_5_.r_6_, bf16[8,256,512]{2,1,0:T(8,128)(2,1)} %pad_maximum_fusion.1.r_2_.r_3_.r_5_.r_6_, ...), custom_call_target="tpu_custom_call" | custom-call | flops 2147483648 | bytes 16777216 | tf_op jit(solution)/shard_map/up/pallas_call | solution.py:643
  233.1 20.0 %down.1 = (f32[8,128]{1,0:T(8,128)}, f32[256,1024]{1,0:T(8,128)}, bf16[256,1024]{1,0:T(8,128)(2,1)}, f32[192,1024]{1,0:T(8,128)}, bf16[256,4096]{1,0:T(8,128)(2,1)}) custom-call(s32[4]{0:T(128)} %pad_add_fusion.r_0_, f32[1]{0:T(128)} %slice.357.r_1_, f32[256,1024]{1,0:T(8,128)} %get-tuple-element.146.r_2_, bf16[256,4096]{1,0:T(8,128)(2,1)} %get-tuple-element.158.r_3_.r_2_, ...), custom_call_target="tpu_custom_call" | custom-call | flops 4294967296 | bytes 33554432 | tf_op jit(solution)/shard_map/down/pallas_call | solution.py:643
  253.1 6.6 %down_grad.1 = (bf16[16,256,512]{2,1,0:T(8,128)(2,1)}, bf16[16,256,512]{2,1,0:T(8,128)(2,1)}) custom-call(s32[4]{0:T(128)} %pad_add_fusion.r_0_, bf16[256,1024]{1,0:T(8,128)(2,1)} %get-tuple-element.167.r_1_, bf16[256,4096]{1,0:T(8,128)(2,1)} %get-tuple-element.158.r_3_.r_2_), custom_call_target="tpu_custom_call" | custom-call | flops 2147483648 | bytes 12582912 | tf_op jit(solution)/shard_map/down_grad/pallas_call | solution.py:643
  259.7 6.8 %up_grad.1 = (bf16[16,256,512]{2,1,0:T(8,128)(2,1)}, bf16[16,256,512]{2,1,0:T(8,128)(2,1)}) custom-call(s32[4]{0:T(128)} %pad_add_fusion.r_0_, bf16[256,1024]{1,0:T(8,128)(2,1)} %get-tuple-element.147.r_1_, bf16[256,4096]{1,0:T(8,128)(2,1)} %get-tuple-element.175.r_2_.r_1_), custom_call_target="tpu_custom_call" | custom-call | flops 2147483648 | bytes 12582912 | tf_op jit(solution)/shard_map/up_grad/pallas_call | solution.py:643
  267.2 3.7 add_convert_fusion.10
  271.5 13.0 %up_back.1 = (f32[256,1024]{1,0:T(8,128)}, bf16[256,1024]{1,0:T(8,128)(2,1)}, f32[1,1024]{1,0:T(1,128)}) custom-call(s32[4]{0:T(128)} %pad_add_fusion.r_0_, bf16[256,4096]{1,0:T(8,128)(2,1)} %get-tuple-element.175.r_2_.r_1_, f32[256,1024]{1,0:T(8,128)} %get-tuple-element.146.r_2_, f32[1,1024]{1,0:T(1,128)} %get-tuple-element.284.r_4_.r_3_, ...), custom_call_target="tpu_custom_call" | custom-call | flops 2147483648 | bytes 16777216 | tf_op jit(solution)/shard_map/up_back/pallas_call | solution.py:643
  284.5 3.9 add_convert_fusion.6
  290.0 14.3 %attend_back.1.r_3_.r_2_ = bf16[256,3072]{1,0:T(8,128)(2,1)} custom-call(s32[4]{0:T(128)} %pad_add_fusion.r_0_, bf16[256,1024]{1,0:T(8,128)(2,1)} %get-tuple-element.180.r_1_.r_4_, bf16[256,3072]{1,0:T(8,128)(2,1)} %get-tuple-element.181.r_2_, f32[16,2,128,128]{3,2,1,0:T(8,128)} %get-tuple-element.182.r_3_, bf16[8,1024,128]{2,1,0:T(8,128)(2,1)} %copy-done, ...), custom_call_target="tpu_custom_call" | custom-call | flops 939524096 | bytes 4194304 | tf_op jit(solution)/shard_map/attend_back/pallas_call | solution.py:643
  306.5 7.3 %attention_grad.1 = (bf16[4,4,1024,128]{3,2,1,0:T(8,128)(2,1)}, bf16[4,4,1024,128]{3,2,1,0:T(8,128)(2,1)}) custom-call(s32[4]{0:T(128)} %pad_add_fusion.r_0_, bf16[256,1024]{1,0:T(8,128)(2,1)} %get-tuple-element.143.r_3_.r_1_, bf16[256,1024]{1,0:T(8,128)(2,1)} %get-tuple-element.186.r_2_, bf16[256,3072]{1,0:T(8,128)(2,1)} %attend_back.1.r_3_.r_2_, ...), custom_call_target="tpu_custom_call" | custom-call | flops 2147483648 | bytes 8388608 | tf_op jit(solution)/shard_map/attention_grad/pallas_call | solution.py:643
  313.8 7.1 %collective-permute-done.47 = bf16[4,256,512]{2,1,0:T(8,128)(2,1)S(1)} collective-permute-done((bf16[4,256,512]{2,1,0:T(8,128)(2,1)}, bf16[4,256,512]{2,1,0:T(8,128)(2,1)S(1)}, u32[]{:S(2)}, u32[]{:S(2)}) %collective-permute-start.47) | collective-permute-done | bytes 1048608 | tf_op jit(solution)/shard_map/ppermute | solution.py:55
  324.5 17.0 %leave.1 = (bf16[256,1024]{1,0:T(8,128)(2,1)}, f32[1,1024]{1,0:T(1,128)}, f32[2,1024]{1,0:T(2,128)}, bf16[256,1024]{1,0:T(8,128)(2,1)}) custom-call(s32[4]{0:T(128)} %pad_add_fusion.r_0_, f32[256,1024]{1,0:T(8,128)} %get-tuple-element.177.r_1_, bf16[256,3072]{1,0:T(8,128)(2,1)} %attend_back.1.r_3_.r_2_, f32[256,1024]{1,0:T(8,128)} %get-tuple-element.142.r_2_.r_3_, ...), custom_call_target="tpu_custom_call" | custom-call | flops 2147483648 | bytes 8388608 | tf_op jit(solution)/shard_map/leave/pallas_call | solution.py:643
  342.8 3.6 collective-permute-done.48
  350.8 11.5 %pool_back.1 = (f32[384,1024]{1,0:T(8,128)}, f32[4,4,384]{2,1,0:T(4,128)}) custom-call(bf16[256,384]{1,0:T(8,128)(2,1)} %fusion.8.x_ref, bf16[384,128]{1,0:T(8,128)(2,1)} %constant.157.clone.e_ref, bf16[384,1024]{1,0:T(8,128)(2,1)} %table_values.1.tv_ref, bf16[16,256,384]{2,1,0:T(8,128)(2,1)} %get-tuple-element.164.a_ref, ...), custom_call_target="tpu_custom_call" | custom-call | flops 2818572288 | bytes 8388608 | tf_op jit(solution)/shard_map/pool_back/pallas_call | solution.py:643
  366.3 3.3 fusion.2
  375.4 5.2 low_grad.1
  380.5 4.4 collective-permute-done.53
  392.8 7.5 %collective-permute-done.55 = bf16[4,1024,128]{2,1,0:T(8,128)(2,1)S(1)} collective-permute-done((bf16[4,1024,128]{2,1,0:T(8,128)(2,1)}, bf16[4,1024,128]{2,1,0:T(8,128)(2,1)S(1)}, u32[]{:S(2)}, u32[]{:S(2)}) %collective-permute-start.55) | collective-permute-done | bytes 1048608 | tf_op jit(solution)/shard_map/ppermute | solution.py:55
  401.9 4.0 add_convert_fusion
  405.9 3.2 collective-permute-done.59
  410.1 2.7 collective-permute-done.56
  412.8 5.2 collective-permute-done.57
  433.0 2.6 multiply_reduce_fusion.1
  437.6 5.8 %squares.1 = (bf16[1024,1024]{1,0:T(8,128)(2,1)}, bf16[1024,1024]{1,0:T(8,128)(2,1)}) custom-call(s32[4]{0:T(128)} %pad_add_fusion.r_0_, bf16[8,512,128]{2,1,0:T(8,128)(2,1)} %copy-done.10, bf16[8,512,128]{2,1,0:T(8,128)(2,1)} %copy-done.10, bf16[8,512,128]{2,1,0:T(8,128)(2,1)} %collective-permute-done.42.r_3_.r_4_, ...), custom_call_target="tpu_custom_call" | custom-call | bytes 1048576 | tf_op jit(solution)/shard_map/squares/pallas_call | solution.py:643
  452.6 2.7 collective-permute-done.69
  484.2 4.4 collective-permute-done.74
  504.0 2.7 collective-permute-start.83
  514.0 4.5 fusion.76
  (430 shorter events, 190.0 us)
Async XLA Ops:
  1.6 36.1 %collective-permute-start.6 = (bf16[2,128,48]{1,2,0:T(8,128)(2,1)S(1)}, bf16[2,128,48]{1,2,0:T(8,128)(2,1)S(1)}, u32[]{:S(2)}, u32[]{:S(2)}) collective-permute-start(bf16[2,128,48]{1,2,0:T(8,128)(2,1)S(1)} %get-tuple-element.299), channel_id=1, source_target_pairs={{0,8},{1,9},{2,10},{3,11},{4,12},{5,13},{6,14},{7,15},{8,0},{9,1},... | collective-permute-start | bytes 73736 | tf_op jit(solution)/shard_map/ppermute | solution.py:55
  2.2 32.1 %collective-permute-start.8 = (bf16[2,128,48]{1,2,0:T(8,128)(2,1)S(1)}, bf16[2,128,48]{1,2,0:T(8,128)(2,1)S(1)}, u32[]{:S(2)}, u32[]{:S(2)}) collective-permute-start(bf16[2,128,48]{1,2,0:T(8,128)(2,1)S(1)} %get-tuple-element.301), channel_id=1, source_target_pairs={{0,24},{1,25},{2,26},{3,27},{4,28},{5,29},{6,30},{7,31},{8,16},{9,... | collective-permute-start | bytes 73736 | tf_op jit(solution)/shard_map/ppermute | solution.py:55
  4.8 27.3 %collective-permute-start.7 = (bf16[2,128,48]{1,2,0:T(8,128)(2,1)S(1)}, bf16[2,128,48]{1,2,0:T(8,128)(2,1)S(1)}, u32[]{:S(2)}, u32[]{:S(2)}) collective-permute-start(bf16[2,128,48]{1,2,0:T(8,128)(2,1)S(1)} %get-tuple-element.302), channel_id=1, source_target_pairs={{0,16},{1,17},{2,18},{3,19},{4,20},{5,21},{6,22},{7,23},{8,24},{9,... | collective-permute-start | bytes 73736 | tf_op jit(solution)/shard_map/ppermute | solution.py:55
  39.8 15.4 %collective-permute-start.10 = (bf16[1024,128]{1,0:T(8,128)(2,1)S(1)}, bf16[1024,128]{1,0:T(8,128)(2,1)S(1)}, u32[]{:S(2)}, u32[]{:S(2)}) collective-permute-start(bf16[1024,128]{1,0:T(8,128)(2,1)S(1)} %bitcast.203), channel_id=1, source_target_pairs={{0,4},{2,6},{4,0},{6,2},{1,5},{3,7},{5,1},{7,3},{8,12},{10,14},{12... | collective-permute-start | bytes 786440 | tf_op jit(solution)/shard_map/ppermute | solution.py:58
  41.9 14.9 %collective-permute-start.9 = (bf16[2,656,128]{2,1,0:T(8,128)(2,1)S(1)}, bf16[2,656,128]{2,1,0:T(8,128)(2,1)S(1)}, u32[]{:S(2)}, u32[]{:S(2)}) collective-permute-start(bf16[2,656,128]{2,1,0:T(8,128)(2,1)S(1)} %pad_maximum_fusion.13), channel_id=1, source_target_pairs={{0,2},{2,0},{4,6},{6,4},{1,3},{3,1},{5,7},{7,5},{8,10},{10,8},{12,... | collective-permute-start | bytes 1007624 | tf_op jit(solution)/shard_map/ppermute | solution.py:58
  44.2 15.3 %collective-permute-start.15 = (f32[1024,16]{0,1:T(8,128)S(1)}, f32[1024,16]{0,1:T(8,128)S(1)}, u32[]{:S(2)}, u32[]{:S(2)}) collective-permute-start(f32[1024,16]{0,1:T(8,128)S(1)} %get-tuple-element.313), channel_id=1, source_target_pairs={{0,1},{1,0},{2,3},{3,2},{4,5},{5,4},{6,7},{7,6},{8,9},{9,8},{10,11... | collective-permute-start | bytes 196616 | tf_op jit(solution)/shard_map/ppermute | solution.py:58
  56.9 17.3 %collective-permute-start.14 = (bf16[2,1024,128]{2,1,0:T(8,128)(2,1)S(1)}, bf16[2,1024,128]{2,1,0:T(8,128)(2,1)S(1)}, u32[]{:S(2)}, u32[]{:S(2)}) collective-permute-start(bf16[2,1024,128]{2,1,0:T(8,128)(2,1)S(1)} %pad_maximum_fusion.9), channel_id=1, source_target_pairs={{0,2},{2,0},{4,6},{6,4},{1,3},{3,1},{5,7},{7,5},{8,10},{10,8},{12,... | collective-permute-start | bytes 1572872 | tf_op jit(solution)/shard_map/ppermute | solution.py:58
  58.0 16.3 %collective-permute-start.13 = (bf16[4,656,128]{2,1,0:T(8,128)(2,1)S(1)}, bf16[4,656,128]{2,1,0:T(8,128)(2,1)S(1)}, u32[]{:S(2)}, u32[]{:S(2)}) collective-permute-start(bf16[4,656,128]{2,1,0:T(8,128)(2,1)S(1)} %pad_maximum_fusion.8), channel_id=1, source_target_pairs={{0,1},{1,0},{2,3},{3,2},{4,5},{5,4},{6,7},{7,6},{8,24},{9,25},{10,... | collective-permute-start | bytes 2015240 | tf_op jit(solution)/shard_map/ppermute | solution.py:55
  74.5 30.2 %collective-permute-start.19 = (bf16[8,656,128]{2,1,0:T(8,128)(2,1)S(1)}, bf16[8,656,128]{2,1,0:T(8,128)(2,1)S(1)}, u32[]{:S(2)}, u32[]{:S(2)}) collective-permute-start(bf16[8,656,128]{2,1,0:T(8,128)(2,1)S(1)} %pad_maximum_fusion.3.r_1_.r_2_.r_3_.r_4_.r_5_.r_13_.r_14_), channel_id=1, source_target_pairs={{0,16},{1,17},{2,18},{3,19},{4,20},{5,21},{6,22},{7,23},{8,9},{9,8... | collective-permute-start | bytes 4030472 | tf_op jit(solution)/shard_map/ppermute | solution.py:55
  76.1 26.1 %collective-permute-start.20 = (bf16[4,1024,128]{2,1,0:T(8,128)(2,1)S(1)}, bf16[4,1024,128]{2,1,0:T(8,128)(2,1)S(1)}, u32[]{:S(2)}, u32[]{:S(2)}) collective-permute-start(bf16[4,1024,128]{2,1,0:T(8,128)(2,1)S(1)} %pad_maximum_fusion.4), channel_id=1, source_target_pairs={{0,1},{1,0},{2,3},{3,2},{4,5},{5,4},{6,7},{7,6},{8,24},{9,25},{10,... | collective-permute-start | bytes 3145736 | tf_op jit(solution)/shard_map/ppermute | solution.py:55
  104.7 26.1 %collective-permute-start.26 = (bf16[8,1024,128]{2,1,0:T(8,128)(2,1)S(1)}, bf16[8,1024,128]{2,1,0:T(8,128)(2,1)S(1)}, u32[]{:S(2)}, u32[]{:S(2)}) collective-permute-start(bf16[8,1024,128]{2,1,0:T(8,128)(2,1)S(1)} %pad_maximum_fusion.r_5_.r_6_.r_13_.r_14_.r_4_), channel_id=1, source_target_pairs={{0,16},{1,17},{2,18},{3,19},{4,20},{5,21},{6,22},{7,23},{8,9},{9,8... | collective-permute-start | bytes 6291464 | tf_op jit(solution)/shard_map/ppermute | solution.py:55
  105.3 18.9 %collective-permute-start.23 = (bf16[8,656,128]{2,1,0:T(8,128)(2,1)S(1)}, bf16[8,656,128]{2,1,0:T(8,128)(2,1)S(1)}, u32[]{:S(2)}, u32[]{:S(2)}) collective-permute-start(bf16[8,656,128]{2,1,0:T(8,128)(2,1)S(1)} %pad_maximum_fusion.3.r_1_.r_2_.r_3_.r_4_.r_5_.r_13_.r_14_), channel_id=1, source_target_pairs={{0,8},{8,0},{1,9},{9,1},{2,10},{10,2},{3,11},{11,3},{4,12},{12,4},... | collective-permute-start | bytes 4030472 | tf_op jit(solution)/shard_map/ppermute | solution.py:58
  105.3 18.9 %collective-permute-start.24 = (bf16[8,656,128]{2,1,0:T(8,128)(2,1)S(1)}, bf16[8,656,128]{2,1,0:T(8,128)(2,1)S(1)}, u32[]{:S(2)}, u32[]{:S(2)}) collective-permute-start(bf16[8,656,128]{2,1,0:T(8,128)(2,1)S(1)} %collective-permute-done.19.r_3_.r_4_.r_5_.r_6_.r_7_.r_15_.r_16_), channel_id=1, source_target_pairs={{0,8},{8,0},{1,9},{9,1},{2,10},{10,2},{3,11},{11,3},{4,12},{12,4},... | collective-permute-start | bytes 4030472 | tf_op jit(solution)/shard_map/ppermute | solution.py:58
  107.6 15.7 %collective-permute-start.27 = (bf16[256,512]{1,0:T(8,128)(2,1)S(1)}, bf16[256,512]{1,0:T(8,128)(2,1)S(1)}, u32[]{:S(2)}, u32[]{:S(2)}) collective-permute-start(bf16[256,512]{1,0:T(8,128)(2,1)S(1)} %get-tuple-element.135), channel_id=1, source_target_pairs={{0,4},{2,6},{4,0},{6,2},{1,5},{3,7},{5,1},{7,3},{8,12},{10,14},{12... | collective-permute-start | bytes 786440 | tf_op jit(solution)/shard_map/ppermute | solution.py:58
  130.8 18.8 %collective-permute-start.29 = (bf16[8,1024,128]{2,1,0:T(8,128)(2,1)S(1)}, bf16[8,1024,128]{2,1,0:T(8,128)(2,1)S(1)}, u32[]{:S(2)}, u32[]{:S(2)}) collective-permute-start(bf16[8,1024,128]{2,1,0:T(8,128)(2,1)S(1)} %pad_maximum_fusion.r_5_.r_6_.r_13_.r_14_.r_4_), channel_id=1, source_target_pairs={{0,8},{8,0},{1,9},{9,1},{2,10},{10,2},{3,11},{11,3},{4,12},{12,4},... | collective-permute-start | bytes 6291464 | tf_op jit(solution)/shard_map/ppermute | solution.py:58
  130.8 18.8 %collective-permute-start.30 = (bf16[8,1024,128]{2,1,0:T(8,128)(2,1)S(1)}, bf16[8,1024,128]{2,1,0:T(8,128)(2,1)}, u32[]{:S(2)}, u32[]{:S(2)}) collective-permute-start(bf16[8,1024,128]{2,1,0:T(8,128)(2,1)S(1)} %collective-permute-done.26.r_7_.r_8_.r_15_.r_16_.r_6_), channel_id=1, source_target_pairs={{0,8},{8,0},{1,9},{9,1},{2,10},{10,2},{3,11},{11,3},{4,12},{12,4},... | collective-permute-start | bytes 6291464 | tf_op jit(solution)/shard_map/ppermute | solution.py:58
  131.3 15.5 %collective-permute-start.28 = (bf16[4,256,512]{2,1,0:T(8,128)(2,1)}, bf16[4,256,512]{2,1,0:T(8,128)(2,1)}, u32[]{:S(2)}, u32[]{:S(2)}) collective-permute-start(bf16[4,256,512]{2,1,0:T(8,128)(2,1)} %pad_maximum_fusion.5), channel_id=1, source_target_pairs={{0,1},{1,0},{2,3},{3,2},{4,5},{5,4},{6,7},{7,6},{8,24},{9,25},{10,... | collective-permute-start | bytes 3145736 | tf_op jit(solution)/shard_map/ppermute | solution.py:55
  131.9 13.8 %collective-permute-start.31 = (bf16[2,256,512]{2,1,0:T(8,128)(2,1)}, bf16[2,256,512]{2,1,0:T(8,128)(2,1)S(1)}, u32[]{:S(2)}, u32[]{:S(2)}) collective-permute-start(bf16[2,256,512]{2,1,0:T(8,128)(2,1)} %pad_maximum_fusion.11), channel_id=1, source_target_pairs={{0,2},{2,0},{4,6},{6,4},{1,3},{3,1},{5,7},{7,5},{8,10},{10,8},{12,... | collective-permute-start | bytes 1572872 | tf_op jit(solution)/shard_map/ppermute | solution.py:58
  151.0 37.5 %collective-permute-start.32 = (bf16[8,256,512]{2,1,0:T(8,128)(2,1)}, bf16[8,256,512]{2,1,0:T(8,128)(2,1)S(1)}, u32[]{:S(2)}, u32[]{:S(2)}) collective-permute-start(bf16[8,256,512]{2,1,0:T(8,128)(2,1)} %pad_maximum_fusion.1.r_2_.r_3_.r_5_.r_6_), channel_id=1, source_target_pairs={{0,16},{1,17},{2,18},{3,19},{4,20},{5,21},{6,22},{7,23},{8,9},{9,8... | collective-permute-start | bytes 6291464 | tf_op jit(solution)/shard_map/ppermute | solution.py:55
  158.8 26.4 %collective-permute-start.33 = (bf16[4,256,512]{2,1,0:T(8,128)(2,1)}, bf16[4,256,512]{2,1,0:T(8,128)(2,1)S(1)}, u32[]{:S(2)}, u32[]{:S(2)}) collective-permute-start(bf16[4,256,512]{2,1,0:T(8,128)(2,1)} %pad_maximum_fusion.6), channel_id=1, source_target_pairs={{0,1},{1,0},{2,3},{3,2},{4,5},{5,4},{6,7},{7,6},{8,24},{9,25},{10,... | collective-permute-start | bytes 3145736 | tf_op jit(solution)/shard_map/ppermute | solution.py:55
  161.8 19.4 %collective-permute-start.34 = (bf16[512,128]{1,0:T(8,128)(2,1)S(1)}, bf16[512,128]{1,0:T(8,128)(2,1)S(1)}, u32[]{:S(2)}, u32[]{:S(2)}) collective-permute-start(bf16[512,128]{1,0:T(8,128)(2,1)S(1)} %bitcast.217), channel_id=1, source_target_pairs={{0,4},{2,6},{4,0},{6,2},{1,5},{3,7},{5,1},{7,3},{8,12},{10,14},{12... | collective-permute-start | bytes 393224 | tf_op jit(solution)/shard_map/ppermute | solution.py:58
  188.5 22.5 %collective-permute-start.35 = (bf16[8,256,512]{2,1,0:T(8,128)(2,1)}, bf16[8,256,512]{2,1,0:T(8,128)(2,1)S(1)}, u32[]{:S(2)}, u32[]{:S(2)}) collective-permute-start(bf16[8,256,512]{2,1,0:T(8,128)(2,1)} %pad_maximum_fusion.1.r_2_.r_3_.r_5_.r_6_), channel_id=1, source_target_pairs={{0,8},{8,0},{1,9},{9,1},{2,10},{10,2},{3,11},{11,3},{4,12},{12,4},... | collective-permute-start | bytes 6291464 | tf_op jit(solution)/shard_map/ppermute | solution.py:58
  188.5 22.5 %collective-permute-start.36 = (bf16[8,256,512]{2,1,0:T(8,128)(2,1)S(1)}, bf16[8,256,512]{2,1,0:T(8,128)(2,1)S(1)}, u32[]{:S(2)}, u32[]{:S(2)}) collective-permute-start(bf16[8,256,512]{2,1,0:T(8,128)(2,1)S(1)} %collective-permute-done.32.r_4_.r_5_.r_7_.r_8_), channel_id=1, source_target_pairs={{0,8},{8,0},{1,9},{9,1},{2,10},{10,2},{3,11},{11,3},{4,12},{12,4},... | collective-permute-start | bytes 6291464 | tf_op jit(solution)/shard_map/ppermute | solution.py:58
  189.0 26.4 %collective-permute-start.37 = (bf16[8,256,512]{2,1,0:T(8,128)(2,1)}, bf16[8,256,512]{2,1,0:T(8,128)(2,1)}, u32[]{:S(2)}, u32[]{:S(2)}) collective-permute-start(bf16[8,256,512]{2,1,0:T(8,128)(2,1)} %pad_maximum_fusion.2.r_8_.r_9_), channel_id=1, source_target_pairs={{0,16},{1,17},{2,18},{3,19},{4,20},{5,21},{6,22},{7,23},{8,9},{9,8... | collective-permute-start | bytes 6291464 | tf_op jit(solution)/shard_map/ppermute | solution.py:55
  190.5 19.6 %collective-permute-start.38 = (bf16[2,512,128]{2,1,0:T(8,128)(2,1)S(1)}, bf16[2,512,128]{2,1,0:T(8,128)(2,1)S(1)}, u32[]{:S(2)}, u32[]{:S(2)}) collective-permute-start(bf16[2,512,128]{2,1,0:T(8,128)(2,1)S(1)} %pad_maximum_fusion.14), channel_id=1, source_target_pairs={{0,2},{2,0},{4,6},{6,4},{1,3},{3,1},{5,7},{7,5},{8,10},{10,8},{12,... | collective-permute-start | bytes 786440 | tf_op jit(solution)/shard_map/ppermute | solution.py:58
  215.3 16.4 %collective-permute-start.40 = (bf16[8,256,512]{2,1,0:T(8,128)(2,1)}, bf16[8,256,512]{2,1,0:T(8,128)(2,1)S(1)}, u32[]{:S(2)}, u32[]{:S(2)}) collective-permute-start(bf16[8,256,512]{2,1,0:T(8,128)(2,1)} %pad_maximum_fusion.2.r_8_.r_9_), channel_id=1, source_target_pairs={{0,8},{8,0},{1,9},{9,1},{2,10},{10,2},{3,11},{11,3},{4,12},{12,4},... | collective-permute-start | bytes 6291464 | tf_op jit(solution)/shard_map/ppermute | solution.py:58
  215.3 16.4 %collective-permute-start.41 = (bf16[8,256,512]{2,1,0:T(8,128)(2,1)}, bf16[8,256,512]{2,1,0:T(8,128)(2,1)}, u32[]{:S(2)}, u32[]{:S(2)}) collective-permute-start(bf16[8,256,512]{2,1,0:T(8,128)(2,1)} %collective-permute-done.37.r_10_.r_11_), channel_id=1, source_target_pairs={{0,8},{8,0},{1,9},{9,1},{2,10},{10,2},{3,11},{11,3},{4,12},{12,4},... | collective-permute-start | bytes 6291464 | tf_op jit(solution)/shard_map/ppermute | solution.py:58
  228.9 30.8 %collective-permute-start.42 = (bf16[8,512,128]{2,1,0:T(8,128)(2,1)S(1)}, bf16[8,512,128]{2,1,0:T(8,128)(2,1)}, u32[]{:S(2)}, u32[]{:S(2)}) collective-permute-start(bf16[8,512,128]{2,1,0:T(8,128)(2,1)S(1)} %pad_maximum_fusion.7.r_1_.r_2_), channel_id=1, source_target_pairs={{0,16},{1,17},{2,18},{3,19},{4,20},{5,21},{6,22},{7,23},{8,9},{9,8... | collective-permute-start | bytes 3145736 | tf_op jit(solution)/shard_map/ppermute | solution.py:55
  266.5 18.0 %collective-permute-start.45 = (bf16[16,256,512]{2,1,0:T(8,128)(2,1)}, bf16[16,256,512]{2,1,0:T(8,128)(2,1)}, u32[]{:S(2)}, u32[]{:S(2)}) collective-permute-start(bf16[16,256,512]{2,1,0:T(8,128)(2,1)} %get-tuple-element.172), channel_id=1, source_target_pairs={{0,8},{8,0},{1,9},{9,1},{2,10},{10,2},{3,11},{11,3},{4,12},{12,4},... | collective-permute-start | bytes 12582920 | tf_op jit(solution)/shard_map/ppermute | solution.py:58
  270.9 17.5 %collective-permute-start.44 = (bf16[4,256,512]{2,1,0:T(8,128)(2,1)}, bf16[4,256,512]{2,1,0:T(8,128)(2,1)}, u32[]{:S(2)}, u32[]{:S(2)}) collective-permute-start(bf16[4,256,512]{2,1,0:T(8,128)(2,1)} %get-tuple-element.179), channel_id=1, source_target_pairs={{0,16},{1,17},{2,18},{3,19},{4,20},{5,21},{6,22},{7,23},{8,9},{9,8... | collective-permute-start | bytes 3145736 | tf_op jit(solution)/shard_map/ppermute | solution.py:55
  288.5 17.3 %collective-permute-start.46 = (bf16[4,256,512]{2,1,0:T(8,128)(2,1)}, bf16[4,256,512]{2,1,0:T(8,128)(2,1)S(1)}, u32[]{:S(2)}, u32[]{:S(2)}) collective-permute-start(bf16[4,256,512]{2,1,0:T(8,128)(2,1)} %get-tuple-element.183), channel_id=1, source_target_pairs={{0,16},{1,17},{2,18},{3,19},{4,20},{5,21},{6,22},{7,23},{8,9},{9,8... | collective-permute-start | bytes 3145736 | tf_op jit(solution)/shard_map/ppermute | solution.py:55
  305.8 15.1 %collective-permute-start.47 = (bf16[4,256,512]{2,1,0:T(8,128)(2,1)}, bf16[4,256,512]{2,1,0:T(8,128)(2,1)S(1)}, u32[]{:S(2)}, u32[]{:S(2)}) collective-permute-start(bf16[4,256,512]{2,1,0:T(8,128)(2,1)} %get-tuple-element.185), channel_id=1, source_target_pairs={{0,16},{1,17},{2,18},{3,19},{4,20},{5,21},{6,22},{7,23},{8,9},{9,8... | collective-permute-start | bytes 3145736 | tf_op jit(solution)/shard_map/ppermute | solution.py:55
  320.9 45.4 %collective-permute-start.50 = (bf16[16,1024,128]{2,1,0:T(8,128)(2,1)}, bf16[16,1024,128]{2,1,0:T(8,128)(2,1)}, u32[]{:S(2)}, u32[]{:S(2)}) collective-permute-start(bf16[16,1024,128]{2,1,0:T(8,128)(2,1)} %bitcast.241), channel_id=1, source_target_pairs={{0,8},{8,0},{1,9},{9,1},{2,10},{10,2},{3,11},{11,3},{4,12},{12,4},... | collective-permute-start | bytes 12582920 | tf_op jit(solution)/shard_map/ppermute | solution.py:58
  320.9 25.5 %collective-permute-start.48 = (bf16[4,256,512]{2,1,0:T(8,128)(2,1)S(1)}, bf16[4,256,512]{2,1,0:T(8,128)(2,1)}, u32[]{:S(2)}, u32[]{:S(2)}) collective-permute-start(bf16[4,256,512]{2,1,0:T(8,128)(2,1)S(1)} %copy-done.45), channel_id=1, source_target_pairs={{0,16},{1,17},{2,18},{3,19},{4,20},{5,21},{6,22},{7,23},{8,9},{9,8... | collective-permute-start | bytes 3145736 | tf_op jit(solution)/shard_map/ppermute | solution.py:55
  321.5 25.0 %collective-permute-start.49 = (bf16[4,256,512]{2,1,0:T(8,128)(2,1)S(1)}, bf16[4,256,512]{2,1,0:T(8,128)(2,1)}, u32[]{:S(2)}, u32[]{:S(2)}) collective-permute-start(bf16[4,256,512]{2,1,0:T(8,128)(2,1)S(1)} %add_convert_fusion.5), channel_id=1, source_target_pairs={{0,1},{1,0},{2,3},{3,2},{4,5},{5,4},{6,7},{7,6},{8,24},{9,25},{10,... | collective-permute-start | bytes 3145736 | tf_op jit(solution)/shard_map/ppermute | solution.py:55
  348.9 15.1 %collective-permute-start.52 = (bf16[4,256,512]{2,1,0:T(8,128)(2,1)}, bf16[4,256,512]{2,1,0:T(8,128)(2,1)}, u32[]{:S(2)}, u32[]{:S(2)}) collective-permute-start(bf16[4,256,512]{2,1,0:T(8,128)(2,1)} %add_convert_fusion.3), channel_id=1, source_target_pairs={{0,1},{1,0},{2,3},{3,2},{4,5},{5,4},{6,7},{7,6},{8,24},{9,25},{10,... | collective-permute-start | bytes 3145736 | tf_op jit(solution)/shard_map/ppermute | solution.py:55
  350.6 19.0 %collective-permute-start.51 = (bf16[2,256,512]{2,1,0:T(8,128)(2,1)}, bf16[2,256,512]{2,1,0:T(8,128)(2,1)S(1)}, u32[]{:S(2)}, u32[]{:S(2)}) collective-permute-start(bf16[2,256,512]{2,1,0:T(8,128)(2,1)} %get-tuple-element.196), channel_id=1, source_target_pairs={{0,2},{2,0},{4,6},{6,4},{1,3},{3,1},{5,7},{7,5},{8,10},{10,8},{12,... | collective-permute-start | bytes 1572872 | tf_op jit(solution)/shard_map/ppermute | solution.py:58
  370.4 14.9 %collective-permute-start.54 = (bf16[4,1024,128]{2,1,0:T(8,128)(2,1)S(1)}, bf16[4,1024,128]{2,1,0:T(8,128)(2,1)}, u32[]{:S(2)}, u32[]{:S(2)}) collective-permute-start(bf16[4,1024,128]{2,1,0:T(8,128)(2,1)S(1)} %get-tuple-element.207), channel_id=1, source_target_pairs={{0,16},{1,17},{2,18},{3,19},{4,20},{5,21},{6,22},{7,23},{8,9},{9,8... | collective-permute-start | bytes 3145736 | tf_op jit(solution)/shard_map/ppermute | solution.py:55
  385.3 15.0 %collective-permute-start.55 = (bf16[4,1024,128]{2,1,0:T(8,128)(2,1)}, bf16[4,1024,128]{2,1,0:T(8,128)(2,1)S(1)}, u32[]{:S(2)}, u32[]{:S(2)}) collective-permute-start(bf16[4,1024,128]{2,1,0:T(8,128)(2,1)} %get-tuple-element.208), channel_id=1, source_target_pairs={{0,16},{1,17},{2,18},{3,19},{4,20},{5,21},{6,22},{7,23},{8,9},{9,8... | collective-permute-start | bytes 3145736 | tf_op jit(solution)/shard_map/ppermute | solution.py:55
  389.6 19.5 %collective-permute-start.59 = (bf16[8,400,128]{2,1,0:T(8,128)(2,1)S(1)}, bf16[8,400,128]{2,1,0:T(8,128)(2,1)S(1)}, u32[]{:S(2)}, u32[]{:S(2)}) collective-permute-start(bf16[8,400,128]{2,1,0:T(8,128)(2,1)S(1)} %get-tuple-element.279), channel_id=1, source_target_pairs={{0,16},{1,17},{2,18},{3,19},{4,20},{5,21},{6,22},{7,23},{8,9},{9,8... | collective-permute-start | bytes 2457608 | tf_op jit(solution)/shard_map/ppermute | solution.py:55
  390.6 45.0 %collective-permute-start.66 = (bf16[8,512,128]{2,1,0:T(8,128)(2,1)S(1)}, bf16[8,512,128]{2,1,0:T(8,128)(2,1)S(1)}, u32[]{:S(2)}, u32[]{:S(2)}) collective-permute-start(bf16[8,512,128]{2,1,0:T(8,128)(2,1)S(1)} %pad_maximum_fusion.7.r_1_.r_2_), channel_id=1, source_target_pairs={{0,8},{8,0},{1,9},{9,1},{2,10},{10,2},{3,11},{11,3},{4,12},{12,4},... | collective-permute-start | bytes 3145736 | tf_op jit(solution)/shard_map/ppermute | solution.py:58
  391.2 44.4 %collective-permute-start.67 = (bf16[8,512,128]{2,1,0:T(8,128)(2,1)}, bf16[8,512,128]{2,1,0:T(8,128)(2,1)S(1)}, u32[]{:S(2)}, u32[]{:S(2)}) collective-permute-start(bf16[8,512,128]{2,1,0:T(8,128)(2,1)} %collective-permute-done.42.r_3_.r_4_), channel_id=1, source_target_pairs={{0,8},{8,0},{1,9},{9,1},{2,10},{10,2},{3,11},{11,3},{4,12},{12,4},... | collective-permute-start | bytes 3145736 | tf_op jit(solution)/shard_map/ppermute | solution.py:58
  391.2 21.6 %collective-permute-start.56 = (bf16[1,256,512]{2,1,0:T(8,128)(2,1)}, bf16[1,256,512]{2,1,0:T(8,128)(2,1)}, u32[]{:S(2)}, u32[]{:S(2)}) collective-permute-start(bf16[1,256,512]{2,1,0:T(8,128)(2,1)} %add_convert_fusion.27), channel_id=1, source_target_pairs={{0,4},{2,6},{4,0},{6,2},{1,5},{3,7},{5,1},{7,3},{8,12},{10,14},{12... | collective-permute-start | bytes 786440 | tf_op jit(solution)/shard_map/ppermute | solution.py:58
  400.3 17.7 %collective-permute-start.57 = (bf16[1,256,512]{2,1,0:T(8,128)(2,1)S(1)}, bf16[1,256,512]{2,1,0:T(8,128)(2,1)}, u32[]{:S(2)}, u32[]{:S(2)}) collective-permute-start(bf16[1,256,512]{2,1,0:T(8,128)(2,1)S(1)} %add_convert_fusion.26), channel_id=1, source_target_pairs={{0,4},{2,6},{4,0},{6,2},{1,5},{3,7},{5,1},{7,3},{8,12},{10,14},{12... | collective-permute-start | bytes 786440 | tf_op jit(solution)/shard_map/ppermute | solution.py:58
  419.2 24.3 %collective-permute-start.65 = (bf16[4,1024,128]{2,1,0:T(8,128)(2,1)}, bf16[4,1024,128]{2,1,0:T(8,128)(2,1)}, u32[]{:S(2)}, u32[]{:S(2)}) collective-permute-start(bf16[4,1024,128]{2,1,0:T(8,128)(2,1)} %get-tuple-element.215), channel_id=1, source_target_pairs={{0,1},{1,0},{2,3},{3,2},{4,5},{5,4},{6,7},{7,6},{8,24},{9,25},{10,... | collective-permute-start | bytes 3145736 | tf_op jit(solution)/shard_map/ppermute | solution.py:55
  429.2 14.2 %collective-permute-start.62 = (f32[16,384]{1,0:T(8,128)S(1)}, f32[16,384]{1,0:T(8,128)S(1)}, u32[]{:S(2)}, u32[]{:S(2)}) collective-permute-start(f32[16,384]{1,0:T(8,128)S(1)} %add.489), channel_id=1, source_target_pairs={{0,4},{2,6},{4,0},{6,2},{1,5},{3,7},{5,1},{7,3},{8,12},{10,14},{12... | collective-permute-start | bytes 73736 | tf_op jit(solution)/shard_map/ppermute | solution.py:58
  448.3 16.4 %collective-permute-start.71 = (bf16[2,1024,128]{2,1,0:T(8,128)(2,1)S(1)}, bf16[2,1024,128]{2,1,0:T(8,128)(2,1)S(1)}, u32[]{:S(2)}, u32[]{:S(2)}) collective-permute-start(bf16[2,1024,128]{2,1,0:T(8,128)(2,1)S(1)} %get-tuple-element.224), channel_id=1, source_target_pairs={{0,2},{2,0},{4,6},{6,4},{1,3},{3,1},{5,7},{7,5},{8,10},{10,8},{12,... | collective-permute-start | bytes 1572872 | tf_op jit(solution)/shard_map/ppermute | solution.py:58
  474.8 13.7 %collective-permute-start.74 = (bf16[1,1024,128]{2,1,0:T(8,128)(2,1)}, bf16[1,1024,128]{2,1,0:T(8,128)(2,1)}, u32[]{:S(2)}, u32[]{:S(2)}) collective-permute-start(bf16[1,1024,128]{2,1,0:T(8,128)(2,1)} %add_convert_fusion.24), channel_id=1, source_target_pairs={{0,4},{2,6},{4,0},{6,2},{1,5},{3,7},{5,1},{7,3},{8,12},{10,14},{12... | collective-permute-start | bytes 786440 | tf_op jit(solution)/shard_map/ppermute | solution.py:58
  (110 other events, 1389.1 us)

commit v5 on v4

--- a/solution.py
+++ b/solution.py
@@ -796,7 +796,7 @@
         masks = half_masks(cap)
         key = lax.broadcasted_iota(jnp.int32, (cap, cap), 1)
 
-        @pl.loop(0, width // 128, unroll=2)
+        @pl.loop(0, width // 128, unroll=4)
         def _(j):
             for m in range(micro):
                 rows = slice(m * cap, (m + 1) * cap)
@@ -998,7 +998,7 @@
         do_ref[...] = acc_ref[...].astype(BF)
         masks = half_masks(cap)
 
-        @pl.loop(0, width // 128, unroll=2)
+        @pl.loop(0, width // 128, unroll=4)
         def _(j):
             for m in range(micro):
                 rows = slice(m * cap, (m + 1) * cap)
@@ -1599,7 +1599,7 @@
         *twice(wq_parts),
     )
     z2l, z1a = grid.begin([na, z1l, s_sum, wq, wk], (z2, l_end[1]), (z1, a_half[1]))
-    s_sum = grid.hop(grid.gate(s_sum, z2l), ("x", 1), ("y", 1))
+    s_sum = grid.rounds(grid.gate(s_sum, z2l), "yx")
     a_end = ends(a_half[0], z1a)
     (z2a,) = grid.begin([z1a], (z2, a_end[1]))
     low_sum, attn_sum = (

time: 530 us -> 532 us (level)
    ppermute x25 -> x26, waiting for transfers between devices: 50.1 us -> 51.4 us  [permute(): return lax.ppermute(value, AXES, self.flat(move))]
    ppermute x25 -> x26, starting transfers between devices: 27.8 us -> 28.1 us  [permute(): return lax.ppermute(value, AXES, self.flat(move))]
  transfers between devices with their start and end apart: 86 -> 87, of which waited for: 47 -> 49; matrix products, arithmetic and copies ran while one was open for 16% -> 16% of each run, Pallas kernels for 32% -> 32%
where the time goes in v5:
time: 532 us; the launch traced here: 522 us
  Pallas kernels  166 us (31%)
  waiting for transfers between devices  145 us (27%)
  starting transfers between devices  88.9 us (17%)
  other arithmetic  77.1 us (14%)
  local copies, waits for them, and re-layouts  22.7 us (4%)
  between operations  13.8 us (3%)
  matrix products  8.63 us (2%)
    pallas_call x16, Pallas kernels, call(): pl.pallas_call(kernel, name=name, grid=grid, in_specs=in_specs, out_shape...  166 us
    ppermute x61, waiting for transfers between devices, swap(): lax.ppermute(value, axis, [(i, i ^ bit) for i in range(self.sizes[axis])])  93.5 us
    ppermute x61, starting transfers between devices, swap(): lax.ppermute(value, axis, [(i, i ^ bit) for i in range(self.sizes[axis])])  60.8 us
    ppermute x26, waiting for transfers between devices, permute(): return lax.ppermute(value, AXES, self.flat(move))  51.4 us
    convert_element_type x18, other arithmetic, plus(): return (left.astype(F32) + right.astype(F32)).astype(BF)  32.1 us
    ppermute x26, starting transfers between devices, permute(): return lax.ppermute(value, AXES, self.flat(move))  28.1 us
  transfers between devices with their start and end apart: 87, of which 49 were waited for; matrix products, arithmetic and copies ran while one was open for 16% of the time, Pallas kernels for 32%

profile of v5, /device:TPU:0, one launch (start us, length us, event | category | flops | bytes accessed | tf_op | source)
XLA Modules:
  0.0 521.8 jit_solution(15921222547773266408)
XLA Ops:
  2.2 2.6 collective-permute-start.8
  7.8 3.1 collective-permute-start
  13.0 5.7 %collective-permute-done = bf16[656,128]{1,0:T(8,128)(2,1)S(1)} collective-permute-done((bf16[656,128]{1,0:T(8,128)(2,1)S(1)}, bf16[656,128]{1,0:T(8,128)(2,1)S(1)}, u32[]{:S(2)}, u32[]{:S(2)}) %collective-permute-start) | collective-permute-done | bytes 167968 | tf_op jit(solution)/shard_map/ppermute | solution.py:58
  19.7 2.6 collective-permute-done.1
  24.5 2.5 collective-permute-done.2
  45.8 9.4 %collective-permute-done.10 = bf16[1024,128]{1,0:T(8,128)(2,1)S(1)} collective-permute-done((bf16[1024,128]{1,0:T(8,128)(2,1)S(1)}, bf16[1024,128]{1,0:T(8,128)(2,1)S(1)}, u32[]{:S(2)}, u32[]{:S(2)}) %collective-permute-start.10) | collective-permute-done | bytes 262176 | tf_op jit(solution)/shard_map/ppermute | solution.py:58
  61.1 3.5 collective-permute-done.16
  64.6 4.2 collective-permute-start.17
  70.9 3.3 collective-permute-done.18
  79.6 11.7 %collective-permute-done.21 = bf16[256,512]{1,0:T(8,128)(2,1)S(1)} collective-permute-done((bf16[256,512]{1,0:T(8,128)(2,1)S(1)}, bf16[256,512]{1,0:T(8,128)(2,1)S(1)}, u32[]{:S(2)}, u32[]{:S(2)}) %collective-permute-start.21) | collective-permute-done | bytes 262176 | tf_op jit(solution)/shard_map/ppermute | solution.py:58
  91.4 10.8 %collective-permute-done.20 = bf16[4,1024,128]{2,1,0:T(8,128)(2,1)S(1)} collective-permute-done((bf16[4,1024,128]{2,1,0:T(8,128)(2,1)S(1)}, bf16[4,1024,128]{2,1,0:T(8,128)(2,1)S(1)}, u32[]{:S(2)}, u32[]{:S(2)}) %collective-permute-start.20) | collective-permute-done | bytes 1048608 | tf_op jit(solution)/shard_map/ppermute | solution.py:55
  108.7 9.3 %collective-permute-done.25 = f32[1024,16]{0,1:T(8,128)S(1)} collective-permute-done((f32[1024,16]{0,1:T(8,128)S(1)}, f32[1024,16]{0,1:T(8,128)S(1)}, u32[]{:S(2)}, u32[]{:S(2)}) %collective-permute-start.25) | collective-permute-done | bytes 65568 | tf_op jit(solution)/shard_map/ppermute | solution.py:58
  119.2 4.2 collective-permute-done.27
  124.3 6.6 %collective-permute-done.26.r_7_.r_8_.r_15_.r_16_.r_6_ = bf16[8,1024,128]{2,1,0:T(8,128)(2,1)S(1)} collective-permute-done((bf16[8,1024,128]{2,1,0:T(8,128)(2,1)S(1)}, bf16[8,1024,128]{2,1,0:T(8,128)(2,1)S(1)}, u32[]{:S(2)}, u32[]{:S(2)}) %collective-permute-start.26) | collective-permute-done | bytes 2097184 | tf_op jit(solution)/shard_map/ppermute | solution.py:55
  133.7 5.6 %assemble.1 = (bf16[384,1024]{1,0:T(8,128)(2,1)}, f32[192,1024]{1,0:T(8,128)}, bf16[1024,1024]{1,0:T(8,128)(2,1)}) custom-call(s32[4]{0:T(128)} %pad_add_fusion.r_0_, bf16[8,656,128]{2,1,0:T(8,128)(2,1)} %copy-done.3, bf16[8,656,128]{2,1,0:T(8,128)(2,1)} %copy-done.3, bf16[8,656,128]{2,1,0:T(8,128)(2,1)} %copy-done.4, bf16[8,656,128]{2,1,0:T(8,128)(2,1)} %copy-done.4, ...), custom_call_target="tpu_custom_call" | custom-call | bytes 8388608 | tf_op jit(solution)/shard_map/assemble/pallas_call | solution.py:643
  139.3 4.8 table_values.1.tv_ref
  146.8 2.8 pad_maximum_fusion.1.r_2_.r_3_.r_5_.r_6_
  162.6 12.9 %pool.1 = (bf16[256,1024]{1,0:T(8,128)(2,1)}, bf16[16,256,384]{2,1,0:T(8,128)(2,1)}, f32[16,256,128]{2,1,0:T(8,128)}) custom-call(bf16[256,384]{1,0:T(8,128)(2,1)} %fusion.8.x_ref, bf16[384,128]{1,0:T(8,128)(2,1)} %constant.157.clone.e_ref, f32[384,128]{1,0:T(8,128)} %pad.10.tu_ref, bf16[384,1024]{1,0:T(8,128)(2,1)} %table_values.1.tv_ref), custom_call_target="tpu_custom_call" | custom-call | flops 2415919104 | bytes 8388608 | tf_op jit(solution)/shard_map/pool/pallas_call | solution.py:643
  175.5 5.2 %enter.1 = (f32[256,1024]{1,0:T(8,128)}, bf16[256,1024]{1,0:T(8,128)(2,1)}) custom-call(s32[4]{0:T(128)} %pad_add_fusion.r_0_, bf16[256,1024]{1,0:T(8,128)(2,1)} %get-tuple-element.141.r_1_.r_2_, f32[2,1024]{1,0:T(2,128)} %fusion.49.r_2_, f32[1,1024]{1,0:T(1,128)} %get-tuple-element.285.r_3_.r_4_, bf16[8,656,128]{2,1,0:T(8,128)(2,1)} %copy-done.3, ...), custom_call_target="tpu_custom_call" | custom-call | flops 536870912 | bytes 4194304 | tf_op jit(solution)/shard_map/enter/pallas_call | solution.py:643
  180.8 4.4 collective-permute-done.33
  190.8 19.6 %attend.1 = (bf16[256,3072]{1,0:T(8,128)(2,1)}, f32[16,2,128,128]{3,2,1,0:T(8,128)}, bf16[256,1024]{1,0:T(8,128)(2,1)}, f32[256,1024]{1,0:T(8,128)}, bf16[256,1024]{1,0:T(8,128)(2,1)}) custom-call(s32[4]{0:T(128)} %pad_add_fusion.r_0_, s32[2]{0:T(128)} %bitcast.239, f32[256,1024]{1,0:T(8,128)} %get-tuple-element.142.r_2_.r_3_, ...), custom_call_target="tpu_custom_call" | custom-call | flops 2415919104 | bytes 16777216 | tf_op jit(solution)/shard_map/attend/pallas_call | solution.py:643
  211.3 4.1 collective-permute-done.37.r_10_.r_11_
  216.4 10.3 %up.1 = (bf16[256,4096]{1,0:T(8,128)(2,1)}, bf16[256,4096]{1,0:T(8,128)(2,1)}) custom-call(s32[4]{0:T(128)} %pad_add_fusion.r_0_, bf16[256,1024]{1,0:T(8,128)(2,1)} %get-tuple-element.147.r_1_, bf16[8,256,512]{2,1,0:T(8,128)(2,1)} %pad_maximum_fusion.1.r_2_.r_3_.r_5_.r_6_, bf16[8,256,512]{2,1,0:T(8,128)(2,1)} %pad_maximum_fusion.1.r_2_.r_3_.r_5_.r_6_, ...), custom_call_target="tpu_custom_call" | custom-call | flops 2147483648 | bytes 16777216 | tf_op jit(solution)/shard_map/up/pallas_call | solution.py:643
  232.9 20.0 %down.1 = (f32[8,128]{1,0:T(8,128)}, f32[256,1024]{1,0:T(8,128)}, bf16[256,1024]{1,0:T(8,128)(2,1)}, f32[192,1024]{1,0:T(8,128)}, bf16[256,4096]{1,0:T(8,128)(2,1)}) custom-call(s32[4]{0:T(128)} %pad_add_fusion.r_0_, f32[1]{0:T(128)} %slice.357.r_1_, f32[256,1024]{1,0:T(8,128)} %get-tuple-element.146.r_2_, bf16[256,4096]{1,0:T(8,128)(2,1)} %get-tuple-element.158.r_3_.r_2_, ...), custom_call_target="tpu_custom_call" | custom-call | flops 4294967296 | bytes 33554432 | tf_op jit(solution)/shard_map/down/pallas_call | solution.py:643
  252.9 6.8 %down_grad.1 = (bf16[16,256,512]{2,1,0:T(8,128)(2,1)}, bf16[16,256,512]{2,1,0:T(8,128)(2,1)}) custom-call(s32[4]{0:T(128)} %pad_add_fusion.r_0_, bf16[256,1024]{1,0:T(8,128)(2,1)} %get-tuple-element.167.r_1_, bf16[256,4096]{1,0:T(8,128)(2,1)} %get-tuple-element.158.r_3_.r_2_), custom_call_target="tpu_custom_call" | custom-call | flops 2147483648 | bytes 12582912 | tf_op jit(solution)/shard_map/down_grad/pallas_call | solution.py:643
  259.8 6.8 %up_grad.1 = (bf16[16,256,512]{2,1,0:T(8,128)(2,1)}, bf16[16,256,512]{2,1,0:T(8,128)(2,1)}) custom-call(s32[4]{0:T(128)} %pad_add_fusion.r_0_, bf16[256,1024]{1,0:T(8,128)(2,1)} %get-tuple-element.147.r_1_, bf16[256,4096]{1,0:T(8,128)(2,1)} %get-tuple-element.175.r_2_.r_1_), custom_call_target="tpu_custom_call" | custom-call | flops 2147483648 | bytes 12582912 | tf_op jit(solution)/shard_map/up_grad/pallas_call | solution.py:643
  267.2 3.7 add_convert_fusion.10
  271.5 13.0 %up_back.1 = (f32[256,1024]{1,0:T(8,128)}, bf16[256,1024]{1,0:T(8,128)(2,1)}, f32[1,1024]{1,0:T(1,128)}) custom-call(s32[4]{0:T(128)} %pad_add_fusion.r_0_, bf16[256,4096]{1,0:T(8,128)(2,1)} %get-tuple-element.175.r_2_.r_1_, f32[256,1024]{1,0:T(8,128)} %get-tuple-element.146.r_2_, f32[1,1024]{1,0:T(1,128)} %get-tuple-element.284.r_4_.r_3_, ...), custom_call_target="tpu_custom_call" | custom-call | flops 2147483648 | bytes 16777216 | tf_op jit(solution)/shard_map/up_back/pallas_call | solution.py:643
  284.5 3.7 add_convert_fusion.6
  289.8 14.0 %attend_back.1.r_3_.r_2_ = bf16[256,3072]{1,0:T(8,128)(2,1)} custom-call(s32[4]{0:T(128)} %pad_add_fusion.r_0_, bf16[256,1024]{1,0:T(8,128)(2,1)} %get-tuple-element.180.r_1_.r_4_, bf16[256,3072]{1,0:T(8,128)(2,1)} %get-tuple-element.181.r_2_, f32[16,2,128,128]{3,2,1,0:T(8,128)} %get-tuple-element.182.r_3_, bf16[8,1024,128]{2,1,0:T(8,128)(2,1)} %copy-done, ...), custom_call_target="tpu_custom_call" | custom-call | flops 939524096 | bytes 4194304 | tf_op jit(solution)/shard_map/attend_back/pallas_call | solution.py:643
  306.0 7.3 %attention_grad.1 = (bf16[4,4,1024,128]{3,2,1,0:T(8,128)(2,1)}, bf16[4,4,1024,128]{3,2,1,0:T(8,128)(2,1)}) custom-call(s32[4]{0:T(128)} %pad_add_fusion.r_0_, bf16[256,1024]{1,0:T(8,128)(2,1)} %get-tuple-element.143.r_3_.r_1_, bf16[256,1024]{1,0:T(8,128)(2,1)} %get-tuple-element.186.r_2_, bf16[256,3072]{1,0:T(8,128)(2,1)} %attend_back.1.r_3_.r_2_, ...), custom_call_target="tpu_custom_call" | custom-call | flops 2147483648 | bytes 8388608 | tf_op jit(solution)/shard_map/attention_grad/pallas_call | solution.py:643
  313.3 7.1 %collective-permute-done.47 = bf16[4,256,512]{2,1,0:T(8,128)(2,1)S(1)} collective-permute-done((bf16[4,256,512]{2,1,0:T(8,128)(2,1)}, bf16[4,256,512]{2,1,0:T(8,128)(2,1)S(1)}, u32[]{:S(2)}, u32[]{:S(2)}) %collective-permute-start.47) | collective-permute-done | bytes 1048608 | tf_op jit(solution)/shard_map/ppermute | solution.py:55
  324.0 17.3 %leave.1 = (bf16[256,1024]{1,0:T(8,128)(2,1)}, f32[1,1024]{1,0:T(1,128)}, f32[2,1024]{1,0:T(2,128)}, bf16[256,1024]{1,0:T(8,128)(2,1)}) custom-call(s32[4]{0:T(128)} %pad_add_fusion.r_0_, f32[256,1024]{1,0:T(8,128)} %get-tuple-element.177.r_1_, bf16[256,3072]{1,0:T(8,128)(2,1)} %attend_back.1.r_3_.r_2_, f32[256,1024]{1,0:T(8,128)} %get-tuple-element.142.r_2_.r_3_, ...), custom_call_target="tpu_custom_call" | custom-call | flops 2147483648 | bytes 8388608 | tf_op jit(solution)/shard_map/leave/pallas_call | solution.py:643
  342.6 3.4 collective-permute-done.48
  350.5 11.1 %pool_back.1 = (f32[384,1024]{1,0:T(8,128)}, f32[4,4,384]{2,1,0:T(4,128)}) custom-call(bf16[256,384]{1,0:T(8,128)(2,1)} %fusion.8.x_ref, bf16[384,128]{1,0:T(8,128)(2,1)} %constant.157.clone.e_ref, bf16[384,1024]{1,0:T(8,128)(2,1)} %table_values.1.tv_ref, bf16[16,256,384]{2,1,0:T(8,128)(2,1)} %get-tuple-element.164.a_ref, ...), custom_call_target="tpu_custom_call" | custom-call | flops 2818572288 | bytes 8388608 | tf_op jit(solution)/shard_map/pool_back/pallas_call | solution.py:643
  365.8 3.3 fusion.2
  374.8 5.4 %low_grad.1 = (bf16[4,4,400,128]{3,2,1,0:T(8,128)(2,1)}, bf16[4,4,400,128]{3,2,1,0:T(8,128)(2,1)}) custom-call(s32[4]{0:T(128)} %pad_add_fusion.r_0_, s32[2]{0:T(128)} %bitcast.237, bf16[256,1024]{1,0:T(8,128)(2,1)} %get-tuple-element.141.r_1_.r_2_, bf16[256,1024]{1,0:T(8,128)(2,1)} %get-tuple-element.201.r_3_, f32[384,1024]{1,0:T(8,128)} %get-tuple-element.198.r_4_, ...), custom_call_target="tpu_custom_call" | custom-call | flops 536870912 | bytes 3276800 | tf_op jit(solution)/shard_map/low_grad/pallas_call | solution.py:643
  380.2 4.2 collective-permute-done.53
  392.0 7.8 %collective-permute-done.55 = bf16[4,1024,128]{2,1,0:T(8,128)(2,1)S(1)} collective-permute-done((bf16[4,1024,128]{2,1,0:T(8,128)(2,1)}, bf16[4,1024,128]{2,1,0:T(8,128)(2,1)S(1)}, u32[]{:S(2)}, u32[]{:S(2)}) %collective-permute-start.55) | collective-permute-done | bytes 1048608 | tf_op jit(solution)/shard_map/ppermute | solution.py:55
  401.4 4.0 add_convert_fusion
  405.4 3.2 collective-permute-done.59
  409.6 2.7 collective-permute-done.56
  412.3 5.2 %collective-permute-done.57 = bf16[1,256,512]{2,1,0:T(8,128)(2,1)} collective-permute-done((bf16[1,256,512]{2,1,0:T(8,128)(2,1)S(1)}, bf16[1,256,512]{2,1,0:T(8,128)(2,1)}, u32[]{:S(2)}, u32[]{:S(2)}) %collective-permute-start.57) | collective-permute-done | bytes 262176 | tf_op jit(solution)/shard_map/ppermute | solution.py:58
  432.2 2.6 multiply_reduce_fusion.1
  436.7 5.6 %squares.1 = (bf16[1024,1024]{1,0:T(8,128)(2,1)}, bf16[1024,1024]{1,0:T(8,128)(2,1)}) custom-call(s32[4]{0:T(128)} %pad_add_fusion.r_0_, bf16[8,512,128]{2,1,0:T(8,128)(2,1)} %copy-done.10, bf16[8,512,128]{2,1,0:T(8,128)(2,1)} %copy-done.10, bf16[8,512,128]{2,1,0:T(8,128)(2,1)} %collective-permute-done.42.r_3_.r_4_, ...), custom_call_target="tpu_custom_call" | custom-call | bytes 1048576 | tf_op jit(solution)/shard_map/squares/pallas_call | solution.py:643
  481.7 4.3 collective-permute-done.75
  512.1 4.5 fusion.76
  516.6 2.5 fusion.74
  (431 shorter events, 189.3 us)
Async XLA Ops:
  1.6 36.1 %collective-permute-start.6 = (bf16[2,128,48]{1,2,0:T(8,128)(2,1)S(1)}, bf16[2,128,48]{1,2,0:T(8,128)(2,1)S(1)}, u32[]{:S(2)}, u32[]{:S(2)}) collective-permute-start(bf16[2,128,48]{1,2,0:T(8,128)(2,1)S(1)} %get-tuple-element.299), channel_id=1, source_target_pairs={{0,8},{1,9},{2,10},{3,11},{4,12},{5,13},{6,14},{7,15},{8,0},{9,1},... | collective-permute-start | bytes 73736 | tf_op jit(solution)/shard_map/ppermute | solution.py:55
  2.2 32.1 %collective-permute-start.8 = (bf16[2,128,48]{1,2,0:T(8,128)(2,1)S(1)}, bf16[2,128,48]{1,2,0:T(8,128)(2,1)S(1)}, u32[]{:S(2)}, u32[]{:S(2)}) collective-permute-start(bf16[2,128,48]{1,2,0:T(8,128)(2,1)S(1)} %get-tuple-element.301), channel_id=1, source_target_pairs={{0,24},{1,25},{2,26},{3,27},{4,28},{5,29},{6,30},{7,31},{8,16},{9,... | collective-permute-start | bytes 73736 | tf_op jit(solution)/shard_map/ppermute | solution.py:55
  4.8 27.3 %collective-permute-start.7 = (bf16[2,128,48]{1,2,0:T(8,128)(2,1)S(1)}, bf16[2,128,48]{1,2,0:T(8,128)(2,1)S(1)}, u32[]{:S(2)}, u32[]{:S(2)}) collective-permute-start(bf16[2,128,48]{1,2,0:T(8,128)(2,1)S(1)} %get-tuple-element.302), channel_id=1, source_target_pairs={{0,16},{1,17},{2,18},{3,19},{4,20},{5,21},{6,22},{7,23},{8,24},{9,... | collective-permute-start | bytes 73736 | tf_op jit(solution)/shard_map/ppermute | solution.py:55
  39.8 15.4 %collective-permute-start.10 = (bf16[1024,128]{1,0:T(8,128)(2,1)S(1)}, bf16[1024,128]{1,0:T(8,128)(2,1)S(1)}, u32[]{:S(2)}, u32[]{:S(2)}) collective-permute-start(bf16[1024,128]{1,0:T(8,128)(2,1)S(1)} %bitcast.203), channel_id=1, source_target_pairs={{0,4},{2,6},{4,0},{6,2},{1,5},{3,7},{5,1},{7,3},{8,12},{10,14},{12... | collective-permute-start | bytes 786440 | tf_op jit(solution)/shard_map/ppermute | solution.py:58
  41.9 14.9 %collective-permute-start.9 = (bf16[2,656,128]{2,1,0:T(8,128)(2,1)S(1)}, bf16[2,656,128]{2,1,0:T(8,128)(2,1)S(1)}, u32[]{:S(2)}, u32[]{:S(2)}) collective-permute-start(bf16[2,656,128]{2,1,0:T(8,128)(2,1)S(1)} %pad_maximum_fusion.13), channel_id=1, source_target_pairs={{0,2},{2,0},{4,6},{6,4},{1,3},{3,1},{5,7},{7,5},{8,10},{10,8},{12,... | collective-permute-start | bytes 1007624 | tf_op jit(solution)/shard_map/ppermute | solution.py:58
  44.2 15.3 %collective-permute-start.15 = (f32[1024,16]{0,1:T(8,128)S(1)}, f32[1024,16]{0,1:T(8,128)S(1)}, u32[]{:S(2)}, u32[]{:S(2)}) collective-permute-start(f32[1024,16]{0,1:T(8,128)S(1)} %get-tuple-element.313), channel_id=1, source_target_pairs={{0,1},{1,0},{2,3},{3,2},{4,5},{5,4},{6,7},{7,6},{8,9},{9,8},{10,11... | collective-permute-start | bytes 196616 | tf_op jit(solution)/shard_map/ppermute | solution.py:58
  56.9 17.3 %collective-permute-start.14 = (bf16[2,1024,128]{2,1,0:T(8,128)(2,1)S(1)}, bf16[2,1024,128]{2,1,0:T(8,128)(2,1)S(1)}, u32[]{:S(2)}, u32[]{:S(2)}) collective-permute-start(bf16[2,1024,128]{2,1,0:T(8,128)(2,1)S(1)} %pad_maximum_fusion.9), channel_id=1, source_target_pairs={{0,2},{2,0},{4,6},{6,4},{1,3},{3,1},{5,7},{7,5},{8,10},{10,8},{12,... | collective-permute-start | bytes 1572872 | tf_op jit(solution)/shard_map/ppermute | solution.py:58
  58.0 16.3 %collective-permute-start.13 = (bf16[4,656,128]{2,1,0:T(8,128)(2,1)S(1)}, bf16[4,656,128]{2,1,0:T(8,128)(2,1)S(1)}, u32[]{:S(2)}, u32[]{:S(2)}) collective-permute-start(bf16[4,656,128]{2,1,0:T(8,128)(2,1)S(1)} %pad_maximum_fusion.8), channel_id=1, source_target_pairs={{0,1},{1,0},{2,3},{3,2},{4,5},{5,4},{6,7},{7,6},{8,24},{9,25},{10,... | collective-permute-start | bytes 2015240 | tf_op jit(solution)/shard_map/ppermute | solution.py:55
  74.5 30.2 %collective-permute-start.19 = (bf16[8,656,128]{2,1,0:T(8,128)(2,1)S(1)}, bf16[8,656,128]{2,1,0:T(8,128)(2,1)S(1)}, u32[]{:S(2)}, u32[]{:S(2)}) collective-permute-start(bf16[8,656,128]{2,1,0:T(8,128)(2,1)S(1)} %pad_maximum_fusion.3.r_1_.r_2_.r_3_.r_4_.r_5_.r_13_.r_14_), channel_id=1, source_target_pairs={{0,16},{1,17},{2,18},{3,19},{4,20},{5,21},{6,22},{7,23},{8,9},{9,8... | collective-permute-start | bytes 4030472 | tf_op jit(solution)/shard_map/ppermute | solution.py:55
  76.1 26.1 %collective-permute-start.20 = (bf16[4,1024,128]{2,1,0:T(8,128)(2,1)S(1)}, bf16[4,1024,128]{2,1,0:T(8,128)(2,1)S(1)}, u32[]{:S(2)}, u32[]{:S(2)}) collective-permute-start(bf16[4,1024,128]{2,1,0:T(8,128)(2,1)S(1)} %pad_maximum_fusion.4), channel_id=1, source_target_pairs={{0,1},{1,0},{2,3},{3,2},{4,5},{5,4},{6,7},{7,6},{8,24},{9,25},{10,... | collective-permute-start | bytes 3145736 | tf_op jit(solution)/shard_map/ppermute | solution.py:55
  77.6 13.7 %collective-permute-start.21 = (bf16[256,512]{1,0:T(8,128)(2,1)S(1)}, bf16[256,512]{1,0:T(8,128)(2,1)S(1)}, u32[]{:S(2)}, u32[]{:S(2)}) collective-permute-start(bf16[256,512]{1,0:T(8,128)(2,1)S(1)} %get-tuple-element.130), channel_id=1, source_target_pairs={{0,4},{2,6},{4,0},{6,2},{1,5},{3,7},{5,1},{7,3},{8,12},{10,14},{12... | collective-permute-start | bytes 786440 | tf_op jit(solution)/shard_map/ppermute | solution.py:58
  104.7 26.1 %collective-permute-start.26 = (bf16[8,1024,128]{2,1,0:T(8,128)(2,1)S(1)}, bf16[8,1024,128]{2,1,0:T(8,128)(2,1)S(1)}, u32[]{:S(2)}, u32[]{:S(2)}) collective-permute-start(bf16[8,1024,128]{2,1,0:T(8,128)(2,1)S(1)} %pad_maximum_fusion.r_5_.r_6_.r_13_.r_14_.r_4_), channel_id=1, source_target_pairs={{0,16},{1,17},{2,18},{3,19},{4,20},{5,21},{6,22},{7,23},{8,9},{9,8... | collective-permute-start | bytes 6291464 | tf_op jit(solution)/shard_map/ppermute | solution.py:55
  105.3 18.9 %collective-permute-start.23 = (bf16[8,656,128]{2,1,0:T(8,128)(2,1)S(1)}, bf16[8,656,128]{2,1,0:T(8,128)(2,1)S(1)}, u32[]{:S(2)}, u32[]{:S(2)}) collective-permute-start(bf16[8,656,128]{2,1,0:T(8,128)(2,1)S(1)} %pad_maximum_fusion.3.r_1_.r_2_.r_3_.r_4_.r_5_.r_13_.r_14_), channel_id=1, source_target_pairs={{0,8},{8,0},{1,9},{9,1},{2,10},{10,2},{3,11},{11,3},{4,12},{12,4},... | collective-permute-start | bytes 4030472 | tf_op jit(solution)/shard_map/ppermute | solution.py:58
  105.3 18.9 %collective-permute-start.24 = (bf16[8,656,128]{2,1,0:T(8,128)(2,1)S(1)}, bf16[8,656,128]{2,1,0:T(8,128)(2,1)S(1)}, u32[]{:S(2)}, u32[]{:S(2)}) collective-permute-start(bf16[8,656,128]{2,1,0:T(8,128)(2,1)S(1)} %collective-permute-done.19.r_3_.r_4_.r_5_.r_6_.r_7_.r_15_.r_16_), channel_id=1, source_target_pairs={{0,8},{8,0},{1,9},{9,1},{2,10},{10,2},{3,11},{11,3},{4,12},{12,4},... | collective-permute-start | bytes 4030472 | tf_op jit(solution)/shard_map/ppermute | solution.py:58
  107.6 15.7 %collective-permute-start.27 = (bf16[256,512]{1,0:T(8,128)(2,1)S(1)}, bf16[256,512]{1,0:T(8,128)(2,1)S(1)}, u32[]{:S(2)}, u32[]{:S(2)}) collective-permute-start(bf16[256,512]{1,0:T(8,128)(2,1)S(1)} %get-tuple-element.135), channel_id=1, source_target_pairs={{0,4},{2,6},{4,0},{6,2},{1,5},{3,7},{5,1},{7,3},{8,12},{10,14},{12... | collective-permute-start | bytes 786440 | tf_op jit(solution)/shard_map/ppermute | solution.py:58
  130.8 18.8 %collective-permute-start.29 = (bf16[8,1024,128]{2,1,0:T(8,128)(2,1)S(1)}, bf16[8,1024,128]{2,1,0:T(8,128)(2,1)S(1)}, u32[]{:S(2)}, u32[]{:S(2)}) collective-permute-start(bf16[8,1024,128]{2,1,0:T(8,128)(2,1)S(1)} %pad_maximum_fusion.r_5_.r_6_.r_13_.r_14_.r_4_), channel_id=1, source_target_pairs={{0,8},{8,0},{1,9},{9,1},{2,10},{10,2},{3,11},{11,3},{4,12},{12,4},... | collective-permute-start | bytes 6291464 | tf_op jit(solution)/shard_map/ppermute | solution.py:58
  130.8 18.8 %collective-permute-start.30 = (bf16[8,1024,128]{2,1,0:T(8,128)(2,1)S(1)}, bf16[8,1024,128]{2,1,0:T(8,128)(2,1)}, u32[]{:S(2)}, u32[]{:S(2)}) collective-permute-start(bf16[8,1024,128]{2,1,0:T(8,128)(2,1)S(1)} %collective-permute-done.26.r_7_.r_8_.r_15_.r_16_.r_6_), channel_id=1, source_target_pairs={{0,8},{8,0},{1,9},{9,1},{2,10},{10,2},{3,11},{11,3},{4,12},{12,4},... | collective-permute-start | bytes 6291464 | tf_op jit(solution)/shard_map/ppermute | solution.py:58
  131.3 15.5 %collective-permute-start.28 = (bf16[4,256,512]{2,1,0:T(8,128)(2,1)}, bf16[4,256,512]{2,1,0:T(8,128)(2,1)}, u32[]{:S(2)}, u32[]{:S(2)}) collective-permute-start(bf16[4,256,512]{2,1,0:T(8,128)(2,1)} %pad_maximum_fusion.5), channel_id=1, source_target_pairs={{0,1},{1,0},{2,3},{3,2},{4,5},{5,4},{6,7},{7,6},{8,24},{9,25},{10,... | collective-permute-start | bytes 3145736 | tf_op jit(solution)/shard_map/ppermute | solution.py:55
  131.9 13.8 %collective-permute-start.31 = (bf16[2,256,512]{2,1,0:T(8,128)(2,1)}, bf16[2,256,512]{2,1,0:T(8,128)(2,1)S(1)}, u32[]{:S(2)}, u32[]{:S(2)}) collective-permute-start(bf16[2,256,512]{2,1,0:T(8,128)(2,1)} %pad_maximum_fusion.11), channel_id=1, source_target_pairs={{0,2},{2,0},{4,6},{6,4},{1,3},{3,1},{5,7},{7,5},{8,10},{10,8},{12,... | collective-permute-start | bytes 1572872 | tf_op jit(solution)/shard_map/ppermute | solution.py:58
  151.0 37.5 %collective-permute-start.32 = (bf16[8,256,512]{2,1,0:T(8,128)(2,1)}, bf16[8,256,512]{2,1,0:T(8,128)(2,1)S(1)}, u32[]{:S(2)}, u32[]{:S(2)}) collective-permute-start(bf16[8,256,512]{2,1,0:T(8,128)(2,1)} %pad_maximum_fusion.1.r_2_.r_3_.r_5_.r_6_), channel_id=1, source_target_pairs={{0,16},{1,17},{2,18},{3,19},{4,20},{5,21},{6,22},{7,23},{8,9},{9,8... | collective-permute-start | bytes 6291464 | tf_op jit(solution)/shard_map/ppermute | solution.py:55
  158.8 26.4 %collective-permute-start.33 = (bf16[4,256,512]{2,1,0:T(8,128)(2,1)}, bf16[4,256,512]{2,1,0:T(8,128)(2,1)S(1)}, u32[]{:S(2)}, u32[]{:S(2)}) collective-permute-start(bf16[4,256,512]{2,1,0:T(8,128)(2,1)} %pad_maximum_fusion.6), channel_id=1, source_target_pairs={{0,1},{1,0},{2,3},{3,2},{4,5},{5,4},{6,7},{7,6},{8,24},{9,25},{10,... | collective-permute-start | bytes 3145736 | tf_op jit(solution)/shard_map/ppermute | solution.py:55
  161.8 18.9 %collective-permute-start.34 = (bf16[512,128]{1,0:T(8,128)(2,1)S(1)}, bf16[512,128]{1,0:T(8,128)(2,1)S(1)}, u32[]{:S(2)}, u32[]{:S(2)}) collective-permute-start(bf16[512,128]{1,0:T(8,128)(2,1)S(1)} %bitcast.217), channel_id=1, source_target_pairs={{0,4},{2,6},{4,0},{6,2},{1,5},{3,7},{5,1},{7,3},{8,12},{10,14},{12... | collective-permute-start | bytes 393224 | tf_op jit(solution)/shard_map/ppermute | solution.py:58
  188.4 22.8 %collective-permute-start.35 = (bf16[8,256,512]{2,1,0:T(8,128)(2,1)}, bf16[8,256,512]{2,1,0:T(8,128)(2,1)S(1)}, u32[]{:S(2)}, u32[]{:S(2)}) collective-permute-start(bf16[8,256,512]{2,1,0:T(8,128)(2,1)} %pad_maximum_fusion.1.r_2_.r_3_.r_5_.r_6_), channel_id=1, source_target_pairs={{0,8},{8,0},{1,9},{9,1},{2,10},{10,2},{3,11},{11,3},{4,12},{12,4},... | collective-permute-start | bytes 6291464 | tf_op jit(solution)/shard_map/ppermute | solution.py:58
  188.4 22.8 %collective-permute-start.36 = (bf16[8,256,512]{2,1,0:T(8,128)(2,1)S(1)}, bf16[8,256,512]{2,1,0:T(8,128)(2,1)S(1)}, u32[]{:S(2)}, u32[]{:S(2)}) collective-permute-start(bf16[8,256,512]{2,1,0:T(8,128)(2,1)S(1)} %collective-permute-done.32.r_4_.r_5_.r_7_.r_8_), channel_id=1, source_target_pairs={{0,8},{8,0},{1,9},{9,1},{2,10},{10,2},{3,11},{11,3},{4,12},{12,4},... | collective-permute-start | bytes 6291464 | tf_op jit(solution)/shard_map/ppermute | solution.py:58
  189.0 26.4 %collective-permute-start.37 = (bf16[8,256,512]{2,1,0:T(8,128)(2,1)}, bf16[8,256,512]{2,1,0:T(8,128)(2,1)}, u32[]{:S(2)}, u32[]{:S(2)}) collective-permute-start(bf16[8,256,512]{2,1,0:T(8,128)(2,1)} %pad_maximum_fusion.2.r_8_.r_9_), channel_id=1, source_target_pairs={{0,16},{1,17},{2,18},{3,19},{4,20},{5,21},{6,22},{7,23},{8,9},{9,8... | collective-permute-start | bytes 6291464 | tf_op jit(solution)/shard_map/ppermute | solution.py:55
  190.5 19.9 %collective-permute-start.38 = (bf16[2,512,128]{2,1,0:T(8,128)(2,1)S(1)}, bf16[2,512,128]{2,1,0:T(8,128)(2,1)S(1)}, u32[]{:S(2)}, u32[]{:S(2)}) collective-permute-start(bf16[2,512,128]{2,1,0:T(8,128)(2,1)S(1)} %pad_maximum_fusion.14), channel_id=1, source_target_pairs={{0,2},{2,0},{4,6},{6,4},{1,3},{3,1},{5,7},{7,5},{8,10},{10,8},{12,... | collective-permute-start | bytes 786440 | tf_op jit(solution)/shard_map/ppermute | solution.py:58
  215.3 16.3 %collective-permute-start.40 = (bf16[8,256,512]{2,1,0:T(8,128)(2,1)}, bf16[8,256,512]{2,1,0:T(8,128)(2,1)S(1)}, u32[]{:S(2)}, u32[]{:S(2)}) collective-permute-start(bf16[8,256,512]{2,1,0:T(8,128)(2,1)} %pad_maximum_fusion.2.r_8_.r_9_), channel_id=1, source_target_pairs={{0,8},{8,0},{1,9},{9,1},{2,10},{10,2},{3,11},{11,3},{4,12},{12,4},... | collective-permute-start | bytes 6291464 | tf_op jit(solution)/shard_map/ppermute | solution.py:58
  215.3 16.3 %collective-permute-start.41 = (bf16[8,256,512]{2,1,0:T(8,128)(2,1)}, bf16[8,256,512]{2,1,0:T(8,128)(2,1)}, u32[]{:S(2)}, u32[]{:S(2)}) collective-permute-start(bf16[8,256,512]{2,1,0:T(8,128)(2,1)} %collective-permute-done.37.r_10_.r_11_), channel_id=1, source_target_pairs={{0,8},{8,0},{1,9},{9,1},{2,10},{10,2},{3,11},{11,3},{4,12},{12,4},... | collective-permute-start | bytes 6291464 | tf_op jit(solution)/shard_map/ppermute | solution.py:58
  228.7 31.1 %collective-permute-start.42 = (bf16[8,512,128]{2,1,0:T(8,128)(2,1)S(1)}, bf16[8,512,128]{2,1,0:T(8,128)(2,1)}, u32[]{:S(2)}, u32[]{:S(2)}) collective-permute-start(bf16[8,512,128]{2,1,0:T(8,128)(2,1)S(1)} %pad_maximum_fusion.7.r_1_.r_2_), channel_id=1, source_target_pairs={{0,16},{1,17},{2,18},{3,19},{4,20},{5,21},{6,22},{7,23},{8,9},{9,8... | collective-permute-start | bytes 3145736 | tf_op jit(solution)/shard_map/ppermute | solution.py:55
  266.5 18.0 %collective-permute-start.45 = (bf16[16,256,512]{2,1,0:T(8,128)(2,1)}, bf16[16,256,512]{2,1,0:T(8,128)(2,1)}, u32[]{:S(2)}, u32[]{:S(2)}) collective-permute-start(bf16[16,256,512]{2,1,0:T(8,128)(2,1)} %get-tuple-element.172), channel_id=1, source_target_pairs={{0,8},{8,0},{1,9},{9,1},{2,10},{10,2},{3,11},{11,3},{4,12},{12,4},... | collective-permute-start | bytes 12582920 | tf_op jit(solution)/shard_map/ppermute | solution.py:58
  271.0 17.3 %collective-permute-start.44 = (bf16[4,256,512]{2,1,0:T(8,128)(2,1)}, bf16[4,256,512]{2,1,0:T(8,128)(2,1)}, u32[]{:S(2)}, u32[]{:S(2)}) collective-permute-start(bf16[4,256,512]{2,1,0:T(8,128)(2,1)} %get-tuple-element.179), channel_id=1, source_target_pairs={{0,16},{1,17},{2,18},{3,19},{4,20},{5,21},{6,22},{7,23},{8,9},{9,8... | collective-permute-start | bytes 3145736 | tf_op jit(solution)/shard_map/ppermute | solution.py:55
  288.2 17.1 %collective-permute-start.46 = (bf16[4,256,512]{2,1,0:T(8,128)(2,1)}, bf16[4,256,512]{2,1,0:T(8,128)(2,1)S(1)}, u32[]{:S(2)}, u32[]{:S(2)}) collective-permute-start(bf16[4,256,512]{2,1,0:T(8,128)(2,1)} %get-tuple-element.183), channel_id=1, source_target_pairs={{0,16},{1,17},{2,18},{3,19},{4,20},{5,21},{6,22},{7,23},{8,9},{9,8... | collective-permute-start | bytes 3145736 | tf_op jit(solution)/shard_map/ppermute | solution.py:55
  305.4 15.1 %collective-permute-start.47 = (bf16[4,256,512]{2,1,0:T(8,128)(2,1)}, bf16[4,256,512]{2,1,0:T(8,128)(2,1)S(1)}, u32[]{:S(2)}, u32[]{:S(2)}) collective-permute-start(bf16[4,256,512]{2,1,0:T(8,128)(2,1)} %get-tuple-element.185), channel_id=1, source_target_pairs={{0,16},{1,17},{2,18},{3,19},{4,20},{5,21},{6,22},{7,23},{8,9},{9,8... | collective-permute-start | bytes 3145736 | tf_op jit(solution)/shard_map/ppermute | solution.py:55
  320.4 45.4 %collective-permute-start.50 = (bf16[16,1024,128]{2,1,0:T(8,128)(2,1)}, bf16[16,1024,128]{2,1,0:T(8,128)(2,1)}, u32[]{:S(2)}, u32[]{:S(2)}) collective-permute-start(bf16[16,1024,128]{2,1,0:T(8,128)(2,1)} %bitcast.241), channel_id=1, source_target_pairs={{0,8},{8,0},{1,9},{9,1},{2,10},{10,2},{3,11},{11,3},{4,12},{12,4},... | collective-permute-start | bytes 12582920 | tf_op jit(solution)/shard_map/ppermute | solution.py:58
  320.4 25.6 %collective-permute-start.48 = (bf16[4,256,512]{2,1,0:T(8,128)(2,1)S(1)}, bf16[4,256,512]{2,1,0:T(8,128)(2,1)}, u32[]{:S(2)}, u32[]{:S(2)}) collective-permute-start(bf16[4,256,512]{2,1,0:T(8,128)(2,1)S(1)} %copy-done.45), channel_id=1, source_target_pairs={{0,16},{1,17},{2,18},{3,19},{4,20},{5,21},{6,22},{7,23},{8,9},{9,8... | collective-permute-start | bytes 3145736 | tf_op jit(solution)/shard_map/ppermute | solution.py:55
  321.1 25.1 %collective-permute-start.49 = (bf16[4,256,512]{2,1,0:T(8,128)(2,1)S(1)}, bf16[4,256,512]{2,1,0:T(8,128)(2,1)}, u32[]{:S(2)}, u32[]{:S(2)}) collective-permute-start(bf16[4,256,512]{2,1,0:T(8,128)(2,1)S(1)} %add_convert_fusion.5), channel_id=1, source_target_pairs={{0,1},{1,0},{2,3},{3,2},{4,5},{5,4},{6,7},{7,6},{8,24},{9,25},{10,... | collective-permute-start | bytes 3145736 | tf_op jit(solution)/shard_map/ppermute | solution.py:55
  348.4 15.1 %collective-permute-start.52 = (bf16[4,256,512]{2,1,0:T(8,128)(2,1)}, bf16[4,256,512]{2,1,0:T(8,128)(2,1)}, u32[]{:S(2)}, u32[]{:S(2)}) collective-permute-start(bf16[4,256,512]{2,1,0:T(8,128)(2,1)} %add_convert_fusion.3), channel_id=1, source_target_pairs={{0,1},{1,0},{2,3},{3,2},{4,5},{5,4},{6,7},{7,6},{8,24},{9,25},{10,... | collective-permute-start | bytes 3145736 | tf_op jit(solution)/shard_map/ppermute | solution.py:55
  350.2 19.0 %collective-permute-start.51 = (bf16[2,256,512]{2,1,0:T(8,128)(2,1)}, bf16[2,256,512]{2,1,0:T(8,128)(2,1)S(1)}, u32[]{:S(2)}, u32[]{:S(2)}) collective-permute-start(bf16[2,256,512]{2,1,0:T(8,128)(2,1)} %get-tuple-element.196), channel_id=1, source_target_pairs={{0,2},{2,0},{4,6},{6,4},{1,3},{3,1},{5,7},{7,5},{8,10},{10,8},{12,... | collective-permute-start | bytes 1572872 | tf_op jit(solution)/shard_map/ppermute | solution.py:58
  369.9 14.9 %collective-permute-start.54 = (bf16[4,1024,128]{2,1,0:T(8,128)(2,1)S(1)}, bf16[4,1024,128]{2,1,0:T(8,128)(2,1)}, u32[]{:S(2)}, u32[]{:S(2)}) collective-permute-start(bf16[4,1024,128]{2,1,0:T(8,128)(2,1)S(1)} %get-tuple-element.207), channel_id=1, source_target_pairs={{0,16},{1,17},{2,18},{3,19},{4,20},{5,21},{6,22},{7,23},{8,9},{9,8... | collective-permute-start | bytes 3145736 | tf_op jit(solution)/shard_map/ppermute | solution.py:55
  370.6 13.9 %collective-permute-start.53 = (bf16[2,256,512]{2,1,0:T(8,128)(2,1)}, bf16[2,256,512]{2,1,0:T(8,128)(2,1)S(1)}, u32[]{:S(2)}, u32[]{:S(2)}) collective-permute-start(bf16[2,256,512]{2,1,0:T(8,128)(2,1)} %get-tuple-element.199), channel_id=1, source_target_pairs={{0,2},{2,0},{4,6},{6,4},{1,3},{3,1},{5,7},{7,5},{8,10},{10,8},{12,... | collective-permute-start | bytes 1572872 | tf_op jit(solution)/shard_map/ppermute | solution.py:58
  384.9 15.0 %collective-permute-start.55 = (bf16[4,1024,128]{2,1,0:T(8,128)(2,1)}, bf16[4,1024,128]{2,1,0:T(8,128)(2,1)S(1)}, u32[]{:S(2)}, u32[]{:S(2)}) collective-permute-start(bf16[4,1024,128]{2,1,0:T(8,128)(2,1)} %get-tuple-element.208), channel_id=1, source_target_pairs={{0,16},{1,17},{2,18},{3,19},{4,20},{5,21},{6,22},{7,23},{8,9},{9,8... | collective-permute-start | bytes 3145736 | tf_op jit(solution)/shard_map/ppermute | solution.py:55
  389.1 19.5 %collective-permute-start.59 = (bf16[8,400,128]{2,1,0:T(8,128)(2,1)S(1)}, bf16[8,400,128]{2,1,0:T(8,128)(2,1)S(1)}, u32[]{:S(2)}, u32[]{:S(2)}) collective-permute-start(bf16[8,400,128]{2,1,0:T(8,128)(2,1)S(1)} %get-tuple-element.279), channel_id=1, source_target_pairs={{0,16},{1,17},{2,18},{3,19},{4,20},{5,21},{6,22},{7,23},{8,9},{9,8... | collective-permute-start | bytes 2457608 | tf_op jit(solution)/shard_map/ppermute | solution.py:55
  389.8 45.0 %collective-permute-start.66 = (bf16[8,512,128]{2,1,0:T(8,128)(2,1)S(1)}, bf16[8,512,128]{2,1,0:T(8,128)(2,1)S(1)}, u32[]{:S(2)}, u32[]{:S(2)}) collective-permute-start(bf16[8,512,128]{2,1,0:T(8,128)(2,1)S(1)} %pad_maximum_fusion.7.r_1_.r_2_), channel_id=1, source_target_pairs={{0,8},{8,0},{1,9},{9,1},{2,10},{10,2},{3,11},{11,3},{4,12},{12,4},... | collective-permute-start | bytes 3145736 | tf_op jit(solution)/shard_map/ppermute | solution.py:58
  390.8 44.0 %collective-permute-start.67 = (bf16[8,512,128]{2,1,0:T(8,128)(2,1)}, bf16[8,512,128]{2,1,0:T(8,128)(2,1)S(1)}, u32[]{:S(2)}, u32[]{:S(2)}) collective-permute-start(bf16[8,512,128]{2,1,0:T(8,128)(2,1)} %collective-permute-done.42.r_3_.r_4_), channel_id=1, source_target_pairs={{0,8},{8,0},{1,9},{9,1},{2,10},{10,2},{3,11},{11,3},{4,12},{12,4},... | collective-permute-start | bytes 3145736 | tf_op jit(solution)/shard_map/ppermute | solution.py:58
  390.8 21.5 %collective-permute-start.56 = (bf16[1,256,512]{2,1,0:T(8,128)(2,1)}, bf16[1,256,512]{2,1,0:T(8,128)(2,1)}, u32[]{:S(2)}, u32[]{:S(2)}) collective-permute-start(bf16[1,256,512]{2,1,0:T(8,128)(2,1)} %add_convert_fusion.27), channel_id=1, source_target_pairs={{0,4},{2,6},{4,0},{6,2},{1,5},{3,7},{5,1},{7,3},{8,12},{10,14},{12... | collective-permute-start | bytes 786440 | tf_op jit(solution)/shard_map/ppermute | solution.py:58
  399.9 17.7 %collective-permute-start.57 = (bf16[1,256,512]{2,1,0:T(8,128)(2,1)S(1)}, bf16[1,256,512]{2,1,0:T(8,128)(2,1)}, u32[]{:S(2)}, u32[]{:S(2)}) collective-permute-start(bf16[1,256,512]{2,1,0:T(8,128)(2,1)S(1)} %add_convert_fusion.26), channel_id=1, source_target_pairs={{0,4},{2,6},{4,0},{6,2},{1,5},{3,7},{5,1},{7,3},{8,12},{10,14},{12... | collective-permute-start | bytes 786440 | tf_op jit(solution)/shard_map/ppermute | solution.py:58
  418.3 24.2 %collective-permute-start.65 = (bf16[4,1024,128]{2,1,0:T(8,128)(2,1)}, bf16[4,1024,128]{2,1,0:T(8,128)(2,1)}, u32[]{:S(2)}, u32[]{:S(2)}) collective-permute-start(bf16[4,1024,128]{2,1,0:T(8,128)(2,1)} %get-tuple-element.215), channel_id=1, source_target_pairs={{0,1},{1,0},{2,3},{3,2},{4,5},{5,4},{6,7},{7,6},{8,24},{9,25},{10,... | collective-permute-start | bytes 3145736 | tf_op jit(solution)/shard_map/ppermute | solution.py:55
  447.7 14.6 %collective-permute-start.72 = (bf16[2,1024,128]{2,1,0:T(8,128)(2,1)S(1)}, bf16[2,1024,128]{2,1,0:T(8,128)(2,1)S(1)}, u32[]{:S(2)}, u32[]{:S(2)}) collective-permute-start(bf16[2,1024,128]{2,1,0:T(8,128)(2,1)S(1)} %get-tuple-element.224), channel_id=1, source_target_pairs={{0,2},{2,0},{4,6},{6,4},{1,3},{3,1},{5,7},{7,5},{8,10},{10,8},{12,... | collective-permute-start | bytes 1572872 | tf_op jit(solution)/shard_map/ppermute | solution.py:58
  (111 other events, 1384.7 us)
